TPU v7x, 32 devices: a whole 2x2x4 slice. The times are simulated.
32 devices in a mesh: dp: 4 (over y, x), expert: 8 (over z, core).
Axes of the slice: x: 2, y: 2, z: 4, core: 2. Of those that a mesh axis runs over, the one named last changes fastest.
Arguments:
- tokens: bfloat16 [1024, 2048], P('expert'), may hold values from -4 to 4
- norm_gain: bfloat16 [2048], replicated, may hold values from 0.5 to 1.5
- routing_projection_matrix: bfloat16 [2048, 8], replicated, may hold values from -0.125 to 0.125
- experts: int32 [1024, 8], P('expert'), may hold values from 0 to 7, as said below
- replica_key: int32 [1024, 8], P('expert'), may hold values from 0 to 1048575
- slot_expert: int32 [16], replicated, may hold values from 0 to 7, as said below
- capacity: int32 [16], replicated, may hold values from 4 to 16, as said below
- slot_gate_up_weight: bfloat16 [16, 2048, 2, 1024], P('expert', None, None, 'dp'), may hold values from -0.125 to 0.125
- down_weight: bfloat16 [16, 1024, 2048], P('expert', 'dp'), may hold values from -0.1875 to 0.1875
Outputs:
- mixed: bfloat16 [1024, 2048], P('expert', 'dp')
Inputs may be any that keep to these rules, and one draw needn't show every extreme that they name: Each row names 8 different experts. `slot_expert`: every expert occupies at least one slot. `capacity`: for every j the capacities of slots 2 * j and 2 * j + 1 sum to at most 24, and to exactly 24 for some j.
All inputs are finite; a program needn't handle non-finite values.
Results may differ from a plain program's by a relative error of at most 0.012.
Values may be sent and summed in bfloat16 or wider, within the bound.
No kernel may reach another device: no remote copies, remote signals or barrier semaphores. Data moves between devices by JAX's collectives and lax.ppermute only.
A program may use at most 128 MiB of HBM per device.

v0:
```python
import jax
import jax.numpy as jnp
from jax import lax
from jax.sharding import PartitionSpec as P

CAPACITY_HIGH = 16


def assign_slots(experts, replica_key, slot_expert):
    flat_experts = experts.reshape(-1)
    holders = (flat_experts[:, None] == slot_expert[None, :]).astype(jnp.int32)
    copies = jnp.sum(holders, axis=1)
    earlier = jnp.cumsum(holders, axis=1) - holders
    wanted = replica_key.reshape(-1) % copies
    matched = holders * (earlier == wanted[:, None]).astype(jnp.int32)
    numbers = jnp.arange(slot_expert.shape[0], dtype=jnp.int32)
    return jnp.sum(matched * numbers[None, :], axis=1)


def expert_part(rows, gate_up_one, down_one):
    model_width = rows.shape[2]
    unit_count = gate_up_one.shape[2]
    flat_rows = rows.reshape(-1, model_width)
    gate_up_out = jnp.dot(
        flat_rows,
        gate_up_one.reshape(model_width, 2 * unit_count),
        preferred_element_type=jnp.float32,
    )
    activated = (jax.nn.silu(gate_up_out[:, :unit_count]) * gate_up_out[:, unit_count:]).astype(
        jnp.bfloat16
    )
    result = jnp.dot(activated, down_one, preferred_element_type=jnp.float32)
    result = lax.optimization_barrier(result.astype(jnp.bfloat16))
    return result.reshape(rows.shape)


def combine(returned, target, weight_kept, rows_here, pick_count):
    flat_rows = returned.reshape(-1, returned.shape[2])
    flat_rows = jnp.concatenate([flat_rows, jnp.zeros((1, flat_rows.shape[1]), flat_rows.dtype)])
    gathered = flat_rows[target].astype(jnp.float32).reshape(rows_here, pick_count, -1)
    return jnp.sum(weight_kept.reshape(rows_here, pick_count)[:, :, None] * gathered, axis=1)


def on_device(
    tokens,
    norm_gain,
    routing_projection_matrix,
    experts,
    replica_key,
    slot_expert,
    capacity,
    slot_gate_up_weight,
    down_weight,
):
    peer_count = lax.axis_size("expert")
    group_pos = lax.axis_index("dp")
    rows_here = tokens.shape[0]
    model_width = tokens.shape[1]
    pick_count = experts.shape[1]
    slot_count = slot_expert.shape[0]
    per_device = slot_count // peer_count
    quarter = model_width // lax.axis_size("dp")
    hidden = tokens.astype(jnp.float32)
    scale = lax.rsqrt(jnp.mean(hidden * hidden, axis=-1, keepdims=True) + 1e-06)
    normed = (hidden * scale * norm_gain.astype(jnp.float32)).astype(jnp.bfloat16)
    logits = jnp.dot(normed, routing_projection_matrix, preferred_element_type=jnp.float32)
    routing_logit_matrix = jax.nn.sigmoid(jnp.take_along_axis(logits, experts, axis=1)).reshape(-1)
    slot_ids = assign_slots(experts, replica_key, slot_expert)
    onehot = (slot_ids[:, None] == jnp.arange(slot_count, dtype=jnp.int32)[None, :]).astype(
        jnp.int32
    )
    position = jnp.sum((jnp.cumsum(onehot, axis=0) - onehot) * onehot, axis=1)
    kept_mask = position < jnp.sum(onehot * capacity[None, :], axis=1)
    slot_parity = jnp.arange(slot_count, dtype=jnp.int32) % per_device
    buffer_rows = per_device * CAPACITY_HIGH
    offsets = slot_parity * CAPACITY_HIGH
    second_start = CAPACITY_HIGH
    row_in = jnp.sum(onehot * offsets[None, :], axis=1) + position
    target = jnp.where(
        kept_mask, slot_ids // per_device * buffer_rows + row_in, peer_count * buffer_rows
    )
    source_rows = jnp.arange(rows_here * pick_count, dtype=jnp.int32) // pick_count
    outgoing = (
        jnp.zeros((peer_count * buffer_rows + 1, model_width), jnp.bfloat16)
        .at[target]
        .set(normed[source_rows])
    )
    outgoing = outgoing[:-1].reshape(peer_count, buffer_rows, model_width)
    incoming = lax.all_to_all(outgoing, "expert", split_axis=0, concat_axis=0, tiled=True)
    first_rows = incoming[:, :CAPACITY_HIGH]
    second_rows = lax.dynamic_slice_in_dim(incoming, second_start, CAPACITY_HIGH, 1)
    first_out = expert_part(first_rows, slot_gate_up_weight[0], down_weight[0])
    second_out = expert_part(second_rows, slot_gate_up_weight[1], down_weight[1])
    first_full = jnp.pad(first_out, ((0, 0), (0, buffer_rows - CAPACITY_HIGH), (0, 0)))
    clamped = jnp.minimum(second_start, buffer_rows - CAPACITY_HIGH)
    second_full = lax.dynamic_update_slice(jnp.zeros_like(first_full), second_out, (0, clamped, 0))
    row_index = jnp.arange(buffer_rows, dtype=jnp.int32)[None, :, None]
    partial_value = jnp.where(row_index < second_start, first_full, second_full)
    weight_kept = jnp.where(kept_mask, routing_logit_matrix, jnp.float32(0.0))
    returned = lax.all_to_all(partial_value, "expert", split_axis=0, concat_axis=0, tiled=True)
    mixture_full = combine(returned, target, weight_kept, rows_here, pick_count)
    mixture = lax.psum_scatter(
        mixture_full.astype(jnp.bfloat16), "dp", scatter_dimension=1, tiled=True
    ).astype(jnp.float32)
    residual = lax.dynamic_slice_in_dim(tokens, group_pos * quarter, quarter, 1).astype(jnp.float32)
    return (residual + mixture).astype(jnp.bfloat16)


def solution(mesh):
    in_specs = (
        P("expert", None),
        P(),
        P(),
        P("expert", None),
        P("expert", None),
        P(),
        P(),
        P("expert", None, None, "dp"),
        P("expert", "dp", None),
    )
    out_specs = P("expert", "dp")
    return jax.shard_map(
        on_device, mesh=mesh, in_specs=in_specs, out_specs=out_specs, check_vma=False
    )
```

profile of v0, /device:TPU:0, one launch (start us, length us, event | category | flops | bytes accessed | tf_op | source)
XLA Modules:
  0.0 153.6 jit_solution(7800581160735194050)
XLA Ops:
  6.6 0.8 copy.22
  7.4 0.1 eq.52
  7.5 0.7 convert_reduce_fusion
  8.2 0.7 compare_convert_fusion
  9.0 1.2 fusion.3
  10.2 0.7 convert_element_type.58
  10.9 0.8 copy.23
  11.7 0.1 reshape.239
  11.8 0.1 add_select_fusion
  11.9 0.1 reduce_window_sum.26
  12.0 0.7 fusion.15
  12.8 4.5 %reduce-window.6 = s32[16,8,128]{2,1,0:T(8,128)S(1)} reduce-window(s32[16,8,128]{2,1,0:T(8,128)S(1)} %fusion.23, s32[]{:T(128)} %constant.87.clone.1), window={size=1x1x128 pad=0_0x0_0x127_0}, to_apply=%region_3.4 | reduce-window | flops 2080768 | bytes 131076 | tf_op jit(solution)/shard_map/reduce-window
  17.3 0.1 slice.54
  17.4 0.1 copy.24
  17.5 0.1 copy.25
  17.6 0.1 broadcast_add_fusion
  17.7 0.8 select_reduce_fusion
  18.5 0.2 fusion.5
  18.7 20.3 %scatter_custom_fusion = bf16[257,2048]{1,0:T(8,128)(2,1)S(1)} fusion(s32[1024]{0:T(1024)S(1)} %bitcast.70, bf16[128,2048]{1,0:T(8,128)(2,1)S(1)} %fusion.5, s32[1024]{0:T(1024)S(1)} %broadcast_clamp_fusion.1, bf16[]{:T(256)} %constant.100.clone.1), kind=kCustom, calls=%fused_computation.6 | custom fusion | bytes 1052674 | tf_op jit(solution)/shard_map/scatter | solution.py:86
  39.0 1.1 slice.56
  40.1 6.3 %all-to-all-start = ((bf16[8,32,2048]{2,1,0:T(8,128)(2,1)}), bf16[8,32,2048]{2,1,0:T(8,128)(2,1)S(1)}, u32[]{:S(2)}, u32[]{:S(2)}) async-start(bf16[8,32,2048]{2,1,0:T(8,128)(2,1)} %bitcast.60), calls=%async_computation | async-start | bytes 2097152 | tf_op jit(solution)/shard_map/all_to_all | solution.py:89
  46.4 4.7 %fusion.27 = (bf16[1,2048,2,256]{3,2,1,0:T(2,128)(2,1)S(1)}, bf16[1,2048,2,256]{3,2,1,0:T(2,128)(2,1)S(1)}) fusion(bf16[2,2048,2,256]{3,2,1,0:T(2,128)(2,1)} %param.16), kind=kLoop, calls=%fused_computation.69 | loop fusion | bytes 8388608 | tf_op jit(solution)/shard_map/slice | solution.py:92
  51.1 0.5 copy.31
  51.6 1.9 %copy.32 = bf16[256,8,2,256]{3,1,2,0:T(8,128)(2,1)} copy(bf16[256,8,2,256]{3,2,1,0:T(2,128)(2,1)S(1)} %bitcast.57) | data formatting | bytes 4194304
  53.5 19.5 %all-to-all-done = bf16[8,32,2048]{2,1,0:T(8,128)(2,1)S(1)} async-done(((bf16[8,32,2048]{2,1,0:T(8,128)(2,1)}), bf16[8,32,2048]{2,1,0:T(8,128)(2,1)S(1)}, u32[]{:S(2)}, u32[]{:S(2)}) %all-to-all-start) | async-done | bytes 1048608 | tf_op jit(solution)/shard_map/all_to_all | solution.py:89
  73.0 0.1 fusion.28
  73.1 1.5 copy-done.1
  74.6 0.4 fusion.31
  75.0 0.2 copy-done.6
  75.2 0.3 convolution_convert_fusion
  75.6 0.4 fusion.30
  76.0 0.3 convolution_convert_fusion.1
  76.4 1.3 pad_select_fusion
  77.6 3.6 %all-to-all-start.1 = ((bf16[8,32,2048]{2,1,0:T(8,128)(2,1)}), bf16[8,32,2048]{2,1,0:T(8,128)(2,1)S(1)}, u32[]{:S(2)}, u32[]{:S(2)}) async-start(bf16[8,32,2048]{2,1,0:T(8,128)(2,1)} %pad_select_fusion), calls=%async_computation.1 | async-start | bytes 2097152 | tf_op jit(solution)/shard_map/all_to_all | solution.py:100
  81.3 0.1 lt.87
  81.4 0.1 copy.26
  81.5 0.1 reshape.265
  81.6 0.1 copy.28
  81.6 0.3 fusion.29
  81.9 4.6 %gather_fusion.1 = f32[1024]{0:T(1024)S(1)} fusion(f32[128,8]{0,1:T(8,128)S(1)} %fusion.29, s32[1024]{0:T(1024)S(1)} %reshape.265), kind=kCustom, calls=%fused_computation.2 | custom fusion | bytes 16384 | tf_op jit(solution)/shard_map/jit(take_along_axis)/gather | solution.py:67
  86.5 0.1 reshape.268
  86.7 0.1 copy.29
  86.8 20.9 %all-to-all-done.1 = bf16[8,32,2048]{2,1,0:T(8,128)(2,1)S(1)} async-done(((bf16[8,32,2048]{2,1,0:T(8,128)(2,1)}), bf16[8,32,2048]{2,1,0:T(8,128)(2,1)S(1)}, u32[]{:S(2)}, u32[]{:S(2)}) %all-to-all-start.1) | async-done | bytes 1048608 | tf_op jit(solution)/shard_map/all_to_all | solution.py:100
  107.7 0.1 concatenate.3
  107.8 6.0 %gather_fusion = bf16[1024,2048]{1,0:T(8,128)(2,1)} fusion(bf16[257,2048]{1,0:T(8,128)(2,1)S(1)} %concatenate.3, s32[1024]{0:T(1024)S(1)} %broadcast_clamp_fusion), kind=kCustom, calls=%fused_computation.1 | custom fusion | bytes 8392704 | tf_op jit(solution)/shard_map/gather | solution.py:40
  113.9 7.3 %fusion = bf16[128,2048]{1,0:T(8,128)(2,1)} fusion(bf16[1024,2048]{1,0:T(8,128)(2,1)} %gather_fusion, f32[128,8]{1,0:T(8,128)S(1)} %copy.29), kind=kLoop, calls=%fused_computation.5 | loop fusion | flops 6029312 | bytes 4722688 | tf_op jit(solution)/shard_map/reduce_sum | solution.py:41
  121.2 23.8 %reduce-scatter.2.cloned.1.call-done = bf16[128,512]{1,0:T(8,128)(2,1)} async-done(((bf16[128,2048]{1,0:T(8,128)(2,1)}), bf16[128,512]{1,0:T(8,128)(2,1)}) %reduce-scatter.2.cloned.1.call-update) | async-done | bytes 131088 | tf_op jit(solution)/shard_map/reduce_scatter | solution.py:102
  145.1 1.7 %add_convert_fusion = bf16[128,512]{1,0:T(8,128)(2,1)} fusion(bf16[128,512]{1,0:T(8,128)(2,1)} %reduce-scatter.2.cloned.1.call-done, bf16[128,2048]{1,0:T(8,128)(2,1)} %param.9, s32[]{:T(128)S(6)} %select_n.105), kind=kLoop, calls=%fused_computation.21 | loop fusion | flops 262144 | bytes 393220 | tf_op jit(solution)/shard_map/convert_element_type | solution.py:106
  (29 shorter events, 0.3 us)
Async XLA Ops:
  6.5 75.1 %copy-start = (bf16[2048,8]{0,1:T(8,128)(2,1)S(1)}, bf16[2048,8]{0,1:T(8,128)(2,1)}, u32[]{:S(2)}) copy-start(bf16[2048,8]{0,1:T(8,128)(2,1)} %param.11) | copy-start | bytes 98308
  6.5 11.9 %copy-start.2 = (bf16[128,2048]{1,0:T(8,128)(2,1)S(1)}, bf16[128,2048]{1,0:T(8,128)(2,1)}, u32[]{:S(2)}) copy-start(bf16[128,2048]{1,0:T(8,128)(2,1)} %param.9) | copy-start | bytes 1572868
  18.7 21.4 %copy-start.3 = (bf16[128,2048]{1,0:T(8,128)(2,1)}, bf16[128,2048]{1,0:T(8,128)(2,1)S(1)}, u32[]{:S(2)}) copy-start(bf16[128,2048]{1,0:T(8,128)(2,1)S(1)} %fusion.5) | copy-start | bytes 1572868
  40.1 32.9 %all-to-all-start = ((bf16[8,32,2048]{2,1,0:T(8,128)(2,1)}), bf16[8,32,2048]{2,1,0:T(8,128)(2,1)S(1)}, u32[]{:S(2)}, u32[]{:S(2)}) async-start(bf16[8,32,2048]{2,1,0:T(8,128)(2,1)} %bitcast.60), calls=%async_computation | async-start | bytes 2097152 | tf_op jit(solution)/shard_map/all_to_all | solution.py:89
  73.0 1.6 %copy-start.1 = (bf16[256,8,2,256]{3,1,2,0:T(8,128)(2,1)S(1)}, bf16[256,8,2,256]{3,1,2,0:T(8,128)(2,1)}, u32[]{:S(2)}) copy-start(bf16[256,8,2,256]{3,1,2,0:T(8,128)(2,1)} %copy.32) | copy-start | bytes 6291460
  73.0 2.2 %copy-start.6 = (bf16[2,256,2048]{2,1,0:T(8,128)(2,1)S(1)}, bf16[2,256,2048]{2,1,0:T(8,128)(2,1)}, u32[]{:S(2)}) copy-start(bf16[2,256,2048]{2,1,0:T(8,128)(2,1)} %param.17) | copy-start | bytes 6291460
  76.3 5.0 %copy-start.5 = (s32[128,8]{0,1:T(8,128)S(1)}, s32[128,8]{0,1:T(8,128)}, u32[]{:S(2)}) copy-start(s32[128,8]{0,1:T(8,128)} %param.12) | copy-start | bytes 12292
  76.4 5.3 %copy-start.4 = (bf16[128,2048]{1,0:T(8,128)(2,1)S(1)}, bf16[128,2048]{1,0:T(8,128)(2,1)}, u32[]{:S(2)}) copy-start(bf16[128,2048]{1,0:T(8,128)(2,1)} %copy-done.3) | copy-start | bytes 1572868
  77.6 30.1 %all-to-all-start.1 = ((bf16[8,32,2048]{2,1,0:T(8,128)(2,1)}), bf16[8,32,2048]{2,1,0:T(8,128)(2,1)S(1)}, u32[]{:S(2)}, u32[]{:S(2)}) async-start(bf16[8,32,2048]{2,1,0:T(8,128)(2,1)} %pad_select_fusion), calls=%async_computation.1 | async-start | bytes 2097152 | tf_op jit(solution)/shard_map/all_to_all | solution.py:100
  81.2 63.8 %reduce-scatter.2.cloned.1.call-start = ((), (), s32[]{:S(2)}) async-start(), calls=%async_computation.3 | async-start | bytes 655360 | tf_op jit(solution)/shard_map/reduce_scatter | solution.py:102
Sparse Core Ops, SparseCore 0:
  121.3 23.6 reduce-scatter.1
where the time goes:
time: 154 us
  waiting for transfers between devices  64.3 us (42%)
  local copies, waits for them, and re-layouts  43.6 us (28%)
  other arithmetic  20.3 us (13%)
  between operations  13.6 us (9%)
  starting transfers between devices  9.92 us (6%)
  matrix products  1.81 us (1%)
    reduce_scatter x1, waiting for transfers between devices, on_device(): lax.psum_scatter(mixture_full.astype(jnp.bfloat16), 'dp', scatter_dimensi...  23.8 us
    all_to_all x1, waiting for transfers between devices, on_device(): lax.all_to_all(partial_value, 'expert', split_axis=0, concat_axis=0, tile...  20.9 us
    scatter x1, local copies, waits for them, and re-layouts, on_device(): outgoing = jnp.zeros((peer_count * buffer_rows + 1, model_width), jnp.bfl...  20.3 us
    all_to_all x1, waiting for transfers between devices, on_device(): lax.all_to_all(outgoing, 'expert', split_axis=0, concat_axis=0, tiled=True)  19.5 us
    reduce_sum x1, other arithmetic, combine(): jnp.sum(weight_kept.reshape(rows_here, pick_count)[:, :, None] * gathered...  7.32 us
    all_to_all x1, starting transfers between devices, on_device(): lax.all_to_all(outgoing, 'expert', split_axis=0, concat_axis=0, tiled=True)  6.33 us
    gather x1, local copies, waits for them, and re-layouts, combine(): flat_rows[target].astype(jnp.float32).reshape(rows_here, pick_count, -1)  6.02 us
    unnamed x18, local copies, waits for them, and re-layouts  5.71 us
  transfers between devices with their start and end apart: 3, of which 3 were waited for; matrix products, arithmetic and copies ran while one was open for 8% of the time, Pallas kernels for 0%

commit v1 on v0

v1 whole, which is shorter than its diff:
```python
import functools

import jax
import jax.numpy as jnp
from jax import lax
from jax.experimental import pallas as pl
from jax.experimental.pallas import tpu as pltpu
from jax.sharding import PartitionSpec as P

CAP_DEV = 24


def to_column(row):
    n = row.shape[1]
    eye = lax.broadcasted_iota(jnp.int32, (n, n), 0) == lax.broadcasted_iota(
        jnp.int32, (n, n), 1
    )
    wide = jnp.where(eye, jnp.broadcast_to(row, (n, n)).astype(jnp.float32), 0.0)
    return jnp.sum(wide, axis=1, keepdims=True)


def place_rows(experts_t, keys_t, slot_row, cap_row, per_device):
    slots = slot_row.shape[1]
    picks, rows = experts_t.shape
    slot_f = slot_row.astype(jnp.float32)
    cap_f = cap_row.astype(jnp.float32)
    slot_col = to_column(slot_row)
    cap_col = to_column(cap_row)
    here = lax.broadcasted_iota(jnp.int32, (slots, slots), 0)
    other = lax.broadcasted_iota(jnp.int32, (slots, slots), 1)
    same = jnp.where(slot_f == slot_col, 1.0, 0.0)
    copies = jnp.sum(same, axis=1, keepdims=True)
    earlier = other < here
    place = jnp.sum(jnp.where(earlier, same, 0.0), axis=1, keepdims=True)
    together = (here // per_device) == (other // per_device)
    offset = jnp.sum(jnp.where(earlier & together, cap_f, 0.0), axis=1, keepdims=True)
    hit = jnp.zeros((slots, rows), jnp.float32)
    key = jnp.zeros((slots, rows), jnp.float32)
    experts_f = experts_t.astype(jnp.float32)
    keys_f = keys_t.astype(jnp.float32)
    for k in range(picks):
        match = experts_f[k : k + 1, :] == slot_col
        hit = jnp.where(match, 1.0, hit)
        key = jnp.where(match, keys_f[k : k + 1, :], key)
    rest = key - jnp.floor(key * (1.0 / copies)) * copies
    rest = jnp.where(rest < 0.0, rest + copies, rest)
    rest = jnp.where(rest >= copies, rest - copies, rest)
    chosen = (hit > 0.0) & (rest == place)
    before = lax.broadcasted_iota(jnp.int32, (rows, rows), 0) < lax.broadcasted_iota(
        jnp.int32, (rows, rows), 1
    )
    position = jnp.dot(
        jnp.where(chosen, 1.0, 0.0).astype(jnp.bfloat16),
        jnp.where(before, 1.0, 0.0).astype(jnp.bfloat16),
        preferred_element_type=jnp.float32,
    )
    return jnp.where(chosen & (position < cap_col), position + offset, -1.0)


def row_scale(hidden):
    return lax.rsqrt(jnp.mean(hidden * hidden, axis=-1, keepdims=True) + 1e-06)


def dispatch_kernel(
    per_device,
    tokens_ref,
    gain_ref,
    experts_ref,
    keys_ref,
    slot_ref,
    cap_ref,
    out_ref,
    local_ref,
):
    slots = slot_ref.shape[1]
    rows = tokens_ref.shape[0]
    width = out_ref.shape[1]
    hidden = tokens_ref[...].astype(jnp.float32)
    scale = row_scale(hidden)
    start = pl.multiple_of(lax.axis_index("dp") * width, width)
    part = tokens_ref[:, pl.ds(start, width)].astype(jnp.float32)
    gain = gain_ref[:, pl.ds(start, width)].astype(jnp.float32)
    normed = (part * scale * gain).astype(jnp.bfloat16)
    local = place_rows(
        experts_ref[...], keys_ref[...], slot_ref[...], cap_ref[...], per_device
    )
    local_ref[...] = local
    number = lax.broadcasted_iota(jnp.int32, (CAP_DEV, rows), 0).astype(jnp.float32)
    blocks = []
    for device in range(slots // per_device):
        block = jnp.zeros((CAP_DEV, rows), jnp.float32)
        for slot in range(device * per_device, (device + 1) * per_device):
            block = jnp.where(local[slot : slot + 1, :] == number, 1.0, block)
        blocks.append(block)
    pick = jnp.concatenate(blocks, axis=0).astype(jnp.bfloat16)
    out_ref[...] = jnp.dot(pick, normed, preferred_element_type=jnp.float32).astype(
        jnp.bfloat16
    )


def weight_kernel(
    per_device, tokens_ref, gain_ref, route_ref, slot_ref, local_ref, out_ref
):
    slots = slot_ref.shape[1]
    rows = tokens_ref.shape[0]
    hidden = tokens_ref[...].astype(jnp.float32)
    normed = (hidden * row_scale(hidden) * gain_ref[...].astype(jnp.float32)).astype(
        jnp.bfloat16
    )
    logits = lax.dot_general(
        route_ref[...],
        normed,
        (((1,), (1,)), ((), ())),
        preferred_element_type=jnp.float32,
    )
    score = 1.0 / (1.0 + jnp.exp(-logits))
    slot_col = to_column(slot_ref[...])
    by_slot = jnp.zeros((slots, rows), jnp.float32)
    for expert in range(route_ref.shape[0]):
        by_slot = jnp.where(slot_col == expert, score[expert : expert + 1, :], by_slot)
    local = local_ref[...]
    number = lax.broadcasted_iota(jnp.int32, (CAP_DEV, rows), 0).astype(jnp.float32)
    blocks = []
    for device in range(slots // per_device):
        block = jnp.zeros((CAP_DEV, rows), jnp.float32)
        for slot in range(device * per_device, (device + 1) * per_device):
            block = jnp.where(
                local[slot : slot + 1, :] == number, by_slot[slot : slot + 1, :], block
            )
        blocks.append(block)
    out_ref[...] = jnp.concatenate(blocks, axis=0).astype(jnp.bfloat16)


def on_device(
    tokens,
    norm_gain,
    routing_projection_matrix,
    experts,
    replica_key,
    slot_expert,
    capacity,
    slot_gate_up_weight,
    down_weight,
):
    peers = lax.axis_size("expert")
    groups = lax.axis_size("dp")
    group = lax.axis_index("dp")
    rows, width = tokens.shape
    slots = slot_expert.shape[0]
    per_device = slots // peers
    units = slot_gate_up_weight.shape[3]
    quarter = width // groups
    total = peers * CAP_DEV

    gain = norm_gain.reshape(1, width)
    slot_row = slot_expert.reshape(1, slots)
    cap_row = capacity.reshape(1, slots)
    outgoing, local = pl.pallas_call(
        functools.partial(dispatch_kernel, per_device),
        out_shape=(
            jax.ShapeDtypeStruct((total, quarter), jnp.bfloat16),
            jax.ShapeDtypeStruct((slots, rows), jnp.float32),
        ),
        name="dispatch",
    )(tokens, gain, experts.T, replica_key.T, slot_row, cap_row)
    weights = pl.pallas_call(
        functools.partial(weight_kernel, per_device),
        out_shape=jax.ShapeDtypeStruct((total, rows), jnp.bfloat16),
        name="combine_weights",
    )(tokens, gain, routing_projection_matrix.T, slot_row, local)

    def swap(value, step):
        return lax.ppermute(value, "dp", [(i, i ^ step) for i in range(groups)])

    def exchange(value):
        return lax.all_to_all(
            value.reshape(peers, CAP_DEV, quarter), "expert", 0, 0, tiled=True
        ).reshape(total, quarter)

    own = exchange(outgoing)
    gate_up = None
    for step in range(groups):
        rows_in = own if step == 0 else swap(own, step)
        start = (group ^ step) * quarter
        part = lax.dynamic_slice_in_dim(slot_gate_up_weight, start, quarter, 1)
        part = part.transpose(1, 0, 2, 3).reshape(quarter, per_device * 2 * units)
        term = jnp.dot(rows_in, part, preferred_element_type=jnp.float32)
        gate_up = term if gate_up is None else gate_up + term

    expert = lax.axis_index("expert")
    caps = lax.dynamic_slice_in_dim(capacity, expert * per_device, per_device)
    ends = jnp.cumsum(caps)
    number = lax.broadcasted_iota(jnp.int32, (peers, CAP_DEV, 1), 1).reshape(total, 1)
    pieces = []
    for slot in range(per_device):
        gate = gate_up[:, 2 * slot * units : (2 * slot + 1) * units]
        up = gate_up[:, (2 * slot + 1) * units : (2 * slot + 2) * units]
        mine = (number >= ends[slot] - caps[slot]) & (number < ends[slot])
        pieces.append(jnp.where(mine, jax.nn.silu(gate) * up, 0.0).astype(jnp.bfloat16))
    activated = jnp.concatenate(pieces, axis=1)
    down = down_weight.reshape(per_device * units, width)
    summed = None
    for step in reversed(range(groups)):
        start = (group ^ step) * quarter
        part = lax.dynamic_slice_in_dim(down, start, quarter, 1)
        term = jnp.dot(activated, part, preferred_element_type=jnp.float32)
        term = term.astype(jnp.bfloat16)
        if step:
            term = swap(term, step)
        term = term.astype(jnp.float32)
        summed = term if summed is None else summed + term
    returned = exchange(summed.astype(jnp.bfloat16))
    mixture = lax.dot_general(
        weights, returned, (((0,), (0,)), ((), ())), preferred_element_type=jnp.float32
    )
    residual = lax.dynamic_slice_in_dim(tokens, group * quarter, quarter, 1)
    return (residual.astype(jnp.float32) + mixture).astype(jnp.bfloat16)


def solution(mesh):
    in_specs = (
        P("expert", None),
        P(),
        P(),
        P("expert", None),
        P("expert", None),
        P(),
        P(),
        P("expert", None, None, "dp"),
        P("expert", "dp", None),
    )
    return jax.shard_map(
        on_device,
        mesh=mesh,
        in_specs=in_specs,
        out_specs=P("expert", "dp"),
        check_vma=False,
    )
```

time: 154 us -> 76.5 us (0.50)
  waiting for transfers between devices: 64.3 us -> 21.3 us
  local copies, waits for them, and re-layouts: 43.6 us -> 21.4 us
  other arithmetic: 20.3 us -> 1.57 us
  between operations: 13.6 us -> 2.75 us
  starting transfers between devices: 9.92 us -> 17.5 us
  matrix products: 1.81 us -> 6.9 us
  Pallas kernels: 0 us -> 4.39 us
    all_to_all x2, waiting for transfers between devices: 40.4 us -> 6.2 us  [exchange(): lax.all_to_all(value.reshape(peers, CAP_DEV, quarter), 'expert', 0, 0, ti...]
    reduce_scatter x1 -> x0, waiting for transfers between devices: 23.8 us -> none  [on_device(): lax.psum_scatter(mixture_full.astype(jnp.bfloat16), 'dp', scatter_dimensi...]
    scatter x1 -> x0, local copies, waits for them, and re-layouts: 20.3 us -> none  [on_device(): outgoing = jnp.zeros((peer_count * buffer_rows + 1, model_width), jnp.bfl...]
    ppermute x0 -> x6, waiting for transfers between devices: none -> 15.1 us  [swap(): return lax.ppermute(value, 'dp', [(i, i ^ step) for i in range(groups)])]
    gather x6 -> x0, local copies, waits for them, and re-layouts: 11 us -> none  [the longest x1 6.02 us: combine(): flat_rows[target].astype(jnp.float32).reshape(rows_here, pick_count, -1)]
    reduce_sum x5 -> x0, other arithmetic: 10.8 us -> none  [the longest x1 7.32 us: combine(): jnp.sum(weight_kept.reshape(rows_here, pick_count)[:, :, None] * gathered...]
    ppermute x0 -> x6, starting transfers between devices: none -> 7.11 us  [swap(): return lax.ppermute(value, 'dp', [(i, i ^ step) for i in range(groups)])]
    unnamed x18 -> x12, local copies, waits for them, and re-layouts: 5.71 us -> 12.3 us
  transfers between devices with their start and end apart: 3 -> 8, of which waited for: 3 -> 6; matrix products, arithmetic and copies ran while one was open for 8% -> 32% of each run, Pallas kernels for 0% -> 3%
where the time goes in v1:
time: 76.5 us; the launch traced here: 75.9 us
  local copies, waits for them, and re-layouts  21.4 us (28%)
  waiting for transfers between devices  21.3 us (28%)
  starting transfers between devices  17.5 us (23%)
  matrix products  6.9 us (9%)
  Pallas kernels  4.39 us (6%)
  between operations  2.75 us (4%)
  other arithmetic  1.57 us (2%)
    ppermute x6, waiting for transfers between devices, swap(): return lax.ppermute(value, 'dp', [(i, i ^ step) for i in range(groups)])  15.1 us
    unnamed x12, local copies, waits for them, and re-layouts  12.3 us
    all_to_all x2, starting transfers between devices, exchange(): lax.all_to_all(value.reshape(peers, CAP_DEV, quarter), 'expert', 0, 0, ti...  10.4 us
    ppermute x6, starting transfers between devices, swap(): return lax.ppermute(value, 'dp', [(i, i ^ step) for i in range(groups)])  7.11 us
    all_to_all x2, waiting for transfers between devices, exchange(): lax.all_to_all(value.reshape(peers, CAP_DEV, quarter), 'expert', 0, 0, ti...  6.2 us
    dynamic_slice x1, local copies, waits for them, and re-layouts, on_device(): part = lax.dynamic_slice_in_dim(slot_gate_up_weight, start, quarter, 1)  5.42 us
    dot_general x4, matrix products, on_device(): term = jnp.dot(rows_in, part, preferred_element_type=jnp.float32)  3.3 us
    pallas_call x1, Pallas kernels, on_device(): pl.pallas_call(functools.partial(dispatch_kernel, per_device), out_shape=...  2.24 us
  transfers between devices with their start and end apart: 8, of which 6 were waited for; matrix products, arithmetic and copies ran while one was open for 32% of the time, Pallas kernels for 3%

profile of v1, /device:TPU:0, one launch (start us, length us, event | category | flops | bytes accessed | tf_op | source)
XLA Modules:
  0.0 75.9 jit_solution(4159086364246309093)
XLA Ops:
  0.0 0.0 copy-start
  0.0 1.4 %reshape.87.gain_ref = bf16[1,2048]{1,0:T(2,128)(2,1)} reshape(bf16[2048]{0:T(1024)(128)(2,1)} %param.10) | data formatting | bytes 8192 | tf_op jit(solution)/shard_map/reshape | solution.py:155
  1.4 2.2 %dispatch.1 = (bf16[192,512]{1,0:T(8,128)(2,1)}, f32[16,128]{1,0:T(8,128)}) custom-call(bf16[128,2048]{1,0:T(8,128)(2,1)} %tokens_ref.3, bf16[1,2048]{1,0:T(2,128)(2,1)} %reshape.87.gain_ref, s32[8,128]{1,0:T(8,128)} %bitcast.57, s32[8,128]{1,0:T(8,128)} %bitcast.58, s32[1,16]{1,0:T(1,128)} %bitcast.59, s32[1,16]{1,0:T(1,128)} %bitcast.61), custom_call_target="tpu_custom_call" | custom-call | tf_op jit(solution)/shard_map/dispatch/pallas_call | solution.py:158
  3.7 6.3 %all-to-all-start = ((bf16[8,24,512]{2,1,0:T(8,128)(2,1)}), bf16[8,24,512]{2,1,0:T(8,128)(2,1)S(1)}, u32[]{:S(2)}, u32[]{:S(2)}) async-start(bf16[8,24,512]{2,1,0:T(8,128)(2,1)} %bitcast.55), calls=%async_computation | async-start | bytes 393216 | tf_op jit(solution)/shard_map/all_to_all | solution.py:176
  10.0 0.7 dynamic-slice_bitcast_fusion
  10.7 0.2 reduce-window.4
  10.9 5.4 %constant_dynamic-slice_fusion.1 = (bf16[2,512,2,256]{3,2,1,0:T(2,128)(2,1)}, bf16[2,512,2,256]{3,2,1,0:T(2,128)(2,1)}, bf16[2,512,2,256]{3,2,1,0:T(2,128)(2,1)}, bf16[2,512,2,256]{3,2,1,0:T(2,128)(2,1)S(1)}) fusion(bf16[2,2048,2,256]{3,2,1,0:T(2,128)(2,1)} %param.16, s32[]{:T(128)S(6)} %select_n.30, s32[]{:T(128)S(6)} %select_n.29, s32[]{:T(128)S(6)} %select_n.27, ...), kind=kLoop, calls=%fused_computation.33 | loop fusion | bytes 8388624 | tf_op jit(solution)/shard_map/dynamic_slice | solution.py:185
  16.3 0.6 fusion.20
  17.0 0.0 copy-done.3
  17.0 0.1 dynamic_slice.31
  17.1 3.7 %copy.14 = bf16[2,512,2,256]{1,3,2,0:T(8,128)(2,1)} copy(bf16[2,512,2,256]{3,2,1,0:T(2,128)(2,1)} %get-tuple-element.11) | data formatting | bytes 2097152
  20.7 3.7 %copy.15 = bf16[2,512,2,256]{1,3,2,0:T(8,128)(2,1)} copy(bf16[2,512,2,256]{3,2,1,0:T(2,128)(2,1)} %get-tuple-element.10) | data formatting | bytes 2097152
  24.4 2.5 %copy.17 = bf16[2,512,2,256]{1,3,2,0:T(8,128)(2,1)} copy(bf16[2,512,2,256]{3,2,1,0:T(2,128)(2,1)S(1)} %get-tuple-element.12) | data formatting | bytes 2097152
  26.9 2.4 %copy.16 = bf16[2,512,2,256]{1,3,2,0:T(8,128)(2,1)S(1)} copy(bf16[2,512,2,256]{3,2,1,0:T(2,128)(2,1)} %get-tuple-element.9) | data formatting | bytes 2097152
  29.3 0.7 fusion.19
  31.2 0.6 fusion.11
  31.8 0.1 and.25
  33.3 0.7 fusion.12
  34.0 0.1 and.27
  34.0 0.0 all-to-all-done
  34.1 0.0 copy-start.2
  34.1 1.6 %collective-permute-start = (bf16[192,512]{1,0:T(8,128)(2,1)S(1)}, bf16[192,512]{1,0:T(8,128)(2,1)S(1)}, u32[]{:S(2)}, u32[]{:S(2)}) collective-permute-start(bf16[192,512]{1,0:T(8,128)(2,1)S(1)} %bitcast.51), channel_id=1, source_target_pairs={{0,8},{8,0},{16,24},{24,16},{1,9},{9,1},{17,25},{25,17},{2,10},{10... | collective-permute-start | bytes 589832 | tf_op jit(solution)/shard_map/ppermute | solution.py:173
  35.6 1.5 %collective-permute-start.2 = (bf16[192,512]{1,0:T(8,128)(2,1)S(1)}, bf16[192,512]{1,0:T(8,128)(2,1)S(1)}, u32[]{:S(2)}, u32[]{:S(2)}) collective-permute-start(bf16[192,512]{1,0:T(8,128)(2,1)S(1)} %bitcast.52), channel_id=1, source_target_pairs={{0,24},{8,16},{16,8},{24,0},{1,25},{9,17},{17,9},{25,1},{2,26},{10... | collective-permute-start | bytes 589832 | tf_op jit(solution)/shard_map/ppermute | solution.py:173
  37.1 0.5 collective-permute-start.1
  37.6 1.8 %fusion.21 = f32[192,1024]{1,0:T(8,128)S(1)} fusion(bf16[192,512]{1,0:T(8,128)(2,1)S(1)} %bitcast.54, bf16[512,1024]{0,1:T(8,128)(2,1)} %bitcast.48), kind=kOutput, calls=%fused_computation.38 | convolution fusion | flops 201326592 | bytes 2031616 | tf_op jit(solution)/shard_map/dot_general | solution.py:187
  39.4 2.4 %collective-permute-done = bf16[192,512]{1,0:T(8,128)(2,1)S(1)} collective-permute-done((bf16[192,512]{1,0:T(8,128)(2,1)S(1)}, bf16[192,512]{1,0:T(8,128)(2,1)S(1)}, u32[]{:S(2)}, u32[]{:S(2)}) %collective-permute-start) | collective-permute-done | bytes 196640 | tf_op jit(solution)/shard_map/ppermute | solution.py:173
  41.8 0.0 copy-done.2
  41.8 0.5 convolution_add_fusion.1
  42.3 4.4 %collective-permute-done.2 = bf16[192,512]{1,0:T(8,128)(2,1)S(1)} collective-permute-done((bf16[192,512]{1,0:T(8,128)(2,1)S(1)}, bf16[192,512]{1,0:T(8,128)(2,1)S(1)}, u32[]{:S(2)}, u32[]{:S(2)}) %collective-permute-start.2) | collective-permute-done | bytes 196640 | tf_op jit(solution)/shard_map/ppermute | solution.py:173
  46.7 0.0 copy-done.1
  46.7 0.5 fusion.22
  47.2 0.9 %collective-permute-done.1 = bf16[192,512]{1,0:T(8,128)(2,1)S(1)} collective-permute-done((bf16[192,512]{1,0:T(8,128)(2,1)S(1)}, bf16[192,512]{1,0:T(8,128)(2,1)S(1)}, u32[]{:S(2)}, u32[]{:S(2)}) %collective-permute-start.1) | collective-permute-done | bytes 196640 | tf_op jit(solution)/shard_map/ppermute | solution.py:173
  48.1 0.5 fusion
  48.6 0.1 fusion.10
  48.7 0.3 convolution_convert_fusion.3
  49.0 0.3 convolution_convert_fusion.2
  49.3 0.3 convolution_convert_fusion.1
  49.6 1.5 %collective-permute-start.3 = (bf16[192,512]{1,0:T(8,128)(2,1)S(1)}, bf16[192,512]{1,0:T(8,128)(2,1)S(1)}, u32[]{:S(2)}, u32[]{:S(2)}) collective-permute-start(bf16[192,512]{1,0:T(8,128)(2,1)S(1)} %convolution_convert_fusion.3), channel_id=1, source_target_pairs={{0,24},{8,16},{16,8},{24,0},{1,25},{9,17},{17,9},{25,1},{2,26},{10... | collective-permute-start | bytes 589832 | tf_op jit(solution)/shard_map/ppermute | solution.py:173
  51.1 1.5 %collective-permute-start.4 = (bf16[192,512]{1,0:T(8,128)(2,1)S(1)}, bf16[192,512]{1,0:T(8,128)(2,1)S(1)}, u32[]{:S(2)}, u32[]{:S(2)}) collective-permute-start(bf16[192,512]{1,0:T(8,128)(2,1)S(1)} %convolution_convert_fusion.2), channel_id=1, source_target_pairs={{0,16},{8,24},{16,0},{24,8},{1,17},{9,25},{17,1},{25,9},{2,18},{10... | collective-permute-start | bytes 589832 | tf_op jit(solution)/shard_map/ppermute | solution.py:173
  52.6 0.6 collective-permute-start.5
  53.2 5.3 %collective-permute-done.3 = bf16[192,512]{1,0:T(8,128)(2,1)S(1)} collective-permute-done((bf16[192,512]{1,0:T(8,128)(2,1)S(1)}, bf16[192,512]{1,0:T(8,128)(2,1)S(1)}, u32[]{:S(2)}, u32[]{:S(2)}) %collective-permute-start.3) | collective-permute-done | bytes 196640 | tf_op jit(solution)/shard_map/ppermute | solution.py:173
  58.5 2.2 %collective-permute-done.4 = bf16[192,512]{1,0:T(8,128)(2,1)S(1)} collective-permute-done((bf16[192,512]{1,0:T(8,128)(2,1)S(1)}, bf16[192,512]{1,0:T(8,128)(2,1)S(1)}, u32[]{:S(2)}, u32[]{:S(2)}) %collective-permute-start.4) | collective-permute-done | bytes 196640 | tf_op jit(solution)/shard_map/ppermute | solution.py:173
  60.7 0.0 collective-permute-done.5
  60.7 1.0 %add_convert_fusion = bf16[192,512]{1,0:T(8,128)(2,1)} fusion(bf16[192,512]{1,0:T(8,128)(2,1)S(1)} %collective-permute-done.5, bf16[192,512]{1,0:T(8,128)(2,1)S(1)} %collective-permute-done.4, bf16[192,512]{1,0:T(8,128)(2,1)S(1)} %collective-permute-done.3, bf16[512,2048]{1,0:T(8,128)(2,1)S(1)} %bitcast.45, s32[]{:T(128)S(6)} %select_n.27, ...), kind=kOutput, calls=%fused_computation.14 | convolution fusion | flops 101941248 | bytes 1507332 | tf_op jit(solution)/shard_map/dot_general | solution.py:206
  61.6 4.1 %all-to-all-start.1 = ((bf16[8,24,512]{2,1,0:T(8,128)(2,1)}), bf16[8,24,512]{2,1,0:T(8,128)(2,1)S(1)}, u32[]{:S(2)}, u32[]{:S(2)}) async-start(bf16[8,24,512]{2,1,0:T(8,128)(2,1)} %bitcast.21), calls=%async_computation.1 | async-start | bytes 393216 | tf_op jit(solution)/shard_map/all_to_all | solution.py:176
  65.7 2.1 %combine_weights.1 = bf16[192,128]{1,0:T(8,128)(2,1)} custom-call(bf16[128,2048]{1,0:T(8,128)(2,1)} %tokens_ref.3, bf16[1,2048]{1,0:T(2,128)(2,1)} %reshape.87.gain_ref, bf16[8,2048]{1,0:T(8,128)(2,1)} %bitcast.56, s32[1,16]{1,0:T(1,128)} %bitcast.60, f32[16,128]{1,0:T(8,128)} %get-tuple-element.7.local_ref), custom_call_target="tpu_custom_call" | custom-call | tf_op jit(solution)/shard_map/combine_weights/pallas_call | solution.py:166
  67.9 6.2 %all-to-all-done.1 = bf16[8,24,512]{2,1,0:T(8,128)(2,1)S(1)} async-done(((bf16[8,24,512]{2,1,0:T(8,128)(2,1)}), bf16[8,24,512]{2,1,0:T(8,128)(2,1)S(1)}, u32[]{:S(2)}, u32[]{:S(2)}) %all-to-all-start.1) | async-done | bytes 196640 | tf_op jit(solution)/shard_map/all_to_all | solution.py:176
  74.0 1.8 %fusion.2 = bf16[128,512]{1,0:T(8,128)(2,1)} fusion(bf16[192,128]{1,0:T(8,128)(2,1)} %combine_weights.1, bf16[192,512]{1,0:T(8,128)(2,1)S(1)} %bitcast.50, bf16[128,2048]{1,0:T(8,128)(2,1)} %tokens_ref.3, s32[]{:T(128)S(6)} %select_n.27), kind=kOutput, calls=%fused_computation.9 | convolution fusion | flops 25362432 | bytes 507908 | tf_op jit(solution)/shard_map/dot_general | solution.py:213
  (3 shorter events, 0.0 us)
Async XLA Ops:
  0.0 48.7 %copy-start = (bf16[2,256,2048]{2,1,0:T(8,128)(2,1)S(1)}, bf16[2,256,2048]{2,1,0:T(8,128)(2,1)}, u32[]{:S(2)}) copy-start(bf16[2,256,2048]{2,1,0:T(8,128)(2,1)} %param.17) | copy-start | bytes 6291460
  3.7 30.4 %all-to-all-start = ((bf16[8,24,512]{2,1,0:T(8,128)(2,1)}), bf16[8,24,512]{2,1,0:T(8,128)(2,1)S(1)}, u32[]{:S(2)}, u32[]{:S(2)}) async-start(bf16[8,24,512]{2,1,0:T(8,128)(2,1)} %bitcast.55), calls=%async_computation | async-start | bytes 393216 | tf_op jit(solution)/shard_map/all_to_all | solution.py:176
  10.9 6.1 %copy-start.3 = (s32[16]{0:T(128)S(1)}, s32[16]{0:T(128)}, u32[]{:S(2)}) copy-start(s32[16]{0:T(128)} %param.15) | copy-start | bytes 196
  34.1 7.8 %copy-start.2 = (bf16[2,512,2,256]{1,3,2,0:T(8,128)(2,1)S(1)}, bf16[2,512,2,256]{1,3,2,0:T(8,128)(2,1)}, u32[]{:S(2)}) copy-start(bf16[2,512,2,256]{1,3,2,0:T(8,128)(2,1)} %copy.15) | copy-start | bytes 3145732
  34.1 7.8 %collective-permute-start = (bf16[192,512]{1,0:T(8,128)(2,1)S(1)}, bf16[192,512]{1,0:T(8,128)(2,1)S(1)}, u32[]{:S(2)}, u32[]{:S(2)}) collective-permute-start(bf16[192,512]{1,0:T(8,128)(2,1)S(1)} %bitcast.51), channel_id=1, source_target_pairs={{0,8},{8,0},{16,24},{24,16},{1,9},{9,1},{17,25},{25,17},{2,10},{10... | collective-permute-start | bytes 589832 | tf_op jit(solution)/shard_map/ppermute | solution.py:173
  35.6 11.1 %collective-permute-start.2 = (bf16[192,512]{1,0:T(8,128)(2,1)S(1)}, bf16[192,512]{1,0:T(8,128)(2,1)S(1)}, u32[]{:S(2)}, u32[]{:S(2)}) collective-permute-start(bf16[192,512]{1,0:T(8,128)(2,1)S(1)} %bitcast.52), channel_id=1, source_target_pairs={{0,24},{8,16},{16,8},{24,0},{1,25},{9,17},{17,9},{25,1},{2,26},{10... | collective-permute-start | bytes 589832 | tf_op jit(solution)/shard_map/ppermute | solution.py:173
  37.1 11.0 %collective-permute-start.1 = (bf16[192,512]{1,0:T(8,128)(2,1)S(1)}, bf16[192,512]{1,0:T(8,128)(2,1)S(1)}, u32[]{:S(2)}, u32[]{:S(2)}) collective-permute-start(bf16[192,512]{1,0:T(8,128)(2,1)S(1)} %bitcast.53), channel_id=1, source_target_pairs={{0,16},{8,24},{16,0},{24,8},{1,17},{9,25},{17,1},{25,9},{2,18},{10... | collective-permute-start | bytes 589832 | tf_op jit(solution)/shard_map/ppermute | solution.py:173
  37.6 9.1 %copy-start.1 = (bf16[2,512,2,256]{1,3,2,0:T(8,128)(2,1)S(1)}, bf16[2,512,2,256]{1,3,2,0:T(8,128)(2,1)}, u32[]{:S(2)}) copy-start(bf16[2,512,2,256]{1,3,2,0:T(8,128)(2,1)} %copy.17) | copy-start | bytes 3145732
  49.6 8.8 %collective-permute-start.3 = (bf16[192,512]{1,0:T(8,128)(2,1)S(1)}, bf16[192,512]{1,0:T(8,128)(2,1)S(1)}, u32[]{:S(2)}, u32[]{:S(2)}) collective-permute-start(bf16[192,512]{1,0:T(8,128)(2,1)S(1)} %convolution_convert_fusion.3), channel_id=1, source_target_pairs={{0,24},{8,16},{16,8},{24,0},{1,25},{9,17},{17,9},{25,1},{2,26},{10... | collective-permute-start | bytes 589832 | tf_op jit(solution)/shard_map/ppermute | solution.py:173
  51.1 9.6 %collective-permute-start.4 = (bf16[192,512]{1,0:T(8,128)(2,1)S(1)}, bf16[192,512]{1,0:T(8,128)(2,1)S(1)}, u32[]{:S(2)}, u32[]{:S(2)}) collective-permute-start(bf16[192,512]{1,0:T(8,128)(2,1)S(1)} %convolution_convert_fusion.2), channel_id=1, source_target_pairs={{0,16},{8,24},{16,0},{24,8},{1,17},{9,25},{17,1},{25,9},{2,18},{10... | collective-permute-start | bytes 589832 | tf_op jit(solution)/shard_map/ppermute | solution.py:173
  52.6 8.1 %collective-permute-start.5 = (bf16[192,512]{1,0:T(8,128)(2,1)S(1)}, bf16[192,512]{1,0:T(8,128)(2,1)S(1)}, u32[]{:S(2)}, u32[]{:S(2)}) collective-permute-start(bf16[192,512]{1,0:T(8,128)(2,1)S(1)} %convolution_convert_fusion.1), channel_id=1, source_target_pairs={{0,8},{8,0},{16,24},{24,16},{1,9},{9,1},{17,25},{25,17},{2,10},{10... | collective-permute-start | bytes 589832 | tf_op jit(solution)/shard_map/ppermute | solution.py:173
  61.6 12.4 %all-to-all-start.1 = ((bf16[8,24,512]{2,1,0:T(8,128)(2,1)}), bf16[8,24,512]{2,1,0:T(8,128)(2,1)S(1)}, u32[]{:S(2)}, u32[]{:S(2)}) async-start(bf16[8,24,512]{2,1,0:T(8,128)(2,1)} %bitcast.21), calls=%async_computation.1 | async-start | bytes 393216 | tf_op jit(solution)/shard_map/all_to_all | solution.py:176

commit v2 on v1

--- a/solution.py
+++ b/solution.py
@@ -61,6 +61,20 @@
     return lax.rsqrt(jnp.mean(hidden * hidden, axis=-1, keepdims=True) + 1e-06)
 
 
+def apply_gain(scaled, gain_ref, first):
+    gain = gain_ref[...].astype(jnp.float32)
+    number = lax.broadcasted_iota(jnp.int32, gain.shape, 0)
+    parts = []
+    for index in range(scaled.shape[1] // 128):
+        row = jnp.sum(
+            jnp.where(number == first + index, gain, 0.0), axis=0, keepdims=True
+        )
+        parts.append(
+            (scaled[:, index * 128 : (index + 1) * 128] * row).astype(jnp.bfloat16)
+        )
+    return jnp.concatenate(parts, axis=1)
+
+
 def dispatch_kernel(
     per_device,
     tokens_ref,
@@ -79,8 +93,7 @@
     scale = row_scale(hidden)
     start = pl.multiple_of(lax.axis_index("dp") * width, width)
     part = tokens_ref[:, pl.ds(start, width)].astype(jnp.float32)
-    gain = gain_ref[:, pl.ds(start, width)].astype(jnp.float32)
-    normed = (part * scale * gain).astype(jnp.bfloat16)
+    normed = apply_gain(part * scale, gain_ref, lax.axis_index("dp") * (width // 128))
     local = place_rows(
         experts_ref[...], keys_ref[...], slot_ref[...], cap_ref[...], per_device
     )
@@ -99,14 +112,22 @@
 
 
 def weight_kernel(
-    per_device, tokens_ref, gain_ref, route_ref, slot_ref, local_ref, out_ref
+    per_device,
+    tokens_ref,
+    gain_ref,
+    route_ref,
+    slot_ref,
+    local_ref,
+    out_ref,
+    residual_ref,
 ):
+    quarter = residual_ref.shape[1]
+    start = pl.multiple_of(lax.axis_index("dp") * quarter, quarter)
+    residual_ref[...] = tokens_ref[:, pl.ds(start, quarter)]
     slots = slot_ref.shape[1]
     rows = tokens_ref.shape[0]
     hidden = tokens_ref[...].astype(jnp.float32)
-    normed = (hidden * row_scale(hidden) * gain_ref[...].astype(jnp.float32)).astype(
-        jnp.bfloat16
-    )
+    normed = apply_gain(hidden * row_scale(hidden), gain_ref, 0)
     logits = lax.dot_general(
         route_ref[...],
         normed,
@@ -128,7 +149,87 @@
                 local[slot : slot + 1, :] == number, by_slot[slot : slot + 1, :], block
             )
         blocks.append(block)
-    out_ref[...] = jnp.concatenate(blocks, axis=0).astype(jnp.bfloat16)
+    out_ref[...] = jnp.concatenate(blocks, axis=0).T.astype(jnp.bfloat16)
+
+
+def split_kernel(halves, per_device, cap_ref, in_ref, out_ref, mask_ref):
+    tile = 256
+    kinds = 2 * halves
+    per_tile = tile // kinds
+    to_row = lax.broadcasted_iota(jnp.int32, (tile, tile), 0)
+    from_row = lax.broadcasted_iota(jnp.int32, (tile, tile), 1)
+    column = to_row // per_tile
+    source = (to_row % per_tile) * kinds + (column % halves) * 2 + column // halves
+    order = jnp.where(source == from_row, 1.0, 0.0).astype(jnp.bfloat16)
+    for index in range(0, in_ref.shape[1] // tile, 2):
+        low = index * tile
+        pair = jnp.concatenate(
+            [in_ref[0, low : low + tile, :], in_ref[0, low + tile : low + 2 * tile, :]],
+            axis=1,
+        )
+        moved = jnp.dot(order, pair, preferred_element_type=jnp.float32)
+        moved = moved.astype(jnp.bfloat16)
+        for side in range(2):
+            top = (index + side) * per_tile
+            for kind in range(kinds):
+                out_ref[0, top : top + per_tile, kind * 128 : (kind + 1) * 128] = moved[
+                    kind * per_tile : (kind + 1) * per_tile,
+                    side * 128 : (side + 1) * 128,
+                ]
+
+    @pl.when((pl.program_id(0) == 0) & (pl.program_id(1) == 0))
+    def _():
+        units = halves * 128
+        first = lax.axis_index("expert") * per_device
+        caps = cap_ref[...].astype(jnp.float32)
+        lane = lax.broadcasted_iota(jnp.int32, caps.shape, 1)
+        number = lax.broadcasted_iota(jnp.int32, (CAP_DEV, units), 0)
+        number = number.astype(jnp.float32)
+        end = jnp.zeros((1, 1), jnp.float32)
+        parts = []
+        for slot in range(per_device):
+            begin = end
+            cap = jnp.sum(
+                jnp.where(lane == first + slot, caps, 0.0), axis=1, keepdims=True
+            )
+            end = begin + cap
+            parts.append(jnp.where((number >= begin) & (number < end), 1.0, 0.0))
+        block = jnp.concatenate(parts, axis=1)
+        copies = mask_ref.shape[0] // CAP_DEV
+        mask_ref[...] = jnp.concatenate([block] * copies, axis=0).astype(jnp.bfloat16)
+
+
+def split_weights(weight, cap_row, groups, peers):
+    slots, width, _, units = weight.shape
+    halves = units // 128
+    quarter = width // groups
+    rows = weight.reshape(slots, width, 2, halves, 128).transpose(0, 1, 3, 2, 4)
+    rows = rows.reshape(slots, width * 2 * halves, 128)
+    return pl.pallas_call(
+        functools.partial(split_kernel, halves, slots),
+        grid=(groups, slots),
+        in_specs=[
+            pl.BlockSpec(cap_row.shape, lambda step, slot: (0, 0)),
+            pl.BlockSpec(
+                (1, quarter * 2 * halves, 128),
+                lambda step, slot: (slot, lax.axis_index("dp") ^ step, 0),
+            ),
+        ],
+        out_specs=(
+            pl.BlockSpec((1, quarter, 2 * units), lambda step, slot: (step, 0, slot)),
+            pl.BlockSpec((peers * CAP_DEV, slots * units), lambda step, slot: (0, 0)),
+        ),
+        out_shape=(
+            jax.ShapeDtypeStruct((groups, quarter, slots * 2 * units), jnp.bfloat16),
+            jax.ShapeDtypeStruct((peers * CAP_DEV, slots * units), jnp.bfloat16),
+        ),
+        cost_estimate=pl.CostEstimate(
+            flops=2 * 256 * weight.size,
+            bytes_accessed=4 * weight.size,
+            transcendentals=0,
+        ),
+        name="split_gate_up",
+    )(cap_row, rows)
 
 
 def on_device(
@@ -152,7 +253,7 @@
     quarter = width // groups
     total = peers * CAP_DEV
 
-    gain = norm_gain.reshape(1, width)
+    gain = norm_gain.reshape(width // 128, 128)
     slot_row = slot_expert.reshape(1, slots)
     cap_row = capacity.reshape(1, slots)
     outgoing, local = pl.pallas_call(
@@ -163,9 +264,12 @@
         ),
         name="dispatch",
     )(tokens, gain, experts.T, replica_key.T, slot_row, cap_row)
-    weights = pl.pallas_call(
+    weights, residual = pl.pallas_call(
         functools.partial(weight_kernel, per_device),
-        out_shape=jax.ShapeDtypeStruct((total, rows), jnp.bfloat16),
+        out_shape=(
+            jax.ShapeDtypeStruct((rows, total), jnp.bfloat16),
+            jax.ShapeDtypeStruct((rows, quarter), jnp.bfloat16),
+        ),
         name="combine_weights",
     )(tokens, gain, routing_projection_matrix.T, slot_row, local)
 
@@ -178,26 +282,19 @@
         ).reshape(total, quarter)
 
     own = exchange(outgoing)
+    gate_up_parts, mask = split_weights(slot_gate_up_weight, cap_row, groups, peers)
     gate_up = None
     for step in range(groups):
         rows_in = own if step == 0 else swap(own, step)
-        start = (group ^ step) * quarter
-        part = lax.dynamic_slice_in_dim(slot_gate_up_weight, start, quarter, 1)
-        part = part.transpose(1, 0, 2, 3).reshape(quarter, per_device * 2 * units)
-        term = jnp.dot(rows_in, part, preferred_element_type=jnp.float32)
+        term = jnp.dot(rows_in, gate_up_parts[step], preferred_element_type=jnp.float32)
         gate_up = term if gate_up is None else gate_up + term
 
-    expert = lax.axis_index("expert")
-    caps = lax.dynamic_slice_in_dim(capacity, expert * per_device, per_device)
-    ends = jnp.cumsum(caps)
-    number = lax.broadcasted_iota(jnp.int32, (peers, CAP_DEV, 1), 1).reshape(total, 1)
     pieces = []
     for slot in range(per_device):
         gate = gate_up[:, 2 * slot * units : (2 * slot + 1) * units]
         up = gate_up[:, (2 * slot + 1) * units : (2 * slot + 2) * units]
-        mine = (number >= ends[slot] - caps[slot]) & (number < ends[slot])
-        pieces.append(jnp.where(mine, jax.nn.silu(gate) * up, 0.0).astype(jnp.bfloat16))
-    activated = jnp.concatenate(pieces, axis=1)
+        pieces.append((jax.nn.silu(gate) * up).astype(jnp.bfloat16))
+    activated = jnp.where(mask > 0, jnp.concatenate(pieces, axis=1), 0)
     down = down_weight.reshape(per_device * units, width)
     summed = None
     for step in reversed(range(groups)):
@@ -210,10 +307,7 @@
         term = term.astype(jnp.float32)
         summed = term if summed is None else summed + term
     returned = exchange(summed.astype(jnp.bfloat16))
-    mixture = lax.dot_general(
-        weights, returned, (((0,), (0,)), ((), ())), preferred_element_type=jnp.float32
-    )
-    residual = lax.dynamic_slice_in_dim(tokens, group * quarter, quarter, 1)
+    mixture = jnp.dot(weights, returned, preferred_element_type=jnp.float32)
     return (residual.astype(jnp.float32) + mixture).astype(jnp.bfloat16)
 
 

time: 76.5 us -> 58 us (0.76)
  local copies, waits for them, and re-layouts: 21.4 us -> 0.01 us
  Pallas kernels: 4.39 us -> 12.4 us
  between operations: 2.75 us -> 0.09 us
  waiting for transfers between devices: 21.3 us -> 18.8 us
  other arithmetic: 1.57 us -> 0.18 us
  starting transfers between devices: 17.5 us -> 18.5 us
    unnamed x12 -> x6, local copies, waits for them, and re-layouts: 12.3 us -> 0.01 us
    pallas_call x1 -> x2, Pallas kernels: 2.14 us -> 9.99 us  [the longest x1 7.75 us: split_weights(): pl.pallas_call(functools.partial(split_kernel, halves, slots), grid=(grou...]
    dynamic_slice x2 -> x0, local copies, waits for them, and re-layouts: 5.49 us -> none  [the longest x1 5.42 us: on_device(): part = lax.dynamic_slice_in_dim(slot_gate_up_weight, start, quarter, 1)]
    ppermute x6, waiting for transfers between devices: 15.1 us -> 12.1 us  [swap(): return lax.ppermute(value, 'dp', [(i, i ^ step) for i in range(groups)])]
    reshape x2 -> x0, local copies, waits for them, and re-layouts: 2.17 us -> none  [the longest x1 1.44 us: on_device(): gain = norm_gain.reshape(1, width)]
    slice x2 -> x0, local copies, waits for them, and re-layouts: 1.31 us -> none  [on_device(): mine = (number >= ends[slot] - caps[slot]) & (number < ends[slot])]
    and x2 -> x0, other arithmetic: 1.25 us -> none  [on_device(): mine = (number >= ends[slot] - caps[slot]) & (number < ends[slot])]
    all_to_all x2, starting transfers between devices: 10.4 us -> 11.3 us  [exchange(): lax.all_to_all(value.reshape(peers, CAP_DEV, quarter), 'expert', 0, 0, ti...]
  transfers between devices with their start and end apart: 8 -> 8, of which waited for: 6 -> 7; matrix products, arithmetic and copies ran while one was open for 32% -> 7% of each run, Pallas kernels for 3% -> 17%
where the time goes in v2:
time: 58 us; the launch traced here: 57.5 us
  waiting for transfers between devices  18.8 us (32%)
  starting transfers between devices  18.5 us (32%)
  Pallas kernels  12.4 us (21%)
  matrix products  7.5 us (13%)
    ppermute x6, waiting for transfers between devices, swap(): return lax.ppermute(value, 'dp', [(i, i ^ step) for i in range(groups)])  12.1 us
    all_to_all x2, starting transfers between devices, exchange(): lax.all_to_all(value.reshape(peers, CAP_DEV, quarter), 'expert', 0, 0, ti...  11.3 us
    pallas_call x1, Pallas kernels, split_weights(): pl.pallas_call(functools.partial(split_kernel, halves, slots), grid=(grou...  7.75 us
    ppermute x6, starting transfers between devices, swap(): return lax.ppermute(value, 'dp', [(i, i ^ step) for i in range(groups)])  7.17 us
    all_to_all x2, waiting for transfers between devices, exchange(): lax.all_to_all(value.reshape(peers, CAP_DEV, quarter), 'expert', 0, 0, ti...  6.69 us
    dot_general x4, matrix products, on_device(): jnp.dot(rows_in, gate_up_parts[step], preferred_element_type=jnp.float32)  3.95 us
    pallas_call x1, Pallas kernels, on_device(): pl.pallas_call(functools.partial(dispatch_kernel, per_device), out_shape=...  2.39 us
    pallas_call x1, Pallas kernels, on_device(): pl.pallas_call(functools.partial(weight_kernel, per_device), out_shape=(j...  2.24 us
  transfers between devices with their start and end apart: 8, of which 7 were waited for; matrix products, arithmetic and copies ran while one was open for 7% of the time, Pallas kernels for 17%

profile of v2, /device:TPU:0, one launch (start us, length us, event | category | flops | bytes accessed | tf_op | source)
XLA Modules:
  0.0 57.5 jit_solution(6875786422578348838)
XLA Ops:
  0.0 0.0 copy-start
  0.0 2.4 %dispatch.1 = (bf16[192,512]{1,0:T(8,128)(2,1)}, f32[16,128]{1,0:T(8,128)}) custom-call(bf16[128,2048]{1,0:T(8,128)(2,1)} %tokens_ref.3, bf16[16,128]{1,0:T(8,128)(2,1)} %bitcast.50, s32[8,128]{1,0:T(8,128)} %bitcast.52, s32[8,128]{1,0:T(8,128)} %bitcast.53, s32[1,16]{1,0:T(1,128)} %bitcast.56, s32[1,16]{1,0:T(1,128)} %bitcast.54), custom_call_target="tpu_custom_call" | custom-call | tf_op jit(solution)/shard_map/dispatch/pallas_call | solution.py:259
  2.4 6.3 %all-to-all-start = ((bf16[8,24,512]{2,1,0:T(8,128)(2,1)}), bf16[8,24,512]{2,1,0:T(8,128)(2,1)S(1)}, u32[]{:S(2)}, u32[]{:S(2)}) async-start(bf16[8,24,512]{2,1,0:T(8,128)(2,1)} %bitcast.48), calls=%async_computation | async-start | bytes 393216 | tf_op jit(solution)/shard_map/all_to_all | solution.py:280
  8.7 7.8 %split_gate_up.1 = (bf16[4,512,1024]{2,1,0:T(8,128)(2,1)}, bf16[192,512]{1,0:T(8,128)(2,1)}) custom-call(s32[1,16]{1,0:T(1,128)} %bitcast.55, bf16[2,8192,128]{2,1,0:T(8,128)(2,1)} %bitcast.42), custom_call_target="tpu_custom_call" | custom-call | flops 1073741824 | bytes 8388608 | tf_op jit(solution)/shard_map/split_gate_up/pallas_call | solution.py:208
  16.5 0.6 %all-to-all-done = bf16[8,24,512]{2,1,0:T(8,128)(2,1)S(1)} async-done(((bf16[8,24,512]{2,1,0:T(8,128)(2,1)}), bf16[8,24,512]{2,1,0:T(8,128)(2,1)S(1)}, u32[]{:S(2)}, u32[]{:S(2)}) %all-to-all-start) | async-done | bytes 196640 | tf_op jit(solution)/shard_map/all_to_all | solution.py:280
  17.1 0.0 copy-start.1
  17.1 1.5 %collective-permute-start = (bf16[192,512]{1,0:T(8,128)(2,1)S(1)}, bf16[192,512]{1,0:T(8,128)(2,1)S(1)}, u32[]{:S(2)}, u32[]{:S(2)}) collective-permute-start(bf16[192,512]{1,0:T(8,128)(2,1)S(1)} %bitcast.44), channel_id=1, source_target_pairs={{0,8},{8,0},{16,24},{24,16},{1,9},{9,1},{17,25},{25,17},{2,10},{10... | collective-permute-start | bytes 589832 | tf_op jit(solution)/shard_map/ppermute | solution.py:277
  18.6 1.5 %collective-permute-start.2 = (bf16[192,512]{1,0:T(8,128)(2,1)S(1)}, bf16[192,512]{1,0:T(8,128)(2,1)S(1)}, u32[]{:S(2)}, u32[]{:S(2)}) collective-permute-start(bf16[192,512]{1,0:T(8,128)(2,1)S(1)} %bitcast.45), channel_id=1, source_target_pairs={{0,24},{8,16},{16,8},{24,0},{1,25},{9,17},{17,9},{25,1},{2,26},{10... | collective-permute-start | bytes 589832 | tf_op jit(solution)/shard_map/ppermute | solution.py:277
  20.0 0.5 collective-permute-start.1
  20.6 1.6 %fusion.7 = f32[192,1024]{1,0:T(8,128)S(1)} fusion(bf16[192,512]{1,0:T(8,128)(2,1)S(1)} %bitcast.47, bf16[4,512,1024]{2,1,0:T(8,128)(2,1)} %get-tuple-element.16), kind=kOutput, calls=%fused_computation.14 | convolution fusion | flops 201326592 | bytes 2031616 | tf_op jit(solution)/shard_map/dot_general | solution.py:289
  22.2 0.0 copy-start.2
  22.2 2.7 %collective-permute-done = bf16[192,512]{1,0:T(8,128)(2,1)S(1)} collective-permute-done((bf16[192,512]{1,0:T(8,128)(2,1)S(1)}, bf16[192,512]{1,0:T(8,128)(2,1)S(1)}, u32[]{:S(2)}, u32[]{:S(2)}) %collective-permute-start) | collective-permute-done | bytes 196640 | tf_op jit(solution)/shard_map/ppermute | solution.py:277
  24.8 1.6 %convolution_add_fusion.1 = f32[192,1024]{1,0:T(8,128)S(1)} fusion(f32[192,1024]{1,0:T(8,128)S(1)} %fusion.7, bf16[192,512]{1,0:T(8,128)(2,1)S(1)} %collective-permute-done, bf16[4,512,1024]{2,1,0:T(8,128)(2,1)} %get-tuple-element.16), kind=kOutput, calls=%fused_computation.2 | convolution fusion | flops 201523200 | bytes 2818048 | tf_op jit(solution)/shard_map/dot_general | solution.py:289
  26.4 2.7 %collective-permute-done.2 = bf16[192,512]{1,0:T(8,128)(2,1)S(1)} collective-permute-done((bf16[192,512]{1,0:T(8,128)(2,1)S(1)}, bf16[192,512]{1,0:T(8,128)(2,1)S(1)}, u32[]{:S(2)}, u32[]{:S(2)}) %collective-permute-start.2) | collective-permute-done | bytes 196640 | tf_op jit(solution)/shard_map/ppermute | solution.py:277
  29.1 0.0 copy-done.1
  29.1 0.4 fusion.3
  29.5 1.0 %collective-permute-done.1 = bf16[192,512]{1,0:T(8,128)(2,1)S(1)} collective-permute-done((bf16[192,512]{1,0:T(8,128)(2,1)S(1)}, bf16[192,512]{1,0:T(8,128)(2,1)S(1)}, u32[]{:S(2)}, u32[]{:S(2)}) %collective-permute-start.1) | collective-permute-done | bytes 196640 | tf_op jit(solution)/shard_map/ppermute | solution.py:277
  30.5 0.4 fusion
  30.9 0.1 fusion.18
  31.0 0.0 copy-done.2
  31.0 0.1 compare_select_fusion
  31.1 0.0 copy-done
  31.1 0.3 convolution_convert_fusion.3
  31.4 1.5 %collective-permute-start.3 = (bf16[192,512]{1,0:T(8,128)(2,1)S(1)}, bf16[192,512]{1,0:T(8,128)(2,1)S(1)}, u32[]{:S(2)}, u32[]{:S(2)}) collective-permute-start(bf16[192,512]{1,0:T(8,128)(2,1)S(1)} %convolution_convert_fusion.3), channel_id=1, source_target_pairs={{0,24},{8,16},{16,8},{24,0},{1,25},{9,17},{17,9},{25,1},{2,26},{10... | collective-permute-start | bytes 589832 | tf_op jit(solution)/shard_map/ppermute | solution.py:277
  32.9 0.3 convolution_convert_fusion.2
  33.1 1.6 %collective-permute-start.4 = (bf16[192,512]{1,0:T(8,128)(2,1)S(1)}, bf16[192,512]{1,0:T(8,128)(2,1)S(1)}, u32[]{:S(2)}, u32[]{:S(2)}) collective-permute-start(bf16[192,512]{1,0:T(8,128)(2,1)S(1)} %convolution_convert_fusion.2), channel_id=1, source_target_pairs={{0,16},{8,24},{16,0},{24,8},{1,17},{9,25},{17,1},{25,9},{2,18},{10... | collective-permute-start | bytes 589832 | tf_op jit(solution)/shard_map/ppermute | solution.py:277
  34.7 0.3 convolution_convert_fusion.1
  35.0 0.6 %collective-permute-start.5 = (bf16[192,512]{1,0:T(8,128)(2,1)S(1)}, bf16[192,512]{1,0:T(8,128)(2,1)S(1)}, u32[]{:S(2)}, u32[]{:S(2)}) collective-permute-start(bf16[192,512]{1,0:T(8,128)(2,1)S(1)} %convolution_convert_fusion.1), channel_id=1, source_target_pairs={{0,8},{8,0},{16,24},{24,16},{1,9},{9,1},{17,25},{25,17},{2,10},{10... | collective-permute-start | bytes 589832 | tf_op jit(solution)/shard_map/ppermute | solution.py:277
  35.6 3.8 %collective-permute-done.3 = bf16[192,512]{1,0:T(8,128)(2,1)S(1)} collective-permute-done((bf16[192,512]{1,0:T(8,128)(2,1)S(1)}, bf16[192,512]{1,0:T(8,128)(2,1)S(1)}, u32[]{:S(2)}, u32[]{:S(2)}) %collective-permute-start.3) | collective-permute-done | bytes 196640 | tf_op jit(solution)/shard_map/ppermute | solution.py:277
  39.4 2.0 %collective-permute-done.4 = bf16[192,512]{1,0:T(8,128)(2,1)S(1)} collective-permute-done((bf16[192,512]{1,0:T(8,128)(2,1)S(1)}, bf16[192,512]{1,0:T(8,128)(2,1)S(1)}, u32[]{:S(2)}, u32[]{:S(2)}) %collective-permute-start.4) | collective-permute-done | bytes 196640 | tf_op jit(solution)/shard_map/ppermute | solution.py:277
  41.4 0.0 collective-permute-done.5
  41.4 1.0 %add_convert_fusion = bf16[192,512]{1,0:T(8,128)(2,1)} fusion(bf16[192,512]{1,0:T(8,128)(2,1)S(1)} %collective-permute-done.5, bf16[192,512]{1,0:T(8,128)(2,1)S(1)} %collective-permute-done.4, bf16[192,512]{1,0:T(8,128)(2,1)S(1)} %collective-permute-done.3, bf16[192,512]{1,0:T(8,128)(2,1)S(1)} %compare_select_fusion, bf16[512,2048]{1,0:T(8,128)(2,1)S(1)} %bitcast.41, ...), kind=kOutput, calls=%fused_computation.24 | convolution fusion | flops 101548032 | bytes 1507332 | tf_op jit(solution)/shard_map/dot_general | solution.py:303
  42.4 5.0 %all-to-all-start.1 = ((bf16[8,24,512]{2,1,0:T(8,128)(2,1)}), bf16[8,24,512]{2,1,0:T(8,128)(2,1)S(1)}, u32[]{:S(2)}, u32[]{:S(2)}) async-start(bf16[8,24,512]{2,1,0:T(8,128)(2,1)} %bitcast.16), calls=%async_computation.1 | async-start | bytes 393216 | tf_op jit(solution)/shard_map/all_to_all | solution.py:280
  47.3 2.2 %combine_weights.1 = (bf16[128,192]{1,0:T(8,128)(2,1)}, bf16[128,512]{1,0:T(8,128)(2,1)}) custom-call(bf16[128,2048]{1,0:T(8,128)(2,1)} %tokens_ref.3, bf16[16,128]{1,0:T(8,128)(2,1)} %bitcast.51, bf16[8,2048]{1,0:T(8,128)(2,1)} %bitcast.49, s32[1,16]{1,0:T(1,128)} %bitcast.57, f32[16,128]{1,0:T(8,128)} %get-tuple-element.11.local_ref), custom_call_target="tpu_custom_call" | custom-call | tf_op jit(solution)/shard_map/combine_weights/pallas_call | solution.py:267
  49.6 6.1 %all-to-all-done.1 = bf16[8,24,512]{2,1,0:T(8,128)(2,1)S(1)} async-done(((bf16[8,24,512]{2,1,0:T(8,128)(2,1)}), bf16[8,24,512]{2,1,0:T(8,128)(2,1)S(1)}, u32[]{:S(2)}, u32[]{:S(2)}) %all-to-all-start.1) | async-done | bytes 196640 | tf_op jit(solution)/shard_map/all_to_all | solution.py:280
  55.7 1.8 %fusion.2 = bf16[128,512]{1,0:T(8,128)(2,1)} fusion(bf16[128,192]{1,0:T(8,128)(2,1)} %get-tuple-element.13, bf16[192,512]{1,0:T(8,128)(2,1)S(1)} %bitcast.43, bf16[128,512]{1,0:T(8,128)(2,1)} %get-tuple-element.12), kind=kOutput, calls=%fused_computation.9 | convolution fusion | flops 25362432 | bytes 507904 | tf_op jit(solution)/shard_map/dot_general | solution.py:310
Async XLA Ops:
  0.0 31.1 %copy-start = (bf16[2,256,2048]{2,1,0:T(8,128)(2,1)S(1)}, bf16[2,256,2048]{2,1,0:T(8,128)(2,1)}, u32[]{:S(2)}) copy-start(bf16[2,256,2048]{2,1,0:T(8,128)(2,1)} %param.17) | copy-start | bytes 6291460
  2.4 14.7 %all-to-all-start = ((bf16[8,24,512]{2,1,0:T(8,128)(2,1)}), bf16[8,24,512]{2,1,0:T(8,128)(2,1)S(1)}, u32[]{:S(2)}, u32[]{:S(2)}) async-start(bf16[8,24,512]{2,1,0:T(8,128)(2,1)} %bitcast.48), calls=%async_computation | async-start | bytes 393216 | tf_op jit(solution)/shard_map/all_to_all | solution.py:280
  17.1 12.1 %copy-start.1 = (bf16[4,512,1024]{2,1,0:T(8,128)(2,1)S(1)}, bf16[4,512,1024]{2,1,0:T(8,128)(2,1)}, u32[]{:S(2)}) copy-start(bf16[4,512,1024]{2,1,0:T(8,128)(2,1)} %get-tuple-element.16) | copy-start | bytes 12582916
  17.1 7.8 %collective-permute-start = (bf16[192,512]{1,0:T(8,128)(2,1)S(1)}, bf16[192,512]{1,0:T(8,128)(2,1)S(1)}, u32[]{:S(2)}, u32[]{:S(2)}) collective-permute-start(bf16[192,512]{1,0:T(8,128)(2,1)S(1)} %bitcast.44), channel_id=1, source_target_pairs={{0,8},{8,0},{16,24},{24,16},{1,9},{9,1},{17,25},{25,17},{2,10},{10... | collective-permute-start | bytes 589832 | tf_op jit(solution)/shard_map/ppermute | solution.py:277
  18.6 10.6 %collective-permute-start.2 = (bf16[192,512]{1,0:T(8,128)(2,1)S(1)}, bf16[192,512]{1,0:T(8,128)(2,1)S(1)}, u32[]{:S(2)}, u32[]{:S(2)}) collective-permute-start(bf16[192,512]{1,0:T(8,128)(2,1)S(1)} %bitcast.45), channel_id=1, source_target_pairs={{0,24},{8,16},{16,8},{24,0},{1,25},{9,17},{17,9},{25,1},{2,26},{10... | collective-permute-start | bytes 589832 | tf_op jit(solution)/shard_map/ppermute | solution.py:277
  20.0 10.4 %collective-permute-start.1 = (bf16[192,512]{1,0:T(8,128)(2,1)S(1)}, bf16[192,512]{1,0:T(8,128)(2,1)S(1)}, u32[]{:S(2)}, u32[]{:S(2)}) collective-permute-start(bf16[192,512]{1,0:T(8,128)(2,1)S(1)} %bitcast.46), channel_id=1, source_target_pairs={{0,16},{8,24},{16,0},{24,8},{1,17},{9,25},{17,1},{25,9},{2,18},{10... | collective-permute-start | bytes 589832 | tf_op jit(solution)/shard_map/ppermute | solution.py:277
  22.2 8.8 %copy-start.2 = (bf16[192,512]{1,0:T(8,128)(2,1)S(1)}, bf16[192,512]{1,0:T(8,128)(2,1)}, u32[]{:S(2)}) copy-start(bf16[192,512]{1,0:T(8,128)(2,1)} %get-tuple-element.14) | copy-start | bytes 589828
  31.4 8.0 %collective-permute-start.3 = (bf16[192,512]{1,0:T(8,128)(2,1)S(1)}, bf16[192,512]{1,0:T(8,128)(2,1)S(1)}, u32[]{:S(2)}, u32[]{:S(2)}) collective-permute-start(bf16[192,512]{1,0:T(8,128)(2,1)S(1)} %convolution_convert_fusion.3), channel_id=1, source_target_pairs={{0,24},{8,16},{16,8},{24,0},{1,25},{9,17},{17,9},{25,1},{2,26},{10... | collective-permute-start | bytes 589832 | tf_op jit(solution)/shard_map/ppermute | solution.py:277
  33.1 8.3 %collective-permute-start.4 = (bf16[192,512]{1,0:T(8,128)(2,1)S(1)}, bf16[192,512]{1,0:T(8,128)(2,1)S(1)}, u32[]{:S(2)}, u32[]{:S(2)}) collective-permute-start(bf16[192,512]{1,0:T(8,128)(2,1)S(1)} %convolution_convert_fusion.2), channel_id=1, source_target_pairs={{0,16},{8,24},{16,0},{24,8},{1,17},{9,25},{17,1},{25,9},{2,18},{10... | collective-permute-start | bytes 589832 | tf_op jit(solution)/shard_map/ppermute | solution.py:277
  35.0 6.4 %collective-permute-start.5 = (bf16[192,512]{1,0:T(8,128)(2,1)S(1)}, bf16[192,512]{1,0:T(8,128)(2,1)S(1)}, u32[]{:S(2)}, u32[]{:S(2)}) collective-permute-start(bf16[192,512]{1,0:T(8,128)(2,1)S(1)} %convolution_convert_fusion.1), channel_id=1, source_target_pairs={{0,8},{8,0},{16,24},{24,16},{1,9},{9,1},{17,25},{25,17},{2,10},{10... | collective-permute-start | bytes 589832 | tf_op jit(solution)/shard_map/ppermute | solution.py:277
  42.4 13.3 %all-to-all-start.1 = ((bf16[8,24,512]{2,1,0:T(8,128)(2,1)}), bf16[8,24,512]{2,1,0:T(8,128)(2,1)S(1)}, u32[]{:S(2)}, u32[]{:S(2)}) async-start(bf16[8,24,512]{2,1,0:T(8,128)(2,1)} %bitcast.16), calls=%async_computation.1 | async-start | bytes 393216 | tf_op jit(solution)/shard_map/all_to_all | solution.py:280

commit v3 on v1

v3 whole, which is shorter than its diff:
```python
import functools

import jax
import jax.numpy as jnp
from jax import lax
from jax.experimental import pallas as pl
from jax.experimental.pallas import tpu as pltpu
from jax.sharding import PartitionSpec as P

CAP_DEV = 24
NEAR = 4


def to_column(row):
    n = row.shape[1]
    eye = lax.broadcasted_iota(jnp.int32, (n, n), 0) == lax.broadcasted_iota(
        jnp.int32, (n, n), 1
    )
    wide = jnp.where(eye, jnp.broadcast_to(row, (n, n)).astype(jnp.float32), 0.0)
    return jnp.sum(wide, axis=1, keepdims=True)


def place_rows(experts_t, keys_t, slot_row, cap_row, per_device):
    slots = slot_row.shape[1]
    picks, rows = experts_t.shape
    slot_f = slot_row.astype(jnp.float32)
    cap_f = cap_row.astype(jnp.float32)
    slot_col = to_column(slot_row)
    cap_col = to_column(cap_row)
    here = lax.broadcasted_iota(jnp.int32, (slots, slots), 0)
    other = lax.broadcasted_iota(jnp.int32, (slots, slots), 1)
    same = jnp.where(slot_f == slot_col, 1.0, 0.0)
    copies = jnp.sum(same, axis=1, keepdims=True)
    earlier = other < here
    place = jnp.sum(jnp.where(earlier, same, 0.0), axis=1, keepdims=True)
    together = (here // per_device) == (other // per_device)
    offset = jnp.sum(jnp.where(earlier & together, cap_f, 0.0), axis=1, keepdims=True)
    hit = jnp.zeros((slots, rows), jnp.float32)
    key = jnp.zeros((slots, rows), jnp.float32)
    experts_f = experts_t.astype(jnp.float32)
    keys_f = keys_t.astype(jnp.float32)
    for k in range(picks):
        match = experts_f[k : k + 1, :] == slot_col
        hit = jnp.where(match, 1.0, hit)
        key = jnp.where(match, keys_f[k : k + 1, :], key)
    rest = key - jnp.floor(key * (1.0 / copies)) * copies
    rest = jnp.where(rest < 0.0, rest + copies, rest)
    rest = jnp.where(rest >= copies, rest - copies, rest)
    chosen = (hit > 0.0) & (rest == place)
    before = lax.broadcasted_iota(jnp.int32, (rows, rows), 0) < lax.broadcasted_iota(
        jnp.int32, (rows, rows), 1
    )
    position = jnp.dot(
        jnp.where(chosen, 1.0, 0.0).astype(jnp.bfloat16),
        jnp.where(before, 1.0, 0.0).astype(jnp.bfloat16),
        preferred_element_type=jnp.float32,
    )
    return jnp.where(chosen & (position < cap_col), position + offset, -1.0)


def row_scale(hidden):
    return lax.rsqrt(jnp.mean(hidden * hidden, axis=-1, keepdims=True) + 1e-06)


def apply_gain(scaled, gain, first):
    number = lax.broadcasted_iota(jnp.int32, gain.shape, 0)
    parts = []
    for index in range(scaled.shape[1] // 128):
        row = jnp.sum(
            jnp.where(number == first + index, gain, 0.0), axis=0, keepdims=True
        )
        parts.append(
            (scaled[:, index * 128 : (index + 1) * 128] * row).astype(jnp.bfloat16)
        )
    return jnp.concatenate(parts, axis=1)


def pick_rows(local_ref, value_ref, steps, per_device):
    rows = local_ref.shape[1]
    me = lax.axis_index("expert")
    number = lax.broadcasted_iota(jnp.int32, (CAP_DEV, rows), 0).astype(jnp.float32)
    blocks = []
    for step in steps:
        block = jnp.zeros((CAP_DEV, rows), jnp.float32)
        for index in range(per_device):
            slot = (me ^ step) * per_device + index
            value = 1.0 if value_ref is None else value_ref[pl.ds(slot, 1), :]
            block = jnp.where(local_ref[pl.ds(slot, 1), :] == number, value, block)
        blocks.append(block)
    return jnp.concatenate(blocks, axis=0)


def store_blocks(refs, value):
    for index, ref in enumerate(refs):
        ref[...] = value[index * CAP_DEV : (index + 1) * CAP_DEV, :].astype(ref.dtype)


def load_blocks(refs):
    return jnp.concatenate([ref[...].astype(jnp.float32) for ref in refs], axis=0)


def dispatch_kernel(per_device, steps, *refs):
    tokens_hbm, *small_hbm = refs[:6]
    tokens_ref, gain_ref, local_ref, *out_refs = refs[6 : 9 + len(steps)]
    experts_ref, keys_ref, slot_ref, cap_ref, arrived = refs[9 + len(steps) :]
    small_refs = (experts_ref, keys_ref, slot_ref, cap_ref, gain_ref)
    copies = [
        pltpu.make_async_copy(source, target, arrived.at[index])
        for index, (source, target) in enumerate(
            zip((*small_hbm, tokens_hbm), (*small_refs, tokens_ref))
        )
    ]
    for copy in copies:
        copy.start()
    for copy in copies[:-1]:
        copy.wait()
    local_ref[...] = place_rows(
        experts_ref[...], keys_ref[...], slot_ref[...], cap_ref[...], per_device
    )
    pick = pick_rows(local_ref, None, steps, per_device).astype(jnp.bfloat16)
    gain = gain_ref[...].astype(jnp.float32)
    width = out_refs[0].shape[1]
    group = lax.axis_index("dp")
    copies[-1].wait()
    scale = row_scale(tokens_ref[...].astype(jnp.float32))
    start = pl.multiple_of(group * width, width)
    part = tokens_ref[:, pl.ds(start, width)].astype(jnp.float32)
    normed = apply_gain(part * scale, gain, group * (width // 128))
    store_blocks(out_refs, jnp.dot(pick, normed, preferred_element_type=jnp.float32))


def near_kernel(
    per_device, groups, steps, tokens_ref, gain_ref, local_ref, *out_refs
):
    gain = gain_ref[...].astype(jnp.float32)
    width = tokens_ref.shape[1] // groups
    group = lax.axis_index("dp")
    scale = row_scale(tokens_ref[...].astype(jnp.float32))
    pick = pick_rows(local_ref, None, steps, per_device).astype(jnp.bfloat16)
    for step in range(groups):
        start = pl.multiple_of((group ^ step) * width, width)
        part = tokens_ref[:, pl.ds(start, width)].astype(jnp.float32)
        normed = apply_gain(part * scale, gain, (group ^ step) * (width // 128))
        value = jnp.dot(pick, normed, preferred_element_type=jnp.float32)
        for index, ref in enumerate(out_refs):
            ref[:, step * width : (step + 1) * width] = value[
                index * CAP_DEV : (index + 1) * CAP_DEV, :
            ].astype(ref.dtype)


def weight_kernel(
    per_device,
    steps,
    tokens_ref,
    gain_ref,
    route_ref,
    slot_ref,
    local_ref,
    out_ref,
    residual_ref,
    score_ref,
):
    quarter = residual_ref.shape[1]
    start = pl.multiple_of(lax.axis_index("dp") * quarter, quarter)
    residual_ref[...] = tokens_ref[:, pl.ds(start, quarter)]
    slots = slot_ref.shape[1]
    rows = tokens_ref.shape[0]
    hidden = tokens_ref[...].astype(jnp.float32)
    gain = gain_ref[...].astype(jnp.float32)
    normed = apply_gain(hidden * row_scale(hidden), gain, 0)
    logits = lax.dot_general(
        route_ref[...],
        normed,
        (((1,), (1,)), ((), ())),
        preferred_element_type=jnp.float32,
    )
    score = 1.0 / (1.0 + jnp.exp(-logits))
    slot_col = to_column(slot_ref[...])
    by_slot = jnp.zeros((slots, rows), jnp.float32)
    for expert in range(route_ref.shape[0]):
        by_slot = jnp.where(slot_col == expert, score[expert : expert + 1, :], by_slot)
    score_ref[...] = by_slot
    weights = pick_rows(local_ref, score_ref, steps, per_device)
    out_ref[...] = weights.T.astype(jnp.bfloat16)


def split_kernel(halves, groups, in_hbm, out_ref, in_ref, arrived):
    tile = 256
    kinds = 2 * halves
    per_tile = tile // kinds
    slots, length, _ = in_hbm.shape
    part = length // groups
    group = lax.axis_index("dp")
    copies = []
    for step in range(groups):
        base = pl.multiple_of((group ^ step) * part, part)
        copies.append(
            pltpu.make_async_copy(
                in_hbm.at[:, pl.ds(base, part), :], in_ref.at[step], arrived.at[step]
            )
        )
        copies[-1].start()
    to_row = lax.broadcasted_iota(jnp.int32, (tile, tile), 0)
    from_row = lax.broadcasted_iota(jnp.int32, (tile, tile), 1)
    column = to_row // per_tile
    source = (to_row % per_tile) * kinds + (column % halves) * 2 + column // halves
    order = jnp.where(source == from_row, 1.0, 0.0).astype(jnp.bfloat16)
    for step in range(groups):
        copies[step].wait()
        for slot in range(slots):
            for index in range(0, part // tile, 2):
                low = index * tile
                pair = [
                    in_ref[step, slot, low + side * tile : low + (side + 1) * tile, :]
                    for side in range(2)
                ]
                moved = jnp.dot(
                    order,
                    jnp.concatenate(pair, axis=1),
                    preferred_element_type=jnp.float32,
                ).astype(jnp.bfloat16)
                for side in range(2):
                    top = (index + side) * per_tile
                    for kind in range(kinds):
                        left = (slot * kinds + kind) * 128
                        out_ref[step, top : top + per_tile, left : left + 128] = moved[
                            kind * per_tile : (kind + 1) * per_tile,
                            side * 128 : (side + 1) * 128,
                        ]


def slot_mask(cap_ref, per_device, units):
    first = lax.axis_index("expert") * per_device
    caps = cap_ref[...].astype(jnp.float32)
    lane = lax.broadcasted_iota(jnp.int32, caps.shape, 1)
    number = lax.broadcasted_iota(jnp.int32, (CAP_DEV, units), 0).astype(jnp.float32)
    end = jnp.zeros((1, 1), jnp.float32)
    parts = []
    for slot in range(per_device):
        begin = end
        end = begin + jnp.sum(
            jnp.where(lane == first + slot, caps, 0.0), axis=1, keepdims=True
        )
        parts.append(jnp.where((number >= begin) & (number < end), 1.0, 0.0))
    return jnp.concatenate(parts, axis=1)


def finish_rows(gate_up, cap_ref, down_ref, out_refs, per_device):
    units = down_ref.shape[0] // per_device
    mask = slot_mask(cap_ref, per_device, units)
    mask = jnp.concatenate([mask] * (gate_up.shape[0] // CAP_DEV), axis=0)
    pieces = []
    for slot in range(per_device):
        left = 2 * slot * units
        gate = gate_up[:, left : left + units]
        up = gate_up[:, left + units : left + 2 * units]
        pieces.append(gate / (1.0 + jnp.exp(-gate)) * up)
    activated = jnp.where(mask > 0.0, jnp.concatenate(pieces, axis=1), 0.0)
    activated = activated.astype(jnp.bfloat16)
    group = lax.axis_index("dp")
    for step, ref in enumerate(out_refs):
        width = ref.shape[1]
        start = pl.multiple_of((group ^ step) * width, width)
        ref[...] = jnp.dot(
            activated,
            down_ref[:, pl.ds(start, width)],
            preferred_element_type=jnp.float32,
        ).astype(ref.dtype)


def far_kernel(
    per_device, sum_ref, last_ref, weight_ref, cap_ref, down_ref, *out_refs
):
    gate_up = sum_ref[...] + jnp.dot(
        last_ref[...],
        weight_ref[weight_ref.shape[0] - 1],
        preferred_element_type=jnp.float32,
    )
    finish_rows(gate_up, cap_ref, down_ref, out_refs, per_device)


def near_expert_kernel(per_device, count, *refs):
    row_refs, (weight_ref, cap_ref, down_ref, *out_refs) = refs[:count], refs[count:]
    rows = load_blocks(row_refs).astype(jnp.bfloat16)
    width = weight_ref.shape[1]
    gate_up = None
    for step in range(weight_ref.shape[0]):
        term = jnp.dot(
            rows[:, step * width : (step + 1) * width],
            weight_ref[step],
            preferred_element_type=jnp.float32,
        )
        gate_up = term if gate_up is None else gate_up + term
    finish_rows(gate_up, cap_ref, down_ref, out_refs, per_device)


def join_kernel(*refs):
    refs[-1][...] = load_blocks(refs[:-1]).astype(refs[-1].dtype)


def sum_kernel(count, *refs):
    total = refs[0][...].astype(jnp.float32)
    for ref in refs[1:count]:
        total = total + ref[...].astype(jnp.float32)
    store_blocks(refs[count:], total)


def combine_kernel(count, weight_ref, residual_ref, *refs):
    rows = load_blocks(refs[:count]).astype(jnp.bfloat16)
    mixture = jnp.dot(weight_ref[...], rows, preferred_element_type=jnp.float32)
    refs[count][...] = (residual_ref[...].astype(jnp.float32) + mixture).astype(
        jnp.bfloat16
    )


def call(kernel, name, outs, *args, scratch=(), in_hbm=False, after=()):
    count = len(after)
    if in_hbm:
        args = [pltpu.with_memory_space_constraint(a, pltpu.HBM) for a in args]
    space = pltpu.HBM if in_hbm else pltpu.VMEM
    size = sum(a.size * a.dtype.itemsize for a in (*args, *outs))
    return pl.pallas_call(
        lambda *refs: kernel(*refs[count:]),
        in_specs=[pl.BlockSpec(memory_space=pl.ANY)] * count
        + [pl.BlockSpec(memory_space=space)] * len(args),
        out_specs=[pl.BlockSpec(memory_space=pltpu.VMEM)] * len(outs),
        out_shape=outs,
        scratch_shapes=scratch,
        compiler_params=pltpu.CompilerParams(vmem_limit_bytes=size + (8 << 20)),
        name=name,
    )(*after, *args)


def on_device(
    tokens,
    norm_gain,
    routing_projection_matrix,
    experts,
    replica_key,
    slot_expert,
    capacity,
    slot_gate_up_weight,
    down_weight,
):
    peers = lax.axis_size("expert")
    groups = lax.axis_size("dp")
    rows, width = tokens.shape
    slots = slot_expert.shape[0]
    per_device = slots // peers
    units = slot_gate_up_weight.shape[3]
    quarter = width // groups
    near = range(min(NEAR, peers))
    far = range(len(near), peers)

    def blocks(count, *shape, dtype=jnp.bfloat16):
        return [jax.ShapeDtypeStruct(shape, dtype)] * count

    def to_group(value, step):
        return lax.ppermute(value, "dp", [(i, i ^ step) for i in range(groups)])

    def to_peer(value, step):
        return lax.ppermute(value, "expert", [(i, i ^ step) for i in range(peers)])

    gain = norm_gain.reshape(width // 128, 128)
    slot_row = slot_expert.reshape(1, slots)
    cap_row = capacity.reshape(1, slots)
    down = down_weight.reshape(per_device * units, width)

    tokens_here, gain_here, local, *far_out = call(
        functools.partial(dispatch_kernel, per_device, far),
        "dispatch",
        blocks(1, rows, width)
        + blocks(1, *gain.shape)
        + blocks(1, slots, rows, dtype=jnp.float32)
        + blocks(len(far), CAP_DEV, quarter),
        tokens,
        experts.T,
        replica_key.T,
        slot_row,
        cap_row,
        gain,
        scratch=[
            pltpu.VMEM((experts.shape[1], rows), jnp.int32),
            pltpu.VMEM((experts.shape[1], rows), jnp.int32),
            pltpu.VMEM((1, slots), jnp.int32),
            pltpu.VMEM((1, slots), jnp.int32),
            pltpu.SemaphoreType.DMA((6,)),
        ],
        in_hbm=True,
    )
    far_in = [to_peer(value, step) for value, step in zip(far_out[::-1], far[::-1])]

    halves = units // 128
    split_in = slot_gate_up_weight.reshape(per_device, width, 2, halves, 128)
    split_in = split_in.transpose(0, 1, 3, 2, 4)
    split_in = split_in.reshape(per_device, width * halves * 2, 128)
    (gate_up,) = call(
        functools.partial(split_kernel, halves, groups),
        "split_gate_up",
        blocks(1, groups, quarter, per_device * 2 * units),
        split_in,
        scratch=[
            pltpu.VMEM(
                (groups, per_device, quarter * halves * 2, 128), jnp.bfloat16
            ),
            pltpu.SemaphoreType.DMA((groups,)),
        ],
        in_hbm=True,
        after=(local,),
    )

    (far_rows,) = call(
        join_kernel,
        "join_far",
        blocks(1, len(far) * CAP_DEV, quarter),
        *far_in[::-1],
        after=(gate_up,),
    )
    near_out = call(
        functools.partial(near_kernel, per_device, groups, near),
        "dispatch_near",
        blocks(len(near), CAP_DEV, width),
        tokens_here,
        gain_here,
        local,
        after=(far_rows,),
    )
    near_in = [near_out[0]] + [to_peer(near_out[step], step) for step in near[1:]]

    far_parts = [far_rows] + [to_group(far_rows, step) for step in range(1, groups)]
    far_sum = None
    for step in range(groups - 1):
        term = jnp.dot(
            far_parts[step], gate_up[step], preferred_element_type=jnp.float32
        )
        far_sum = term if far_sum is None else far_sum + term
    far_partials = call(
        functools.partial(far_kernel, per_device),
        "expert_far",
        blocks(groups, len(far) * CAP_DEV, quarter),
        far_sum,
        far_parts[-1],
        gate_up,
        cap_row,
        down,
    )
    near_partials = call(
        functools.partial(near_expert_kernel, per_device, len(near)),
        "expert_near",
        blocks(groups, len(near) * CAP_DEV, quarter),
        *near_in,
        gate_up,
        cap_row,
        down,
        after=(far_partials[1],),
    )

    def reduce_groups(partials, name, count, after=()):
        received = [to_group(partials[step], step) for step in range(1, groups)]
        return call(
            functools.partial(sum_kernel, groups),
            name,
            blocks(count, CAP_DEV, quarter),
            partials[0],
            *received,
            after=after,
        )

    far_back = reduce_groups(far_partials, "sum_far", len(far))
    near_back = reduce_groups(near_partials, "sum_near", len(near), far_back[:1])
    far_back = [to_peer(value, step) for value, step in zip(far_back[::-1], far[::-1])]
    near_back = [near_back[0]] + [to_peer(near_back[step], step) for step in near[1:]]

    weights, residual = call(
        functools.partial(weight_kernel, per_device, range(peers)),
        "combine_weights",
        blocks(1, rows, peers * CAP_DEV) + blocks(1, rows, quarter),
        tokens_here,
        gain_here,
        routing_projection_matrix.T,
        slot_row,
        local,
        scratch=[pltpu.VMEM((slots, rows), jnp.float32)],
    )
    (mixed,) = call(
        functools.partial(combine_kernel, peers),
        "combine",
        blocks(1, rows, quarter),
        weights,
        residual,
        *near_back,
        *far_back[::-1],
    )
    return mixed


def solution(mesh):
    in_specs = (
        P("expert", None),
        P(),
        P(),
        P("expert", None),
        P("expert", None),
        P(),
        P(),
        P("expert", None, None, "dp"),
        P("expert", "dp", None),
    )
    return jax.shard_map(
        on_device,
        mesh=mesh,
        in_specs=in_specs,
        out_specs=P("expert", "dp"),
        check_vma=False,
    )
```

time: 76.5 us -> 46.1 us (0.60)
  local copies, waits for them, and re-layouts: 21.4 us -> 0.03 us
  waiting for transfers between devices: 21.3 us -> 12.4 us
  starting transfers between devices: 17.5 us -> 23.7 us
  matrix products: 6.9 us -> 0.92 us
  Pallas kernels: 4.39 us -> 8.69 us
  between operations: 2.75 us -> 0.19 us
  other arithmetic: 1.57 us -> 0 us
    ppermute x6 -> x23, starting transfers between devices: 7.11 us -> 23.7 us  [the longest x14 13 us: to_peer(): return lax.ppermute(value, 'expert', [(i, i ^ step) for i in range(peers)])]
    unnamed x12 -> x8, local copies, waits for them, and re-layouts: 12.3 us -> 0.03 us
    all_to_all x2 -> x0, starting transfers between devices: 10.4 us -> none  [exchange(): lax.all_to_all(value.reshape(peers, CAP_DEV, quarter), 'expert', 0, 0, ti...]
    all_to_all x2 -> x0, waiting for transfers between devices: 6.2 us -> none  [exchange(): lax.all_to_all(value.reshape(peers, CAP_DEV, quarter), 'expert', 0, 0, ti...]
    dot_general x9 -> x3, matrix products: 6.9 us -> 0.92 us  [on_device(): jnp.dot(far_parts[step], gate_up[step], preferred_element_type=jnp.float32)]
    dynamic_slice x2 -> x0, local copies, waits for them, and re-layouts: 5.49 us -> none  [the longest x1 5.42 us: on_device(): part = lax.dynamic_slice_in_dim(slot_gate_up_weight, start, quarter, 1)]
    pallas_call x2 -> x10, Pallas kernels: 4.39 us -> 8.69 us  [call(): pl.pallas_call(lambda *refs: kernel(*refs[count:]), in_specs=[pl.BlockSpe...]
    ppermute x6 -> x23, waiting for transfers between devices: 15.1 us -> 12.4 us  [the longest x9 7.58 us: to_group(): return lax.ppermute(value, 'dp', [(i, i ^ step) for i in range(groups)])]
  transfers between devices with their start and end apart: 8 -> 23, of which waited for: 6 -> 9; matrix products, arithmetic and copies ran while one was open for 32% -> 2% of each run, Pallas kernels for 3% -> 14%
where the time goes in v3:
time: 46.1 us; the launch traced here: 45.9 us
  starting transfers between devices  23.7 us (51%)
  waiting for transfers between devices  12.4 us (27%)
  Pallas kernels  8.69 us (19%)
  matrix products  0.92 us (2%)
    ppermute x14, starting transfers between devices, to_peer(): return lax.ppermute(value, 'expert', [(i, i ^ step) for i in range(peers)])  13 us
    ppermute x9, starting transfers between devices, to_group(): return lax.ppermute(value, 'dp', [(i, i ^ step) for i in range(groups)])  10.7 us
    pallas_call x10, Pallas kernels, call(): pl.pallas_call(lambda *refs: kernel(*refs[count:]), in_specs=[pl.BlockSpe...  8.69 us
    ppermute x9, waiting for transfers between devices, to_group(): return lax.ppermute(value, 'dp', [(i, i ^ step) for i in range(groups)])  7.58 us
    ppermute x14, waiting for transfers between devices, to_peer(): return lax.ppermute(value, 'expert', [(i, i ^ step) for i in range(peers)])  4.83 us
    dot_general x3, matrix products, on_device(): jnp.dot(far_parts[step], gate_up[step], preferred_element_type=jnp.float32)  0.92 us
  transfers between devices with their start and end apart: 23, of which 9 were waited for; matrix products, arithmetic and copies ran while one was open for 2% of the time, Pallas kernels for 14%

profile of v3, /device:TPU:0, one launch (start us, length us, event | category | flops | bytes accessed | tf_op | source)
XLA Modules:
  0.0 45.9 jit_solution(214709539904725257)
XLA Ops:
  0.0 1.5 %dispatch.1 = (bf16[128,2048]{1,0:T(8,128)(2,1)S(1)}, bf16[16,128]{1,0:T(8,128)(2,1)S(1)}, f32[16,128]{1,0:T(8,128)S(1)}, bf16[24,512]{1,0:T(8,128)(2,1)S(1)}, b...) custom-call(bf16[128,2048]{1,0:T(8,128)(2,1)} %refs_0_.1, s32[8,128]{1,0:T(8,128)} %bitcast.33, ...), custom_call_target="tpu_custom_call" | custom-call | tf_op jit(solution)/shard_map/dispatch/pallas_call | solution.py:322
  1.5 4.1 %collective-permute-start = (bf16[24,512]{1,0:T(8,128)(2,1)S(1)}, bf16[24,512]{1,0:T(8,128)(2,1)S(1)}, u32[]{:S(2)}, u32[]{:S(2)}) collective-permute-start(bf16[24,512]{1,0:T(8,128)(2,1)S(1)} %get-tuple-element.39), channel_id=1, source_target_pairs={{0,4},{1,5},{2,6},{3,7},{4,0},{5,1},{6,2},{7,3},{8,12},{9,13},{10,... | collective-permute-start | bytes 73736 | tf_op jit(solution)/shard_map/ppermute | solution.py:362
  5.6 0.0 collective-permute-start.1
  5.6 3.1 %collective-permute-start.2 = (bf16[24,512]{1,0:T(8,128)(2,1)S(1)}, bf16[24,512]{1,0:T(8,128)(2,1)S(1)}, u32[]{:S(2)}, u32[]{:S(2)}) collective-permute-start(bf16[24,512]{1,0:T(8,128)(2,1)S(1)} %get-tuple-element.41), channel_id=1, source_target_pairs={{0,6},{1,7},{2,4},{3,5},{4,2},{5,3},{6,0},{7,1},{8,14},{9,15},{10,... | collective-permute-start | bytes 73736 | tf_op jit(solution)/shard_map/ppermute | solution.py:362
  8.7 0.6 %collective-permute-start.3 = (bf16[24,512]{1,0:T(8,128)(2,1)S(1)}, bf16[24,512]{1,0:T(8,128)(2,1)S(1)}, u32[]{:S(2)}, u32[]{:S(2)}) collective-permute-start(bf16[24,512]{1,0:T(8,128)(2,1)S(1)} %get-tuple-element.42), channel_id=1, source_target_pairs={{0,7},{1,6},{2,5},{3,4},{4,3},{5,2},{6,1},{7,0},{8,15},{9,14},{10,... | collective-permute-start | bytes 73736 | tf_op jit(solution)/shard_map/ppermute | solution.py:362
  9.3 3.3 %split_gate_up.1.refs_0_.refs_2_.refs_5_ = bf16[4,512,1024]{2,1,0:T(8,128)(2,1)S(1)} custom-call(f32[16,128]{1,0:T(8,128)S(1)} %get-tuple-element.36.refs_4_.refs_0_.refs_3_, bf16[2,8192,128]{2,1,0:T(8,128)(2,1)} %bitcast.32), custom_call_target="tpu_custom_call" | custom-call | tf_op jit(solution)/shard_map/split_gate_up/pallas_call | solution.py:322
  12.6 0.0 copy-start
  12.6 0.0 copy-start.2
  12.7 1.1 %collective-permute-done.3.refs_4_ = bf16[24,512]{1,0:T(8,128)(2,1)S(1)} collective-permute-done((bf16[24,512]{1,0:T(8,128)(2,1)S(1)}, bf16[24,512]{1,0:T(8,128)(2,1)S(1)}, u32[]{:S(2)}, u32[]{:S(2)}) %collective-permute-start.3) | collective-permute-done | bytes 24608 | tf_op jit(solution)/shard_map/ppermute | solution.py:362
  13.8 1.6 %collective-permute-start.4 = (bf16[96,512]{1,0:T(8,128)(2,1)S(1)}, bf16[96,512]{1,0:T(8,128)(2,1)S(1)}, u32[]{:S(2)}, u32[]{:S(2)}) collective-permute-start(bf16[96,512]{1,0:T(8,128)(2,1)S(1)} %join_far.1.refs_0_), channel_id=1, source_target_pairs={{0,8},{8,0},{16,24},{24,16},{1,9},{9,1},{17,25},{25,17},{2,10},{10... | collective-permute-start | bytes 294920 | tf_op jit(solution)/shard_map/ppermute | solution.py:359
  15.4 1.5 %collective-permute-start.6 = (bf16[96,512]{1,0:T(8,128)(2,1)S(1)}, bf16[96,512]{1,0:T(8,128)(2,1)S(1)}, u32[]{:S(2)}, u32[]{:S(2)}) collective-permute-start(bf16[96,512]{1,0:T(8,128)(2,1)S(1)} %join_far.1.refs_0_), channel_id=1, source_target_pairs={{0,24},{8,16},{16,8},{24,0},{1,25},{9,17},{17,9},{25,1},{2,26},{10... | collective-permute-start | bytes 294920 | tf_op jit(solution)/shard_map/ppermute | solution.py:359
  16.8 0.5 %collective-permute-start.5 = (bf16[96,512]{1,0:T(8,128)(2,1)S(1)}, bf16[96,512]{1,0:T(8,128)(2,1)S(1)}, u32[]{:S(2)}, u32[]{:S(2)}) collective-permute-start(bf16[96,512]{1,0:T(8,128)(2,1)S(1)} %join_far.1.refs_0_), channel_id=1, source_target_pairs={{0,16},{8,24},{16,0},{24,8},{1,17},{9,25},{17,1},{25,9},{2,18},{10... | collective-permute-start | bytes 294920 | tf_op jit(solution)/shard_map/ppermute | solution.py:359
  17.3 0.4 dispatch_near.1
  17.8 0.1 collective-permute-start.10
  17.9 0.1 collective-permute-start.11
  18.0 1.3 %collective-permute-done.4 = bf16[96,512]{1,0:T(8,128)(2,1)S(1)} collective-permute-done((bf16[96,512]{1,0:T(8,128)(2,1)S(1)}, bf16[96,512]{1,0:T(8,128)(2,1)S(1)}, u32[]{:S(2)}, u32[]{:S(2)}) %collective-permute-start.4) | collective-permute-done | bytes 98336 | tf_op jit(solution)/shard_map/ppermute | solution.py:359
  19.2 0.5 %collective-permute-start.12 = (bf16[24,2048]{1,0:T(8,128)(2,1)S(1)}, bf16[24,2048]{1,0:T(8,128)(2,1)S(1)}, u32[]{:S(2)}, u32[]{:S(2)}) collective-permute-start(bf16[24,2048]{1,0:T(8,128)(2,1)S(1)} %get-tuple-element.51), channel_id=1, source_target_pairs={{0,3},{1,2},{2,1},{3,0},{4,7},{5,6},{6,5},{7,4},{8,11},{9,10},{10,... | collective-permute-start | bytes 294920 | tf_op jit(solution)/shard_map/ppermute | solution.py:362
  19.7 0.3 fusion.2
  20.1 3.7 %collective-permute-done.5 = bf16[96,512]{1,0:T(8,128)(2,1)S(1)} collective-permute-done((bf16[96,512]{1,0:T(8,128)(2,1)S(1)}, bf16[96,512]{1,0:T(8,128)(2,1)S(1)}, u32[]{:S(2)}, u32[]{:S(2)}) %collective-permute-start.5) | collective-permute-done | bytes 98336 | tf_op jit(solution)/shard_map/ppermute | solution.py:359
  23.8 0.3 fusion.1
  24.1 0.3 fusion.refs_0_
  24.5 0.7 %expert_far.1 = (bf16[96,512]{1,0:T(8,128)(2,1)S(1)}, bf16[96,512]{1,0:T(8,128)(2,1)S(1)}, bf16[96,512]{1,0:T(8,128)(2,1)S(1)}, bf16[96,512]{1,0:T(8,128)(2,1)S(1)}) custom-call(f32[96,1024]{1,0:T(8,128)S(1)} %fusion.refs_0_, bf16[96,512]{1,0:T(8,128)(2,1)S(1)} %collective-permute-done.6.refs_1_, ...), custom_call_target="tpu_custom_call" | custom-call | tf_op jit(solution)/shard_map/expert_far/pallas_call | solution.py:322
  25.2 0.0 copy-start.1
  25.2 0.0 copy-start.3
  25.2 0.6 %collective-permute-start.8 = (bf16[96,512]{1,0:T(8,128)(2,1)S(1)}, bf16[96,512]{1,0:T(8,128)(2,1)S(1)}, u32[]{:S(2)}, u32[]{:S(2)}) collective-permute-start(bf16[96,512]{1,0:T(8,128)(2,1)S(1)} %get-tuple-element.45), channel_id=1, source_target_pairs={{0,16},{8,24},{16,0},{24,8},{1,17},{9,25},{17,1},{25,9},{2,18},{10... | collective-permute-start | bytes 294920 | tf_op jit(solution)/shard_map/ppermute | solution.py:359
  25.8 2.4 %collective-permute-start.9 = (bf16[96,512]{1,0:T(8,128)(2,1)S(1)}, bf16[96,512]{1,0:T(8,128)(2,1)S(1)}, u32[]{:S(2)}, u32[]{:S(2)}) collective-permute-start(bf16[96,512]{1,0:T(8,128)(2,1)S(1)} %get-tuple-element.46), channel_id=1, source_target_pairs={{0,24},{8,16},{16,8},{24,0},{1,25},{9,17},{17,9},{25,1},{2,26},{10... | collective-permute-start | bytes 294920 | tf_op jit(solution)/shard_map/ppermute | solution.py:359
  28.2 0.5 %collective-permute-start.7 = (bf16[96,512]{1,0:T(8,128)(2,1)S(1)}, bf16[96,512]{1,0:T(8,128)(2,1)S(1)}, u32[]{:S(2)}, u32[]{:S(2)}) collective-permute-start(bf16[96,512]{1,0:T(8,128)(2,1)S(1)} %get-tuple-element.44.refs_0_), channel_id=1, source_target_pairs={{0,8},{8,0},{16,24},{24,16},{1,9},{9,1},{17,25},{25,17},{2,10},{10... | collective-permute-start | bytes 294920 | tf_op jit(solution)/shard_map/ppermute | solution.py:359
  28.8 1.2 %expert_near.1 = (bf16[96,512]{1,0:T(8,128)(2,1)S(1)}, bf16[96,512]{1,0:T(8,128)(2,1)S(1)}, bf16[96,512]{1,0:T(8,128)(2,1)S(1)}, bf16[96,512]{1,0:T(8,128)(2,1)S(1)}) custom-call(bf16[96,512]{1,0:T(8,128)(2,1)S(1)} %get-tuple-element.44.refs_0_, bf16[24,2048]{1,0:T(8,128)(2,1)S(1)} %get-tuple-element.48.refs_1_, ...), custom_call_target="tpu_custom_call" | custom-call | tf_op jit(solution)/shard_map/expert_near/pallas_call | solution.py:322
  30.0 1.6 %collective-permute-start.13 = (bf16[96,512]{1,0:T(8,128)(2,1)S(1)}, bf16[96,512]{1,0:T(8,128)(2,1)S(1)}, u32[]{:S(2)}, u32[]{:S(2)}) collective-permute-start(bf16[96,512]{1,0:T(8,128)(2,1)S(1)} %get-tuple-element.53), channel_id=1, source_target_pairs={{0,8},{8,0},{16,24},{24,16},{1,9},{9,1},{17,25},{25,17},{2,10},{10... | collective-permute-start | bytes 294920 | tf_op jit(solution)/shard_map/ppermute | solution.py:359
  31.5 0.5 %collective-permute-start.14 = (bf16[96,512]{1,0:T(8,128)(2,1)S(1)}, bf16[96,512]{1,0:T(8,128)(2,1)S(1)}, u32[]{:S(2)}, u32[]{:S(2)}) collective-permute-start(bf16[96,512]{1,0:T(8,128)(2,1)S(1)} %get-tuple-element.54), channel_id=1, source_target_pairs={{0,16},{8,24},{16,0},{24,8},{1,17},{9,25},{17,1},{25,9},{2,18},{10... | collective-permute-start | bytes 294920 | tf_op jit(solution)/shard_map/ppermute | solution.py:359
  32.1 1.5 %collective-permute-start.15 = (bf16[96,512]{1,0:T(8,128)(2,1)S(1)}, bf16[96,512]{1,0:T(8,128)(2,1)S(1)}, u32[]{:S(2)}, u32[]{:S(2)}) collective-permute-start(bf16[96,512]{1,0:T(8,128)(2,1)S(1)} %get-tuple-element.55), channel_id=1, source_target_pairs={{0,24},{8,16},{16,8},{24,0},{1,25},{9,17},{17,9},{25,1},{2,26},{10... | collective-permute-start | bytes 294920 | tf_op jit(solution)/shard_map/ppermute | solution.py:359
  33.5 0.7 %collective-permute-done.7.refs_1_ = bf16[96,512]{1,0:T(8,128)(2,1)S(1)} collective-permute-done((bf16[96,512]{1,0:T(8,128)(2,1)S(1)}, bf16[96,512]{1,0:T(8,128)(2,1)S(1)}, u32[]{:S(2)}, u32[]{:S(2)}) %collective-permute-start.7) | collective-permute-done | bytes 98336 | tf_op jit(solution)/shard_map/ppermute | solution.py:359
  34.3 0.1 sum_far.1
  34.3 0.1 collective-permute-start.20
  34.4 1.0 %collective-permute-start.21 = (bf16[24,512]{1,0:T(8,128)(2,1)S(1)}, bf16[24,512]{1,0:T(8,128)(2,1)S(1)}, u32[]{:S(2)}, u32[]{:S(2)}) collective-permute-start(bf16[24,512]{1,0:T(8,128)(2,1)S(1)} %get-tuple-element.61), channel_id=1, source_target_pairs={{0,6},{1,7},{2,4},{3,5},{4,2},{5,3},{6,0},{7,1},{8,14},{9,15},{10,... | collective-permute-start | bytes 73736 | tf_op jit(solution)/shard_map/ppermute | solution.py:362
  35.4 0.7 %collective-permute-done.13.refs_2_ = bf16[96,512]{1,0:T(8,128)(2,1)S(1)} collective-permute-done((bf16[96,512]{1,0:T(8,128)(2,1)S(1)}, bf16[96,512]{1,0:T(8,128)(2,1)S(1)}, u32[]{:S(2)}, u32[]{:S(2)}) %collective-permute-start.13) | collective-permute-done | bytes 98336 | tf_op jit(solution)/shard_map/ppermute | solution.py:359
  36.2 0.4 collective-permute-start.22
  36.5 0.0 collective-permute-done.14.refs_3_
  36.5 1.1 %collective-permute-done.15.refs_4_ = bf16[96,512]{1,0:T(8,128)(2,1)S(1)} collective-permute-done((bf16[96,512]{1,0:T(8,128)(2,1)S(1)}, bf16[96,512]{1,0:T(8,128)(2,1)S(1)}, u32[]{:S(2)}, u32[]{:S(2)}) %collective-permute-start.15) | collective-permute-done | bytes 98336 | tf_op jit(solution)/shard_map/ppermute | solution.py:359
  37.6 0.1 sum_near.1
  37.7 0.9 %collective-permute-start.16 = (bf16[24,512]{1,0:T(8,128)(2,1)S(1)}, bf16[24,512]{1,0:T(8,128)(2,1)S(1)}, u32[]{:S(2)}, u32[]{:S(2)}) collective-permute-start(bf16[24,512]{1,0:T(8,128)(2,1)S(1)} %get-tuple-element.57), channel_id=1, source_target_pairs={{0,1},{1,0},{2,3},{3,2},{4,5},{5,4},{6,7},{7,6},{8,9},{9,8},{10,11... | collective-permute-start | bytes 73736 | tf_op jit(solution)/shard_map/ppermute | solution.py:362
  38.5 1.4 %collective-permute-start.18 = (bf16[24,512]{1,0:T(8,128)(2,1)S(1)}, bf16[24,512]{1,0:T(8,128)(2,1)S(1)}, u32[]{:S(2)}, u32[]{:S(2)}) collective-permute-start(bf16[24,512]{1,0:T(8,128)(2,1)S(1)} %get-tuple-element.59), channel_id=1, source_target_pairs={{0,3},{1,2},{2,1},{3,0},{4,7},{5,6},{6,5},{7,4},{8,11},{9,10},{10,... | collective-permute-start | bytes 73736 | tf_op jit(solution)/shard_map/ppermute | solution.py:362
  40.0 0.1 collective-permute-done.21.refs_8_
  40.1 0.8 %collective-permute-start.19 = (bf16[24,512]{1,0:T(8,128)(2,1)S(1)}, bf16[24,512]{1,0:T(8,128)(2,1)S(1)}, u32[]{:S(2)}, u32[]{:S(2)}) collective-permute-start(bf16[24,512]{1,0:T(8,128)(2,1)S(1)} %get-tuple-element.47.refs_0_), channel_id=1, source_target_pairs={{0,4},{1,5},{2,6},{3,7},{4,0},{5,1},{6,2},{7,3},{8,12},{9,13},{10,... | collective-permute-start | bytes 73736 | tf_op jit(solution)/shard_map/ppermute | solution.py:362
  40.9 0.5 %combine_weights.1 = (bf16[128,192]{1,0:T(8,128)(2,1)S(1)}, bf16[128,512]{1,0:T(8,128)(2,1)S(1)}) custom-call(bf16[128,2048]{1,0:T(8,128)(2,1)S(1)} %get-tuple-element.34.refs_0_.refs_1_, bf16[16,128]{1,0:T(8,128)(2,1)S(1)} %get-tuple-element.35.refs_1_.refs_2_, bf16[8,2048]{1,0:T(8,128)(2,1)S(1)} %bitcast.26, s32[1,16]{1,0:T(1,128)S(1)} %bitcast.31, ...), custom_call_target="tpu_custom_call" | custom-call | tf_op jit(solution)/shard_map/combine_weights/pallas_call | solution.py:322
  41.5 0.9 %collective-permute-done.17.refs_4_ = bf16[24,512]{1,0:T(8,128)(2,1)S(1)} collective-permute-done((bf16[24,512]{1,0:T(8,128)(2,1)S(1)}, bf16[24,512]{1,0:T(8,128)(2,1)S(1)}, u32[]{:S(2)}, u32[]{:S(2)}) %collective-permute-start.17) | collective-permute-done | bytes 24608 | tf_op jit(solution)/shard_map/ppermute | solution.py:362
  42.4 2.7 %collective-permute-done.19.refs_6_ = bf16[24,512]{1,0:T(8,128)(2,1)S(1)} collective-permute-done((bf16[24,512]{1,0:T(8,128)(2,1)S(1)}, bf16[24,512]{1,0:T(8,128)(2,1)S(1)}, u32[]{:S(2)}, u32[]{:S(2)}) %collective-permute-start.19) | collective-permute-done | bytes 24608 | tf_op jit(solution)/shard_map/ppermute | solution.py:362
  45.1 0.8 %combine.1 = bf16[128,512]{1,0:T(8,128)(2,1)} custom-call(bf16[128,192]{1,0:T(8,128)(2,1)S(1)} %get-tuple-element.37.refs_0_, bf16[128,512]{1,0:T(8,128)(2,1)S(1)} %get-tuple-element.38.refs_1_, bf16[24,512]{1,0:T(8,128)(2,1)S(1)} %get-tuple-element.56.refs_2_, bf16[24,512]{1,0:T(8,128)(2,1)S(1)} %collective-permute-done.16.refs_3_, ...), custom_call_target="tpu_custom_call" | custom-call | tf_op jit(solution)/shard_map/combine/pallas_call | solution.py:322
  (19 shorter events, 0.1 us)
Async XLA Ops:
  1.5 11.1 %collective-permute-start = (bf16[24,512]{1,0:T(8,128)(2,1)S(1)}, bf16[24,512]{1,0:T(8,128)(2,1)S(1)}, u32[]{:S(2)}, u32[]{:S(2)}) collective-permute-start(bf16[24,512]{1,0:T(8,128)(2,1)S(1)} %get-tuple-element.39), channel_id=1, source_target_pairs={{0,4},{1,5},{2,6},{3,7},{4,0},{5,1},{6,2},{7,3},{8,12},{9,13},{10,... | collective-permute-start | bytes 73736 | tf_op jit(solution)/shard_map/ppermute | solution.py:362
  5.6 7.0 %collective-permute-start.1 = (bf16[24,512]{1,0:T(8,128)(2,1)S(1)}, bf16[24,512]{1,0:T(8,128)(2,1)S(1)}, u32[]{:S(2)}, u32[]{:S(2)}) collective-permute-start(bf16[24,512]{1,0:T(8,128)(2,1)S(1)} %get-tuple-element.40), channel_id=1, source_target_pairs={{0,5},{1,4},{2,7},{3,6},{4,1},{5,0},{6,3},{7,2},{8,13},{9,12},{10,... | collective-permute-start | bytes 73736 | tf_op jit(solution)/shard_map/ppermute | solution.py:362
  5.6 7.0 %collective-permute-start.2 = (bf16[24,512]{1,0:T(8,128)(2,1)S(1)}, bf16[24,512]{1,0:T(8,128)(2,1)S(1)}, u32[]{:S(2)}, u32[]{:S(2)}) collective-permute-start(bf16[24,512]{1,0:T(8,128)(2,1)S(1)} %get-tuple-element.41), channel_id=1, source_target_pairs={{0,6},{1,7},{2,4},{3,5},{4,2},{5,3},{6,0},{7,1},{8,14},{9,15},{10,... | collective-permute-start | bytes 73736 | tf_op jit(solution)/shard_map/ppermute | solution.py:362
  8.7 5.0 %collective-permute-start.3 = (bf16[24,512]{1,0:T(8,128)(2,1)S(1)}, bf16[24,512]{1,0:T(8,128)(2,1)S(1)}, u32[]{:S(2)}, u32[]{:S(2)}) collective-permute-start(bf16[24,512]{1,0:T(8,128)(2,1)S(1)} %get-tuple-element.42), channel_id=1, source_target_pairs={{0,7},{1,6},{2,5},{3,4},{4,3},{5,2},{6,1},{7,0},{8,15},{9,14},{10,... | collective-permute-start | bytes 73736 | tf_op jit(solution)/shard_map/ppermute | solution.py:362
  12.6 11.8 %copy-start = (bf16[2,256,2048]{2,1,0:T(8,128)(2,1)S(1)}, bf16[2,256,2048]{2,1,0:T(8,128)(2,1)}, u32[]{:S(2)}) copy-start(bf16[2,256,2048]{2,1,0:T(8,128)(2,1)} %param.17) | copy-start | bytes 6291460
  12.6 11.8 %copy-start.2 = (s32[16]{0:T(128)S(1)}, s32[16]{0:T(128)}, u32[]{:S(2)}) copy-start(s32[16]{0:T(128)} %param.15) | copy-start | bytes 196
  13.8 5.4 %collective-permute-start.4 = (bf16[96,512]{1,0:T(8,128)(2,1)S(1)}, bf16[96,512]{1,0:T(8,128)(2,1)S(1)}, u32[]{:S(2)}, u32[]{:S(2)}) collective-permute-start(bf16[96,512]{1,0:T(8,128)(2,1)S(1)} %join_far.1.refs_0_), channel_id=1, source_target_pairs={{0,8},{8,0},{16,24},{24,16},{1,9},{9,1},{17,25},{25,17},{2,10},{10... | collective-permute-start | bytes 294920 | tf_op jit(solution)/shard_map/ppermute | solution.py:359
  15.4 9.1 %collective-permute-start.6 = (bf16[96,512]{1,0:T(8,128)(2,1)S(1)}, bf16[96,512]{1,0:T(8,128)(2,1)S(1)}, u32[]{:S(2)}, u32[]{:S(2)}) collective-permute-start(bf16[96,512]{1,0:T(8,128)(2,1)S(1)} %join_far.1.refs_0_), channel_id=1, source_target_pairs={{0,24},{8,16},{16,8},{24,0},{1,25},{9,17},{17,9},{25,1},{2,26},{10... | collective-permute-start | bytes 294920 | tf_op jit(solution)/shard_map/ppermute | solution.py:359
  16.8 7.0 %collective-permute-start.5 = (bf16[96,512]{1,0:T(8,128)(2,1)S(1)}, bf16[96,512]{1,0:T(8,128)(2,1)S(1)}, u32[]{:S(2)}, u32[]{:S(2)}) collective-permute-start(bf16[96,512]{1,0:T(8,128)(2,1)S(1)} %join_far.1.refs_0_), channel_id=1, source_target_pairs={{0,16},{8,24},{16,0},{24,8},{1,17},{9,25},{17,1},{25,9},{2,18},{10... | collective-permute-start | bytes 294920 | tf_op jit(solution)/shard_map/ppermute | solution.py:359
  17.8 10.4 %collective-permute-start.10 = (bf16[24,2048]{1,0:T(8,128)(2,1)S(1)}, bf16[24,2048]{1,0:T(8,128)(2,1)S(1)}, u32[]{:S(2)}, u32[]{:S(2)}) collective-permute-start(bf16[24,2048]{1,0:T(8,128)(2,1)S(1)} %get-tuple-element.49), channel_id=1, source_target_pairs={{0,1},{1,0},{2,3},{3,2},{4,5},{5,4},{6,7},{7,6},{8,9},{9,8},{10,11... | collective-permute-start | bytes 294920 | tf_op jit(solution)/shard_map/ppermute | solution.py:362
  17.9 10.9 %collective-permute-start.11 = (bf16[24,2048]{1,0:T(8,128)(2,1)S(1)}, bf16[24,2048]{1,0:T(8,128)(2,1)S(1)}, u32[]{:S(2)}, u32[]{:S(2)}) collective-permute-start(bf16[24,2048]{1,0:T(8,128)(2,1)S(1)} %get-tuple-element.50), channel_id=1, source_target_pairs={{0,2},{1,3},{2,0},{3,1},{4,6},{5,7},{6,4},{7,5},{8,10},{9,11},{10,... | collective-permute-start | bytes 294920 | tf_op jit(solution)/shard_map/ppermute | solution.py:362
  19.2 9.5 %collective-permute-start.12 = (bf16[24,2048]{1,0:T(8,128)(2,1)S(1)}, bf16[24,2048]{1,0:T(8,128)(2,1)S(1)}, u32[]{:S(2)}, u32[]{:S(2)}) collective-permute-start(bf16[24,2048]{1,0:T(8,128)(2,1)S(1)} %get-tuple-element.51), channel_id=1, source_target_pairs={{0,3},{1,2},{2,1},{3,0},{4,7},{5,6},{6,5},{7,4},{8,11},{9,10},{10,... | collective-permute-start | bytes 294920 | tf_op jit(solution)/shard_map/ppermute | solution.py:362
  25.2 15.7 %copy-start.1 = (bf16[2048,8]{0,1:T(8,128)(2,1)S(1)}, bf16[2048,8]{0,1:T(8,128)(2,1)}, u32[]{:S(2)}) copy-start(bf16[2048,8]{0,1:T(8,128)(2,1)} %param.11) | copy-start | bytes 98308
  25.2 15.7 %copy-start.3 = (s32[16]{0:T(128)S(1)}, s32[16]{0:T(128)}, u32[]{:S(2)}) copy-start(s32[16]{0:T(128)} %param.14) | copy-start | bytes 196
  25.2 6.9 %collective-permute-start.8 = (bf16[96,512]{1,0:T(8,128)(2,1)S(1)}, bf16[96,512]{1,0:T(8,128)(2,1)S(1)}, u32[]{:S(2)}, u32[]{:S(2)}) collective-permute-start(bf16[96,512]{1,0:T(8,128)(2,1)S(1)} %get-tuple-element.45), channel_id=1, source_target_pairs={{0,16},{8,24},{16,0},{24,8},{1,17},{9,25},{17,1},{25,9},{2,18},{10... | collective-permute-start | bytes 294920 | tf_op jit(solution)/shard_map/ppermute | solution.py:359
  25.8 7.8 %collective-permute-start.9 = (bf16[96,512]{1,0:T(8,128)(2,1)S(1)}, bf16[96,512]{1,0:T(8,128)(2,1)S(1)}, u32[]{:S(2)}, u32[]{:S(2)}) collective-permute-start(bf16[96,512]{1,0:T(8,128)(2,1)S(1)} %get-tuple-element.46), channel_id=1, source_target_pairs={{0,24},{8,16},{16,8},{24,0},{1,25},{9,17},{17,9},{25,1},{2,26},{10... | collective-permute-start | bytes 294920 | tf_op jit(solution)/shard_map/ppermute | solution.py:359
  28.2 6.0 %collective-permute-start.7 = (bf16[96,512]{1,0:T(8,128)(2,1)S(1)}, bf16[96,512]{1,0:T(8,128)(2,1)S(1)}, u32[]{:S(2)}, u32[]{:S(2)}) collective-permute-start(bf16[96,512]{1,0:T(8,128)(2,1)S(1)} %get-tuple-element.44.refs_0_), channel_id=1, source_target_pairs={{0,8},{8,0},{16,24},{24,16},{1,9},{9,1},{17,25},{25,17},{2,10},{10... | collective-permute-start | bytes 294920 | tf_op jit(solution)/shard_map/ppermute | solution.py:359
  30.0 6.2 %collective-permute-start.13 = (bf16[96,512]{1,0:T(8,128)(2,1)S(1)}, bf16[96,512]{1,0:T(8,128)(2,1)S(1)}, u32[]{:S(2)}, u32[]{:S(2)}) collective-permute-start(bf16[96,512]{1,0:T(8,128)(2,1)S(1)} %get-tuple-element.53), channel_id=1, source_target_pairs={{0,8},{8,0},{16,24},{24,16},{1,9},{9,1},{17,25},{25,17},{2,10},{10... | collective-permute-start | bytes 294920 | tf_op jit(solution)/shard_map/ppermute | solution.py:359
  31.5 5.0 %collective-permute-start.14 = (bf16[96,512]{1,0:T(8,128)(2,1)S(1)}, bf16[96,512]{1,0:T(8,128)(2,1)S(1)}, u32[]{:S(2)}, u32[]{:S(2)}) collective-permute-start(bf16[96,512]{1,0:T(8,128)(2,1)S(1)} %get-tuple-element.54), channel_id=1, source_target_pairs={{0,16},{8,24},{16,0},{24,8},{1,17},{9,25},{17,1},{25,9},{2,18},{10... | collective-permute-start | bytes 294920 | tf_op jit(solution)/shard_map/ppermute | solution.py:359
  32.1 5.5 %collective-permute-start.15 = (bf16[96,512]{1,0:T(8,128)(2,1)S(1)}, bf16[96,512]{1,0:T(8,128)(2,1)S(1)}, u32[]{:S(2)}, u32[]{:S(2)}) collective-permute-start(bf16[96,512]{1,0:T(8,128)(2,1)S(1)} %get-tuple-element.55), channel_id=1, source_target_pairs={{0,24},{8,16},{16,8},{24,0},{1,25},{9,17},{17,9},{25,1},{2,26},{10... | collective-permute-start | bytes 294920 | tf_op jit(solution)/shard_map/ppermute | solution.py:359
  34.3 4.2 %collective-permute-start.20 = (bf16[24,512]{1,0:T(8,128)(2,1)S(1)}, bf16[24,512]{1,0:T(8,128)(2,1)S(1)}, u32[]{:S(2)}, u32[]{:S(2)}) collective-permute-start(bf16[24,512]{1,0:T(8,128)(2,1)S(1)} %get-tuple-element.60), channel_id=1, source_target_pairs={{0,5},{1,4},{2,7},{3,6},{4,1},{5,0},{6,3},{7,2},{8,13},{9,12},{10,... | collective-permute-start | bytes 73736 | tf_op jit(solution)/shard_map/ppermute | solution.py:362
  34.4 5.7 %collective-permute-start.21 = (bf16[24,512]{1,0:T(8,128)(2,1)S(1)}, bf16[24,512]{1,0:T(8,128)(2,1)S(1)}, u32[]{:S(2)}, u32[]{:S(2)}) collective-permute-start(bf16[24,512]{1,0:T(8,128)(2,1)S(1)} %get-tuple-element.61), channel_id=1, source_target_pairs={{0,6},{1,7},{2,4},{3,5},{4,2},{5,3},{6,0},{7,1},{8,14},{9,15},{10,... | collective-permute-start | bytes 73736 | tf_op jit(solution)/shard_map/ppermute | solution.py:362
  36.2 5.3 %collective-permute-start.22 = (bf16[24,512]{1,0:T(8,128)(2,1)S(1)}, bf16[24,512]{1,0:T(8,128)(2,1)S(1)}, u32[]{:S(2)}, u32[]{:S(2)}) collective-permute-start(bf16[24,512]{1,0:T(8,128)(2,1)S(1)} %get-tuple-element.62), channel_id=1, source_target_pairs={{0,7},{1,6},{2,5},{3,4},{4,3},{5,2},{6,1},{7,0},{8,15},{9,14},{10,... | collective-permute-start | bytes 73736 | tf_op jit(solution)/shard_map/ppermute | solution.py:362
  37.7 3.8 %collective-permute-start.16 = (bf16[24,512]{1,0:T(8,128)(2,1)S(1)}, bf16[24,512]{1,0:T(8,128)(2,1)S(1)}, u32[]{:S(2)}, u32[]{:S(2)}) collective-permute-start(bf16[24,512]{1,0:T(8,128)(2,1)S(1)} %get-tuple-element.57), channel_id=1, source_target_pairs={{0,1},{1,0},{2,3},{3,2},{4,5},{5,4},{6,7},{7,6},{8,9},{9,8},{10,11... | collective-permute-start | bytes 73736 | tf_op jit(solution)/shard_map/ppermute | solution.py:362
  38.5 3.8 %collective-permute-start.17 = (bf16[24,512]{1,0:T(8,128)(2,1)S(1)}, bf16[24,512]{1,0:T(8,128)(2,1)S(1)}, u32[]{:S(2)}, u32[]{:S(2)}) collective-permute-start(bf16[24,512]{1,0:T(8,128)(2,1)S(1)} %get-tuple-element.58), channel_id=1, source_target_pairs={{0,2},{1,3},{2,0},{3,1},{4,6},{5,7},{6,4},{7,5},{8,10},{9,11},{10,... | collective-permute-start | bytes 73736 | tf_op jit(solution)/shard_map/ppermute | solution.py:362
  38.5 3.8 %collective-permute-start.18 = (bf16[24,512]{1,0:T(8,128)(2,1)S(1)}, bf16[24,512]{1,0:T(8,128)(2,1)S(1)}, u32[]{:S(2)}, u32[]{:S(2)}) collective-permute-start(bf16[24,512]{1,0:T(8,128)(2,1)S(1)} %get-tuple-element.59), channel_id=1, source_target_pairs={{0,3},{1,2},{2,1},{3,0},{4,7},{5,6},{6,5},{7,4},{8,11},{9,10},{10,... | collective-permute-start | bytes 73736 | tf_op jit(solution)/shard_map/ppermute | solution.py:362
  40.1 5.0 %collective-permute-start.19 = (bf16[24,512]{1,0:T(8,128)(2,1)S(1)}, bf16[24,512]{1,0:T(8,128)(2,1)S(1)}, u32[]{:S(2)}, u32[]{:S(2)}) collective-permute-start(bf16[24,512]{1,0:T(8,128)(2,1)S(1)} %get-tuple-element.47.refs_0_), channel_id=1, source_target_pairs={{0,4},{1,5},{2,6},{3,7},{4,0},{5,1},{6,2},{7,3},{8,12},{9,13},{10,... | collective-permute-start | bytes 73736 | tf_op jit(solution)/shard_map/ppermute | solution.py:362

commit v4 on v3

--- a/solution.py
+++ b/solution.py
@@ -91,18 +91,23 @@
 
 
 def store_blocks(refs, value):
-    for index, ref in enumerate(refs):
-        ref[...] = value[index * CAP_DEV : (index + 1) * CAP_DEV, :].astype(ref.dtype)
-
-
-def load_blocks(refs):
-    return jnp.concatenate([ref[...].astype(jnp.float32) for ref in refs], axis=0)
+    top = 0
+    for ref in refs:
+        ref[...] = value[top : top + ref.shape[0], :].astype(ref.dtype)
+        top += ref.shape[0]
+
+
+def load_blocks(refs, half=None):
+    values = [ref[...].astype(jnp.float32) for ref in refs]
+    if half is not None:
+        values = [v[half * CAP_DEV : (half + 1) * CAP_DEV, :] for v in values]
+    return jnp.concatenate(values, axis=0)
 
 
 def dispatch_kernel(per_device, steps, *refs):
     tokens_hbm, *small_hbm = refs[:6]
-    tokens_ref, gain_ref, local_ref, *out_refs = refs[6 : 9 + len(steps)]
-    experts_ref, keys_ref, slot_ref, cap_ref, arrived = refs[9 + len(steps) :]
+    tokens_ref, gain_ref, local_ref, *out_refs = refs[6:11]
+    experts_ref, keys_ref, slot_ref, cap_ref, arrived = refs[11:]
     small_refs = (experts_ref, keys_ref, slot_ref, cap_ref, gain_ref)
     copies = [
         pltpu.make_async_copy(source, target, arrived.at[index])
@@ -129,23 +134,23 @@
     store_blocks(out_refs, jnp.dot(pick, normed, preferred_element_type=jnp.float32))
 
 
-def near_kernel(
-    per_device, groups, steps, tokens_ref, gain_ref, local_ref, *out_refs
-):
+def near_kernel(per_device, groups, steps, tokens_ref, gain_ref, local_ref, *out_refs):
     gain = gain_ref[...].astype(jnp.float32)
     width = tokens_ref.shape[1] // groups
     group = lax.axis_index("dp")
     scale = row_scale(tokens_ref[...].astype(jnp.float32))
-    pick = pick_rows(local_ref, None, steps, per_device).astype(jnp.bfloat16)
+    pick = pick_rows(local_ref, None, sum(steps, ()), per_device).astype(jnp.bfloat16)
     for step in range(groups):
         start = pl.multiple_of((group ^ step) * width, width)
         part = tokens_ref[:, pl.ds(start, width)].astype(jnp.float32)
         normed = apply_gain(part * scale, gain, (group ^ step) * (width // 128))
         value = jnp.dot(pick, normed, preferred_element_type=jnp.float32)
-        for index, ref in enumerate(out_refs):
+        top = 0
+        for ref in out_refs:
             ref[:, step * width : (step + 1) * width] = value[
-                index * CAP_DEV : (index + 1) * CAP_DEV, :
+                top : top + ref.shape[0], :
             ].astype(ref.dtype)
+            top += ref.shape[0]
 
 
 def weight_kernel(
@@ -184,7 +189,7 @@
     out_ref[...] = weights.T.astype(jnp.bfloat16)
 
 
-def split_kernel(halves, groups, in_hbm, out_ref, in_ref, arrived):
+def split_kernel(halves, groups, steps, in_hbm, out_ref, in_ref, arrived):
     tile = 256
     kinds = 2 * halves
     per_tile = tile // kinds
@@ -192,11 +197,11 @@
     part = length // groups
     group = lax.axis_index("dp")
     copies = []
-    for step in range(groups):
+    for place, step in enumerate(steps):
         base = pl.multiple_of((group ^ step) * part, part)
         copies.append(
             pltpu.make_async_copy(
-                in_hbm.at[:, pl.ds(base, part), :], in_ref.at[step], arrived.at[step]
+                in_hbm.at[:, pl.ds(base, part), :], in_ref.at[place], arrived.at[place]
             )
         )
         copies[-1].start()
@@ -205,13 +210,13 @@
     column = to_row // per_tile
     source = (to_row % per_tile) * kinds + (column % halves) * 2 + column // halves
     order = jnp.where(source == from_row, 1.0, 0.0).astype(jnp.bfloat16)
-    for step in range(groups):
-        copies[step].wait()
+    for place in range(len(steps)):
+        copies[place].wait()
         for slot in range(slots):
             for index in range(0, part // tile, 2):
                 low = index * tile
                 pair = [
-                    in_ref[step, slot, low + side * tile : low + (side + 1) * tile, :]
+                    in_ref[place, slot, low + side * tile : low + (side + 1) * tile, :]
                     for side in range(2)
                 ]
                 moved = jnp.dot(
@@ -223,7 +228,7 @@
                     top = (index + side) * per_tile
                     for kind in range(kinds):
                         left = (slot * kinds + kind) * 128
-                        out_ref[step, top : top + per_tile, left : left + 128] = moved[
+                        out_ref[place, top : top + per_tile, left : left + 128] = moved[
                             kind * per_tile : (kind + 1) * per_tile,
                             side * 128 : (side + 1) * 128,
                         ]
@@ -268,9 +273,16 @@
         ).astype(ref.dtype)
 
 
-def far_kernel(
-    per_device, sum_ref, last_ref, weight_ref, cap_ref, down_ref, *out_refs
-):
+def product_kernel(index, rows_ref, weight_ref, *refs):
+    value = jnp.dot(
+        rows_ref[...], weight_ref[index], preferred_element_type=jnp.float32
+    )
+    for ref in refs[:-1]:
+        value = value + ref[...]
+    refs[-1][...] = value
+
+
+def far_kernel(per_device, sum_ref, last_ref, weight_ref, cap_ref, down_ref, *out_refs):
     gate_up = sum_ref[...] + jnp.dot(
         last_ref[...],
         weight_ref[weight_ref.shape[0] - 1],
@@ -279,15 +291,24 @@
     finish_rows(gate_up, cap_ref, down_ref, out_refs, per_device)
 
 
-def near_expert_kernel(per_device, count, *refs):
-    row_refs, (weight_ref, cap_ref, down_ref, *out_refs) = refs[:count], refs[count:]
-    rows = load_blocks(row_refs).astype(jnp.bfloat16)
-    width = weight_ref.shape[1]
+def near_expert_kernel(
+    per_device, own_ref, core_ref, chip_ref, first_ref, second_ref, cap_ref, down_ref, *out_refs
+):
+    rows = jnp.concatenate(
+        [load_blocks([own_ref]), load_blocks([core_ref], 0), load_blocks([chip_ref])],
+        axis=0,
+    ).astype(jnp.bfloat16)
+    width = first_ref.shape[1]
     gate_up = None
-    for step in range(weight_ref.shape[0]):
+    for index in range(first_ref.shape[0] + second_ref.shape[0]):
+        weight = (
+            first_ref[index]
+            if index < first_ref.shape[0]
+            else second_ref[index - first_ref.shape[0]]
+        )
         term = jnp.dot(
-            rows[:, step * width : (step + 1) * width],
-            weight_ref[step],
+            rows[:, index * width : (index + 1) * width],
+            weight,
             preferred_element_type=jnp.float32,
         )
         gate_up = term if gate_up is None else gate_up + term
@@ -296,6 +317,23 @@
 
 def join_kernel(*refs):
     refs[-1][...] = load_blocks(refs[:-1]).astype(refs[-1].dtype)
+
+
+def pair_kernel(same_ref, core_ref, *out_refs):
+    same, core = load_blocks([same_ref]), load_blocks([core_ref])
+    for index, ref in enumerate(out_refs):
+        rows = slice(index * CAP_DEV, (index + 1) * CAP_DEV)
+        ref[...] = jnp.concatenate([same[rows], core[rows]], axis=0).astype(ref.dtype)
+
+
+def forward_kernel(same_ref, core_ref, out_ref):
+    out_ref[...] = jnp.concatenate(
+        [load_blocks([same_ref]), load_blocks([core_ref], 1)], axis=0
+    ).astype(out_ref.dtype)
+
+
+def flip_kernel(*refs):
+    refs[-1][...] = load_blocks(refs[:-1], 1).astype(refs[-1].dtype)
 
 
 def sum_kernel(count, *refs):
@@ -305,12 +343,21 @@
     store_blocks(refs[count:], total)
 
 
-def combine_kernel(count, weight_ref, residual_ref, *refs):
-    rows = load_blocks(refs[:count]).astype(jnp.bfloat16)
-    mixture = jnp.dot(weight_ref[...], rows, preferred_element_type=jnp.float32)
-    refs[count][...] = (residual_ref[...].astype(jnp.float32) + mixture).astype(
-        jnp.bfloat16
-    )
+def combine_kernel(weight_ref, residual_ref, *refs):
+    rows = load_blocks(refs[:-1], 0).astype(jnp.bfloat16)
+    mixture = jnp.dot(
+        weight_ref[:, : rows.shape[0]], rows, preferred_element_type=jnp.float32
+    )
+    refs[-1][...] = residual_ref[...].astype(jnp.float32) + mixture
+
+
+def finish_kernel(weight_ref, sum_ref, core_ref, out_ref):
+    mixture = jnp.dot(
+        weight_ref[:, core_ref.shape[0] :],
+        core_ref[...],
+        preferred_element_type=jnp.float32,
+    )
+    out_ref[...] = (sum_ref[...] + mixture).astype(jnp.bfloat16)
 
 
 def call(kernel, name, outs, *args, scratch=(), in_hbm=False, after=()):
@@ -327,6 +374,7 @@
         out_shape=outs,
         scratch_shapes=scratch,
         compiler_params=pltpu.CompilerParams(vmem_limit_bytes=size + (8 << 20)),
+        cost_estimate=pl.CostEstimate(flops=1, bytes_accessed=1, transcendentals=0),
         name=name,
     )(*after, *args)
 
@@ -349,8 +397,7 @@
     per_device = slots // peers
     units = slot_gate_up_weight.shape[3]
     quarter = width // groups
-    near = range(min(NEAR, peers))
-    far = range(len(near), peers)
+    chips = peers // 2
 
     def blocks(count, *shape, dtype=jnp.bfloat16):
         return [jax.ShapeDtypeStruct(shape, dtype)] * count
@@ -366,13 +413,15 @@
     cap_row = capacity.reshape(1, slots)
     down = down_weight.reshape(per_device * units, width)
 
-    tokens_here, gain_here, local, *far_out = call(
-        functools.partial(dispatch_kernel, per_device, far),
+    tokens_here, gain_here, local, far_same, far_flip = call(
+        functools.partial(
+            dispatch_kernel, per_device, [*range(4, peers, 2), *range(5, peers, 2)]
+        ),
         "dispatch",
         blocks(1, rows, width)
         + blocks(1, *gain.shape)
         + blocks(1, slots, rows, dtype=jnp.float32)
-        + blocks(len(far), CAP_DEV, quarter),
+        + blocks(2, (chips - 2) * CAP_DEV, quarter),
         tokens,
         experts.T,
         replica_key.T,
@@ -388,68 +437,104 @@
         ],
         in_hbm=True,
     )
-    far_in = [to_peer(value, step) for value, step in zip(far_out[::-1], far[::-1])]
+    core_far = to_peer(far_flip, 1)
+    own_rows, same_rows, flip_rows = call(
+        functools.partial(near_kernel, per_device, groups, ((0,), (2,), (1, 3))),
+        "dispatch_near",
+        blocks(2, CAP_DEV, width) + blocks(1, 2 * CAP_DEV, width),
+        tokens_here,
+        gain_here,
+        local,
+    )
+    core_rows = to_peer(flip_rows, 1)
+    far_out = call(
+        pair_kernel,
+        "pair_far",
+        blocks(chips - 2, 2 * CAP_DEV, quarter),
+        far_same,
+        core_far,
+    )
+    far_in = [
+        to_peer(value, 2 * chip) for chip, value in reversed([*enumerate(far_out, 2)])
+    ]
+    (chip_rows,) = call(
+        forward_kernel,
+        "forward_near",
+        blocks(1, 2 * CAP_DEV, width),
+        same_rows,
+        core_rows,
+        after=(far_out[0],),
+    )
+    near_ready = chip_rows
+    chip_rows = to_peer(chip_rows, 2)
 
     halves = units // 128
     split_in = slot_gate_up_weight.reshape(per_device, width, 2, halves, 128)
     split_in = split_in.transpose(0, 1, 3, 2, 4)
     split_in = split_in.reshape(per_device, width * halves * 2, 128)
-    (gate_up,) = call(
-        functools.partial(split_kernel, halves, groups),
-        "split_gate_up",
-        blocks(1, groups, quarter, per_device * 2 * units),
-        split_in,
-        scratch=[
-            pltpu.VMEM(
-                (groups, per_device, quarter * halves * 2, 128), jnp.bfloat16
-            ),
-            pltpu.SemaphoreType.DMA((groups,)),
-        ],
-        in_hbm=True,
-        after=(local,),
-    )
-
+    half = groups // 2
+
+    def split(steps, after):
+        return call(
+            functools.partial(split_kernel, halves, groups, steps),
+            "split_gate_up",
+            blocks(1, len(steps), quarter, per_device * 2 * units),
+            split_in,
+            scratch=[
+                pltpu.VMEM(
+                    (len(steps), per_device, quarter * halves * 2, 128), jnp.bfloat16
+                ),
+                pltpu.SemaphoreType.DMA((len(steps),)),
+            ],
+            in_hbm=True,
+            after=after,
+        )[0]
+
+    first_weights = split(range(half), (near_ready,))
     (far_rows,) = call(
         join_kernel,
         "join_far",
-        blocks(1, len(far) * CAP_DEV, quarter),
+        blocks(1, (peers - NEAR) * CAP_DEV, quarter),
         *far_in[::-1],
-        after=(gate_up,),
-    )
-    near_out = call(
-        functools.partial(near_kernel, per_device, groups, near),
-        "dispatch_near",
-        blocks(len(near), CAP_DEV, width),
-        tokens_here,
-        gain_here,
-        local,
-        after=(far_rows,),
-    )
-    near_in = [near_out[0]] + [to_peer(near_out[step], step) for step in near[1:]]
+        after=(first_weights,),
+    )
+    second_weights = split(range(half, groups), (far_rows,))
 
     far_parts = [far_rows] + [to_group(far_rows, step) for step in range(1, groups)]
-    far_sum = None
+    far_sum = ()
     for step in range(groups - 1):
-        term = jnp.dot(
-            far_parts[step], gate_up[step], preferred_element_type=jnp.float32
-        )
-        far_sum = term if far_sum is None else far_sum + term
+        weights, index = (
+            (first_weights, step) if step < half else (second_weights, step - half)
+        )
+        far_sum = call(
+            functools.partial(product_kernel, index),
+            "product_far",
+            blocks(
+                1, far_rows.shape[0], per_device * 2 * units, dtype=jnp.float32
+            ),
+            far_parts[step],
+            weights,
+            *far_sum,
+        )
     far_partials = call(
         functools.partial(far_kernel, per_device),
         "expert_far",
-        blocks(groups, len(far) * CAP_DEV, quarter),
-        far_sum,
+        blocks(groups, (peers - NEAR) * CAP_DEV, quarter),
+        *far_sum,
         far_parts[-1],
-        gate_up,
+        second_weights,
         cap_row,
         down,
     )
     near_partials = call(
-        functools.partial(near_expert_kernel, per_device, len(near)),
+        functools.partial(near_expert_kernel, per_device),
         "expert_near",
-        blocks(groups, len(near) * CAP_DEV, quarter),
-        *near_in,
-        gate_up,
+        blocks(groups, NEAR * CAP_DEV, quarter),
+        own_rows,
+        core_rows,
+        chip_rows,
+        first_weights,
+        second_weights,
         cap_row,
         down,
         after=(far_partials[1],),
@@ -460,19 +545,26 @@
         return call(
             functools.partial(sum_kernel, groups),
             name,
-            blocks(count, CAP_DEV, quarter),
+            blocks(count, 2 * CAP_DEV, quarter),
             partials[0],
             *received,
             after=after,
         )
 
-    far_back = reduce_groups(far_partials, "sum_far", len(far))
-    near_back = reduce_groups(near_partials, "sum_near", len(near), far_back[:1])
-    far_back = [to_peer(value, step) for value, step in zip(far_back[::-1], far[::-1])]
-    near_back = [near_back[0]] + [to_peer(near_back[step], step) for step in near[1:]]
-
+    far_back = reduce_groups(far_partials, "sum_far", chips - 2)
+    near_back = reduce_groups(near_partials, "sum_near", 2, far_back[:1])
+    far_back = [
+        to_peer(value, 2 * chip) for chip, value in reversed([*enumerate(far_back, 2)])
+    ]
+    back = [near_back[0], to_peer(near_back[1], 2), *far_back[::-1]]
+    (flip_back,) = call(
+        flip_kernel, "flip_back", blocks(1, chips * CAP_DEV, quarter), *back
+    )
+    core_back = to_peer(flip_back, 1)
+
+    order = [*range(0, peers, 2), *range(1, peers, 2)]
     weights, residual = call(
-        functools.partial(weight_kernel, per_device, range(peers)),
+        functools.partial(weight_kernel, per_device, order),
         "combine_weights",
         blocks(1, rows, peers * CAP_DEV) + blocks(1, rows, quarter),
         tokens_here,
@@ -482,14 +574,16 @@
         local,
         scratch=[pltpu.VMEM((slots, rows), jnp.float32)],
     )
-    (mixed,) = call(
-        functools.partial(combine_kernel, peers),
+    (mixed_half,) = call(
+        combine_kernel,
         "combine",
-        blocks(1, rows, quarter),
+        blocks(1, rows, quarter, dtype=jnp.float32),
         weights,
         residual,
-        *near_back,
-        *far_back[::-1],
+        *back,
+    )
+    (mixed,) = call(
+        finish_kernel, "finish", blocks(1, rows, quarter), weights, mixed_half, core_back
     )
     return mixed
 

time: 46.1 us -> 42.5 us (0.922)
  waiting for transfers between devices: 12.4 us -> 8.79 us
  Pallas kernels: 8.69 us -> 11.1 us
  starting transfers between devices: 23.7 us -> 22.3 us
  matrix products: 0.92 us -> 0 us
    ppermute x9, waiting for transfers between devices: 7.58 us -> 2.31 us  [to_group(): return lax.ppermute(value, 'dp', [(i, i ^ step) for i in range(groups)])]
    pallas_call x10 -> x18, Pallas kernels: 8.69 us -> 11.1 us  [call(): pl.pallas_call(lambda *refs: kernel(*refs[count:]), in_specs=[pl.BlockSpe...]
    ppermute x14 -> x9, waiting for transfers between devices: 4.83 us -> 6.48 us  [to_peer(): return lax.ppermute(value, 'expert', [(i, i ^ step) for i in range(peers)])]
    ppermute x14 -> x9, starting transfers between devices: 13 us -> 11.6 us  [to_peer(): return lax.ppermute(value, 'expert', [(i, i ^ step) for i in range(peers)])]
    dot_general x3 -> x0, matrix products: 0.92 us -> none  [on_device(): jnp.dot(far_parts[step], gate_up[step], preferred_element_type=jnp.float32)]
  transfers between devices with their start and end apart: 23 -> 18, of which waited for: 9 -> 9; matrix products, arithmetic and copies ran while one was open for 2% -> 0% of each run, Pallas kernels for 14% -> 19%
where the time goes in v4:
time: 42.5 us; the launch traced here: 42.3 us
  starting transfers between devices  22.3 us (52%)
  Pallas kernels  11.1 us (26%)
  waiting for transfers between devices  8.79 us (21%)
    ppermute x9, starting transfers between devices, to_peer(): return lax.ppermute(value, 'expert', [(i, i ^ step) for i in range(peers)])  11.6 us
    pallas_call x18, Pallas kernels, call(): pl.pallas_call(lambda *refs: kernel(*refs[count:]), in_specs=[pl.BlockSpe...  11.1 us
    ppermute x9, starting transfers between devices, to_group(): return lax.ppermute(value, 'dp', [(i, i ^ step) for i in range(groups)])  10.7 us
    ppermute x9, waiting for transfers between devices, to_peer(): return lax.ppermute(value, 'expert', [(i, i ^ step) for i in range(peers)])  6.48 us
    ppermute x9, waiting for transfers between devices, to_group(): return lax.ppermute(value, 'dp', [(i, i ^ step) for i in range(groups)])  2.31 us
  transfers between devices with their start and end apart: 18, of which 9 were waited for; matrix products, arithmetic and copies ran while one was open for 0% of the time, Pallas kernels for 19%

profile of v4, /device:TPU:0, one launch (start us, length us, event | category | flops | bytes accessed | tf_op | source)
XLA Modules:
  0.0 42.3 jit_solution(2533195783781501216)
XLA Ops:
  0.0 1.5 %dispatch.1 = (bf16[128,2048]{1,0:T(8,128)(2,1)S(1)}, bf16[16,128]{1,0:T(8,128)(2,1)S(1)}, f32[16,128]{1,0:T(8,128)S(1)}, bf16[48,512]{1,0:T(8,128)(2,1)S(1)}, bf16[48,512]{1,0:T(8,128)(2,1)S(1)}) custom-call(bf16[128,2048]{1,0:T(8,128)(2,1)} %refs_0_.1, s32[8,128]{1,0:T(8,128)} %bitcast.22, s32[8,128]{1,0:T(8,128)} %bitcast.23, s32[1,16]{1,0:T(1,128)} %bitcast.18, ...), custom_call_target="tpu_custom_call" | custom-call | flops 1 | bytes 1 | tf_op jit(solution)/shard_map/dispatch/pallas_call | solution.py:369
  1.5 0.4 %dispatch_near.1 = (bf16[24,2048]{1,0:T(8,128)(2,1)S(1)}, bf16[24,2048]{1,0:T(8,128)(2,1)S(1)}, bf16[48,2048]{1,0:T(8,128)(2,1)S(1)}) custom-call(bf16[128,2048]{1,0:T(8,128)(2,1)S(1)} %get-tuple-element.29.refs_0_, bf16[16,128]{1,0:T(8,128)(2,1)S(1)} %get-tuple-element.30.refs_1_, f32[16,128]{1,0:T(8,128)S(1)} %get-tuple-element.31.refs_4_.refs_2_), custom_call_target="tpu_custom_call" | custom-call | flops 1 | bytes 1 | tf_op jit(solution)/shard_map/dispatch_near/pallas_call | solution.py:369
  2.0 0.5 %collective-permute-start.1 = (bf16[48,2048]{1,0:T(8,128)(2,1)S(1)}, bf16[48,2048]{1,0:T(8,128)(2,1)S(1)}, u32[]{:S(2)}, u32[]{:S(2)}) collective-permute-start(bf16[48,2048]{1,0:T(8,128)(2,1)S(1)} %get-tuple-element.38), channel_id=1, source_target_pairs={{0,1},{1,0},{2,3},{3,2},{4,5},{5,4},{6,7},{7,6},{8,9},{9,8},{10,11... | collective-permute-start | bytes 589832 | tf_op jit(solution)/shard_map/ppermute | solution.py:409
  2.5 0.1 collective-permute-start
  2.6 1.2 %collective-permute-done.refs_1_ = bf16[48,512]{1,0:T(8,128)(2,1)S(1)} collective-permute-done((bf16[48,512]{1,0:T(8,128)(2,1)S(1)}, bf16[48,512]{1,0:T(8,128)(2,1)S(1)}, u32[]{:S(2)}, u32[]{:S(2)}) %collective-permute-start) | collective-permute-done | bytes 49184 | tf_op jit(solution)/shard_map/ppermute | solution.py:409
  3.7 4.9 %collective-permute-start.3 = (bf16[48,512]{1,0:T(8,128)(2,1)S(1)}, bf16[48,512]{1,0:T(8,128)(2,1)S(1)}, u32[]{:S(2)}, u32[]{:S(2)}) collective-permute-start(bf16[48,512]{1,0:T(8,128)(2,1)S(1)} %get-tuple-element.39), channel_id=1, source_target_pairs={{0,6},{1,7},{2,4},{3,5},{4,2},{5,3},{6,0},{7,1},{8,14},{9,15},{10,... | collective-permute-start | bytes 147464 | tf_op jit(solution)/shard_map/ppermute | solution.py:409
  8.7 0.0 collective-permute-start.2
  8.7 2.3 %split_gate_up.2.refs_0_.refs_1_.refs_4_ = bf16[2,512,1024]{2,1,0:T(8,128)(2,1)S(1)} custom-call(bf16[48,2048]{1,0:T(8,128)(2,1)S(1)} %forward_near.1.refs_0_, bf16[2,8192,128]{2,1,0:T(8,128)(2,1)} %bitcast.20), custom_call_target="tpu_custom_call" | custom-call | flops 1 | bytes 1 | tf_op jit(solution)/shard_map/split_gate_up/pallas_call | solution.py:369
  11.0 0.0 collective-permute-done.3.refs_2_
  11.0 2.7 %collective-permute-done.2.refs_1_ = bf16[48,512]{1,0:T(8,128)(2,1)S(1)} collective-permute-done((bf16[48,512]{1,0:T(8,128)(2,1)S(1)}, bf16[48,512]{1,0:T(8,128)(2,1)S(1)}, u32[]{:S(2)}, u32[]{:S(2)}) %collective-permute-start.2) | collective-permute-done | bytes 49184 | tf_op jit(solution)/shard_map/ppermute | solution.py:409
  13.7 1.6 %collective-permute-start.5 = (bf16[96,512]{1,0:T(8,128)(2,1)S(1)}, bf16[96,512]{1,0:T(8,128)(2,1)S(1)}, u32[]{:S(2)}, u32[]{:S(2)}) collective-permute-start(bf16[96,512]{1,0:T(8,128)(2,1)S(1)} %join_far.1.refs_0_), channel_id=1, source_target_pairs={{0,8},{8,0},{16,24},{24,16},{1,9},{9,1},{17,25},{25,17},{2,10},{10... | collective-permute-start | bytes 294920 | tf_op jit(solution)/shard_map/ppermute | solution.py:406
  15.3 1.5 %collective-permute-start.4 = (bf16[96,512]{1,0:T(8,128)(2,1)S(1)}, bf16[96,512]{1,0:T(8,128)(2,1)S(1)}, u32[]{:S(2)}, u32[]{:S(2)}) collective-permute-start(bf16[96,512]{1,0:T(8,128)(2,1)S(1)} %join_far.1.refs_0_), channel_id=1, source_target_pairs={{0,16},{8,24},{16,0},{24,8},{1,17},{9,25},{17,1},{25,9},{2,18},{10... | collective-permute-start | bytes 294920 | tf_op jit(solution)/shard_map/ppermute | solution.py:406
  16.8 0.5 %collective-permute-start.6 = (bf16[96,512]{1,0:T(8,128)(2,1)S(1)}, bf16[96,512]{1,0:T(8,128)(2,1)S(1)}, u32[]{:S(2)}, u32[]{:S(2)}) collective-permute-start(bf16[96,512]{1,0:T(8,128)(2,1)S(1)} %join_far.1.refs_0_), channel_id=1, source_target_pairs={{0,24},{8,16},{16,8},{24,0},{1,25},{9,17},{17,9},{25,1},{2,26},{10... | collective-permute-start | bytes 294920 | tf_op jit(solution)/shard_map/ppermute | solution.py:406
  17.3 0.3 product_far.3.refs_2_
  17.6 2.3 %split_gate_up.3.refs_1_.refs_2_.refs_5_ = bf16[2,512,1024]{2,1,0:T(8,128)(2,1)S(1)} custom-call(bf16[96,512]{1,0:T(8,128)(2,1)S(1)} %join_far.1.refs_0_, bf16[2,8192,128]{2,1,0:T(8,128)(2,1)} %bitcast.21), custom_call_target="tpu_custom_call" | custom-call | flops 1 | bytes 1 | tf_op jit(solution)/shard_map/split_gate_up/pallas_call | solution.py:369
  19.9 0.3 product_far.4.refs_2_
  20.2 0.0 copy-start
  20.2 0.0 copy-start.2
  20.2 0.7 %collective-permute-done.4.refs_0_ = bf16[96,512]{1,0:T(8,128)(2,1)S(1)} collective-permute-done((bf16[96,512]{1,0:T(8,128)(2,1)S(1)}, bf16[96,512]{1,0:T(8,128)(2,1)S(1)}, u32[]{:S(2)}, u32[]{:S(2)}) %collective-permute-start.4) | collective-permute-done | bytes 98336 | tf_op jit(solution)/shard_map/ppermute | solution.py:406
  21.0 0.3 product_far.5.refs_0_
  21.3 1.1 %collective-permute-done.6.refs_1_ = bf16[96,512]{1,0:T(8,128)(2,1)S(1)} collective-permute-done((bf16[96,512]{1,0:T(8,128)(2,1)S(1)}, bf16[96,512]{1,0:T(8,128)(2,1)S(1)}, u32[]{:S(2)}, u32[]{:S(2)}) %collective-permute-start.6) | collective-permute-done | bytes 98336 | tf_op jit(solution)/shard_map/ppermute | solution.py:406
  22.3 0.7 %expert_far.1 = (bf16[96,512]{1,0:T(8,128)(2,1)S(1)}, bf16[96,512]{1,0:T(8,128)(2,1)S(1)}, bf16[96,512]{1,0:T(8,128)(2,1)S(1)}, bf16[96,512]{1,0:T(8,128)(2,1)S(1)}) custom-call(f32[96,1024]{1,0:T(8,128)S(1)} %product_far.5.refs_0_, bf16[96,512]{1,0:T(8,128)(2,1)S(1)} %collective-permute-done.6.refs_1_, ...), custom_call_target="tpu_custom_call" | custom-call | flops 1 | bytes 1 | tf_op jit(solution)/shard_map/expert_far/pallas_call | solution.py:369
  23.0 1.1 %collective-permute-start.8 = (bf16[96,512]{1,0:T(8,128)(2,1)S(1)}, bf16[96,512]{1,0:T(8,128)(2,1)S(1)}, u32[]{:S(2)}, u32[]{:S(2)}) collective-permute-start(bf16[96,512]{1,0:T(8,128)(2,1)S(1)} %get-tuple-element.42), channel_id=1, source_target_pairs={{0,16},{8,24},{16,0},{24,8},{1,17},{9,25},{17,1},{25,9},{2,18},{10... | collective-permute-start | bytes 294920 | tf_op jit(solution)/shard_map/ppermute | solution.py:406
  24.2 1.4 %collective-permute-start.9 = (bf16[96,512]{1,0:T(8,128)(2,1)S(1)}, bf16[96,512]{1,0:T(8,128)(2,1)S(1)}, u32[]{:S(2)}, u32[]{:S(2)}) collective-permute-start(bf16[96,512]{1,0:T(8,128)(2,1)S(1)} %get-tuple-element.43), channel_id=1, source_target_pairs={{0,24},{8,16},{16,8},{24,0},{1,25},{9,17},{17,9},{25,1},{2,26},{10... | collective-permute-start | bytes 294920 | tf_op jit(solution)/shard_map/ppermute | solution.py:406
  25.5 1.1 %collective-permute-start.7 = (bf16[96,512]{1,0:T(8,128)(2,1)S(1)}, bf16[96,512]{1,0:T(8,128)(2,1)S(1)}, u32[]{:S(2)}, u32[]{:S(2)}) collective-permute-start(bf16[96,512]{1,0:T(8,128)(2,1)S(1)} %get-tuple-element.41.refs_0_), channel_id=1, source_target_pairs={{0,8},{8,0},{16,24},{24,16},{1,9},{9,1},{17,25},{25,17},{2,10},{10... | collective-permute-start | bytes 294920 | tf_op jit(solution)/shard_map/ppermute | solution.py:406
  26.6 0.0 collective-permute-done.10.refs_3_
  26.6 1.2 %expert_near.1 = (bf16[96,512]{1,0:T(8,128)(2,1)S(1)}, bf16[96,512]{1,0:T(8,128)(2,1)S(1)}, bf16[96,512]{1,0:T(8,128)(2,1)S(1)}, bf16[96,512]{1,0:T(8,128)(2,1)S(1)}) custom-call(bf16[96,512]{1,0:T(8,128)(2,1)S(1)} %get-tuple-element.41.refs_0_, bf16[24,2048]{1,0:T(8,128)(2,1)S(1)} %get-tuple-element.45.refs_1_, ...), custom_call_target="tpu_custom_call" | custom-call | flops 1 | bytes 1 | tf_op jit(solution)/shard_map/expert_near/pallas_call | solution.py:369
  27.8 1.0 %collective-permute-start.11 = (bf16[96,512]{1,0:T(8,128)(2,1)S(1)}, bf16[96,512]{1,0:T(8,128)(2,1)S(1)}, u32[]{:S(2)}, u32[]{:S(2)}) collective-permute-start(bf16[96,512]{1,0:T(8,128)(2,1)S(1)} %get-tuple-element.47), channel_id=1, source_target_pairs={{0,8},{8,0},{16,24},{24,16},{1,9},{9,1},{17,25},{25,17},{2,10},{10... | collective-permute-start | bytes 294920 | tf_op jit(solution)/shard_map/ppermute | solution.py:406
  28.8 1.5 %collective-permute-start.12 = (bf16[96,512]{1,0:T(8,128)(2,1)S(1)}, bf16[96,512]{1,0:T(8,128)(2,1)S(1)}, u32[]{:S(2)}, u32[]{:S(2)}) collective-permute-start(bf16[96,512]{1,0:T(8,128)(2,1)S(1)} %get-tuple-element.48), channel_id=1, source_target_pairs={{0,16},{8,24},{16,0},{24,8},{1,17},{9,25},{17,1},{25,9},{2,18},{10... | collective-permute-start | bytes 294920 | tf_op jit(solution)/shard_map/ppermute | solution.py:406
  30.4 0.0 collective-permute-done.8.refs_2_
  30.4 1.0 %collective-permute-start.13 = (bf16[96,512]{1,0:T(8,128)(2,1)S(1)}, bf16[96,512]{1,0:T(8,128)(2,1)S(1)}, u32[]{:S(2)}, u32[]{:S(2)}) collective-permute-start(bf16[96,512]{1,0:T(8,128)(2,1)S(1)} %get-tuple-element.49), channel_id=1, source_target_pairs={{0,24},{8,16},{16,8},{24,0},{1,25},{9,17},{17,9},{25,1},{2,26},{10... | collective-permute-start | bytes 294920 | tf_op jit(solution)/shard_map/ppermute | solution.py:406
  31.4 0.3 collective-permute-done.7.refs_1_
  31.7 0.1 sum_far.1
  31.7 2.5 %collective-permute-start.16 = (bf16[48,512]{1,0:T(8,128)(2,1)S(1)}, bf16[48,512]{1,0:T(8,128)(2,1)S(1)}, u32[]{:S(2)}, u32[]{:S(2)}) collective-permute-start(bf16[48,512]{1,0:T(8,128)(2,1)S(1)} %get-tuple-element.52), channel_id=1, source_target_pairs={{0,6},{1,7},{2,4},{3,5},{4,2},{5,3},{6,0},{7,1},{8,14},{9,15},{10,... | collective-permute-start | bytes 147464 | tf_op jit(solution)/shard_map/ppermute | solution.py:409
  34.2 1.4 %collective-permute-start.15 = (bf16[48,512]{1,0:T(8,128)(2,1)S(1)}, bf16[48,512]{1,0:T(8,128)(2,1)S(1)}, u32[]{:S(2)}, u32[]{:S(2)}) collective-permute-start(bf16[48,512]{1,0:T(8,128)(2,1)S(1)} %get-tuple-element.44.refs_0_), channel_id=1, source_target_pairs={{0,4},{1,5},{2,6},{3,7},{4,0},{5,1},{6,2},{7,3},{8,12},{9,13},{10,... | collective-permute-start | bytes 147464 | tf_op jit(solution)/shard_map/ppermute | solution.py:409
  35.7 0.0 collective-permute-done.11.refs_2_
  35.7 0.0 collective-permute-done.12.refs_3_
  35.7 0.2 collective-permute-done.13.refs_4_
  35.9 0.1 sum_near.1
  35.9 2.1 %collective-permute-start.14 = (bf16[48,512]{1,0:T(8,128)(2,1)S(1)}, bf16[48,512]{1,0:T(8,128)(2,1)S(1)}, u32[]{:S(2)}, u32[]{:S(2)}) collective-permute-start(bf16[48,512]{1,0:T(8,128)(2,1)S(1)} %get-tuple-element.51), channel_id=1, source_target_pairs={{0,2},{1,3},{2,0},{3,1},{4,6},{5,7},{6,4},{7,5},{8,10},{9,11},{10,... | collective-permute-start | bytes 147464 | tf_op jit(solution)/shard_map/ppermute | solution.py:409
  38.0 0.0 collective-permute-done.16.refs_5_.refs_3_
  38.0 1.2 %collective-permute-done.15.refs_4_.refs_2_ = bf16[48,512]{1,0:T(8,128)(2,1)S(1)} collective-permute-done((bf16[48,512]{1,0:T(8,128)(2,1)S(1)}, bf16[48,512]{1,0:T(8,128)(2,1)S(1)}, u32[]{:S(2)}, u32[]{:S(2)}) %collective-permute-start.15) | collective-permute-done | bytes 49184 | tf_op jit(solution)/shard_map/ppermute | solution.py:409
  39.2 0.9 %collective-permute-done.14.refs_3_.refs_1_ = bf16[48,512]{1,0:T(8,128)(2,1)S(1)} collective-permute-done((bf16[48,512]{1,0:T(8,128)(2,1)S(1)}, bf16[48,512]{1,0:T(8,128)(2,1)S(1)}, u32[]{:S(2)}, u32[]{:S(2)}) %collective-permute-start.14) | collective-permute-done | bytes 49184 | tf_op jit(solution)/shard_map/ppermute | solution.py:409
  40.1 0.1 collective-permute-start.17
  40.2 0.5 %combine_weights.1 = (bf16[128,192]{1,0:T(8,128)(2,1)S(1)}, bf16[128,512]{1,0:T(8,128)(2,1)S(1)}) custom-call(bf16[128,2048]{1,0:T(8,128)(2,1)S(1)} %get-tuple-element.29.refs_0_, bf16[16,128]{1,0:T(8,128)(2,1)S(1)} %get-tuple-element.30.refs_1_, bf16[8,2048]{1,0:T(8,128)(2,1)S(1)} %bitcast.14, s32[1,16]{1,0:T(1,128)S(1)} %bitcast.19, ...), custom_call_target="tpu_custom_call" | custom-call | flops 1 | bytes 1 | tf_op jit(solution)/shard_map/combine_weights/pallas_call | solution.py:369
  40.7 0.2 combine.1.refs_1_
  40.9 0.5 %collective-permute-done.17.refs_2_ = bf16[96,512]{1,0:T(8,128)(2,1)S(1)} collective-permute-done((bf16[96,512]{1,0:T(8,128)(2,1)S(1)}, bf16[96,512]{1,0:T(8,128)(2,1)S(1)}, u32[]{:S(2)}, u32[]{:S(2)}) %collective-permute-start.17) | collective-permute-done | bytes 98336 | tf_op jit(solution)/shard_map/ppermute | solution.py:409
  41.5 0.9 %finish.1 = bf16[128,512]{1,0:T(8,128)(2,1)} custom-call(bf16[128,192]{1,0:T(8,128)(2,1)S(1)} %get-tuple-element.32.refs_0_, f32[128,512]{1,0:T(8,128)S(1)} %combine.1.refs_1_, bf16[96,512]{1,0:T(8,128)(2,1)S(1)} %collective-permute-done.17.refs_2_), custom_call_target="tpu_custom_call" | custom-call | flops 1 | bytes 1 | tf_op jit(solution)/shard_map/finish/pallas_call | solution.py:369
  (14 shorter events, 0.1 us)
Async XLA Ops:
  2.0 6.7 %collective-permute-start.1 = (bf16[48,2048]{1,0:T(8,128)(2,1)S(1)}, bf16[48,2048]{1,0:T(8,128)(2,1)S(1)}, u32[]{:S(2)}, u32[]{:S(2)}) collective-permute-start(bf16[48,2048]{1,0:T(8,128)(2,1)S(1)} %get-tuple-element.38), channel_id=1, source_target_pairs={{0,1},{1,0},{2,3},{3,2},{4,5},{5,4},{6,7},{7,6},{8,9},{9,8},{10,11... | collective-permute-start | bytes 589832 | tf_op jit(solution)/shard_map/ppermute | solution.py:409
  2.5 1.2 %collective-permute-start = (bf16[48,512]{1,0:T(8,128)(2,1)S(1)}, bf16[48,512]{1,0:T(8,128)(2,1)S(1)}, u32[]{:S(2)}, u32[]{:S(2)}) collective-permute-start(bf16[48,512]{1,0:T(8,128)(2,1)S(1)} %get-tuple-element.35), channel_id=1, source_target_pairs={{0,1},{1,0},{2,3},{3,2},{4,5},{5,4},{6,7},{7,6},{8,9},{9,8},{10,11... | collective-permute-start | bytes 147464 | tf_op jit(solution)/shard_map/ppermute | solution.py:409
  3.7 7.2 %collective-permute-start.3 = (bf16[48,512]{1,0:T(8,128)(2,1)S(1)}, bf16[48,512]{1,0:T(8,128)(2,1)S(1)}, u32[]{:S(2)}, u32[]{:S(2)}) collective-permute-start(bf16[48,512]{1,0:T(8,128)(2,1)S(1)} %get-tuple-element.39), channel_id=1, source_target_pairs={{0,6},{1,7},{2,4},{3,5},{4,2},{5,3},{6,0},{7,1},{8,14},{9,15},{10,... | collective-permute-start | bytes 147464 | tf_op jit(solution)/shard_map/ppermute | solution.py:409
  8.7 5.0 %collective-permute-start.2 = (bf16[48,512]{1,0:T(8,128)(2,1)S(1)}, bf16[48,512]{1,0:T(8,128)(2,1)S(1)}, u32[]{:S(2)}, u32[]{:S(2)}) collective-permute-start(bf16[48,512]{1,0:T(8,128)(2,1)S(1)} %get-tuple-element.36.refs_0_), channel_id=1, source_target_pairs={{0,4},{1,5},{2,6},{3,7},{4,0},{5,1},{6,2},{7,3},{8,12},{9,13},{10,... | collective-permute-start | bytes 147464 | tf_op jit(solution)/shard_map/ppermute | solution.py:409
  13.7 6.1 %collective-permute-start.5 = (bf16[96,512]{1,0:T(8,128)(2,1)S(1)}, bf16[96,512]{1,0:T(8,128)(2,1)S(1)}, u32[]{:S(2)}, u32[]{:S(2)}) collective-permute-start(bf16[96,512]{1,0:T(8,128)(2,1)S(1)} %join_far.1.refs_0_), channel_id=1, source_target_pairs={{0,8},{8,0},{16,24},{24,16},{1,9},{9,1},{17,25},{25,17},{2,10},{10... | collective-permute-start | bytes 294920 | tf_op jit(solution)/shard_map/ppermute | solution.py:406
  15.3 11.3 %collective-permute-start.10 = (bf16[48,2048]{1,0:T(8,128)(2,1)S(1)}, bf16[48,2048]{1,0:T(8,128)(2,1)S(1)}, u32[]{:S(2)}, u32[]{:S(2)}) collective-permute-start(bf16[48,2048]{1,0:T(8,128)(2,1)S(1)} %forward_near.1.refs_0_), channel_id=1, source_target_pairs={{0,2},{1,3},{2,0},{3,1},{4,6},{5,7},{6,4},{7,5},{8,10},{9,11},{10,... | collective-permute-start | bytes 589832 | tf_op jit(solution)/shard_map/ppermute | solution.py:409
  15.3 5.7 %collective-permute-start.4 = (bf16[96,512]{1,0:T(8,128)(2,1)S(1)}, bf16[96,512]{1,0:T(8,128)(2,1)S(1)}, u32[]{:S(2)}, u32[]{:S(2)}) collective-permute-start(bf16[96,512]{1,0:T(8,128)(2,1)S(1)} %join_far.1.refs_0_), channel_id=1, source_target_pairs={{0,16},{8,24},{16,0},{24,8},{1,17},{9,25},{17,1},{25,9},{2,18},{10... | collective-permute-start | bytes 294920 | tf_op jit(solution)/shard_map/ppermute | solution.py:406
  16.8 5.5 %collective-permute-start.6 = (bf16[96,512]{1,0:T(8,128)(2,1)S(1)}, bf16[96,512]{1,0:T(8,128)(2,1)S(1)}, u32[]{:S(2)}, u32[]{:S(2)}) collective-permute-start(bf16[96,512]{1,0:T(8,128)(2,1)S(1)} %join_far.1.refs_0_), channel_id=1, source_target_pairs={{0,24},{8,16},{16,8},{24,0},{1,25},{9,17},{17,9},{25,1},{2,26},{10... | collective-permute-start | bytes 294920 | tf_op jit(solution)/shard_map/ppermute | solution.py:406
  20.2 2.1 %copy-start = (bf16[2,256,2048]{2,1,0:T(8,128)(2,1)S(1)}, bf16[2,256,2048]{2,1,0:T(8,128)(2,1)}, u32[]{:S(2)}) copy-start(bf16[2,256,2048]{2,1,0:T(8,128)(2,1)} %param.17) | copy-start | bytes 6291460
  20.2 2.1 %copy-start.2 = (s32[16]{0:T(128)S(1)}, s32[16]{0:T(128)}, u32[]{:S(2)}) copy-start(s32[16]{0:T(128)} %param.15) | copy-start | bytes 196
  23.0 7.3 %collective-permute-start.8 = (bf16[96,512]{1,0:T(8,128)(2,1)S(1)}, bf16[96,512]{1,0:T(8,128)(2,1)S(1)}, u32[]{:S(2)}, u32[]{:S(2)}) collective-permute-start(bf16[96,512]{1,0:T(8,128)(2,1)S(1)} %get-tuple-element.42), channel_id=1, source_target_pairs={{0,16},{8,24},{16,0},{24,8},{1,17},{9,25},{17,1},{25,9},{2,18},{10... | collective-permute-start | bytes 294920 | tf_op jit(solution)/shard_map/ppermute | solution.py:406
  24.2 7.2 %collective-permute-start.9 = (bf16[96,512]{1,0:T(8,128)(2,1)S(1)}, bf16[96,512]{1,0:T(8,128)(2,1)S(1)}, u32[]{:S(2)}, u32[]{:S(2)}) collective-permute-start(bf16[96,512]{1,0:T(8,128)(2,1)S(1)} %get-tuple-element.43), channel_id=1, source_target_pairs={{0,24},{8,16},{16,8},{24,0},{1,25},{9,17},{17,9},{25,1},{2,26},{10... | collective-permute-start | bytes 294920 | tf_op jit(solution)/shard_map/ppermute | solution.py:406
  25.5 6.1 %collective-permute-start.7 = (bf16[96,512]{1,0:T(8,128)(2,1)S(1)}, bf16[96,512]{1,0:T(8,128)(2,1)S(1)}, u32[]{:S(2)}, u32[]{:S(2)}) collective-permute-start(bf16[96,512]{1,0:T(8,128)(2,1)S(1)} %get-tuple-element.41.refs_0_), channel_id=1, source_target_pairs={{0,8},{8,0},{16,24},{24,16},{1,9},{9,1},{17,25},{25,17},{2,10},{10... | collective-permute-start | bytes 294920 | tf_op jit(solution)/shard_map/ppermute | solution.py:406
  26.6 13.6 %copy-start.1 = (bf16[2048,8]{0,1:T(8,128)(2,1)S(1)}, bf16[2048,8]{0,1:T(8,128)(2,1)}, u32[]{:S(2)}) copy-start(bf16[2048,8]{0,1:T(8,128)(2,1)} %param.11) | copy-start | bytes 98308
  26.6 13.6 %copy-start.3 = (s32[16]{0:T(128)S(1)}, s32[16]{0:T(128)}, u32[]{:S(2)}) copy-start(s32[16]{0:T(128)} %param.14) | copy-start | bytes 196
  27.8 7.8 %collective-permute-start.11 = (bf16[96,512]{1,0:T(8,128)(2,1)S(1)}, bf16[96,512]{1,0:T(8,128)(2,1)S(1)}, u32[]{:S(2)}, u32[]{:S(2)}) collective-permute-start(bf16[96,512]{1,0:T(8,128)(2,1)S(1)} %get-tuple-element.47), channel_id=1, source_target_pairs={{0,8},{8,0},{16,24},{24,16},{1,9},{9,1},{17,25},{25,17},{2,10},{10... | collective-permute-start | bytes 294920 | tf_op jit(solution)/shard_map/ppermute | solution.py:406
  28.8 6.8 %collective-permute-start.12 = (bf16[96,512]{1,0:T(8,128)(2,1)S(1)}, bf16[96,512]{1,0:T(8,128)(2,1)S(1)}, u32[]{:S(2)}, u32[]{:S(2)}) collective-permute-start(bf16[96,512]{1,0:T(8,128)(2,1)S(1)} %get-tuple-element.48), channel_id=1, source_target_pairs={{0,16},{8,24},{16,0},{24,8},{1,17},{9,25},{17,1},{25,9},{2,18},{10... | collective-permute-start | bytes 294920 | tf_op jit(solution)/shard_map/ppermute | solution.py:406
  30.4 5.5 %collective-permute-start.13 = (bf16[96,512]{1,0:T(8,128)(2,1)S(1)}, bf16[96,512]{1,0:T(8,128)(2,1)S(1)}, u32[]{:S(2)}, u32[]{:S(2)}) collective-permute-start(bf16[96,512]{1,0:T(8,128)(2,1)S(1)} %get-tuple-element.49), channel_id=1, source_target_pairs={{0,24},{8,16},{16,8},{24,0},{1,25},{9,17},{17,9},{25,1},{2,26},{10... | collective-permute-start | bytes 294920 | tf_op jit(solution)/shard_map/ppermute | solution.py:406
  31.7 6.3 %collective-permute-start.16 = (bf16[48,512]{1,0:T(8,128)(2,1)S(1)}, bf16[48,512]{1,0:T(8,128)(2,1)S(1)}, u32[]{:S(2)}, u32[]{:S(2)}) collective-permute-start(bf16[48,512]{1,0:T(8,128)(2,1)S(1)} %get-tuple-element.52), channel_id=1, source_target_pairs={{0,6},{1,7},{2,4},{3,5},{4,2},{5,3},{6,0},{7,1},{8,14},{9,15},{10,... | collective-permute-start | bytes 147464 | tf_op jit(solution)/shard_map/ppermute | solution.py:409
  34.2 5.0 %collective-permute-start.15 = (bf16[48,512]{1,0:T(8,128)(2,1)S(1)}, bf16[48,512]{1,0:T(8,128)(2,1)S(1)}, u32[]{:S(2)}, u32[]{:S(2)}) collective-permute-start(bf16[48,512]{1,0:T(8,128)(2,1)S(1)} %get-tuple-element.44.refs_0_), channel_id=1, source_target_pairs={{0,4},{1,5},{2,6},{3,7},{4,0},{5,1},{6,2},{7,3},{8,12},{9,13},{10,... | collective-permute-start | bytes 147464 | tf_op jit(solution)/shard_map/ppermute | solution.py:409
  35.9 4.2 %collective-permute-start.14 = (bf16[48,512]{1,0:T(8,128)(2,1)S(1)}, bf16[48,512]{1,0:T(8,128)(2,1)S(1)}, u32[]{:S(2)}, u32[]{:S(2)}) collective-permute-start(bf16[48,512]{1,0:T(8,128)(2,1)S(1)} %get-tuple-element.51), channel_id=1, source_target_pairs={{0,2},{1,3},{2,0},{3,1},{4,6},{5,7},{6,4},{7,5},{8,10},{9,11},{10,... | collective-permute-start | bytes 147464 | tf_op jit(solution)/shard_map/ppermute | solution.py:409
  40.1 1.4 %collective-permute-start.17 = (bf16[96,512]{1,0:T(8,128)(2,1)S(1)}, bf16[96,512]{1,0:T(8,128)(2,1)S(1)}, u32[]{:S(2)}, u32[]{:S(2)}) collective-permute-start(bf16[96,512]{1,0:T(8,128)(2,1)S(1)} %flip_back.1), channel_id=1, source_target_pairs={{0,1},{1,0},{2,3},{3,2},{4,5},{5,4},{6,7},{7,6},{8,9},{9,8},{10,11... | collective-permute-start | bytes 294920 | tf_op jit(solution)/shard_map/ppermute | solution.py:409

commit v5 on v4

--- a/solution.py
+++ b/solution.py
@@ -106,9 +106,9 @@
 
 def dispatch_kernel(per_device, steps, *refs):
     tokens_hbm, *small_hbm = refs[:6]
-    tokens_ref, gain_ref, local_ref, *out_refs = refs[6:11]
-    experts_ref, keys_ref, slot_ref, cap_ref, arrived = refs[11:]
-    small_refs = (experts_ref, keys_ref, slot_ref, cap_ref, gain_ref)
+    tokens_ref, gain_ref, slot_ref, cap_ref, local_ref, *out_refs = refs[6:13]
+    experts_ref, keys_ref, arrived = refs[13:]
+    small_refs = (experts_ref, keys_ref, gain_ref, slot_ref, cap_ref)
     copies = [
         pltpu.make_async_copy(source, target, arrived.at[index])
         for index, (source, target) in enumerate(
@@ -134,20 +134,20 @@
     store_blocks(out_refs, jnp.dot(pick, normed, preferred_element_type=jnp.float32))
 
 
-def near_kernel(per_device, groups, steps, tokens_ref, gain_ref, local_ref, *out_refs):
+def near_kernel(per_device, meet, steps, tokens_ref, gain_ref, local_ref, *out_refs):
     gain = gain_ref[...].astype(jnp.float32)
-    width = tokens_ref.shape[1] // groups
+    width = tokens_ref.shape[1] // len(meet)
     group = lax.axis_index("dp")
     scale = row_scale(tokens_ref[...].astype(jnp.float32))
     pick = pick_rows(local_ref, None, sum(steps, ()), per_device).astype(jnp.bfloat16)
-    for step in range(groups):
+    for place, step in enumerate(meet):
         start = pl.multiple_of((group ^ step) * width, width)
         part = tokens_ref[:, pl.ds(start, width)].astype(jnp.float32)
         normed = apply_gain(part * scale, gain, (group ^ step) * (width // 128))
         value = jnp.dot(pick, normed, preferred_element_type=jnp.float32)
         top = 0
         for ref in out_refs:
-            ref[:, step * width : (step + 1) * width] = value[
+            ref[:, place * width : (place + 1) * width] = value[
                 top : top + ref.shape[0], :
             ].astype(ref.dtype)
             top += ref.shape[0]
@@ -189,49 +189,65 @@
     out_ref[...] = weights.T.astype(jnp.bfloat16)
 
 
-def split_kernel(halves, groups, steps, in_hbm, out_ref, in_ref, arrived):
+def split_rows(halves, in_ref, out_ref):
     tile = 256
     kinds = 2 * halves
     per_tile = tile // kinds
-    slots, length, _ = in_hbm.shape
-    part = length // groups
-    group = lax.axis_index("dp")
-    copies = []
-    for place, step in enumerate(steps):
-        base = pl.multiple_of((group ^ step) * part, part)
-        copies.append(
-            pltpu.make_async_copy(
-                in_hbm.at[:, pl.ds(base, part), :], in_ref.at[place], arrived.at[place]
-            )
-        )
-        copies[-1].start()
+    slots, length, _ = in_ref.shape
     to_row = lax.broadcasted_iota(jnp.int32, (tile, tile), 0)
     from_row = lax.broadcasted_iota(jnp.int32, (tile, tile), 1)
     column = to_row // per_tile
     source = (to_row % per_tile) * kinds + (column % halves) * 2 + column // halves
     order = jnp.where(source == from_row, 1.0, 0.0).astype(jnp.bfloat16)
-    for place in range(len(steps)):
-        copies[place].wait()
-        for slot in range(slots):
-            for index in range(0, part // tile, 2):
-                low = index * tile
-                pair = [
-                    in_ref[place, slot, low + side * tile : low + (side + 1) * tile, :]
-                    for side in range(2)
-                ]
-                moved = jnp.dot(
-                    order,
-                    jnp.concatenate(pair, axis=1),
-                    preferred_element_type=jnp.float32,
-                ).astype(jnp.bfloat16)
-                for side in range(2):
-                    top = (index + side) * per_tile
-                    for kind in range(kinds):
-                        left = (slot * kinds + kind) * 128
-                        out_ref[place, top : top + per_tile, left : left + 128] = moved[
-                            kind * per_tile : (kind + 1) * per_tile,
-                            side * 128 : (side + 1) * 128,
-                        ]
+    for slot in range(slots):
+        for index in range(0, length // tile, 2):
+            low = index * tile
+            pair = [
+                in_ref[slot, low + side * tile : low + (side + 1) * tile, :]
+                for side in range(2)
+            ]
+            moved = jnp.dot(
+                order,
+                jnp.concatenate(pair, axis=1),
+                preferred_element_type=jnp.float32,
+            ).astype(jnp.bfloat16)
+            for side in range(2):
+                top = (index + side) * per_tile
+                for kind in range(kinds):
+                    left = (slot * kinds + kind) * 128
+                    out_ref[top : top + per_tile, left : left + 128] = moved[
+                        kind * per_tile : (kind + 1) * per_tile,
+                        side * 128 : (side + 1) * 128,
+                    ]
+
+
+def split_first_kernel(halves, meet, in_hbm, out_ref, rest_ref, in_ref, arrived):
+    first, second = out_ref.shape[0], rest_ref.shape[0]
+    part = in_hbm.shape[1] // (first + second)
+    group = lax.axis_index("dp")
+    copies = []
+    for step in range(first + second):
+        base = pl.multiple_of((group ^ meet[step]) * part, part)
+        target = in_ref.at[step] if step < first else rest_ref.at[step - first]
+        copies.append(
+            pltpu.make_async_copy(
+                in_hbm.at[:, pl.ds(base, part), :], target, arrived.at[step]
+            )
+        )
+        copies[-1].start()
+    for step in range(first):
+        copies[step].wait()
+        split_rows(halves, in_ref.at[step], out_ref.at[step])
+    for copy in copies[first:]:
+        copy.wait()
+
+
+def split_second_kernel(halves, down_hbm, in_ref, out_ref, down_ref, arrived):
+    copy = pltpu.make_async_copy(down_hbm, down_ref, arrived)
+    copy.start()
+    for index in range(in_ref.shape[0]):
+        split_rows(halves, in_ref.at[index], out_ref.at[index])
+    copy.wait()
 
 
 def slot_mask(cap_ref, per_device, units):
@@ -360,23 +376,22 @@
     out_ref[...] = (sum_ref[...] + mixture).astype(jnp.bfloat16)
 
 
-def call(kernel, name, outs, *args, scratch=(), in_hbm=False, after=()):
+def call(kernel, name, outs, *args, scratch=(), hbm=(), after=()):
     count = len(after)
-    if in_hbm:
-        args = [pltpu.with_memory_space_constraint(a, pltpu.HBM) for a in args]
-    space = pltpu.HBM if in_hbm else pltpu.VMEM
+    hbm = [pltpu.with_memory_space_constraint(a, pltpu.HBM) for a in hbm]
     size = sum(a.size * a.dtype.itemsize for a in (*args, *outs))
     return pl.pallas_call(
         lambda *refs: kernel(*refs[count:]),
         in_specs=[pl.BlockSpec(memory_space=pl.ANY)] * count
-        + [pl.BlockSpec(memory_space=space)] * len(args),
+        + [pl.BlockSpec(memory_space=pltpu.HBM)] * len(hbm)
+        + [pl.BlockSpec(memory_space=pltpu.VMEM)] * len(args),
         out_specs=[pl.BlockSpec(memory_space=pltpu.VMEM)] * len(outs),
         out_shape=outs,
         scratch_shapes=scratch,
         compiler_params=pltpu.CompilerParams(vmem_limit_bytes=size + (8 << 20)),
         cost_estimate=pl.CostEstimate(flops=1, bytes_accessed=1, transcendentals=0),
         name=name,
-    )(*after, *args)
+    )(*after, *hbm, *args)
 
 
 def on_device(
@@ -398,6 +413,8 @@
     units = slot_gate_up_weight.shape[3]
     quarter = width // groups
     chips = peers // 2
+    far = range(2, chips)[::-1]
+    meet = [0, groups - 1, *range(1, groups - 1)]
 
     def blocks(count, *shape, dtype=jnp.bfloat16):
         return [jax.ShapeDtypeStruct(shape, dtype)] * count
@@ -413,33 +430,28 @@
     cap_row = capacity.reshape(1, slots)
     down = down_weight.reshape(per_device * units, width)
 
-    tokens_here, gain_here, local, far_same, far_flip = call(
+    (
+        tokens_here, gain_here, slot_here, cap_here, local, far_same, far_flip
+    ) = call(
         functools.partial(
-            dispatch_kernel, per_device, [*range(4, peers, 2), *range(5, peers, 2)]
+            dispatch_kernel, per_device, [2 * c for c in far] + [2 * c + 1 for c in far]
         ),
         "dispatch",
         blocks(1, rows, width)
         + blocks(1, *gain.shape)
+        + blocks(2, 1, slots, dtype=jnp.int32)
         + blocks(1, slots, rows, dtype=jnp.float32)
         + blocks(2, (chips - 2) * CAP_DEV, quarter),
-        tokens,
-        experts.T,
-        replica_key.T,
-        slot_row,
-        cap_row,
-        gain,
+        hbm=[tokens, experts.T, replica_key.T, gain, slot_row, cap_row],
         scratch=[
             pltpu.VMEM((experts.shape[1], rows), jnp.int32),
             pltpu.VMEM((experts.shape[1], rows), jnp.int32),
-            pltpu.VMEM((1, slots), jnp.int32),
-            pltpu.VMEM((1, slots), jnp.int32),
             pltpu.SemaphoreType.DMA((6,)),
         ],
-        in_hbm=True,
     )
     core_far = to_peer(far_flip, 1)
     own_rows, same_rows, flip_rows = call(
-        functools.partial(near_kernel, per_device, groups, ((0,), (2,), (1, 3))),
+        functools.partial(near_kernel, per_device, meet, ((0,), (2,), (1, 3))),
         "dispatch_near",
         blocks(2, CAP_DEV, width) + blocks(1, 2 * CAP_DEV, width),
         tokens_here,
@@ -454,9 +466,7 @@
         far_same,
         core_far,
     )
-    far_in = [
-        to_peer(value, 2 * chip) for chip, value in reversed([*enumerate(far_out, 2)])
-    ]
+    far_in = [to_peer(value, 2 * chip) for chip, value in zip(far, far_out)]
     (chip_rows,) = call(
         forward_kernel,
         "forward_near",
@@ -474,33 +484,37 @@
     split_in = split_in.reshape(per_device, width * halves * 2, 128)
     half = groups // 2
 
-    def split(steps, after):
-        return call(
-            functools.partial(split_kernel, halves, groups, steps),
-            "split_gate_up",
-            blocks(1, len(steps), quarter, per_device * 2 * units),
-            split_in,
-            scratch=[
-                pltpu.VMEM(
-                    (len(steps), per_device, quarter * halves * 2, 128), jnp.bfloat16
-                ),
-                pltpu.SemaphoreType.DMA((len(steps),)),
-            ],
-            in_hbm=True,
-            after=after,
-        )[0]
-
-    first_weights = split(range(half), (near_ready,))
+    part = (per_device, quarter * halves * 2, 128)
+    out = (quarter, per_device * 2 * units)
+    first_weights, rest = call(
+        functools.partial(split_first_kernel, halves, meet),
+        "split_first",
+        blocks(1, half, *out) + blocks(1, groups - half, *part),
+        hbm=[split_in],
+        scratch=[
+            pltpu.VMEM((half, *part), jnp.bfloat16),
+            pltpu.SemaphoreType.DMA((groups,)),
+        ],
+        after=(near_ready,),
+    )
     (far_rows,) = call(
         join_kernel,
         "join_far",
         blocks(1, (peers - NEAR) * CAP_DEV, quarter),
-        *far_in[::-1],
+        *far_in,
         after=(first_weights,),
     )
-    second_weights = split(range(half, groups), (far_rows,))
-
-    far_parts = [far_rows] + [to_group(far_rows, step) for step in range(1, groups)]
+    second_weights, down_here = call(
+        functools.partial(split_second_kernel, halves),
+        "split_second",
+        blocks(1, groups - half, *out) + blocks(1, *down.shape),
+        rest,
+        hbm=[down],
+        scratch=[pltpu.SemaphoreType.DMA],
+        after=(far_rows,),
+    )
+
+    far_parts = [far_rows] + [to_group(far_rows, step) for step in meet[1:]]
     far_sum = ()
     for step in range(groups - 1):
         weights, index = (
@@ -523,8 +537,8 @@
         *far_sum,
         far_parts[-1],
         second_weights,
-        cap_row,
-        down,
+        cap_here,
+        down_here,
     )
     near_partials = call(
         functools.partial(near_expert_kernel, per_device),
@@ -535,13 +549,15 @@
         chip_rows,
         first_weights,
         second_weights,
-        cap_row,
-        down,
+        cap_here,
+        down_here,
         after=(far_partials[1],),
     )
 
     def reduce_groups(partials, name, count, after=()):
-        received = [to_group(partials[step], step) for step in range(1, groups)]
+        received = [
+            to_group(partials[step], step) for step in meet[1:]
+        ]
         return call(
             functools.partial(sum_kernel, groups),
             name,
@@ -553,16 +569,15 @@
 
     far_back = reduce_groups(far_partials, "sum_far", chips - 2)
     near_back = reduce_groups(near_partials, "sum_near", 2, far_back[:1])
-    far_back = [
-        to_peer(value, 2 * chip) for chip, value in reversed([*enumerate(far_back, 2)])
-    ]
-    back = [near_back[0], to_peer(near_back[1], 2), *far_back[::-1]]
+    far_back = [to_peer(value, 2 * chip) for chip, value in zip(far, far_back)]
+    back = [*far_back, near_back[0], to_peer(near_back[1], 2)]
     (flip_back,) = call(
         flip_kernel, "flip_back", blocks(1, chips * CAP_DEV, quarter), *back
     )
     core_back = to_peer(flip_back, 1)
 
-    order = [*range(0, peers, 2), *range(1, peers, 2)]
+    order = [2 * c for c in (*far, 0, 1)]
+    order += [step + 1 for step in order]
     weights, residual = call(
         functools.partial(weight_kernel, per_device, order),
         "combine_weights",
@@ -570,7 +585,7 @@
         tokens_here,
         gain_here,
         routing_projection_matrix.T,
-        slot_row,
+        slot_here,
         local,
         scratch=[pltpu.VMEM((slots, rows), jnp.float32)],
     )

time: 42.5 us -> 41.1 us (0.967)
  starting transfers between devices: 22.3 us -> 21.1 us
  Pallas kernels: 11.1 us -> 10.4 us
  waiting for transfers between devices: 8.79 us -> 9.22 us
    ppermute x9, starting transfers between devices: 11.6 us -> 10.5 us  [to_peer(): return lax.ppermute(value, 'expert', [(i, i ^ step) for i in range(peers)])]
    ppermute x9, waiting for transfers between devices: 6.48 us -> 7.38 us  [to_peer(): return lax.ppermute(value, 'expert', [(i, i ^ step) for i in range(peers)])]
    pallas_call x18, Pallas kernels: 11.1 us -> 10.4 us  [call(): pl.pallas_call(lambda *refs: kernel(*refs[count:]), in_specs=[pl.BlockSpe...]
    ppermute x9, waiting for transfers between devices: 2.31 us -> 1.84 us  [to_group(): return lax.ppermute(value, 'dp', [(i, i ^ step) for i in range(groups)])]
  transfers between devices with their start and end apart: 18 -> 18, of which waited for: 9 -> 8; matrix products, arithmetic and copies ran while one was open for 0% -> 0% of each run, Pallas kernels for 19% -> 19%
where the time goes in v5:
time: 41.1 us; the launch traced here: 40.9 us
  starting transfers between devices  21.1 us (51%)
  Pallas kernels  10.4 us (25%)
  waiting for transfers between devices  9.22 us (22%)
    ppermute x9, starting transfers between devices, to_group(): return lax.ppermute(value, 'dp', [(i, i ^ step) for i in range(groups)])  10.7 us
    ppermute x9, starting transfers between devices, to_peer(): return lax.ppermute(value, 'expert', [(i, i ^ step) for i in range(peers)])  10.5 us
    pallas_call x18, Pallas kernels, call(): pl.pallas_call(lambda *refs: kernel(*refs[count:]), in_specs=[pl.BlockSpe...  10.4 us
    ppermute x9, waiting for transfers between devices, to_peer(): return lax.ppermute(value, 'expert', [(i, i ^ step) for i in range(peers)])  7.38 us
    ppermute x9, waiting for transfers between devices, to_group(): return lax.ppermute(value, 'dp', [(i, i ^ step) for i in range(groups)])  1.84 us
  transfers between devices with their start and end apart: 18, of which 8 were waited for; matrix products, arithmetic and copies ran while one was open for 0% of the time, Pallas kernels for 19%

profile of v5, /device:TPU:0, one launch (start us, length us, event | category | flops | bytes accessed | tf_op | source)
XLA Modules:
  0.0 40.9 jit_solution(15198962438248425035)
XLA Ops:
  0.0 1.5 %dispatch.1 = (bf16[128,2048]{1,0:T(8,128)(2,1)S(1)}, bf16[16,128]{1,0:T(8,128)(2,1)S(1)}, s32[1,16]{1,0:T(1,128)S(1)}, s32[1,16]{1,0:T(1,128)S(1)}, f32[16,128]...) custom-call(bf16[128,2048]{1,0:T(8,128)(2,1)} %refs_0_.1, s32[8,128]{1,0:T(8,128)} %bitcast.15, ...), custom_call_target="tpu_custom_call" | custom-call | flops 1 | bytes 1 | tf_op jit(solution)/shard_map/dispatch/pallas_call | solution.py:383
  1.5 0.4 %dispatch_near.1 = (bf16[24,2048]{1,0:T(8,128)(2,1)S(1)}, bf16[24,2048]{1,0:T(8,128)(2,1)S(1)}, bf16[48,2048]{1,0:T(8,128)(2,1)S(1)}) custom-call(bf16[128,2048]{1,0:T(8,128)(2,1)S(1)} %get-tuple-element.35.refs_0_, bf16[16,128]{1,0:T(8,128)(2,1)S(1)} %get-tuple-element.36.refs_1_, f32[16,128]{1,0:T(8,128)S(1)} %get-tuple-element.38.refs_4_.refs_2_), custom_call_target="tpu_custom_call" | custom-call | flops 1 | bytes 1 | tf_op jit(solution)/shard_map/dispatch_near/pallas_call | solution.py:383
  2.0 0.5 %collective-permute-start.1 = (bf16[48,2048]{1,0:T(8,128)(2,1)S(1)}, bf16[48,2048]{1,0:T(8,128)(2,1)S(1)}, u32[]{:S(2)}, u32[]{:S(2)}) collective-permute-start(bf16[48,2048]{1,0:T(8,128)(2,1)S(1)} %get-tuple-element.45), channel_id=1, source_target_pairs={{0,1},{1,0},{2,3},{3,2},{4,5},{5,4},{6,7},{7,6},{8,9},{9,8},{10,11... | collective-permute-start | bytes 589832 | tf_op jit(solution)/shard_map/ppermute | solution.py:426
  2.5 0.1 collective-permute-start
  2.6 1.2 %collective-permute-done.refs_1_ = bf16[48,512]{1,0:T(8,128)(2,1)S(1)} collective-permute-done((bf16[48,512]{1,0:T(8,128)(2,1)S(1)}, bf16[48,512]{1,0:T(8,128)(2,1)S(1)}, u32[]{:S(2)}, u32[]{:S(2)}) %collective-permute-start) | collective-permute-done | bytes 49184 | tf_op jit(solution)/shard_map/ppermute | solution.py:426
  3.7 4.9 %collective-permute-start.2 = (bf16[48,512]{1,0:T(8,128)(2,1)S(1)}, bf16[48,512]{1,0:T(8,128)(2,1)S(1)}, u32[]{:S(2)}, u32[]{:S(2)}) collective-permute-start(bf16[48,512]{1,0:T(8,128)(2,1)S(1)} %get-tuple-element.43.refs_0_), channel_id=1, source_target_pairs={{0,6},{1,7},{2,4},{3,5},{4,2},{5,3},{6,0},{7,1},{8,14},{9,15},{10,... | collective-permute-start | bytes 147464 | tf_op jit(solution)/shard_map/ppermute | solution.py:426
  8.7 0.0 collective-permute-start.3
  8.7 0.0 collective-permute-done.1.refs_2_
  8.7 2.3 %split_first.1 = (bf16[2,512,1024]{2,1,0:T(8,128)(2,1)S(1)}, bf16[2,2,2048,128]{3,2,1,0:T(8,128)(2,1)S(1)}) custom-call(bf16[48,2048]{1,0:T(8,128)(2,1)S(1)} %forward_near.1.refs_0_, bf16[2,8192,128]{2,1,0:T(8,128)(2,1)} %bitcast.13), custom_call_target="tpu_custom_call" | custom-call | flops 1 | bytes 1 | tf_op jit(solution)/shard_map/split_first/pallas_call | solution.py:383
  11.0 0.0 collective-permute-done.2.refs_1_
  11.0 2.7 %collective-permute-done.3.refs_2_ = bf16[48,512]{1,0:T(8,128)(2,1)S(1)} collective-permute-done((bf16[48,512]{1,0:T(8,128)(2,1)S(1)}, bf16[48,512]{1,0:T(8,128)(2,1)S(1)}, u32[]{:S(2)}, u32[]{:S(2)}) %collective-permute-start.3) | collective-permute-done | bytes 49184 | tf_op jit(solution)/shard_map/ppermute | solution.py:426
  13.7 2.5 %collective-permute-start.5 = (bf16[96,512]{1,0:T(8,128)(2,1)S(1)}, bf16[96,512]{1,0:T(8,128)(2,1)S(1)}, u32[]{:S(2)}, u32[]{:S(2)}) collective-permute-start(bf16[96,512]{1,0:T(8,128)(2,1)S(1)} %join_far.1.refs_0_), channel_id=1, source_target_pairs={{0,24},{8,16},{16,8},{24,0},{1,25},{9,17},{17,9},{25,1},{2,26},{10... | collective-permute-start | bytes 294920 | tf_op jit(solution)/shard_map/ppermute | solution.py:423
  16.2 0.5 %collective-permute-start.4 = (bf16[96,512]{1,0:T(8,128)(2,1)S(1)}, bf16[96,512]{1,0:T(8,128)(2,1)S(1)}, u32[]{:S(2)}, u32[]{:S(2)}) collective-permute-start(bf16[96,512]{1,0:T(8,128)(2,1)S(1)} %join_far.1.refs_0_), channel_id=1, source_target_pairs={{0,8},{8,0},{16,24},{24,16},{1,9},{9,1},{17,25},{25,17},{2,10},{10... | collective-permute-start | bytes 294920 | tf_op jit(solution)/shard_map/ppermute | solution.py:423
  16.8 0.0 collective-permute-start.12
  16.8 0.5 %collective-permute-start.6 = (bf16[96,512]{1,0:T(8,128)(2,1)S(1)}, bf16[96,512]{1,0:T(8,128)(2,1)S(1)}, u32[]{:S(2)}, u32[]{:S(2)}) collective-permute-start(bf16[96,512]{1,0:T(8,128)(2,1)S(1)} %join_far.1.refs_0_), channel_id=1, source_target_pairs={{0,16},{8,24},{16,0},{24,8},{1,17},{9,25},{17,1},{25,9},{2,18},{10... | collective-permute-start | bytes 294920 | tf_op jit(solution)/shard_map/ppermute | solution.py:423
  17.3 0.3 product_far.3.refs_2_
  17.6 1.6 %split_second.1 = (bf16[2,512,1024]{2,1,0:T(8,128)(2,1)S(1)}, bf16[512,2048]{1,0:T(8,128)(2,1)S(1)}) custom-call(bf16[96,512]{1,0:T(8,128)(2,1)S(1)} %join_far.1.refs_0_, bf16[512,2048]{1,0:T(8,128)(2,1)} %bitcast.14, bf16[2,2,2048,128]{3,2,1,0:T(8,128)(2,1)S(1)} %get-tuple-element.48.refs_2_), custom_call_target="tpu_custom_call" | custom-call | flops 1 | bytes 1 | tf_op jit(solution)/shard_map/split_second/pallas_call | solution.py:383
  19.2 1.1 %collective-permute-done.5.refs_0_ = bf16[96,512]{1,0:T(8,128)(2,1)S(1)} collective-permute-done((bf16[96,512]{1,0:T(8,128)(2,1)S(1)}, bf16[96,512]{1,0:T(8,128)(2,1)S(1)}, u32[]{:S(2)}, u32[]{:S(2)}) %collective-permute-start.5) | collective-permute-done | bytes 98336 | tf_op jit(solution)/shard_map/ppermute | solution.py:423
  20.3 0.3 product_far.4.refs_2_
  20.6 0.7 %collective-permute-done.4.refs_0_ = bf16[96,512]{1,0:T(8,128)(2,1)S(1)} collective-permute-done((bf16[96,512]{1,0:T(8,128)(2,1)S(1)}, bf16[96,512]{1,0:T(8,128)(2,1)S(1)}, u32[]{:S(2)}, u32[]{:S(2)}) %collective-permute-start.4) | collective-permute-done | bytes 98336 | tf_op jit(solution)/shard_map/ppermute | solution.py:423
  21.3 0.3 product_far.5.refs_0_
  21.6 0.0 collective-permute-done.6.refs_1_
  21.6 0.7 %expert_far.1 = (bf16[96,512]{1,0:T(8,128)(2,1)S(1)}, bf16[96,512]{1,0:T(8,128)(2,1)S(1)}, bf16[96,512]{1,0:T(8,128)(2,1)S(1)}, bf16[96,512]{1,0:T(8,128)(2,1)S(1)}) custom-call(f32[96,1024]{1,0:T(8,128)S(1)} %product_far.5.refs_0_, bf16[96,512]{1,0:T(8,128)(2,1)S(1)} %collective-permute-done.6.refs_1_, ...), custom_call_target="tpu_custom_call" | custom-call | flops 1 | bytes 1 | tf_op jit(solution)/shard_map/expert_far/pallas_call | solution.py:383
  22.4 2.0 %collective-permute-start.7 = (bf16[96,512]{1,0:T(8,128)(2,1)S(1)}, bf16[96,512]{1,0:T(8,128)(2,1)S(1)}, u32[]{:S(2)}, u32[]{:S(2)}) collective-permute-start(bf16[96,512]{1,0:T(8,128)(2,1)S(1)} %get-tuple-element.53), channel_id=1, source_target_pairs={{0,24},{8,16},{16,8},{24,0},{1,25},{9,17},{17,9},{25,1},{2,26},{10... | collective-permute-start | bytes 294920 | tf_op jit(solution)/shard_map/ppermute | solution.py:423
  24.4 0.5 %collective-permute-start.8 = (bf16[96,512]{1,0:T(8,128)(2,1)S(1)}, bf16[96,512]{1,0:T(8,128)(2,1)S(1)}, u32[]{:S(2)}, u32[]{:S(2)}) collective-permute-start(bf16[96,512]{1,0:T(8,128)(2,1)S(1)} %get-tuple-element.54.refs_0_), channel_id=1, source_target_pairs={{0,8},{8,0},{16,24},{24,16},{1,9},{9,1},{17,25},{25,17},{2,10},{10... | collective-permute-start | bytes 294920 | tf_op jit(solution)/shard_map/ppermute | solution.py:423
  24.9 1.0 %collective-permute-start.9 = (bf16[96,512]{1,0:T(8,128)(2,1)S(1)}, bf16[96,512]{1,0:T(8,128)(2,1)S(1)}, u32[]{:S(2)}, u32[]{:S(2)}) collective-permute-start(bf16[96,512]{1,0:T(8,128)(2,1)S(1)} %get-tuple-element.55), channel_id=1, source_target_pairs={{0,16},{8,24},{16,0},{24,8},{1,17},{9,25},{17,1},{25,9},{2,18},{10... | collective-permute-start | bytes 294920 | tf_op jit(solution)/shard_map/ppermute | solution.py:423
  25.9 0.0 collective-permute-done.12.refs_3_
  25.9 1.2 %expert_near.1 = (bf16[96,512]{1,0:T(8,128)(2,1)S(1)}, bf16[96,512]{1,0:T(8,128)(2,1)S(1)}, bf16[96,512]{1,0:T(8,128)(2,1)S(1)}, bf16[96,512]{1,0:T(8,128)(2,1)S(1)}) custom-call(bf16[96,512]{1,0:T(8,128)(2,1)S(1)} %get-tuple-element.54.refs_0_, bf16[24,2048]{1,0:T(8,128)(2,1)S(1)} %get-tuple-element.58.refs_1_, ...), custom_call_target="tpu_custom_call" | custom-call | flops 1 | bytes 1 | tf_op jit(solution)/shard_map/expert_near/pallas_call | solution.py:383
  27.1 2.0 %collective-permute-start.13 = (bf16[96,512]{1,0:T(8,128)(2,1)S(1)}, bf16[96,512]{1,0:T(8,128)(2,1)S(1)}, u32[]{:S(2)}, u32[]{:S(2)}) collective-permute-start(bf16[96,512]{1,0:T(8,128)(2,1)S(1)} %get-tuple-element.60), channel_id=1, source_target_pairs={{0,24},{8,16},{16,8},{24,0},{1,25},{9,17},{17,9},{25,1},{2,26},{10... | collective-permute-start | bytes 294920 | tf_op jit(solution)/shard_map/ppermute | solution.py:423
  29.1 0.5 %collective-permute-start.14 = (bf16[96,512]{1,0:T(8,128)(2,1)S(1)}, bf16[96,512]{1,0:T(8,128)(2,1)S(1)}, u32[]{:S(2)}, u32[]{:S(2)}) collective-permute-start(bf16[96,512]{1,0:T(8,128)(2,1)S(1)} %get-tuple-element.61), channel_id=1, source_target_pairs={{0,8},{8,0},{16,24},{24,16},{1,9},{9,1},{17,25},{25,17},{2,10},{10... | collective-permute-start | bytes 294920 | tf_op jit(solution)/shard_map/ppermute | solution.py:423
  29.6 0.0 collective-permute-done.7.refs_1_
  29.7 1.0 %collective-permute-start.15 = (bf16[96,512]{1,0:T(8,128)(2,1)S(1)}, bf16[96,512]{1,0:T(8,128)(2,1)S(1)}, u32[]{:S(2)}, u32[]{:S(2)}) collective-permute-start(bf16[96,512]{1,0:T(8,128)(2,1)S(1)} %get-tuple-element.62), channel_id=1, source_target_pairs={{0,16},{8,24},{16,0},{24,8},{1,17},{9,25},{17,1},{25,9},{2,18},{10... | collective-permute-start | bytes 294920 | tf_op jit(solution)/shard_map/ppermute | solution.py:423
  30.7 0.0 collective-permute-done.8.refs_2_
  30.7 0.0 collective-permute-done.9.refs_3_
  30.7 0.1 sum_far.1
  30.8 2.2 %collective-permute-start.10 = (bf16[48,512]{1,0:T(8,128)(2,1)S(1)}, bf16[48,512]{1,0:T(8,128)(2,1)S(1)}, u32[]{:S(2)}, u32[]{:S(2)}) collective-permute-start(bf16[48,512]{1,0:T(8,128)(2,1)S(1)} %get-tuple-element.56.refs_0_), channel_id=1, source_target_pairs={{0,6},{1,7},{2,4},{3,5},{4,2},{5,3},{6,0},{7,1},{8,14},{9,15},{10,... | collective-permute-start | bytes 147464 | tf_op jit(solution)/shard_map/ppermute | solution.py:426
  32.9 1.5 %collective-permute-start.11 = (bf16[48,512]{1,0:T(8,128)(2,1)S(1)}, bf16[48,512]{1,0:T(8,128)(2,1)S(1)}, u32[]{:S(2)}, u32[]{:S(2)}) collective-permute-start(bf16[48,512]{1,0:T(8,128)(2,1)S(1)} %get-tuple-element.57), channel_id=1, source_target_pairs={{0,4},{1,5},{2,6},{3,7},{4,0},{5,1},{6,2},{7,3},{8,12},{9,13},{10,... | collective-permute-start | bytes 147464 | tf_op jit(solution)/shard_map/ppermute | solution.py:426
  34.4 0.0 collective-permute-done.13.refs_2_
  34.4 0.1 sum_near.1
  34.5 1.2 %collective-permute-start.16 = (bf16[48,512]{1,0:T(8,128)(2,1)S(1)}, bf16[48,512]{1,0:T(8,128)(2,1)S(1)}, u32[]{:S(2)}, u32[]{:S(2)}) collective-permute-start(bf16[48,512]{1,0:T(8,128)(2,1)S(1)} %get-tuple-element.64), channel_id=1, source_target_pairs={{0,2},{1,3},{2,0},{3,1},{4,6},{5,7},{6,4},{7,5},{8,10},{9,11},{10,... | collective-permute-start | bytes 147464 | tf_op jit(solution)/shard_map/ppermute | solution.py:426
  35.7 1.3 %collective-permute-done.10.refs_2_.refs_0_ = bf16[48,512]{1,0:T(8,128)(2,1)S(1)} collective-permute-done((bf16[48,512]{1,0:T(8,128)(2,1)S(1)}, bf16[48,512]{1,0:T(8,128)(2,1)S(1)}, u32[]{:S(2)}, u32[]{:S(2)}) %collective-permute-start.10) | collective-permute-done | bytes 49184 | tf_op jit(solution)/shard_map/ppermute | solution.py:426
  37.0 0.9 %collective-permute-done.11.refs_3_.refs_1_ = bf16[48,512]{1,0:T(8,128)(2,1)S(1)} collective-permute-done((bf16[48,512]{1,0:T(8,128)(2,1)S(1)}, bf16[48,512]{1,0:T(8,128)(2,1)S(1)}, u32[]{:S(2)}, u32[]{:S(2)}) %collective-permute-start.11) | collective-permute-done | bytes 49184 | tf_op jit(solution)/shard_map/ppermute | solution.py:426
  37.9 0.7 %collective-permute-done.16.refs_5_.refs_3_ = bf16[48,512]{1,0:T(8,128)(2,1)S(1)} collective-permute-done((bf16[48,512]{1,0:T(8,128)(2,1)S(1)}, bf16[48,512]{1,0:T(8,128)(2,1)S(1)}, u32[]{:S(2)}, u32[]{:S(2)}) %collective-permute-start.16) | collective-permute-done | bytes 49184 | tf_op jit(solution)/shard_map/ppermute | solution.py:426
  38.7 0.1 collective-permute-start.17
  38.8 0.5 %combine_weights.1 = (bf16[128,192]{1,0:T(8,128)(2,1)S(1)}, bf16[128,512]{1,0:T(8,128)(2,1)S(1)}) custom-call(bf16[128,2048]{1,0:T(8,128)(2,1)S(1)} %get-tuple-element.35.refs_0_, bf16[16,128]{1,0:T(8,128)(2,1)S(1)} %get-tuple-element.36.refs_1_, bf16[8,2048]{1,0:T(8,128)(2,1)S(1)} %bitcast.12, s32[1,16]{1,0:T(1,128)S(1)} %get-tuple-element.37.refs_3_, ...), custom_call_target="tpu_custom_call" | custom-call | flops 1 | bytes 1 | tf_op jit(solution)/shard_map/combine_weights/pallas_call | solution.py:383
  39.3 0.2 combine.1.refs_1_
  39.5 0.6 %collective-permute-done.17.refs_2_ = bf16[96,512]{1,0:T(8,128)(2,1)S(1)} collective-permute-done((bf16[96,512]{1,0:T(8,128)(2,1)S(1)}, bf16[96,512]{1,0:T(8,128)(2,1)S(1)}, u32[]{:S(2)}, u32[]{:S(2)}) %collective-permute-start.17) | collective-permute-done | bytes 98336 | tf_op jit(solution)/shard_map/ppermute | solution.py:426
  40.0 0.9 %finish.1 = bf16[128,512]{1,0:T(8,128)(2,1)} custom-call(bf16[128,192]{1,0:T(8,128)(2,1)S(1)} %get-tuple-element.39.refs_0_, f32[128,512]{1,0:T(8,128)S(1)} %combine.1.refs_1_, bf16[96,512]{1,0:T(8,128)(2,1)S(1)} %collective-permute-done.17.refs_2_), custom_call_target="tpu_custom_call" | custom-call | flops 1 | bytes 1 | tf_op jit(solution)/shard_map/finish/pallas_call | solution.py:383
  (8 shorter events, 0.0 us)
Async XLA Ops:
  2.0 6.7 %collective-permute-start.1 = (bf16[48,2048]{1,0:T(8,128)(2,1)S(1)}, bf16[48,2048]{1,0:T(8,128)(2,1)S(1)}, u32[]{:S(2)}, u32[]{:S(2)}) collective-permute-start(bf16[48,2048]{1,0:T(8,128)(2,1)S(1)} %get-tuple-element.45), channel_id=1, source_target_pairs={{0,1},{1,0},{2,3},{3,2},{4,5},{5,4},{6,7},{7,6},{8,9},{9,8},{10,11... | collective-permute-start | bytes 589832 | tf_op jit(solution)/shard_map/ppermute | solution.py:426
  2.5 1.2 %collective-permute-start = (bf16[48,512]{1,0:T(8,128)(2,1)S(1)}, bf16[48,512]{1,0:T(8,128)(2,1)S(1)}, u32[]{:S(2)}, u32[]{:S(2)}) collective-permute-start(bf16[48,512]{1,0:T(8,128)(2,1)S(1)} %get-tuple-element.42), channel_id=1, source_target_pairs={{0,1},{1,0},{2,3},{3,2},{4,5},{5,4},{6,7},{7,6},{8,9},{9,8},{10,11... | collective-permute-start | bytes 147464 | tf_op jit(solution)/shard_map/ppermute | solution.py:426
  3.7 7.3 %collective-permute-start.2 = (bf16[48,512]{1,0:T(8,128)(2,1)S(1)}, bf16[48,512]{1,0:T(8,128)(2,1)S(1)}, u32[]{:S(2)}, u32[]{:S(2)}) collective-permute-start(bf16[48,512]{1,0:T(8,128)(2,1)S(1)} %get-tuple-element.43.refs_0_), channel_id=1, source_target_pairs={{0,6},{1,7},{2,4},{3,5},{4,2},{5,3},{6,0},{7,1},{8,14},{9,15},{10,... | collective-permute-start | bytes 147464 | tf_op jit(solution)/shard_map/ppermute | solution.py:426
  8.7 5.0 %collective-permute-start.3 = (bf16[48,512]{1,0:T(8,128)(2,1)S(1)}, bf16[48,512]{1,0:T(8,128)(2,1)S(1)}, u32[]{:S(2)}, u32[]{:S(2)}) collective-permute-start(bf16[48,512]{1,0:T(8,128)(2,1)S(1)} %get-tuple-element.47), channel_id=1, source_target_pairs={{0,4},{1,5},{2,6},{3,7},{4,0},{5,1},{6,2},{7,3},{8,12},{9,13},{10,... | collective-permute-start | bytes 147464 | tf_op jit(solution)/shard_map/ppermute | solution.py:426
  13.7 6.6 %collective-permute-start.5 = (bf16[96,512]{1,0:T(8,128)(2,1)S(1)}, bf16[96,512]{1,0:T(8,128)(2,1)S(1)}, u32[]{:S(2)}, u32[]{:S(2)}) collective-permute-start(bf16[96,512]{1,0:T(8,128)(2,1)S(1)} %join_far.1.refs_0_), channel_id=1, source_target_pairs={{0,24},{8,16},{16,8},{24,0},{1,25},{9,17},{17,9},{25,1},{2,26},{10... | collective-permute-start | bytes 294920 | tf_op jit(solution)/shard_map/ppermute | solution.py:423
  16.2 5.1 %collective-permute-start.4 = (bf16[96,512]{1,0:T(8,128)(2,1)S(1)}, bf16[96,512]{1,0:T(8,128)(2,1)S(1)}, u32[]{:S(2)}, u32[]{:S(2)}) collective-permute-start(bf16[96,512]{1,0:T(8,128)(2,1)S(1)} %join_far.1.refs_0_), channel_id=1, source_target_pairs={{0,8},{8,0},{16,24},{24,16},{1,9},{9,1},{17,25},{25,17},{2,10},{10... | collective-permute-start | bytes 294920 | tf_op jit(solution)/shard_map/ppermute | solution.py:423
  16.8 9.2 %collective-permute-start.12 = (bf16[48,2048]{1,0:T(8,128)(2,1)S(1)}, bf16[48,2048]{1,0:T(8,128)(2,1)S(1)}, u32[]{:S(2)}, u32[]{:S(2)}) collective-permute-start(bf16[48,2048]{1,0:T(8,128)(2,1)S(1)} %forward_near.1.refs_0_), channel_id=1, source_target_pairs={{0,2},{1,3},{2,0},{3,1},{4,6},{5,7},{6,4},{7,5},{8,10},{9,11},{10,... | collective-permute-start | bytes 589832 | tf_op jit(solution)/shard_map/ppermute | solution.py:426
  16.8 4.9 %collective-permute-start.6 = (bf16[96,512]{1,0:T(8,128)(2,1)S(1)}, bf16[96,512]{1,0:T(8,128)(2,1)S(1)}, u32[]{:S(2)}, u32[]{:S(2)}) collective-permute-start(bf16[96,512]{1,0:T(8,128)(2,1)S(1)} %join_far.1.refs_0_), channel_id=1, source_target_pairs={{0,16},{8,24},{16,0},{24,8},{1,17},{9,25},{17,1},{25,9},{2,18},{10... | collective-permute-start | bytes 294920 | tf_op jit(solution)/shard_map/ppermute | solution.py:423
  22.4 7.3 %collective-permute-start.7 = (bf16[96,512]{1,0:T(8,128)(2,1)S(1)}, bf16[96,512]{1,0:T(8,128)(2,1)S(1)}, u32[]{:S(2)}, u32[]{:S(2)}) collective-permute-start(bf16[96,512]{1,0:T(8,128)(2,1)S(1)} %get-tuple-element.53), channel_id=1, source_target_pairs={{0,24},{8,16},{16,8},{24,0},{1,25},{9,17},{17,9},{25,1},{2,26},{10... | collective-permute-start | bytes 294920 | tf_op jit(solution)/shard_map/ppermute | solution.py:423
  24.4 6.3 %collective-permute-start.8 = (bf16[96,512]{1,0:T(8,128)(2,1)S(1)}, bf16[96,512]{1,0:T(8,128)(2,1)S(1)}, u32[]{:S(2)}, u32[]{:S(2)}) collective-permute-start(bf16[96,512]{1,0:T(8,128)(2,1)S(1)} %get-tuple-element.54.refs_0_), channel_id=1, source_target_pairs={{0,8},{8,0},{16,24},{24,16},{1,9},{9,1},{17,25},{25,17},{2,10},{10... | collective-permute-start | bytes 294920 | tf_op jit(solution)/shard_map/ppermute | solution.py:423
  24.9 5.8 %collective-permute-start.9 = (bf16[96,512]{1,0:T(8,128)(2,1)S(1)}, bf16[96,512]{1,0:T(8,128)(2,1)S(1)}, u32[]{:S(2)}, u32[]{:S(2)}) collective-permute-start(bf16[96,512]{1,0:T(8,128)(2,1)S(1)} %get-tuple-element.55), channel_id=1, source_target_pairs={{0,16},{8,24},{16,0},{24,8},{1,17},{9,25},{17,1},{25,9},{2,18},{10... | collective-permute-start | bytes 294920 | tf_op jit(solution)/shard_map/ppermute | solution.py:423
  25.9 12.8 %copy-start = (bf16[2048,8]{0,1:T(8,128)(2,1)S(1)}, bf16[2048,8]{0,1:T(8,128)(2,1)}, u32[]{:S(2)}) copy-start(bf16[2048,8]{0,1:T(8,128)(2,1)} %param.11) | copy-start | bytes 98308
  27.1 7.3 %collective-permute-start.13 = (bf16[96,512]{1,0:T(8,128)(2,1)S(1)}, bf16[96,512]{1,0:T(8,128)(2,1)S(1)}, u32[]{:S(2)}, u32[]{:S(2)}) collective-permute-start(bf16[96,512]{1,0:T(8,128)(2,1)S(1)} %get-tuple-element.60), channel_id=1, source_target_pairs={{0,24},{8,16},{16,8},{24,0},{1,25},{9,17},{17,9},{25,1},{2,26},{10... | collective-permute-start | bytes 294920 | tf_op jit(solution)/shard_map/ppermute | solution.py:423
  29.1 5.3 %collective-permute-start.14 = (bf16[96,512]{1,0:T(8,128)(2,1)S(1)}, bf16[96,512]{1,0:T(8,128)(2,1)S(1)}, u32[]{:S(2)}, u32[]{:S(2)}) collective-permute-start(bf16[96,512]{1,0:T(8,128)(2,1)S(1)} %get-tuple-element.61), channel_id=1, source_target_pairs={{0,8},{8,0},{16,24},{24,16},{1,9},{9,1},{17,25},{25,17},{2,10},{10... | collective-permute-start | bytes 294920 | tf_op jit(solution)/shard_map/ppermute | solution.py:423
  29.7 4.8 %collective-permute-start.15 = (bf16[96,512]{1,0:T(8,128)(2,1)S(1)}, bf16[96,512]{1,0:T(8,128)(2,1)S(1)}, u32[]{:S(2)}, u32[]{:S(2)}) collective-permute-start(bf16[96,512]{1,0:T(8,128)(2,1)S(1)} %get-tuple-element.62), channel_id=1, source_target_pairs={{0,16},{8,24},{16,0},{24,8},{1,17},{9,25},{17,1},{25,9},{2,18},{10... | collective-permute-start | bytes 294920 | tf_op jit(solution)/shard_map/ppermute | solution.py:423
  30.8 6.3 %collective-permute-start.10 = (bf16[48,512]{1,0:T(8,128)(2,1)S(1)}, bf16[48,512]{1,0:T(8,128)(2,1)S(1)}, u32[]{:S(2)}, u32[]{:S(2)}) collective-permute-start(bf16[48,512]{1,0:T(8,128)(2,1)S(1)} %get-tuple-element.56.refs_0_), channel_id=1, source_target_pairs={{0,6},{1,7},{2,4},{3,5},{4,2},{5,3},{6,0},{7,1},{8,14},{9,15},{10,... | collective-permute-start | bytes 147464 | tf_op jit(solution)/shard_map/ppermute | solution.py:426
  32.9 5.0 %collective-permute-start.11 = (bf16[48,512]{1,0:T(8,128)(2,1)S(1)}, bf16[48,512]{1,0:T(8,128)(2,1)S(1)}, u32[]{:S(2)}, u32[]{:S(2)}) collective-permute-start(bf16[48,512]{1,0:T(8,128)(2,1)S(1)} %get-tuple-element.57), channel_id=1, source_target_pairs={{0,4},{1,5},{2,6},{3,7},{4,0},{5,1},{6,2},{7,3},{8,12},{9,13},{10,... | collective-permute-start | bytes 147464 | tf_op jit(solution)/shard_map/ppermute | solution.py:426
  34.5 4.2 %collective-permute-start.16 = (bf16[48,512]{1,0:T(8,128)(2,1)S(1)}, bf16[48,512]{1,0:T(8,128)(2,1)S(1)}, u32[]{:S(2)}, u32[]{:S(2)}) collective-permute-start(bf16[48,512]{1,0:T(8,128)(2,1)S(1)} %get-tuple-element.64), channel_id=1, source_target_pairs={{0,2},{1,3},{2,0},{3,1},{4,6},{5,7},{6,4},{7,5},{8,10},{9,11},{10,... | collective-permute-start | bytes 147464 | tf_op jit(solution)/shard_map/ppermute | solution.py:426
  38.7 1.4 %collective-permute-start.17 = (bf16[96,512]{1,0:T(8,128)(2,1)S(1)}, bf16[96,512]{1,0:T(8,128)(2,1)S(1)}, u32[]{:S(2)}, u32[]{:S(2)}) collective-permute-start(bf16[96,512]{1,0:T(8,128)(2,1)S(1)} %flip_back.1), channel_id=1, source_target_pairs={{0,1},{1,0},{2,3},{3,2},{4,5},{5,4},{6,7},{7,6},{8,9},{9,8},{10,11... | collective-permute-start | bytes 294920 | tf_op jit(solution)/shard_map/ppermute | solution.py:426

commit v6 on v5

--- a/solution.py
+++ b/solution.py
@@ -104,53 +104,90 @@
     return jnp.concatenate(values, axis=0)
 
 
-def dispatch_kernel(per_device, steps, *refs):
-    tokens_hbm, *small_hbm = refs[:6]
-    tokens_ref, gain_ref, slot_ref, cap_ref, local_ref, *out_refs = refs[6:13]
-    experts_ref, keys_ref, arrived = refs[13:]
-    small_refs = (experts_ref, keys_ref, gain_ref, slot_ref, cap_ref)
+def normed_part(tokens_ref, gain, start, width):
+    scale = row_scale(tokens_ref[...].astype(jnp.float32))
+    left = pl.multiple_of(start * width, width)
+    part = tokens_ref[:, pl.ds(left, width)].astype(jnp.float32)
+    return apply_gain(part * scale, gain, start * (width // 128))
+
+
+def place_kernel(per_device, *refs):
+    in_refs, out_refs, scratch = refs[:6], refs[6:11], refs[11:]
+    tokens_ref, gain_ref, slot_ref, cap_ref, local_ref = out_refs
+    experts_ref, keys_ref, arrived = scratch
+    targets = (tokens_ref, experts_ref, keys_ref, gain_ref, slot_ref, cap_ref)
     copies = [
         pltpu.make_async_copy(source, target, arrived.at[index])
-        for index, (source, target) in enumerate(
-            zip((*small_hbm, tokens_hbm), (*small_refs, tokens_ref))
-        )
+        for index, (source, target) in enumerate(zip(in_refs, targets))
     ]
     for copy in copies:
         copy.start()
-    for copy in copies[:-1]:
+    for copy in copies[1:]:
         copy.wait()
     local_ref[...] = place_rows(
         experts_ref[...], keys_ref[...], slot_ref[...], cap_ref[...], per_device
     )
-    pick = pick_rows(local_ref, None, steps, per_device).astype(jnp.bfloat16)
+    copies[0].wait()
+
+
+def dispatch_kernel(
+    per_device,
+    steps,
+    tokens_ref,
+    core_ref,
+    gain_ref,
+    local_ref,
+    experts_ref,
+    keys_ref,
+    slot_ref,
+    cap_ref,
+    core_local_ref,
+    *out_refs,
+):
+    core_local_ref[...] = place_rows(
+        experts_ref[...], keys_ref[...], slot_ref[...], cap_ref[...], per_device
+    )
     gain = gain_ref[...].astype(jnp.float32)
     width = out_refs[0].shape[1]
     group = lax.axis_index("dp")
-    copies[-1].wait()
-    scale = row_scale(tokens_ref[...].astype(jnp.float32))
-    start = pl.multiple_of(group * width, width)
-    part = tokens_ref[:, pl.ds(start, width)].astype(jnp.float32)
-    normed = apply_gain(part * scale, gain, group * (width // 128))
-    store_blocks(out_refs, jnp.dot(pick, normed, preferred_element_type=jnp.float32))
-
-
-def near_kernel(per_device, meet, steps, tokens_ref, gain_ref, local_ref, *out_refs):
+    rows = []
+    for here, places in ((tokens_ref, local_ref), (core_ref, core_local_ref)):
+        pick = pick_rows(places, None, steps, per_device).astype(jnp.bfloat16)
+        normed = normed_part(here, gain, group, width)
+        rows.append(jnp.dot(pick, normed, preferred_element_type=jnp.float32))
+    for index, ref in enumerate(out_refs):
+        block = slice(index * CAP_DEV, (index + 1) * CAP_DEV)
+        ref[...] = jnp.concatenate([r[block] for r in rows], axis=0).astype(ref.dtype)
+
+
+def near_kernel(
+    per_device,
+    meet,
+    steps,
+    tokens_ref,
+    core_ref,
+    gain_ref,
+    local_ref,
+    core_local_ref,
+    *out_refs,
+):
     gain = gain_ref[...].astype(jnp.float32)
     width = tokens_ref.shape[1] // len(meet)
     group = lax.axis_index("dp")
-    scale = row_scale(tokens_ref[...].astype(jnp.float32))
-    pick = pick_rows(local_ref, None, sum(steps, ()), per_device).astype(jnp.bfloat16)
-    for place, step in enumerate(meet):
-        start = pl.multiple_of((group ^ step) * width, width)
-        part = tokens_ref[:, pl.ds(start, width)].astype(jnp.float32)
-        normed = apply_gain(part * scale, gain, (group ^ step) * (width // 128))
-        value = jnp.dot(pick, normed, preferred_element_type=jnp.float32)
-        top = 0
-        for ref in out_refs:
-            ref[:, place * width : (place + 1) * width] = value[
-                top : top + ref.shape[0], :
-            ].astype(ref.dtype)
-            top += ref.shape[0]
+    sources = ((tokens_ref, local_ref), (core_ref, core_local_ref))
+    for side, (here, places) in enumerate(sources):
+        pick = pick_rows(places, None, steps, per_device).astype(jnp.bfloat16)
+        scale = row_scale(here[...].astype(jnp.float32))
+        for place, step in enumerate(meet):
+            start = pl.multiple_of((group ^ step) * width, width)
+            part = here[:, pl.ds(start, width)].astype(jnp.float32)
+            normed = apply_gain(part * scale, gain, (group ^ step) * (width // 128))
+            value = jnp.dot(pick, normed, preferred_element_type=jnp.float32)
+            for index, ref in enumerate(out_refs):
+                ref[
+                    side * CAP_DEV : (side + 1) * CAP_DEV,
+                    place * width : (place + 1) * width,
+                ] = value[index * CAP_DEV : (index + 1) * CAP_DEV, :].astype(ref.dtype)
 
 
 def weight_kernel(
@@ -308,12 +345,9 @@
 
 
 def near_expert_kernel(
-    per_device, own_ref, core_ref, chip_ref, first_ref, second_ref, cap_ref, down_ref, *out_refs
+    per_device, here_ref, chip_ref, first_ref, second_ref, cap_ref, down_ref, *out_refs
 ):
-    rows = jnp.concatenate(
-        [load_blocks([own_ref]), load_blocks([core_ref], 0), load_blocks([chip_ref])],
-        axis=0,
-    ).astype(jnp.bfloat16)
+    rows = jnp.concatenate([here_ref[...], chip_ref[...]], axis=0)
     width = first_ref.shape[1]
     gate_up = None
     for index in range(first_ref.shape[0] + second_ref.shape[0]):
@@ -333,19 +367,6 @@
 
 def join_kernel(*refs):
     refs[-1][...] = load_blocks(refs[:-1]).astype(refs[-1].dtype)
-
-
-def pair_kernel(same_ref, core_ref, *out_refs):
-    same, core = load_blocks([same_ref]), load_blocks([core_ref])
-    for index, ref in enumerate(out_refs):
-        rows = slice(index * CAP_DEV, (index + 1) * CAP_DEV)
-        ref[...] = jnp.concatenate([same[rows], core[rows]], axis=0).astype(ref.dtype)
-
-
-def forward_kernel(same_ref, core_ref, out_ref):
-    out_ref[...] = jnp.concatenate(
-        [load_blocks([same_ref]), load_blocks([core_ref], 1)], axis=0
-    ).astype(out_ref.dtype)
 
 
 def flip_kernel(*refs):
@@ -430,18 +451,16 @@
     cap_row = capacity.reshape(1, slots)
     down = down_weight.reshape(per_device * units, width)
 
-    (
-        tokens_here, gain_here, slot_here, cap_here, local, far_same, far_flip
-    ) = call(
-        functools.partial(
-            dispatch_kernel, per_device, [2 * c for c in far] + [2 * c + 1 for c in far]
-        ),
-        "dispatch",
+    core_tokens, core_experts, core_keys = (
+        to_peer(value, 1) for value in (tokens, experts.T, replica_key.T)
+    )
+    tokens_here, gain_here, slot_here, cap_here, local = call(
+        functools.partial(place_kernel, per_device),
+        "place",
         blocks(1, rows, width)
         + blocks(1, *gain.shape)
         + blocks(2, 1, slots, dtype=jnp.int32)
-        + blocks(1, slots, rows, dtype=jnp.float32)
-        + blocks(2, (chips - 2) * CAP_DEV, quarter),
+        + blocks(1, slots, rows, dtype=jnp.float32),
         hbm=[tokens, experts.T, replica_key.T, gain, slot_row, cap_row],
         scratch=[
             pltpu.VMEM((experts.shape[1], rows), jnp.int32),
@@ -449,30 +468,30 @@
             pltpu.SemaphoreType.DMA((6,)),
         ],
     )
-    core_far = to_peer(far_flip, 1)
-    own_rows, same_rows, flip_rows = call(
-        functools.partial(near_kernel, per_device, meet, ((0,), (2,), (1, 3))),
-        "dispatch_near",
-        blocks(2, CAP_DEV, width) + blocks(1, 2 * CAP_DEV, width),
+    core_local, *far_out = call(
+        functools.partial(dispatch_kernel, per_device, [2 * c for c in far]),
+        "dispatch",
+        blocks(1, slots, rows, dtype=jnp.float32)
+        + blocks(len(far), 2 * CAP_DEV, quarter),
         tokens_here,
+        core_tokens,
         gain_here,
         local,
-    )
-    core_rows = to_peer(flip_rows, 1)
-    far_out = call(
-        pair_kernel,
-        "pair_far",
-        blocks(chips - 2, 2 * CAP_DEV, quarter),
-        far_same,
-        core_far,
+        core_experts,
+        core_keys,
+        slot_here,
+        cap_here,
     )
     far_in = [to_peer(value, 2 * chip) for chip, value in zip(far, far_out)]
-    (chip_rows,) = call(
-        forward_kernel,
-        "forward_near",
-        blocks(1, 2 * CAP_DEV, width),
-        same_rows,
-        core_rows,
+    here_rows, chip_rows = call(
+        functools.partial(near_kernel, per_device, meet, (0, 2)),
+        "dispatch_near",
+        blocks(2, 2 * CAP_DEV, width),
+        tokens_here,
+        core_tokens,
+        gain_here,
+        local,
+        core_local,
         after=(far_out[0],),
     )
     near_ready = chip_rows
@@ -544,8 +563,7 @@
         functools.partial(near_expert_kernel, per_device),
         "expert_near",
         blocks(groups, NEAR * CAP_DEV, quarter),
-        own_rows,
-        core_rows,
+        here_rows,
         chip_rows,
         first_weights,
         second_weights,

time: 41.1 us -> 40.3 us (0.981)
  waiting for transfers between devices: 9.22 us -> 7.81 us
    ppermute x9 -> x10, waiting for transfers between devices: 7.38 us -> 5.75 us  [to_peer(): return lax.ppermute(value, 'expert', [(i, i ^ step) for i in range(peers)])]
    pallas_call x18 -> x17, Pallas kernels: 10.4 us -> 10.8 us  [call(): pl.pallas_call(lambda *refs: kernel(*refs[count:]), in_specs=[pl.BlockSpe...]
    ppermute x9 -> x10, starting transfers between devices: 10.5 us -> 10.7 us  [to_peer(): return lax.ppermute(value, 'expert', [(i, i ^ step) for i in range(peers)])]
  transfers between devices with their start and end apart: 18 -> 19, of which waited for: 8 -> 8; matrix products, arithmetic and copies ran while one was open for 0% -> 0% of each run, Pallas kernels for 19% -> 23%
where the time goes in v6:
time: 40.3 us; the launch traced here: 40.2 us
  starting transfers between devices  21.4 us (53%)
  Pallas kernels  10.8 us (27%)
  waiting for transfers between devices  7.81 us (19%)
    pallas_call x17, Pallas kernels, call(): pl.pallas_call(lambda *refs: kernel(*refs[count:]), in_specs=[pl.BlockSpe...  10.8 us
    ppermute x10, starting transfers between devices, to_peer(): return lax.ppermute(value, 'expert', [(i, i ^ step) for i in range(peers)])  10.7 us
    ppermute x9, starting transfers between devices, to_group(): return lax.ppermute(value, 'dp', [(i, i ^ step) for i in range(groups)])  10.7 us
    ppermute x10, waiting for transfers between devices, to_peer(): return lax.ppermute(value, 'expert', [(i, i ^ step) for i in range(peers)])  5.75 us
    ppermute x9, waiting for transfers between devices, to_group(): return lax.ppermute(value, 'dp', [(i, i ^ step) for i in range(groups)])  2.06 us
  transfers between devices with their start and end apart: 19, of which 8 were waited for; matrix products, arithmetic and copies ran while one was open for 0% of the time, Pallas kernels for 23%

profile of v6, /device:TPU:0, one launch (start us, length us, event | category | flops | bytes accessed | tf_op | source)
XLA Modules:
  0.0 40.2 jit_solution(15562306479614898423)
XLA Ops:
  0.0 0.5 %collective-permute-start = (bf16[128,2048]{1,0:T(8,128)(2,1)}, bf16[128,2048]{1,0:T(8,128)(2,1)S(1)}, u32[]{:S(2)}, u32[]{:S(2)}) collective-permute-start(bf16[128,2048]{1,0:T(8,128)(2,1)} %refs_0_.1), channel_id=1, source_target_pairs={{0,1},{1,0},{2,3},{3,2},{4,5},{5,4},{6,7},{7,6},{8,9},{9,8},{10,11... | collective-permute-start | bytes 1572872 | tf_op jit(solution)/shard_map/ppermute | solution.py:447
  0.5 0.1 collective-permute-start.1
  0.5 0.5 %collective-permute-start.2 = (s32[8,128]{1,0:T(8,128)}, s32[8,128]{1,0:T(8,128)S(1)}, u32[]{:S(2)}, u32[]{:S(2)}) collective-permute-start(s32[8,128]{1,0:T(8,128)} %bitcast.18), channel_id=1, source_target_pairs={{0,1},{1,0},{2,3},{3,2},{4,5},{5,4},{6,7},{7,6},{8,9},{9,8},{10,11... | collective-permute-start | bytes 12296 | tf_op jit(solution)/shard_map/ppermute | solution.py:447
  1.0 1.2 %place.1 = (bf16[128,2048]{1,0:T(8,128)(2,1)S(1)}, bf16[16,128]{1,0:T(8,128)(2,1)S(1)}, s32[1,16]{1,0:T(1,128)S(1)}, s32[1,16]{1,0:T(1,128)S(1)}, f32[16,128]{1,0:T(8,128)S(1)}) custom-call(bf16[128,2048]{1,0:T(8,128)(2,1)} %refs_0_.1, s32[8,128]{1,0:T(8,128)} %bitcast.17, s32[8,128]{1,0:T(8,128)} %bitcast.19, bf16[16,128]{1,0:T(8,128)(2,1)} %bitcast.15, ...), custom_call_target="tpu_custom_call" | custom-call | flops 1 | bytes 1 | tf_op jit(solution)/shard_map/place/pallas_call | solution.py:404
  2.2 0.0 collective-permute-done.1.refs_4_
  2.2 0.0 collective-permute-done.2.refs_5_
  2.2 0.0 collective-permute-done.refs_1_.refs_2_
  2.2 0.5 %dispatch.1 = (f32[16,128]{1,0:T(8,128)S(1)}, bf16[48,512]{1,0:T(8,128)(2,1)S(1)}, bf16[48,512]{1,0:T(8,128)(2,1)S(1)}) custom-call(bf16[128,2048]{1,0:T(8,128)(2,1)S(1)} %get-tuple-element.33.refs_0_.refs_1_, bf16[128,2048]{1,0:T(8,128)(2,1)S(1)} %collective-permute-done.refs_1_.refs_2_, bf16[16,128]{1,0:T(8,128)(2,1)S(1)} %get-tuple-element.34.refs_1_.refs_2_.refs_3_, ...), custom_call_target="tpu_custom_call" | custom-call | flops 1 | bytes 1 | tf_op jit(solution)/shard_map/dispatch/pallas_call | solution.py:404
  2.8 5.0 %collective-permute-start.3 = (bf16[48,512]{1,0:T(8,128)(2,1)S(1)}, bf16[48,512]{1,0:T(8,128)(2,1)S(1)}, u32[]{:S(2)}, u32[]{:S(2)}) collective-permute-start(bf16[48,512]{1,0:T(8,128)(2,1)S(1)} %get-tuple-element.40.refs_0_), channel_id=1, source_target_pairs={{0,6},{1,7},{2,4},{3,5},{4,2},{5,3},{6,0},{7,1},{8,14},{9,15},{10,... | collective-permute-start | bytes 147464 | tf_op jit(solution)/shard_map/ppermute | solution.py:447
  7.8 0.7 %dispatch_near.1 = (bf16[48,2048]{1,0:T(8,128)(2,1)S(1)}, bf16[48,2048]{1,0:T(8,128)(2,1)S(1)}) custom-call(bf16[48,512]{1,0:T(8,128)(2,1)S(1)} %get-tuple-element.40.refs_0_, bf16[128,2048]{1,0:T(8,128)(2,1)S(1)} %get-tuple-element.33.refs_0_.refs_1_, bf16[128,2048]{1,0:T(8,128)(2,1)S(1)} %collective-permute-done.refs_1_.refs_2_, ...), custom_call_target="tpu_custom_call" | custom-call | flops 1 | bytes 1 | tf_op jit(solution)/shard_map/dispatch_near/pallas_call | solution.py:404
  8.4 2.3 %split_first.1 = (bf16[2,512,1024]{2,1,0:T(8,128)(2,1)S(1)}, bf16[2,2,2048,128]{3,2,1,0:T(8,128)(2,1)S(1)}) custom-call(bf16[48,2048]{1,0:T(8,128)(2,1)S(1)} %get-tuple-element.42.refs_0_, bf16[2,8192,128]{2,1,0:T(8,128)(2,1)} %bitcast.13), custom_call_target="tpu_custom_call" | custom-call | flops 1 | bytes 1 | tf_op jit(solution)/shard_map/split_first/pallas_call | solution.py:404
  10.7 0.0 collective-permute-done.3.refs_1_
  10.7 2.0 %collective-permute-done.4.refs_2_ = bf16[48,512]{1,0:T(8,128)(2,1)S(1)} collective-permute-done((bf16[48,512]{1,0:T(8,128)(2,1)S(1)}, bf16[48,512]{1,0:T(8,128)(2,1)S(1)}, u32[]{:S(2)}, u32[]{:S(2)}) %collective-permute-start.4) | collective-permute-done | bytes 49184 | tf_op jit(solution)/shard_map/ppermute | solution.py:447
  12.8 2.5 %collective-permute-start.6 = (bf16[96,512]{1,0:T(8,128)(2,1)S(1)}, bf16[96,512]{1,0:T(8,128)(2,1)S(1)}, u32[]{:S(2)}, u32[]{:S(2)}) collective-permute-start(bf16[96,512]{1,0:T(8,128)(2,1)S(1)} %join_far.1.refs_0_), channel_id=1, source_target_pairs={{0,24},{8,16},{16,8},{24,0},{1,25},{9,17},{17,9},{25,1},{2,26},{10... | collective-permute-start | bytes 294920 | tf_op jit(solution)/shard_map/ppermute | solution.py:444
  15.3 0.5 %collective-permute-start.5 = (bf16[96,512]{1,0:T(8,128)(2,1)S(1)}, bf16[96,512]{1,0:T(8,128)(2,1)S(1)}, u32[]{:S(2)}, u32[]{:S(2)}) collective-permute-start(bf16[96,512]{1,0:T(8,128)(2,1)S(1)} %join_far.1.refs_0_), channel_id=1, source_target_pairs={{0,8},{8,0},{16,24},{24,16},{1,9},{9,1},{17,25},{25,17},{2,10},{10... | collective-permute-start | bytes 294920 | tf_op jit(solution)/shard_map/ppermute | solution.py:444
  15.8 0.5 %collective-permute-start.7 = (bf16[96,512]{1,0:T(8,128)(2,1)S(1)}, bf16[96,512]{1,0:T(8,128)(2,1)S(1)}, u32[]{:S(2)}, u32[]{:S(2)}) collective-permute-start(bf16[96,512]{1,0:T(8,128)(2,1)S(1)} %join_far.1.refs_0_), channel_id=1, source_target_pairs={{0,16},{8,24},{16,0},{24,8},{1,17},{9,25},{17,1},{25,9},{2,18},{10... | collective-permute-start | bytes 294920 | tf_op jit(solution)/shard_map/ppermute | solution.py:444
  16.3 0.3 product_far.3.refs_2_
  16.6 1.6 %split_second.1 = (bf16[2,512,1024]{2,1,0:T(8,128)(2,1)S(1)}, bf16[512,2048]{1,0:T(8,128)(2,1)S(1)}) custom-call(bf16[96,512]{1,0:T(8,128)(2,1)S(1)} %join_far.1.refs_0_, bf16[512,2048]{1,0:T(8,128)(2,1)} %bitcast.14, bf16[2,2,2048,128]{3,2,1,0:T(8,128)(2,1)S(1)} %get-tuple-element.45.refs_2_), custom_call_target="tpu_custom_call" | custom-call | flops 1 | bytes 1 | tf_op jit(solution)/shard_map/split_second/pallas_call | solution.py:404
  18.3 0.7 %collective-permute-done.6.refs_0_ = bf16[96,512]{1,0:T(8,128)(2,1)S(1)} collective-permute-done((bf16[96,512]{1,0:T(8,128)(2,1)S(1)}, bf16[96,512]{1,0:T(8,128)(2,1)S(1)}, u32[]{:S(2)}, u32[]{:S(2)}) %collective-permute-start.6) | collective-permute-done | bytes 98336 | tf_op jit(solution)/shard_map/ppermute | solution.py:444
  19.0 0.3 product_far.4.refs_2_
  19.3 0.8 %collective-permute-done.5.refs_0_ = bf16[96,512]{1,0:T(8,128)(2,1)S(1)} collective-permute-done((bf16[96,512]{1,0:T(8,128)(2,1)S(1)}, bf16[96,512]{1,0:T(8,128)(2,1)S(1)}, u32[]{:S(2)}, u32[]{:S(2)}) %collective-permute-start.5) | collective-permute-done | bytes 98336 | tf_op jit(solution)/shard_map/ppermute | solution.py:444
  20.0 0.3 product_far.5.refs_0_
  20.3 0.1 collective-permute-done.7.refs_1_
  20.5 0.7 %expert_far.1 = (bf16[96,512]{1,0:T(8,128)(2,1)S(1)}, bf16[96,512]{1,0:T(8,128)(2,1)S(1)}, bf16[96,512]{1,0:T(8,128)(2,1)S(1)}, bf16[96,512]{1,0:T(8,128)(2,1)S(1)}) custom-call(f32[96,1024]{1,0:T(8,128)S(1)} %product_far.5.refs_0_, bf16[96,512]{1,0:T(8,128)(2,1)S(1)} %collective-permute-done.7.refs_1_, ...), custom_call_target="tpu_custom_call" | custom-call | flops 1 | bytes 1 | tf_op jit(solution)/shard_map/expert_far/pallas_call | solution.py:404
  21.2 1.9 %collective-permute-start.8 = (bf16[96,512]{1,0:T(8,128)(2,1)S(1)}, bf16[96,512]{1,0:T(8,128)(2,1)S(1)}, u32[]{:S(2)}, u32[]{:S(2)}) collective-permute-start(bf16[96,512]{1,0:T(8,128)(2,1)S(1)} %get-tuple-element.49), channel_id=1, source_target_pairs={{0,24},{8,16},{16,8},{24,0},{1,25},{9,17},{17,9},{25,1},{2,26},{10... | collective-permute-start | bytes 294920 | tf_op jit(solution)/shard_map/ppermute | solution.py:444
  23.0 0.6 %collective-permute-start.9 = (bf16[96,512]{1,0:T(8,128)(2,1)S(1)}, bf16[96,512]{1,0:T(8,128)(2,1)S(1)}, u32[]{:S(2)}, u32[]{:S(2)}) collective-permute-start(bf16[96,512]{1,0:T(8,128)(2,1)S(1)} %get-tuple-element.50.refs_0_), channel_id=1, source_target_pairs={{0,8},{8,0},{16,24},{24,16},{1,9},{9,1},{17,25},{25,17},{2,10},{10... | collective-permute-start | bytes 294920 | tf_op jit(solution)/shard_map/ppermute | solution.py:444
  23.7 1.0 %collective-permute-start.10 = (bf16[96,512]{1,0:T(8,128)(2,1)S(1)}, bf16[96,512]{1,0:T(8,128)(2,1)S(1)}, u32[]{:S(2)}, u32[]{:S(2)}) collective-permute-start(bf16[96,512]{1,0:T(8,128)(2,1)S(1)} %get-tuple-element.51), channel_id=1, source_target_pairs={{0,16},{8,24},{16,0},{24,8},{1,17},{9,25},{17,1},{25,9},{2,18},{10... | collective-permute-start | bytes 294920 | tf_op jit(solution)/shard_map/ppermute | solution.py:444
  24.7 0.0 collective-permute-done.13.refs_2_
  24.7 1.2 %expert_near.1 = (bf16[96,512]{1,0:T(8,128)(2,1)S(1)}, bf16[96,512]{1,0:T(8,128)(2,1)S(1)}, bf16[96,512]{1,0:T(8,128)(2,1)S(1)}, bf16[96,512]{1,0:T(8,128)(2,1)S(1)}) custom-call(bf16[96,512]{1,0:T(8,128)(2,1)S(1)} %get-tuple-element.50.refs_0_, bf16[48,2048]{1,0:T(8,128)(2,1)S(1)} %get-tuple-element.54.refs_1_, ...), custom_call_target="tpu_custom_call" | custom-call | flops 1 | bytes 1 | tf_op jit(solution)/shard_map/expert_near/pallas_call | solution.py:404
  25.9 1.9 %collective-permute-start.14 = (bf16[96,512]{1,0:T(8,128)(2,1)S(1)}, bf16[96,512]{1,0:T(8,128)(2,1)S(1)}, u32[]{:S(2)}, u32[]{:S(2)}) collective-permute-start(bf16[96,512]{1,0:T(8,128)(2,1)S(1)} %get-tuple-element.56), channel_id=1, source_target_pairs={{0,24},{8,16},{16,8},{24,0},{1,25},{9,17},{17,9},{25,1},{2,26},{10... | collective-permute-start | bytes 294920 | tf_op jit(solution)/shard_map/ppermute | solution.py:444
  27.8 0.6 %collective-permute-start.15 = (bf16[96,512]{1,0:T(8,128)(2,1)S(1)}, bf16[96,512]{1,0:T(8,128)(2,1)S(1)}, u32[]{:S(2)}, u32[]{:S(2)}) collective-permute-start(bf16[96,512]{1,0:T(8,128)(2,1)S(1)} %get-tuple-element.57), channel_id=1, source_target_pairs={{0,8},{8,0},{16,24},{24,16},{1,9},{9,1},{17,25},{25,17},{2,10},{10... | collective-permute-start | bytes 294920 | tf_op jit(solution)/shard_map/ppermute | solution.py:444
  28.5 1.0 %collective-permute-start.16 = (bf16[96,512]{1,0:T(8,128)(2,1)S(1)}, bf16[96,512]{1,0:T(8,128)(2,1)S(1)}, u32[]{:S(2)}, u32[]{:S(2)}) collective-permute-start(bf16[96,512]{1,0:T(8,128)(2,1)S(1)} %get-tuple-element.58), channel_id=1, source_target_pairs={{0,16},{8,24},{16,0},{24,8},{1,17},{9,25},{17,1},{25,9},{2,18},{10... | collective-permute-start | bytes 294920 | tf_op jit(solution)/shard_map/ppermute | solution.py:444
  29.5 0.5 %collective-permute-done.10.refs_3_ = bf16[96,512]{1,0:T(8,128)(2,1)S(1)} collective-permute-done((bf16[96,512]{1,0:T(8,128)(2,1)S(1)}, bf16[96,512]{1,0:T(8,128)(2,1)S(1)}, u32[]{:S(2)}, u32[]{:S(2)}) %collective-permute-start.10) | collective-permute-done | bytes 98336 | tf_op jit(solution)/shard_map/ppermute | solution.py:444
  30.0 0.1 sum_far.1
  30.0 2.3 %collective-permute-start.11 = (bf16[48,512]{1,0:T(8,128)(2,1)S(1)}, bf16[48,512]{1,0:T(8,128)(2,1)S(1)}, u32[]{:S(2)}, u32[]{:S(2)}) collective-permute-start(bf16[48,512]{1,0:T(8,128)(2,1)S(1)} %get-tuple-element.52.refs_0_), channel_id=1, source_target_pairs={{0,6},{1,7},{2,4},{3,5},{4,2},{5,3},{6,0},{7,1},{8,14},{9,15},{10,... | collective-permute-start | bytes 147464 | tf_op jit(solution)/shard_map/ppermute | solution.py:447
  32.4 1.1 %collective-permute-start.12 = (bf16[48,512]{1,0:T(8,128)(2,1)S(1)}, bf16[48,512]{1,0:T(8,128)(2,1)S(1)}, u32[]{:S(2)}, u32[]{:S(2)}) collective-permute-start(bf16[48,512]{1,0:T(8,128)(2,1)S(1)} %get-tuple-element.53), channel_id=1, source_target_pairs={{0,4},{1,5},{2,6},{3,7},{4,0},{5,1},{6,2},{7,3},{8,12},{9,13},{10,... | collective-permute-start | bytes 147464 | tf_op jit(solution)/shard_map/ppermute | solution.py:447
  33.5 0.0 collective-permute-done.15.refs_3_
  33.5 0.0 collective-permute-done.16.refs_4_
  33.5 0.1 sum_near.1
  33.6 1.2 %collective-permute-start.17 = (bf16[48,512]{1,0:T(8,128)(2,1)S(1)}, bf16[48,512]{1,0:T(8,128)(2,1)S(1)}, u32[]{:S(2)}, u32[]{:S(2)}) collective-permute-start(bf16[48,512]{1,0:T(8,128)(2,1)S(1)} %get-tuple-element.60), channel_id=1, source_target_pairs={{0,2},{1,3},{2,0},{3,1},{4,6},{5,7},{6,4},{7,5},{8,10},{9,11},{10,... | collective-permute-start | bytes 147464 | tf_op jit(solution)/shard_map/ppermute | solution.py:447
  34.7 1.3 %collective-permute-done.11.refs_2_.refs_0_ = bf16[48,512]{1,0:T(8,128)(2,1)S(1)} collective-permute-done((bf16[48,512]{1,0:T(8,128)(2,1)S(1)}, bf16[48,512]{1,0:T(8,128)(2,1)S(1)}, u32[]{:S(2)}, u32[]{:S(2)}) %collective-permute-start.11) | collective-permute-done | bytes 49184 | tf_op jit(solution)/shard_map/ppermute | solution.py:447
  36.1 1.8 %collective-permute-done.12.refs_3_.refs_1_ = bf16[48,512]{1,0:T(8,128)(2,1)S(1)} collective-permute-done((bf16[48,512]{1,0:T(8,128)(2,1)S(1)}, bf16[48,512]{1,0:T(8,128)(2,1)S(1)}, u32[]{:S(2)}, u32[]{:S(2)}) %collective-permute-start.12) | collective-permute-done | bytes 49184 | tf_op jit(solution)/shard_map/ppermute | solution.py:447
  37.9 0.0 collective-permute-done.17.refs_5_.refs_3_
  37.9 0.1 collective-permute-start.18
  38.0 0.5 %combine_weights.1 = (bf16[128,192]{1,0:T(8,128)(2,1)S(1)}, bf16[128,512]{1,0:T(8,128)(2,1)S(1)}) custom-call(bf16[128,2048]{1,0:T(8,128)(2,1)S(1)} %get-tuple-element.33.refs_0_.refs_1_, bf16[16,128]{1,0:T(8,128)(2,1)S(1)} %get-tuple-element.34.refs_1_.refs_2_.refs_3_, bf16[8,2048]{1,0:T(8,128)(2,1)S(1)} %bitcast.12, ...), custom_call_target="tpu_custom_call" | custom-call | flops 1 | bytes 1 | tf_op jit(solution)/shard_map/combine_weights/pallas_call | solution.py:404
  38.5 0.2 combine.1.refs_1_
  38.7 0.6 %collective-permute-done.18.refs_2_ = bf16[96,512]{1,0:T(8,128)(2,1)S(1)} collective-permute-done((bf16[96,512]{1,0:T(8,128)(2,1)S(1)}, bf16[96,512]{1,0:T(8,128)(2,1)S(1)}, u32[]{:S(2)}, u32[]{:S(2)}) %collective-permute-start.18) | collective-permute-done | bytes 98336 | tf_op jit(solution)/shard_map/ppermute | solution.py:447
  39.3 0.9 %finish.1 = bf16[128,512]{1,0:T(8,128)(2,1)} custom-call(bf16[128,192]{1,0:T(8,128)(2,1)S(1)} %get-tuple-element.37.refs_0_, f32[128,512]{1,0:T(8,128)S(1)} %combine.1.refs_1_, bf16[96,512]{1,0:T(8,128)(2,1)S(1)} %collective-permute-done.18.refs_2_), custom_call_target="tpu_custom_call" | custom-call | flops 1 | bytes 1 | tf_op jit(solution)/shard_map/finish/pallas_call | solution.py:404
  (9 shorter events, 0.0 us)
Async XLA Ops:
  0.0 2.2 %collective-permute-start = (bf16[128,2048]{1,0:T(8,128)(2,1)}, bf16[128,2048]{1,0:T(8,128)(2,1)S(1)}, u32[]{:S(2)}, u32[]{:S(2)}) collective-permute-start(bf16[128,2048]{1,0:T(8,128)(2,1)} %refs_0_.1), channel_id=1, source_target_pairs={{0,1},{1,0},{2,3},{3,2},{4,5},{5,4},{6,7},{7,6},{8,9},{9,8},{10,11... | collective-permute-start | bytes 1572872 | tf_op jit(solution)/shard_map/ppermute | solution.py:447
  0.5 1.8 %collective-permute-start.1 = (s32[8,128]{1,0:T(8,128)}, s32[8,128]{1,0:T(8,128)S(1)}, u32[]{:S(2)}, u32[]{:S(2)}) collective-permute-start(s32[8,128]{1,0:T(8,128)} %bitcast.16), channel_id=1, source_target_pairs={{0,1},{1,0},{2,3},{3,2},{4,5},{5,4},{6,7},{7,6},{8,9},{9,8},{10,11... | collective-permute-start | bytes 12296 | tf_op jit(solution)/shard_map/ppermute | solution.py:447
  0.5 1.7 %collective-permute-start.2 = (s32[8,128]{1,0:T(8,128)}, s32[8,128]{1,0:T(8,128)S(1)}, u32[]{:S(2)}, u32[]{:S(2)}) collective-permute-start(s32[8,128]{1,0:T(8,128)} %bitcast.18), channel_id=1, source_target_pairs={{0,1},{1,0},{2,3},{3,2},{4,5},{5,4},{6,7},{7,6},{8,9},{9,8},{10,11... | collective-permute-start | bytes 12296 | tf_op jit(solution)/shard_map/ppermute | solution.py:447
  2.8 8.0 %collective-permute-start.3 = (bf16[48,512]{1,0:T(8,128)(2,1)S(1)}, bf16[48,512]{1,0:T(8,128)(2,1)S(1)}, u32[]{:S(2)}, u32[]{:S(2)}) collective-permute-start(bf16[48,512]{1,0:T(8,128)(2,1)S(1)} %get-tuple-element.40.refs_0_), channel_id=1, source_target_pairs={{0,6},{1,7},{2,4},{3,5},{4,2},{5,3},{6,0},{7,1},{8,14},{9,15},{10,... | collective-permute-start | bytes 147464 | tf_op jit(solution)/shard_map/ppermute | solution.py:447
  7.8 5.0 %collective-permute-start.4 = (bf16[48,512]{1,0:T(8,128)(2,1)S(1)}, bf16[48,512]{1,0:T(8,128)(2,1)S(1)}, u32[]{:S(2)}, u32[]{:S(2)}) collective-permute-start(bf16[48,512]{1,0:T(8,128)(2,1)S(1)} %get-tuple-element.44), channel_id=1, source_target_pairs={{0,4},{1,5},{2,6},{3,7},{4,0},{5,1},{6,2},{7,3},{8,12},{9,13},{10,... | collective-permute-start | bytes 147464 | tf_op jit(solution)/shard_map/ppermute | solution.py:447
  12.8 6.2 %collective-permute-start.6 = (bf16[96,512]{1,0:T(8,128)(2,1)S(1)}, bf16[96,512]{1,0:T(8,128)(2,1)S(1)}, u32[]{:S(2)}, u32[]{:S(2)}) collective-permute-start(bf16[96,512]{1,0:T(8,128)(2,1)S(1)} %join_far.1.refs_0_), channel_id=1, source_target_pairs={{0,24},{8,16},{16,8},{24,0},{1,25},{9,17},{17,9},{25,1},{2,26},{10... | collective-permute-start | bytes 294920 | tf_op jit(solution)/shard_map/ppermute | solution.py:444
  15.3 9.4 %collective-permute-start.13 = (bf16[48,2048]{1,0:T(8,128)(2,1)S(1)}, bf16[48,2048]{1,0:T(8,128)(2,1)S(1)}, u32[]{:S(2)}, u32[]{:S(2)}) collective-permute-start(bf16[48,2048]{1,0:T(8,128)(2,1)S(1)} %get-tuple-element.42.refs_0_), channel_id=1, source_target_pairs={{0,2},{1,3},{2,0},{3,1},{4,6},{5,7},{6,4},{7,5},{8,10},{9,11},{10,... | collective-permute-start | bytes 589832 | tf_op jit(solution)/shard_map/ppermute | solution.py:447
  15.3 4.7 %collective-permute-start.5 = (bf16[96,512]{1,0:T(8,128)(2,1)S(1)}, bf16[96,512]{1,0:T(8,128)(2,1)S(1)}, u32[]{:S(2)}, u32[]{:S(2)}) collective-permute-start(bf16[96,512]{1,0:T(8,128)(2,1)S(1)} %join_far.1.refs_0_), channel_id=1, source_target_pairs={{0,8},{8,0},{16,24},{24,16},{1,9},{9,1},{17,25},{25,17},{2,10},{10... | collective-permute-start | bytes 294920 | tf_op jit(solution)/shard_map/ppermute | solution.py:444
  15.8 4.6 %collective-permute-start.7 = (bf16[96,512]{1,0:T(8,128)(2,1)S(1)}, bf16[96,512]{1,0:T(8,128)(2,1)S(1)}, u32[]{:S(2)}, u32[]{:S(2)}) collective-permute-start(bf16[96,512]{1,0:T(8,128)(2,1)S(1)} %join_far.1.refs_0_), channel_id=1, source_target_pairs={{0,16},{8,24},{16,0},{24,8},{1,17},{9,25},{17,1},{25,9},{2,18},{10... | collective-permute-start | bytes 294920 | tf_op jit(solution)/shard_map/ppermute | solution.py:444
  21.2 7.3 %collective-permute-start.8 = (bf16[96,512]{1,0:T(8,128)(2,1)S(1)}, bf16[96,512]{1,0:T(8,128)(2,1)S(1)}, u32[]{:S(2)}, u32[]{:S(2)}) collective-permute-start(bf16[96,512]{1,0:T(8,128)(2,1)S(1)} %get-tuple-element.49), channel_id=1, source_target_pairs={{0,24},{8,16},{16,8},{24,0},{1,25},{9,17},{17,9},{25,1},{2,26},{10... | collective-permute-start | bytes 294920 | tf_op jit(solution)/shard_map/ppermute | solution.py:444
  23.0 6.5 %collective-permute-start.9 = (bf16[96,512]{1,0:T(8,128)(2,1)S(1)}, bf16[96,512]{1,0:T(8,128)(2,1)S(1)}, u32[]{:S(2)}, u32[]{:S(2)}) collective-permute-start(bf16[96,512]{1,0:T(8,128)(2,1)S(1)} %get-tuple-element.50.refs_0_), channel_id=1, source_target_pairs={{0,8},{8,0},{16,24},{24,16},{1,9},{9,1},{17,25},{25,17},{2,10},{10... | collective-permute-start | bytes 294920 | tf_op jit(solution)/shard_map/ppermute | solution.py:444
  23.7 6.3 %collective-permute-start.10 = (bf16[96,512]{1,0:T(8,128)(2,1)S(1)}, bf16[96,512]{1,0:T(8,128)(2,1)S(1)}, u32[]{:S(2)}, u32[]{:S(2)}) collective-permute-start(bf16[96,512]{1,0:T(8,128)(2,1)S(1)} %get-tuple-element.51), channel_id=1, source_target_pairs={{0,16},{8,24},{16,0},{24,8},{1,17},{9,25},{17,1},{25,9},{2,18},{10... | collective-permute-start | bytes 294920 | tf_op jit(solution)/shard_map/ppermute | solution.py:444
  24.7 13.2 %copy-start = (bf16[2048,8]{0,1:T(8,128)(2,1)S(1)}, bf16[2048,8]{0,1:T(8,128)(2,1)}, u32[]{:S(2)}) copy-start(bf16[2048,8]{0,1:T(8,128)(2,1)} %param.11) | copy-start | bytes 98308
  25.9 7.6 %collective-permute-start.14 = (bf16[96,512]{1,0:T(8,128)(2,1)S(1)}, bf16[96,512]{1,0:T(8,128)(2,1)S(1)}, u32[]{:S(2)}, u32[]{:S(2)}) collective-permute-start(bf16[96,512]{1,0:T(8,128)(2,1)S(1)} %get-tuple-element.56), channel_id=1, source_target_pairs={{0,24},{8,16},{16,8},{24,0},{1,25},{9,17},{17,9},{25,1},{2,26},{10... | collective-permute-start | bytes 294920 | tf_op jit(solution)/shard_map/ppermute | solution.py:444
  27.8 5.7 %collective-permute-start.15 = (bf16[96,512]{1,0:T(8,128)(2,1)S(1)}, bf16[96,512]{1,0:T(8,128)(2,1)S(1)}, u32[]{:S(2)}, u32[]{:S(2)}) collective-permute-start(bf16[96,512]{1,0:T(8,128)(2,1)S(1)} %get-tuple-element.57), channel_id=1, source_target_pairs={{0,8},{8,0},{16,24},{24,16},{1,9},{9,1},{17,25},{25,17},{2,10},{10... | collective-permute-start | bytes 294920 | tf_op jit(solution)/shard_map/ppermute | solution.py:444
  28.5 5.1 %collective-permute-start.16 = (bf16[96,512]{1,0:T(8,128)(2,1)S(1)}, bf16[96,512]{1,0:T(8,128)(2,1)S(1)}, u32[]{:S(2)}, u32[]{:S(2)}) collective-permute-start(bf16[96,512]{1,0:T(8,128)(2,1)S(1)} %get-tuple-element.58), channel_id=1, source_target_pairs={{0,16},{8,24},{16,0},{24,8},{1,17},{9,25},{17,1},{25,9},{2,18},{10... | collective-permute-start | bytes 294920 | tf_op jit(solution)/shard_map/ppermute | solution.py:444
  30.0 6.1 %collective-permute-start.11 = (bf16[48,512]{1,0:T(8,128)(2,1)S(1)}, bf16[48,512]{1,0:T(8,128)(2,1)S(1)}, u32[]{:S(2)}, u32[]{:S(2)}) collective-permute-start(bf16[48,512]{1,0:T(8,128)(2,1)S(1)} %get-tuple-element.52.refs_0_), channel_id=1, source_target_pairs={{0,6},{1,7},{2,4},{3,5},{4,2},{5,3},{6,0},{7,1},{8,14},{9,15},{10,... | collective-permute-start | bytes 147464 | tf_op jit(solution)/shard_map/ppermute | solution.py:447
  32.4 5.5 %collective-permute-start.12 = (bf16[48,512]{1,0:T(8,128)(2,1)S(1)}, bf16[48,512]{1,0:T(8,128)(2,1)S(1)}, u32[]{:S(2)}, u32[]{:S(2)}) collective-permute-start(bf16[48,512]{1,0:T(8,128)(2,1)S(1)} %get-tuple-element.53), channel_id=1, source_target_pairs={{0,4},{1,5},{2,6},{3,7},{4,0},{5,1},{6,2},{7,3},{8,12},{9,13},{10,... | collective-permute-start | bytes 147464 | tf_op jit(solution)/shard_map/ppermute | solution.py:447
  33.6 4.3 %collective-permute-start.17 = (bf16[48,512]{1,0:T(8,128)(2,1)S(1)}, bf16[48,512]{1,0:T(8,128)(2,1)S(1)}, u32[]{:S(2)}, u32[]{:S(2)}) collective-permute-start(bf16[48,512]{1,0:T(8,128)(2,1)S(1)} %get-tuple-element.60), channel_id=1, source_target_pairs={{0,2},{1,3},{2,0},{3,1},{4,6},{5,7},{6,4},{7,5},{8,10},{9,11},{10,... | collective-permute-start | bytes 147464 | tf_op jit(solution)/shard_map/ppermute | solution.py:447
  37.9 1.4 %collective-permute-start.18 = (bf16[96,512]{1,0:T(8,128)(2,1)S(1)}, bf16[96,512]{1,0:T(8,128)(2,1)S(1)}, u32[]{:S(2)}, u32[]{:S(2)}) collective-permute-start(bf16[96,512]{1,0:T(8,128)(2,1)S(1)} %flip_back.1), channel_id=1, source_target_pairs={{0,1},{1,0},{2,3},{3,2},{4,5},{5,4},{6,7},{7,6},{8,9},{9,8},{10,11... | collective-permute-start | bytes 294920 | tf_op jit(solution)/shard_map/ppermute | solution.py:447

commit v7 on v6

--- a/solution.py
+++ b/solution.py
@@ -174,20 +174,22 @@
     gain = gain_ref[...].astype(jnp.float32)
     width = tokens_ref.shape[1] // len(meet)
     group = lax.axis_index("dp")
-    sources = ((tokens_ref, local_ref), (core_ref, core_local_ref))
-    for side, (here, places) in enumerate(sources):
+    sources = []
+    for here, places in ((tokens_ref, local_ref), (core_ref, core_local_ref)):
         pick = pick_rows(places, None, steps, per_device).astype(jnp.bfloat16)
-        scale = row_scale(here[...].astype(jnp.float32))
-        for place, step in enumerate(meet):
-            start = pl.multiple_of((group ^ step) * width, width)
+        sources.append((here, pick, row_scale(here[...].astype(jnp.float32))))
+    for place, step in enumerate(meet):
+        start = pl.multiple_of((group ^ step) * width, width)
+        values = []
+        for here, pick, scale in sources:
             part = here[:, pl.ds(start, width)].astype(jnp.float32)
             normed = apply_gain(part * scale, gain, (group ^ step) * (width // 128))
-            value = jnp.dot(pick, normed, preferred_element_type=jnp.float32)
-            for index, ref in enumerate(out_refs):
-                ref[
-                    side * CAP_DEV : (side + 1) * CAP_DEV,
-                    place * width : (place + 1) * width,
-                ] = value[index * CAP_DEV : (index + 1) * CAP_DEV, :].astype(ref.dtype)
+            values.append(jnp.dot(pick, normed, preferred_element_type=jnp.float32))
+        for index, ref in enumerate(out_refs):
+            block = slice(index * CAP_DEV, (index + 1) * CAP_DEV)
+            ref[:, place * width : (place + 1) * width] = jnp.concatenate(
+                [value[block] for value in values], axis=0
+            ).astype(ref.dtype)
 
 
 def weight_kernel(

time: 40.3 us -> 40.3 us (level)
  no operation moved by 1% of the time
where the time goes in v7:
time: 40.3 us; the launch traced here: 40.2 us
  starting transfers between devices  21.4 us (53%)
  Pallas kernels  10.9 us (27%)
  waiting for transfers between devices  7.8 us (19%)
    pallas_call x17, Pallas kernels, call(): pl.pallas_call(lambda *refs: kernel(*refs[count:]), in_specs=[pl.BlockSpe...  10.9 us
    ppermute x10, starting transfers between devices, to_peer(): return lax.ppermute(value, 'expert', [(i, i ^ step) for i in range(peers)])  10.7 us
    ppermute x9, starting transfers between devices, to_group(): return lax.ppermute(value, 'dp', [(i, i ^ step) for i in range(groups)])  10.7 us
    ppermute x10, waiting for transfers between devices, to_peer(): return lax.ppermute(value, 'expert', [(i, i ^ step) for i in range(peers)])  5.74 us
    ppermute x9, waiting for transfers between devices, to_group(): return lax.ppermute(value, 'dp', [(i, i ^ step) for i in range(groups)])  2.06 us
  transfers between devices with their start and end apart: 19, of which 8 were waited for; matrix products, arithmetic and copies ran while one was open for 0% of the time, Pallas kernels for 23%

profile of v7, /device:TPU:0, one launch (start us, length us, event | category | flops | bytes accessed | tf_op | source)
XLA Modules:
  0.0 40.2 jit_solution(16490862348350530150)
XLA Ops:
  0.0 0.5 %collective-permute-start = (bf16[128,2048]{1,0:T(8,128)(2,1)}, bf16[128,2048]{1,0:T(8,128)(2,1)S(1)}, u32[]{:S(2)}, u32[]{:S(2)}) collective-permute-start(bf16[128,2048]{1,0:T(8,128)(2,1)} %refs_0_.1), channel_id=1, source_target_pairs={{0,1},{1,0},{2,3},{3,2},{4,5},{5,4},{6,7},{7,6},{8,9},{9,8},{10,11... | collective-permute-start | bytes 1572872 | tf_op jit(solution)/shard_map/ppermute | solution.py:449
  0.5 0.1 collective-permute-start.1
  0.5 0.5 %collective-permute-start.2 = (s32[8,128]{1,0:T(8,128)}, s32[8,128]{1,0:T(8,128)S(1)}, u32[]{:S(2)}, u32[]{:S(2)}) collective-permute-start(s32[8,128]{1,0:T(8,128)} %bitcast.18), channel_id=1, source_target_pairs={{0,1},{1,0},{2,3},{3,2},{4,5},{5,4},{6,7},{7,6},{8,9},{9,8},{10,11... | collective-permute-start | bytes 12296 | tf_op jit(solution)/shard_map/ppermute | solution.py:449
  1.0 1.2 %place.1 = (bf16[128,2048]{1,0:T(8,128)(2,1)S(1)}, bf16[16,128]{1,0:T(8,128)(2,1)S(1)}, s32[1,16]{1,0:T(1,128)S(1)}, s32[1,16]{1,0:T(1,128)S(1)}, f32[16,128]{1,0:T(8,128)S(1)}) custom-call(bf16[128,2048]{1,0:T(8,128)(2,1)} %refs_0_.1, s32[8,128]{1,0:T(8,128)} %bitcast.17, s32[8,128]{1,0:T(8,128)} %bitcast.19, bf16[16,128]{1,0:T(8,128)(2,1)} %bitcast.15, ...), custom_call_target="tpu_custom_call" | custom-call | flops 1 | bytes 1 | tf_op jit(solution)/shard_map/place/pallas_call | solution.py:406
  2.2 0.0 collective-permute-done.1.refs_4_
  2.2 0.0 collective-permute-done.2.refs_5_
  2.2 0.0 collective-permute-done.refs_1_.refs_2_
  2.2 0.5 %dispatch.1 = (f32[16,128]{1,0:T(8,128)S(1)}, bf16[48,512]{1,0:T(8,128)(2,1)S(1)}, bf16[48,512]{1,0:T(8,128)(2,1)S(1)}) custom-call(bf16[128,2048]{1,0:T(8,128)(2,1)S(1)} %get-tuple-element.33.refs_0_.refs_1_, bf16[128,2048]{1,0:T(8,128)(2,1)S(1)} %collective-permute-done.refs_1_.refs_2_, bf16[16,128]{1,0:T(8,128)(2,1)S(1)} %get-tuple-element.34.refs_1_.refs_2_.refs_3_, ...), custom_call_target="tpu_custom_call" | custom-call | flops 1 | bytes 1 | tf_op jit(solution)/shard_map/dispatch/pallas_call | solution.py:406
  2.8 5.0 %collective-permute-start.3 = (bf16[48,512]{1,0:T(8,128)(2,1)S(1)}, bf16[48,512]{1,0:T(8,128)(2,1)S(1)}, u32[]{:S(2)}, u32[]{:S(2)}) collective-permute-start(bf16[48,512]{1,0:T(8,128)(2,1)S(1)} %get-tuple-element.40.refs_0_), channel_id=1, source_target_pairs={{0,6},{1,7},{2,4},{3,5},{4,2},{5,3},{6,0},{7,1},{8,14},{9,15},{10,... | collective-permute-start | bytes 147464 | tf_op jit(solution)/shard_map/ppermute | solution.py:449
  7.8 0.0 collective-permute-start.4
  7.8 0.7 %dispatch_near.1 = (bf16[48,2048]{1,0:T(8,128)(2,1)S(1)}, bf16[48,2048]{1,0:T(8,128)(2,1)S(1)}) custom-call(bf16[48,512]{1,0:T(8,128)(2,1)S(1)} %get-tuple-element.40.refs_0_, bf16[128,2048]{1,0:T(8,128)(2,1)S(1)} %get-tuple-element.33.refs_0_.refs_1_, bf16[128,2048]{1,0:T(8,128)(2,1)S(1)} %collective-permute-done.refs_1_.refs_2_, ...), custom_call_target="tpu_custom_call" | custom-call | flops 1 | bytes 1 | tf_op jit(solution)/shard_map/dispatch_near/pallas_call | solution.py:406
  8.5 2.3 %split_first.1 = (bf16[2,512,1024]{2,1,0:T(8,128)(2,1)S(1)}, bf16[2,2,2048,128]{3,2,1,0:T(8,128)(2,1)S(1)}) custom-call(bf16[48,2048]{1,0:T(8,128)(2,1)S(1)} %get-tuple-element.42.refs_0_, bf16[2,8192,128]{2,1,0:T(8,128)(2,1)} %bitcast.13), custom_call_target="tpu_custom_call" | custom-call | flops 1 | bytes 1 | tf_op jit(solution)/shard_map/split_first/pallas_call | solution.py:406
  10.8 0.0 collective-permute-done.3.refs_1_
  10.8 2.0 %collective-permute-done.4.refs_2_ = bf16[48,512]{1,0:T(8,128)(2,1)S(1)} collective-permute-done((bf16[48,512]{1,0:T(8,128)(2,1)S(1)}, bf16[48,512]{1,0:T(8,128)(2,1)S(1)}, u32[]{:S(2)}, u32[]{:S(2)}) %collective-permute-start.4) | collective-permute-done | bytes 49184 | tf_op jit(solution)/shard_map/ppermute | solution.py:449
  12.8 2.5 %collective-permute-start.6 = (bf16[96,512]{1,0:T(8,128)(2,1)S(1)}, bf16[96,512]{1,0:T(8,128)(2,1)S(1)}, u32[]{:S(2)}, u32[]{:S(2)}) collective-permute-start(bf16[96,512]{1,0:T(8,128)(2,1)S(1)} %join_far.1.refs_0_), channel_id=1, source_target_pairs={{0,24},{8,16},{16,8},{24,0},{1,25},{9,17},{17,9},{25,1},{2,26},{10... | collective-permute-start | bytes 294920 | tf_op jit(solution)/shard_map/ppermute | solution.py:446
  15.3 0.0 collective-permute-start.13
  15.3 0.5 %collective-permute-start.5 = (bf16[96,512]{1,0:T(8,128)(2,1)S(1)}, bf16[96,512]{1,0:T(8,128)(2,1)S(1)}, u32[]{:S(2)}, u32[]{:S(2)}) collective-permute-start(bf16[96,512]{1,0:T(8,128)(2,1)S(1)} %join_far.1.refs_0_), channel_id=1, source_target_pairs={{0,8},{8,0},{16,24},{24,16},{1,9},{9,1},{17,25},{25,17},{2,10},{10... | collective-permute-start | bytes 294920 | tf_op jit(solution)/shard_map/ppermute | solution.py:446
  15.8 0.5 %collective-permute-start.7 = (bf16[96,512]{1,0:T(8,128)(2,1)S(1)}, bf16[96,512]{1,0:T(8,128)(2,1)S(1)}, u32[]{:S(2)}, u32[]{:S(2)}) collective-permute-start(bf16[96,512]{1,0:T(8,128)(2,1)S(1)} %join_far.1.refs_0_), channel_id=1, source_target_pairs={{0,16},{8,24},{16,0},{24,8},{1,17},{9,25},{17,1},{25,9},{2,18},{10... | collective-permute-start | bytes 294920 | tf_op jit(solution)/shard_map/ppermute | solution.py:446
  16.3 0.3 product_far.3.refs_2_
  16.6 1.6 %split_second.1 = (bf16[2,512,1024]{2,1,0:T(8,128)(2,1)S(1)}, bf16[512,2048]{1,0:T(8,128)(2,1)S(1)}) custom-call(bf16[96,512]{1,0:T(8,128)(2,1)S(1)} %join_far.1.refs_0_, bf16[512,2048]{1,0:T(8,128)(2,1)} %bitcast.14, bf16[2,2,2048,128]{3,2,1,0:T(8,128)(2,1)S(1)} %get-tuple-element.45.refs_2_), custom_call_target="tpu_custom_call" | custom-call | flops 1 | bytes 1 | tf_op jit(solution)/shard_map/split_second/pallas_call | solution.py:406
  18.3 0.7 %collective-permute-done.6.refs_0_ = bf16[96,512]{1,0:T(8,128)(2,1)S(1)} collective-permute-done((bf16[96,512]{1,0:T(8,128)(2,1)S(1)}, bf16[96,512]{1,0:T(8,128)(2,1)S(1)}, u32[]{:S(2)}, u32[]{:S(2)}) %collective-permute-start.6) | collective-permute-done | bytes 98336 | tf_op jit(solution)/shard_map/ppermute | solution.py:446
  19.0 0.3 product_far.4.refs_2_
  19.3 0.8 %collective-permute-done.5.refs_0_ = bf16[96,512]{1,0:T(8,128)(2,1)S(1)} collective-permute-done((bf16[96,512]{1,0:T(8,128)(2,1)S(1)}, bf16[96,512]{1,0:T(8,128)(2,1)S(1)}, u32[]{:S(2)}, u32[]{:S(2)}) %collective-permute-start.5) | collective-permute-done | bytes 98336 | tf_op jit(solution)/shard_map/ppermute | solution.py:446
  20.0 0.3 product_far.5.refs_0_
  20.3 0.1 collective-permute-done.7.refs_1_
  20.5 0.7 %expert_far.1 = (bf16[96,512]{1,0:T(8,128)(2,1)S(1)}, bf16[96,512]{1,0:T(8,128)(2,1)S(1)}, bf16[96,512]{1,0:T(8,128)(2,1)S(1)}, bf16[96,512]{1,0:T(8,128)(2,1)S(1)}) custom-call(f32[96,1024]{1,0:T(8,128)S(1)} %product_far.5.refs_0_, bf16[96,512]{1,0:T(8,128)(2,1)S(1)} %collective-permute-done.7.refs_1_, ...), custom_call_target="tpu_custom_call" | custom-call | flops 1 | bytes 1 | tf_op jit(solution)/shard_map/expert_far/pallas_call | solution.py:406
  21.2 1.9 %collective-permute-start.8 = (bf16[96,512]{1,0:T(8,128)(2,1)S(1)}, bf16[96,512]{1,0:T(8,128)(2,1)S(1)}, u32[]{:S(2)}, u32[]{:S(2)}) collective-permute-start(bf16[96,512]{1,0:T(8,128)(2,1)S(1)} %get-tuple-element.49), channel_id=1, source_target_pairs={{0,24},{8,16},{16,8},{24,0},{1,25},{9,17},{17,9},{25,1},{2,26},{10... | collective-permute-start | bytes 294920 | tf_op jit(solution)/shard_map/ppermute | solution.py:446
  23.0 0.6 %collective-permute-start.9 = (bf16[96,512]{1,0:T(8,128)(2,1)S(1)}, bf16[96,512]{1,0:T(8,128)(2,1)S(1)}, u32[]{:S(2)}, u32[]{:S(2)}) collective-permute-start(bf16[96,512]{1,0:T(8,128)(2,1)S(1)} %get-tuple-element.50.refs_0_), channel_id=1, source_target_pairs={{0,8},{8,0},{16,24},{24,16},{1,9},{9,1},{17,25},{25,17},{2,10},{10... | collective-permute-start | bytes 294920 | tf_op jit(solution)/shard_map/ppermute | solution.py:446
  23.7 1.0 %collective-permute-start.10 = (bf16[96,512]{1,0:T(8,128)(2,1)S(1)}, bf16[96,512]{1,0:T(8,128)(2,1)S(1)}, u32[]{:S(2)}, u32[]{:S(2)}) collective-permute-start(bf16[96,512]{1,0:T(8,128)(2,1)S(1)} %get-tuple-element.51), channel_id=1, source_target_pairs={{0,16},{8,24},{16,0},{24,8},{1,17},{9,25},{17,1},{25,9},{2,18},{10... | collective-permute-start | bytes 294920 | tf_op jit(solution)/shard_map/ppermute | solution.py:446
  24.7 0.0 collective-permute-done.13.refs_2_
  24.7 1.2 %expert_near.1 = (bf16[96,512]{1,0:T(8,128)(2,1)S(1)}, bf16[96,512]{1,0:T(8,128)(2,1)S(1)}, bf16[96,512]{1,0:T(8,128)(2,1)S(1)}, bf16[96,512]{1,0:T(8,128)(2,1)S(1)}) custom-call(bf16[96,512]{1,0:T(8,128)(2,1)S(1)} %get-tuple-element.50.refs_0_, bf16[48,2048]{1,0:T(8,128)(2,1)S(1)} %get-tuple-element.54.refs_1_, ...), custom_call_target="tpu_custom_call" | custom-call | flops 1 | bytes 1 | tf_op jit(solution)/shard_map/expert_near/pallas_call | solution.py:406
  25.9 1.9 %collective-permute-start.14 = (bf16[96,512]{1,0:T(8,128)(2,1)S(1)}, bf16[96,512]{1,0:T(8,128)(2,1)S(1)}, u32[]{:S(2)}, u32[]{:S(2)}) collective-permute-start(bf16[96,512]{1,0:T(8,128)(2,1)S(1)} %get-tuple-element.56), channel_id=1, source_target_pairs={{0,24},{8,16},{16,8},{24,0},{1,25},{9,17},{17,9},{25,1},{2,26},{10... | collective-permute-start | bytes 294920 | tf_op jit(solution)/shard_map/ppermute | solution.py:446
  27.8 0.6 %collective-permute-start.15 = (bf16[96,512]{1,0:T(8,128)(2,1)S(1)}, bf16[96,512]{1,0:T(8,128)(2,1)S(1)}, u32[]{:S(2)}, u32[]{:S(2)}) collective-permute-start(bf16[96,512]{1,0:T(8,128)(2,1)S(1)} %get-tuple-element.57), channel_id=1, source_target_pairs={{0,8},{8,0},{16,24},{24,16},{1,9},{9,1},{17,25},{25,17},{2,10},{10... | collective-permute-start | bytes 294920 | tf_op jit(solution)/shard_map/ppermute | solution.py:446
  28.5 1.0 %collective-permute-start.16 = (bf16[96,512]{1,0:T(8,128)(2,1)S(1)}, bf16[96,512]{1,0:T(8,128)(2,1)S(1)}, u32[]{:S(2)}, u32[]{:S(2)}) collective-permute-start(bf16[96,512]{1,0:T(8,128)(2,1)S(1)} %get-tuple-element.58), channel_id=1, source_target_pairs={{0,16},{8,24},{16,0},{24,8},{1,17},{9,25},{17,1},{25,9},{2,18},{10... | collective-permute-start | bytes 294920 | tf_op jit(solution)/shard_map/ppermute | solution.py:446
  29.5 0.0 collective-permute-done.9.refs_2_
  29.5 0.5 %collective-permute-done.10.refs_3_ = bf16[96,512]{1,0:T(8,128)(2,1)S(1)} collective-permute-done((bf16[96,512]{1,0:T(8,128)(2,1)S(1)}, bf16[96,512]{1,0:T(8,128)(2,1)S(1)}, u32[]{:S(2)}, u32[]{:S(2)}) %collective-permute-start.10) | collective-permute-done | bytes 98336 | tf_op jit(solution)/shard_map/ppermute | solution.py:446
  30.0 0.1 sum_far.1
  30.0 2.3 %collective-permute-start.11 = (bf16[48,512]{1,0:T(8,128)(2,1)S(1)}, bf16[48,512]{1,0:T(8,128)(2,1)S(1)}, u32[]{:S(2)}, u32[]{:S(2)}) collective-permute-start(bf16[48,512]{1,0:T(8,128)(2,1)S(1)} %get-tuple-element.52.refs_0_), channel_id=1, source_target_pairs={{0,6},{1,7},{2,4},{3,5},{4,2},{5,3},{6,0},{7,1},{8,14},{9,15},{10,... | collective-permute-start | bytes 147464 | tf_op jit(solution)/shard_map/ppermute | solution.py:449
  32.4 1.1 %collective-permute-start.12 = (bf16[48,512]{1,0:T(8,128)(2,1)S(1)}, bf16[48,512]{1,0:T(8,128)(2,1)S(1)}, u32[]{:S(2)}, u32[]{:S(2)}) collective-permute-start(bf16[48,512]{1,0:T(8,128)(2,1)S(1)} %get-tuple-element.53), channel_id=1, source_target_pairs={{0,4},{1,5},{2,6},{3,7},{4,0},{5,1},{6,2},{7,3},{8,12},{9,13},{10,... | collective-permute-start | bytes 147464 | tf_op jit(solution)/shard_map/ppermute | solution.py:449
  33.5 0.1 sum_near.1
  33.6 1.2 %collective-permute-start.17 = (bf16[48,512]{1,0:T(8,128)(2,1)S(1)}, bf16[48,512]{1,0:T(8,128)(2,1)S(1)}, u32[]{:S(2)}, u32[]{:S(2)}) collective-permute-start(bf16[48,512]{1,0:T(8,128)(2,1)S(1)} %get-tuple-element.60), channel_id=1, source_target_pairs={{0,2},{1,3},{2,0},{3,1},{4,6},{5,7},{6,4},{7,5},{8,10},{9,11},{10,... | collective-permute-start | bytes 147464 | tf_op jit(solution)/shard_map/ppermute | solution.py:449
  34.7 1.3 %collective-permute-done.11.refs_2_.refs_0_ = bf16[48,512]{1,0:T(8,128)(2,1)S(1)} collective-permute-done((bf16[48,512]{1,0:T(8,128)(2,1)S(1)}, bf16[48,512]{1,0:T(8,128)(2,1)S(1)}, u32[]{:S(2)}, u32[]{:S(2)}) %collective-permute-start.11) | collective-permute-done | bytes 49184 | tf_op jit(solution)/shard_map/ppermute | solution.py:449
  36.1 1.8 %collective-permute-done.12.refs_3_.refs_1_ = bf16[48,512]{1,0:T(8,128)(2,1)S(1)} collective-permute-done((bf16[48,512]{1,0:T(8,128)(2,1)S(1)}, bf16[48,512]{1,0:T(8,128)(2,1)S(1)}, u32[]{:S(2)}, u32[]{:S(2)}) %collective-permute-start.12) | collective-permute-done | bytes 49184 | tf_op jit(solution)/shard_map/ppermute | solution.py:449
  37.9 0.1 collective-permute-start.18
  38.0 0.5 %combine_weights.1 = (bf16[128,192]{1,0:T(8,128)(2,1)S(1)}, bf16[128,512]{1,0:T(8,128)(2,1)S(1)}) custom-call(bf16[128,2048]{1,0:T(8,128)(2,1)S(1)} %get-tuple-element.33.refs_0_.refs_1_, bf16[16,128]{1,0:T(8,128)(2,1)S(1)} %get-tuple-element.34.refs_1_.refs_2_.refs_3_, bf16[8,2048]{1,0:T(8,128)(2,1)S(1)} %bitcast.12, ...), custom_call_target="tpu_custom_call" | custom-call | flops 1 | bytes 1 | tf_op jit(solution)/shard_map/combine_weights/pallas_call | solution.py:406
  38.5 0.2 combine.1.refs_1_
  38.7 0.6 %collective-permute-done.18.refs_2_ = bf16[96,512]{1,0:T(8,128)(2,1)S(1)} collective-permute-done((bf16[96,512]{1,0:T(8,128)(2,1)S(1)}, bf16[96,512]{1,0:T(8,128)(2,1)S(1)}, u32[]{:S(2)}, u32[]{:S(2)}) %collective-permute-start.18) | collective-permute-done | bytes 98336 | tf_op jit(solution)/shard_map/ppermute | solution.py:449
  39.3 0.9 %finish.1 = bf16[128,512]{1,0:T(8,128)(2,1)} custom-call(bf16[128,192]{1,0:T(8,128)(2,1)S(1)} %get-tuple-element.37.refs_0_, f32[128,512]{1,0:T(8,128)S(1)} %combine.1.refs_1_, bf16[96,512]{1,0:T(8,128)(2,1)S(1)} %collective-permute-done.18.refs_2_), custom_call_target="tpu_custom_call" | custom-call | flops 1 | bytes 1 | tf_op jit(solution)/shard_map/finish/pallas_call | solution.py:406
  (9 shorter events, 0.0 us)
Async XLA Ops:
  0.0 2.2 %collective-permute-start = (bf16[128,2048]{1,0:T(8,128)(2,1)}, bf16[128,2048]{1,0:T(8,128)(2,1)S(1)}, u32[]{:S(2)}, u32[]{:S(2)}) collective-permute-start(bf16[128,2048]{1,0:T(8,128)(2,1)} %refs_0_.1), channel_id=1, source_target_pairs={{0,1},{1,0},{2,3},{3,2},{4,5},{5,4},{6,7},{7,6},{8,9},{9,8},{10,11... | collective-permute-start | bytes 1572872 | tf_op jit(solution)/shard_map/ppermute | solution.py:449
  0.5 1.8 %collective-permute-start.1 = (s32[8,128]{1,0:T(8,128)}, s32[8,128]{1,0:T(8,128)S(1)}, u32[]{:S(2)}, u32[]{:S(2)}) collective-permute-start(s32[8,128]{1,0:T(8,128)} %bitcast.16), channel_id=1, source_target_pairs={{0,1},{1,0},{2,3},{3,2},{4,5},{5,4},{6,7},{7,6},{8,9},{9,8},{10,11... | collective-permute-start | bytes 12296 | tf_op jit(solution)/shard_map/ppermute | solution.py:449
  0.5 1.7 %collective-permute-start.2 = (s32[8,128]{1,0:T(8,128)}, s32[8,128]{1,0:T(8,128)S(1)}, u32[]{:S(2)}, u32[]{:S(2)}) collective-permute-start(s32[8,128]{1,0:T(8,128)} %bitcast.18), channel_id=1, source_target_pairs={{0,1},{1,0},{2,3},{3,2},{4,5},{5,4},{6,7},{7,6},{8,9},{9,8},{10,11... | collective-permute-start | bytes 12296 | tf_op jit(solution)/shard_map/ppermute | solution.py:449
  2.8 8.0 %collective-permute-start.3 = (bf16[48,512]{1,0:T(8,128)(2,1)S(1)}, bf16[48,512]{1,0:T(8,128)(2,1)S(1)}, u32[]{:S(2)}, u32[]{:S(2)}) collective-permute-start(bf16[48,512]{1,0:T(8,128)(2,1)S(1)} %get-tuple-element.40.refs_0_), channel_id=1, source_target_pairs={{0,6},{1,7},{2,4},{3,5},{4,2},{5,3},{6,0},{7,1},{8,14},{9,15},{10,... | collective-permute-start | bytes 147464 | tf_op jit(solution)/shard_map/ppermute | solution.py:449
  7.8 5.0 %collective-permute-start.4 = (bf16[48,512]{1,0:T(8,128)(2,1)S(1)}, bf16[48,512]{1,0:T(8,128)(2,1)S(1)}, u32[]{:S(2)}, u32[]{:S(2)}) collective-permute-start(bf16[48,512]{1,0:T(8,128)(2,1)S(1)} %get-tuple-element.44), channel_id=1, source_target_pairs={{0,4},{1,5},{2,6},{3,7},{4,0},{5,1},{6,2},{7,3},{8,12},{9,13},{10,... | collective-permute-start | bytes 147464 | tf_op jit(solution)/shard_map/ppermute | solution.py:449
  12.8 6.2 %collective-permute-start.6 = (bf16[96,512]{1,0:T(8,128)(2,1)S(1)}, bf16[96,512]{1,0:T(8,128)(2,1)S(1)}, u32[]{:S(2)}, u32[]{:S(2)}) collective-permute-start(bf16[96,512]{1,0:T(8,128)(2,1)S(1)} %join_far.1.refs_0_), channel_id=1, source_target_pairs={{0,24},{8,16},{16,8},{24,0},{1,25},{9,17},{17,9},{25,1},{2,26},{10... | collective-permute-start | bytes 294920 | tf_op jit(solution)/shard_map/ppermute | solution.py:446
  15.3 9.4 %collective-permute-start.13 = (bf16[48,2048]{1,0:T(8,128)(2,1)S(1)}, bf16[48,2048]{1,0:T(8,128)(2,1)S(1)}, u32[]{:S(2)}, u32[]{:S(2)}) collective-permute-start(bf16[48,2048]{1,0:T(8,128)(2,1)S(1)} %get-tuple-element.42.refs_0_), channel_id=1, source_target_pairs={{0,2},{1,3},{2,0},{3,1},{4,6},{5,7},{6,4},{7,5},{8,10},{9,11},{10,... | collective-permute-start | bytes 589832 | tf_op jit(solution)/shard_map/ppermute | solution.py:449
  15.3 4.7 %collective-permute-start.5 = (bf16[96,512]{1,0:T(8,128)(2,1)S(1)}, bf16[96,512]{1,0:T(8,128)(2,1)S(1)}, u32[]{:S(2)}, u32[]{:S(2)}) collective-permute-start(bf16[96,512]{1,0:T(8,128)(2,1)S(1)} %join_far.1.refs_0_), channel_id=1, source_target_pairs={{0,8},{8,0},{16,24},{24,16},{1,9},{9,1},{17,25},{25,17},{2,10},{10... | collective-permute-start | bytes 294920 | tf_op jit(solution)/shard_map/ppermute | solution.py:446
  15.8 4.6 %collective-permute-start.7 = (bf16[96,512]{1,0:T(8,128)(2,1)S(1)}, bf16[96,512]{1,0:T(8,128)(2,1)S(1)}, u32[]{:S(2)}, u32[]{:S(2)}) collective-permute-start(bf16[96,512]{1,0:T(8,128)(2,1)S(1)} %join_far.1.refs_0_), channel_id=1, source_target_pairs={{0,16},{8,24},{16,0},{24,8},{1,17},{9,25},{17,1},{25,9},{2,18},{10... | collective-permute-start | bytes 294920 | tf_op jit(solution)/shard_map/ppermute | solution.py:446
  21.2 7.3 %collective-permute-start.8 = (bf16[96,512]{1,0:T(8,128)(2,1)S(1)}, bf16[96,512]{1,0:T(8,128)(2,1)S(1)}, u32[]{:S(2)}, u32[]{:S(2)}) collective-permute-start(bf16[96,512]{1,0:T(8,128)(2,1)S(1)} %get-tuple-element.49), channel_id=1, source_target_pairs={{0,24},{8,16},{16,8},{24,0},{1,25},{9,17},{17,9},{25,1},{2,26},{10... | collective-permute-start | bytes 294920 | tf_op jit(solution)/shard_map/ppermute | solution.py:446
  23.0 6.5 %collective-permute-start.9 = (bf16[96,512]{1,0:T(8,128)(2,1)S(1)}, bf16[96,512]{1,0:T(8,128)(2,1)S(1)}, u32[]{:S(2)}, u32[]{:S(2)}) collective-permute-start(bf16[96,512]{1,0:T(8,128)(2,1)S(1)} %get-tuple-element.50.refs_0_), channel_id=1, source_target_pairs={{0,8},{8,0},{16,24},{24,16},{1,9},{9,1},{17,25},{25,17},{2,10},{10... | collective-permute-start | bytes 294920 | tf_op jit(solution)/shard_map/ppermute | solution.py:446
  23.7 6.3 %collective-permute-start.10 = (bf16[96,512]{1,0:T(8,128)(2,1)S(1)}, bf16[96,512]{1,0:T(8,128)(2,1)S(1)}, u32[]{:S(2)}, u32[]{:S(2)}) collective-permute-start(bf16[96,512]{1,0:T(8,128)(2,1)S(1)} %get-tuple-element.51), channel_id=1, source_target_pairs={{0,16},{8,24},{16,0},{24,8},{1,17},{9,25},{17,1},{25,9},{2,18},{10... | collective-permute-start | bytes 294920 | tf_op jit(solution)/shard_map/ppermute | solution.py:446
  24.7 13.3 %copy-start = (bf16[2048,8]{0,1:T(8,128)(2,1)S(1)}, bf16[2048,8]{0,1:T(8,128)(2,1)}, u32[]{:S(2)}) copy-start(bf16[2048,8]{0,1:T(8,128)(2,1)} %param.11) | copy-start | bytes 98308
  25.9 7.6 %collective-permute-start.14 = (bf16[96,512]{1,0:T(8,128)(2,1)S(1)}, bf16[96,512]{1,0:T(8,128)(2,1)S(1)}, u32[]{:S(2)}, u32[]{:S(2)}) collective-permute-start(bf16[96,512]{1,0:T(8,128)(2,1)S(1)} %get-tuple-element.56), channel_id=1, source_target_pairs={{0,24},{8,16},{16,8},{24,0},{1,25},{9,17},{17,9},{25,1},{2,26},{10... | collective-permute-start | bytes 294920 | tf_op jit(solution)/shard_map/ppermute | solution.py:446
  27.8 5.7 %collective-permute-start.15 = (bf16[96,512]{1,0:T(8,128)(2,1)S(1)}, bf16[96,512]{1,0:T(8,128)(2,1)S(1)}, u32[]{:S(2)}, u32[]{:S(2)}) collective-permute-start(bf16[96,512]{1,0:T(8,128)(2,1)S(1)} %get-tuple-element.57), channel_id=1, source_target_pairs={{0,8},{8,0},{16,24},{24,16},{1,9},{9,1},{17,25},{25,17},{2,10},{10... | collective-permute-start | bytes 294920 | tf_op jit(solution)/shard_map/ppermute | solution.py:446
  28.5 5.1 %collective-permute-start.16 = (bf16[96,512]{1,0:T(8,128)(2,1)S(1)}, bf16[96,512]{1,0:T(8,128)(2,1)S(1)}, u32[]{:S(2)}, u32[]{:S(2)}) collective-permute-start(bf16[96,512]{1,0:T(8,128)(2,1)S(1)} %get-tuple-element.58), channel_id=1, source_target_pairs={{0,16},{8,24},{16,0},{24,8},{1,17},{9,25},{17,1},{25,9},{2,18},{10... | collective-permute-start | bytes 294920 | tf_op jit(solution)/shard_map/ppermute | solution.py:446
  30.0 6.1 %collective-permute-start.11 = (bf16[48,512]{1,0:T(8,128)(2,1)S(1)}, bf16[48,512]{1,0:T(8,128)(2,1)S(1)}, u32[]{:S(2)}, u32[]{:S(2)}) collective-permute-start(bf16[48,512]{1,0:T(8,128)(2,1)S(1)} %get-tuple-element.52.refs_0_), channel_id=1, source_target_pairs={{0,6},{1,7},{2,4},{3,5},{4,2},{5,3},{6,0},{7,1},{8,14},{9,15},{10,... | collective-permute-start | bytes 147464 | tf_op jit(solution)/shard_map/ppermute | solution.py:449
  32.4 5.5 %collective-permute-start.12 = (bf16[48,512]{1,0:T(8,128)(2,1)S(1)}, bf16[48,512]{1,0:T(8,128)(2,1)S(1)}, u32[]{:S(2)}, u32[]{:S(2)}) collective-permute-start(bf16[48,512]{1,0:T(8,128)(2,1)S(1)} %get-tuple-element.53), channel_id=1, source_target_pairs={{0,4},{1,5},{2,6},{3,7},{4,0},{5,1},{6,2},{7,3},{8,12},{9,13},{10,... | collective-permute-start | bytes 147464 | tf_op jit(solution)/shard_map/ppermute | solution.py:449
  33.6 4.3 %collective-permute-start.17 = (bf16[48,512]{1,0:T(8,128)(2,1)S(1)}, bf16[48,512]{1,0:T(8,128)(2,1)S(1)}, u32[]{:S(2)}, u32[]{:S(2)}) collective-permute-start(bf16[48,512]{1,0:T(8,128)(2,1)S(1)} %get-tuple-element.60), channel_id=1, source_target_pairs={{0,2},{1,3},{2,0},{3,1},{4,6},{5,7},{6,4},{7,5},{8,10},{9,11},{10,... | collective-permute-start | bytes 147464 | tf_op jit(solution)/shard_map/ppermute | solution.py:449
  37.9 1.4 %collective-permute-start.18 = (bf16[96,512]{1,0:T(8,128)(2,1)S(1)}, bf16[96,512]{1,0:T(8,128)(2,1)S(1)}, u32[]{:S(2)}, u32[]{:S(2)}) collective-permute-start(bf16[96,512]{1,0:T(8,128)(2,1)S(1)} %flip_back.1), channel_id=1, source_target_pairs={{0,1},{1,0},{2,3},{3,2},{4,5},{5,4},{6,7},{7,6},{8,9},{9,8},{10,11... | collective-permute-start | bytes 294920 | tf_op jit(solution)/shard_map/ppermute | solution.py:449

commit v8 on v7

--- a/solution.py
+++ b/solution.py
@@ -90,6 +90,18 @@
     return jnp.concatenate(blocks, axis=0)
 
 
+def pick_pairs(local_ref, core_local_ref, steps, per_device):
+    own = pick_rows(local_ref, None, steps, per_device)
+    core = pick_rows(core_local_ref, None, steps, per_device)
+    blocks = []
+    for index in range(len(steps)):
+        block = slice(index * CAP_DEV, (index + 1) * CAP_DEV)
+        none = jnp.zeros_like(own[block])
+        blocks.append(jnp.concatenate([own[block], none], axis=1))
+        blocks.append(jnp.concatenate([none, core[block]], axis=1))
+    return jnp.concatenate(blocks, axis=0).astype(jnp.bfloat16)
+
+
 def store_blocks(refs, value):
     top = 0
     for ref in refs:
@@ -150,14 +162,12 @@
     gain = gain_ref[...].astype(jnp.float32)
     width = out_refs[0].shape[1]
     group = lax.axis_index("dp")
-    rows = []
-    for here, places in ((tokens_ref, local_ref), (core_ref, core_local_ref)):
-        pick = pick_rows(places, None, steps, per_device).astype(jnp.bfloat16)
-        normed = normed_part(here, gain, group, width)
-        rows.append(jnp.dot(pick, normed, preferred_element_type=jnp.float32))
-    for index, ref in enumerate(out_refs):
-        block = slice(index * CAP_DEV, (index + 1) * CAP_DEV)
-        ref[...] = jnp.concatenate([r[block] for r in rows], axis=0).astype(ref.dtype)
+    pick = pick_pairs(local_ref, core_local_ref, steps, per_device)
+    normed = jnp.concatenate(
+        [normed_part(here, gain, group, width) for here in (tokens_ref, core_ref)],
+        axis=0,
+    )
+    store_blocks(out_refs, jnp.dot(pick, normed, preferred_element_type=jnp.float32))
 
 
 def near_kernel(
@@ -174,22 +184,23 @@
     gain = gain_ref[...].astype(jnp.float32)
     width = tokens_ref.shape[1] // len(meet)
     group = lax.axis_index("dp")
-    sources = []
-    for here, places in ((tokens_ref, local_ref), (core_ref, core_local_ref)):
-        pick = pick_rows(places, None, steps, per_device).astype(jnp.bfloat16)
-        sources.append((here, pick, row_scale(here[...].astype(jnp.float32))))
+    pick = pick_pairs(local_ref, core_local_ref, steps, per_device)
+    scales = [row_scale(here[...].astype(jnp.float32)) for here in (tokens_ref, core_ref)]
     for place, step in enumerate(meet):
         start = pl.multiple_of((group ^ step) * width, width)
-        values = []
-        for here, pick, scale in sources:
+        parts = []
+        for here, scale in zip((tokens_ref, core_ref), scales):
             part = here[:, pl.ds(start, width)].astype(jnp.float32)
-            normed = apply_gain(part * scale, gain, (group ^ step) * (width // 128))
-            values.append(jnp.dot(pick, normed, preferred_element_type=jnp.float32))
-        for index, ref in enumerate(out_refs):
-            block = slice(index * CAP_DEV, (index + 1) * CAP_DEV)
-            ref[:, place * width : (place + 1) * width] = jnp.concatenate(
-                [value[block] for value in values], axis=0
-            ).astype(ref.dtype)
+            parts.append(apply_gain(part * scale, gain, (group ^ step) * (width // 128)))
+        value = jnp.dot(
+            pick, jnp.concatenate(parts, axis=0), preferred_element_type=jnp.float32
+        )
+        top = 0
+        for ref in out_refs:
+            ref[:, place * width : (place + 1) * width] = value[
+                top : top + ref.shape[0], :
+            ].astype(ref.dtype)
+            top += ref.shape[0]
 
 
 def weight_kernel(
@@ -412,7 +423,9 @@
         out_shape=outs,
         scratch_shapes=scratch,
         compiler_params=pltpu.CompilerParams(vmem_limit_bytes=size + (8 << 20)),
-        cost_estimate=pl.CostEstimate(flops=1, bytes_accessed=1, transcendentals=0),
+        cost_estimate=pl.CostEstimate(
+            flops=10**8, bytes_accessed=10**5, transcendentals=0
+        ),
         name=name,
     )(*after, *hbm, *args)
 

time: 40.3 us -> 40.1 us (level)
  transfers between devices with their start and end apart: 19 -> 19, of which waited for: 8 -> 9; matrix products, arithmetic and copies ran while one was open for 0% -> 0% of each run, Pallas kernels for 23% -> 24%
where the time goes in v8:
time: 40.1 us; the launch traced here: 40 us
  starting transfers between devices  21.4 us (53%)
  Pallas kernels  10.8 us (27%)
  waiting for transfers between devices  7.63 us (19%)
    pallas_call x17, Pallas kernels, call(): pl.pallas_call(lambda *refs: kernel(*refs[count:]), in_specs=[pl.BlockSpe...  10.8 us
    ppermute x10, starting transfers between devices, to_peer(): return lax.ppermute(value, 'expert', [(i, i ^ step) for i in range(peers)])  10.7 us
    ppermute x9, starting transfers between devices, to_group(): return lax.ppermute(value, 'dp', [(i, i ^ step) for i in range(groups)])  10.7 us
    ppermute x10, waiting for transfers between devices, to_peer(): return lax.ppermute(value, 'expert', [(i, i ^ step) for i in range(peers)])  5.6 us
    ppermute x9, waiting for transfers between devices, to_group(): return lax.ppermute(value, 'dp', [(i, i ^ step) for i in range(groups)])  2.03 us
  transfers between devices with their start and end apart: 19, of which 9 were waited for; matrix products, arithmetic and copies ran while one was open for 0% of the time, Pallas kernels for 24%

profile of v8, /device:TPU:0, one launch (start us, length us, event | category | flops | bytes accessed | tf_op | source)
XLA Modules:
  0.0 40.0 jit_solution(1254119926714721311)
XLA Ops:
  0.0 0.5 %collective-permute-start = (bf16[128,2048]{1,0:T(8,128)(2,1)}, bf16[128,2048]{1,0:T(8,128)(2,1)S(1)}, u32[]{:S(2)}, u32[]{:S(2)}) collective-permute-start(bf16[128,2048]{1,0:T(8,128)(2,1)} %refs_0_.1), channel_id=1, source_target_pairs={{0,1},{1,0},{2,3},{3,2},{4,5},{5,4},{6,7},{7,6},{8,9},{9,8},{10,11... | collective-permute-start | bytes 1572872 | tf_op jit(solution)/shard_map/ppermute | solution.py:462
  0.5 0.1 collective-permute-start.1
  0.5 0.5 %collective-permute-start.2 = (s32[8,128]{1,0:T(8,128)}, s32[8,128]{1,0:T(8,128)S(1)}, u32[]{:S(2)}, u32[]{:S(2)}) collective-permute-start(s32[8,128]{1,0:T(8,128)} %bitcast.18), channel_id=1, source_target_pairs={{0,1},{1,0},{2,3},{3,2},{4,5},{5,4},{6,7},{7,6},{8,9},{9,8},{10,11... | collective-permute-start | bytes 12296 | tf_op jit(solution)/shard_map/ppermute | solution.py:462
  1.0 1.2 %place.1 = (bf16[128,2048]{1,0:T(8,128)(2,1)S(1)}, bf16[16,128]{1,0:T(8,128)(2,1)S(1)}, s32[1,16]{1,0:T(1,128)S(1)}, s32[1,16]{1,0:T(1,128)S(1)}, f32[16,128]{1,0:T(8,128)S(1)}) custom-call(bf16[128,2048]{1,0:T(8,128)(2,1)} %refs_0_.1, s32[8,128]{1,0:T(8,128)} %bitcast.17, s32[8,128]{1,0:T(8,128)} %bitcast.19, bf16[16,128]{1,0:T(8,128)(2,1)} %bitcast.15, ...), custom_call_target="tpu_custom_call" | custom-call | flops 100000000 | bytes 100000 | tf_op jit(solution)/shard_map/place/pallas_call | solution.py:417
  2.2 0.0 collective-permute-done.1.refs_4_
  2.2 0.0 collective-permute-done.2.refs_5_
  2.2 0.0 collective-permute-done.refs_1_.refs_2_
  2.2 0.5 %dispatch.1 = (f32[16,128]{1,0:T(8,128)S(1)}, bf16[48,512]{1,0:T(8,128)(2,1)S(1)}, bf16[48,512]{1,0:T(8,128)(2,1)S(1)}) custom-call(bf16[128,2048]{1,0:T(8,128)(2,1)S(1)} %get-tuple-element.33.refs_0_.refs_1_, bf16[128,2048]{1,0:T(8,128)(2,1)S(1)} %collective-permute-done.refs_1_.refs_2_, bf16[16,128]{1,0:T(8,128)(2,1)S(1)} %get-tuple-element.34.refs_1_.refs_2_.refs_3_, ...), custom_call_target="tpu_custom_call" | custom-call | flops 100000000 | bytes 100000 | tf_op jit(solution)/shard_map/dispatch/pallas_call | solution.py:417
  2.7 5.0 %collective-permute-start.3 = (bf16[48,512]{1,0:T(8,128)(2,1)S(1)}, bf16[48,512]{1,0:T(8,128)(2,1)S(1)}, u32[]{:S(2)}, u32[]{:S(2)}) collective-permute-start(bf16[48,512]{1,0:T(8,128)(2,1)S(1)} %get-tuple-element.40.refs_0_), channel_id=1, source_target_pairs={{0,6},{1,7},{2,4},{3,5},{4,2},{5,3},{6,0},{7,1},{8,14},{9,15},{10,... | collective-permute-start | bytes 147464 | tf_op jit(solution)/shard_map/ppermute | solution.py:462
  7.8 0.6 %dispatch_near.1 = (bf16[48,2048]{1,0:T(8,128)(2,1)S(1)}, bf16[48,2048]{1,0:T(8,128)(2,1)S(1)}) custom-call(bf16[48,512]{1,0:T(8,128)(2,1)S(1)} %get-tuple-element.40.refs_0_, bf16[128,2048]{1,0:T(8,128)(2,1)S(1)} %get-tuple-element.33.refs_0_.refs_1_, bf16[128,2048]{1,0:T(8,128)(2,1)S(1)} %collective-permute-done.refs_1_.refs_2_, ...), custom_call_target="tpu_custom_call" | custom-call | flops 100000000 | bytes 100000 | tf_op jit(solution)/shard_map/dispatch_near/pallas_call | solution.py:417
  8.4 2.3 %split_first.1 = (bf16[2,512,1024]{2,1,0:T(8,128)(2,1)S(1)}, bf16[2,2,2048,128]{3,2,1,0:T(8,128)(2,1)S(1)}) custom-call(bf16[48,2048]{1,0:T(8,128)(2,1)S(1)} %get-tuple-element.42.refs_0_, bf16[2,8192,128]{2,1,0:T(8,128)(2,1)} %bitcast.13), custom_call_target="tpu_custom_call" | custom-call | flops 100000000 | bytes 100000 | tf_op jit(solution)/shard_map/split_first/pallas_call | solution.py:417
  10.7 2.0 %collective-permute-done.4.refs_2_ = bf16[48,512]{1,0:T(8,128)(2,1)S(1)} collective-permute-done((bf16[48,512]{1,0:T(8,128)(2,1)S(1)}, bf16[48,512]{1,0:T(8,128)(2,1)S(1)}, u32[]{:S(2)}, u32[]{:S(2)}) %collective-permute-start.4) | collective-permute-done | bytes 49184 | tf_op jit(solution)/shard_map/ppermute | solution.py:462
  12.8 2.5 %collective-permute-start.6 = (bf16[96,512]{1,0:T(8,128)(2,1)S(1)}, bf16[96,512]{1,0:T(8,128)(2,1)S(1)}, u32[]{:S(2)}, u32[]{:S(2)}) collective-permute-start(bf16[96,512]{1,0:T(8,128)(2,1)S(1)} %join_far.1.refs_0_), channel_id=1, source_target_pairs={{0,24},{8,16},{16,8},{24,0},{1,25},{9,17},{17,9},{25,1},{2,26},{10... | collective-permute-start | bytes 294920 | tf_op jit(solution)/shard_map/ppermute | solution.py:459
  15.3 0.5 %collective-permute-start.5 = (bf16[96,512]{1,0:T(8,128)(2,1)S(1)}, bf16[96,512]{1,0:T(8,128)(2,1)S(1)}, u32[]{:S(2)}, u32[]{:S(2)}) collective-permute-start(bf16[96,512]{1,0:T(8,128)(2,1)S(1)} %join_far.1.refs_0_), channel_id=1, source_target_pairs={{0,8},{8,0},{16,24},{24,16},{1,9},{9,1},{17,25},{25,17},{2,10},{10... | collective-permute-start | bytes 294920 | tf_op jit(solution)/shard_map/ppermute | solution.py:459
  15.8 0.5 %collective-permute-start.7 = (bf16[96,512]{1,0:T(8,128)(2,1)S(1)}, bf16[96,512]{1,0:T(8,128)(2,1)S(1)}, u32[]{:S(2)}, u32[]{:S(2)}) collective-permute-start(bf16[96,512]{1,0:T(8,128)(2,1)S(1)} %join_far.1.refs_0_), channel_id=1, source_target_pairs={{0,16},{8,24},{16,0},{24,8},{1,17},{9,25},{17,1},{25,9},{2,18},{10... | collective-permute-start | bytes 294920 | tf_op jit(solution)/shard_map/ppermute | solution.py:459
  16.3 0.3 product_far.3.refs_2_
  16.6 1.6 %split_second.1 = (bf16[2,512,1024]{2,1,0:T(8,128)(2,1)S(1)}, bf16[512,2048]{1,0:T(8,128)(2,1)S(1)}) custom-call(bf16[96,512]{1,0:T(8,128)(2,1)S(1)} %join_far.1.refs_0_, bf16[512,2048]{1,0:T(8,128)(2,1)} %bitcast.14, bf16[2,2,2048,128]{3,2,1,0:T(8,128)(2,1)S(1)} %get-tuple-element.45.refs_2_), custom_call_target="tpu_custom_call" | custom-call | flops 100000000 | bytes 100000 | tf_op jit(solution)/shard_map/split_second/pallas_call | solution.py:417
  18.2 0.7 %collective-permute-done.6.refs_0_ = bf16[96,512]{1,0:T(8,128)(2,1)S(1)} collective-permute-done((bf16[96,512]{1,0:T(8,128)(2,1)S(1)}, bf16[96,512]{1,0:T(8,128)(2,1)S(1)}, u32[]{:S(2)}, u32[]{:S(2)}) %collective-permute-start.6) | collective-permute-done | bytes 98336 | tf_op jit(solution)/shard_map/ppermute | solution.py:459
  18.9 0.3 product_far.4.refs_2_
  19.2 0.8 %collective-permute-done.5.refs_0_ = bf16[96,512]{1,0:T(8,128)(2,1)S(1)} collective-permute-done((bf16[96,512]{1,0:T(8,128)(2,1)S(1)}, bf16[96,512]{1,0:T(8,128)(2,1)S(1)}, u32[]{:S(2)}, u32[]{:S(2)}) %collective-permute-start.5) | collective-permute-done | bytes 98336 | tf_op jit(solution)/shard_map/ppermute | solution.py:459
  20.0 0.3 product_far.5.refs_0_
  20.3 0.1 collective-permute-done.7.refs_1_
  20.4 0.7 %expert_far.1 = (bf16[96,512]{1,0:T(8,128)(2,1)S(1)}, bf16[96,512]{1,0:T(8,128)(2,1)S(1)}, bf16[96,512]{1,0:T(8,128)(2,1)S(1)}, bf16[96,512]{1,0:T(8,128)(2,1)S(1)}) custom-call(f32[96,1024]{1,0:T(8,128)S(1)} %product_far.5.refs_0_, bf16[96,512]{1,0:T(8,128)(2,1)S(1)} %collective-permute-done.7.refs_1_, ...), custom_call_target="tpu_custom_call" | custom-call | flops 100000000 | bytes 100000 | tf_op jit(solution)/shard_map/expert_far/pallas_call | solution.py:417
  21.1 1.9 %collective-permute-start.8 = (bf16[96,512]{1,0:T(8,128)(2,1)S(1)}, bf16[96,512]{1,0:T(8,128)(2,1)S(1)}, u32[]{:S(2)}, u32[]{:S(2)}) collective-permute-start(bf16[96,512]{1,0:T(8,128)(2,1)S(1)} %get-tuple-element.49), channel_id=1, source_target_pairs={{0,24},{8,16},{16,8},{24,0},{1,25},{9,17},{17,9},{25,1},{2,26},{10... | collective-permute-start | bytes 294920 | tf_op jit(solution)/shard_map/ppermute | solution.py:459
  23.0 0.7 %collective-permute-start.9 = (bf16[96,512]{1,0:T(8,128)(2,1)S(1)}, bf16[96,512]{1,0:T(8,128)(2,1)S(1)}, u32[]{:S(2)}, u32[]{:S(2)}) collective-permute-start(bf16[96,512]{1,0:T(8,128)(2,1)S(1)} %get-tuple-element.50.refs_0_), channel_id=1, source_target_pairs={{0,8},{8,0},{16,24},{24,16},{1,9},{9,1},{17,25},{25,17},{2,10},{10... | collective-permute-start | bytes 294920 | tf_op jit(solution)/shard_map/ppermute | solution.py:459
  23.7 1.0 %collective-permute-start.10 = (bf16[96,512]{1,0:T(8,128)(2,1)S(1)}, bf16[96,512]{1,0:T(8,128)(2,1)S(1)}, u32[]{:S(2)}, u32[]{:S(2)}) collective-permute-start(bf16[96,512]{1,0:T(8,128)(2,1)S(1)} %get-tuple-element.51), channel_id=1, source_target_pairs={{0,16},{8,24},{16,0},{24,8},{1,17},{9,25},{17,1},{25,9},{2,18},{10... | collective-permute-start | bytes 294920 | tf_op jit(solution)/shard_map/ppermute | solution.py:459
  24.7 1.2 %expert_near.1 = (bf16[96,512]{1,0:T(8,128)(2,1)S(1)}, bf16[96,512]{1,0:T(8,128)(2,1)S(1)}, bf16[96,512]{1,0:T(8,128)(2,1)S(1)}, bf16[96,512]{1,0:T(8,128)(2,1)S(1)}) custom-call(bf16[96,512]{1,0:T(8,128)(2,1)S(1)} %get-tuple-element.50.refs_0_, bf16[48,2048]{1,0:T(8,128)(2,1)S(1)} %get-tuple-element.54.refs_1_, ...), custom_call_target="tpu_custom_call" | custom-call | flops 100000000 | bytes 100000 | tf_op jit(solution)/shard_map/expert_near/pallas_call | solution.py:417
  25.9 1.9 %collective-permute-start.14 = (bf16[96,512]{1,0:T(8,128)(2,1)S(1)}, bf16[96,512]{1,0:T(8,128)(2,1)S(1)}, u32[]{:S(2)}, u32[]{:S(2)}) collective-permute-start(bf16[96,512]{1,0:T(8,128)(2,1)S(1)} %get-tuple-element.56), channel_id=1, source_target_pairs={{0,24},{8,16},{16,8},{24,0},{1,25},{9,17},{17,9},{25,1},{2,26},{10... | collective-permute-start | bytes 294920 | tf_op jit(solution)/shard_map/ppermute | solution.py:459
  27.8 0.6 %collective-permute-start.15 = (bf16[96,512]{1,0:T(8,128)(2,1)S(1)}, bf16[96,512]{1,0:T(8,128)(2,1)S(1)}, u32[]{:S(2)}, u32[]{:S(2)}) collective-permute-start(bf16[96,512]{1,0:T(8,128)(2,1)S(1)} %get-tuple-element.57), channel_id=1, source_target_pairs={{0,8},{8,0},{16,24},{24,16},{1,9},{9,1},{17,25},{25,17},{2,10},{10... | collective-permute-start | bytes 294920 | tf_op jit(solution)/shard_map/ppermute | solution.py:459
  28.4 0.0 collective-permute-done.8.refs_1_
  28.4 1.0 %collective-permute-start.16 = (bf16[96,512]{1,0:T(8,128)(2,1)S(1)}, bf16[96,512]{1,0:T(8,128)(2,1)S(1)}, u32[]{:S(2)}, u32[]{:S(2)}) collective-permute-start(bf16[96,512]{1,0:T(8,128)(2,1)S(1)} %get-tuple-element.58), channel_id=1, source_target_pairs={{0,16},{8,24},{16,0},{24,8},{1,17},{9,25},{17,1},{25,9},{2,18},{10... | collective-permute-start | bytes 294920 | tf_op jit(solution)/shard_map/ppermute | solution.py:459
  29.5 0.0 collective-permute-done.9.refs_2_
  29.5 0.4 %collective-permute-done.10.refs_3_ = bf16[96,512]{1,0:T(8,128)(2,1)S(1)} collective-permute-done((bf16[96,512]{1,0:T(8,128)(2,1)S(1)}, bf16[96,512]{1,0:T(8,128)(2,1)S(1)}, u32[]{:S(2)}, u32[]{:S(2)}) %collective-permute-start.10) | collective-permute-done | bytes 98336 | tf_op jit(solution)/shard_map/ppermute | solution.py:459
  29.9 0.1 sum_far.1
  30.0 2.0 %collective-permute-start.11 = (bf16[48,512]{1,0:T(8,128)(2,1)S(1)}, bf16[48,512]{1,0:T(8,128)(2,1)S(1)}, u32[]{:S(2)}, u32[]{:S(2)}) collective-permute-start(bf16[48,512]{1,0:T(8,128)(2,1)S(1)} %get-tuple-element.52.refs_0_), channel_id=1, source_target_pairs={{0,6},{1,7},{2,4},{3,5},{4,2},{5,3},{6,0},{7,1},{8,14},{9,15},{10,... | collective-permute-start | bytes 147464 | tf_op jit(solution)/shard_map/ppermute | solution.py:462
  32.0 1.5 %collective-permute-start.12 = (bf16[48,512]{1,0:T(8,128)(2,1)S(1)}, bf16[48,512]{1,0:T(8,128)(2,1)S(1)}, u32[]{:S(2)}, u32[]{:S(2)}) collective-permute-start(bf16[48,512]{1,0:T(8,128)(2,1)S(1)} %get-tuple-element.53), channel_id=1, source_target_pairs={{0,4},{1,5},{2,6},{3,7},{4,0},{5,1},{6,2},{7,3},{8,12},{9,13},{10,... | collective-permute-start | bytes 147464 | tf_op jit(solution)/shard_map/ppermute | solution.py:462
  33.5 0.0 collective-permute-done.15.refs_3_
  33.5 0.0 collective-permute-done.16.refs_4_
  33.5 0.1 sum_near.1
  33.5 1.2 %collective-permute-start.17 = (bf16[48,512]{1,0:T(8,128)(2,1)S(1)}, bf16[48,512]{1,0:T(8,128)(2,1)S(1)}, u32[]{:S(2)}, u32[]{:S(2)}) collective-permute-start(bf16[48,512]{1,0:T(8,128)(2,1)S(1)} %get-tuple-element.60), channel_id=1, source_target_pairs={{0,2},{1,3},{2,0},{3,1},{4,6},{5,7},{6,4},{7,5},{8,10},{9,11},{10,... | collective-permute-start | bytes 147464 | tf_op jit(solution)/shard_map/ppermute | solution.py:462
  34.7 1.3 %collective-permute-done.11.refs_2_.refs_0_ = bf16[48,512]{1,0:T(8,128)(2,1)S(1)} collective-permute-done((bf16[48,512]{1,0:T(8,128)(2,1)S(1)}, bf16[48,512]{1,0:T(8,128)(2,1)S(1)}, u32[]{:S(2)}, u32[]{:S(2)}) %collective-permute-start.11) | collective-permute-done | bytes 49184 | tf_op jit(solution)/shard_map/ppermute | solution.py:462
  36.0 0.9 %collective-permute-done.12.refs_3_.refs_1_ = bf16[48,512]{1,0:T(8,128)(2,1)S(1)} collective-permute-done((bf16[48,512]{1,0:T(8,128)(2,1)S(1)}, bf16[48,512]{1,0:T(8,128)(2,1)S(1)}, u32[]{:S(2)}, u32[]{:S(2)}) %collective-permute-start.12) | collective-permute-done | bytes 49184 | tf_op jit(solution)/shard_map/ppermute | solution.py:462
  37.0 0.7 %collective-permute-done.17.refs_5_.refs_3_ = bf16[48,512]{1,0:T(8,128)(2,1)S(1)} collective-permute-done((bf16[48,512]{1,0:T(8,128)(2,1)S(1)}, bf16[48,512]{1,0:T(8,128)(2,1)S(1)}, u32[]{:S(2)}, u32[]{:S(2)}) %collective-permute-start.17) | collective-permute-done | bytes 49184 | tf_op jit(solution)/shard_map/ppermute | solution.py:462
  37.7 0.1 collective-permute-start.18
  37.8 0.5 %combine_weights.1 = (bf16[128,192]{1,0:T(8,128)(2,1)S(1)}, bf16[128,512]{1,0:T(8,128)(2,1)S(1)}) custom-call(bf16[128,2048]{1,0:T(8,128)(2,1)S(1)} %get-tuple-element.33.refs_0_.refs_1_, bf16[16,128]{1,0:T(8,128)(2,1)S(1)} %get-tuple-element.34.refs_1_.refs_2_.refs_3_, bf16[8,2048]{1,0:T(8,128)(2,1)S(1)} %bitcast.12, ...), custom_call_target="tpu_custom_call" | custom-call | flops 100000000 | bytes 100000 | tf_op jit(solution)/shard_map/combine_weights/pallas_call | solution.py:417
  38.3 0.2 combine.1.refs_1_
  38.5 0.6 %collective-permute-done.18.refs_2_ = bf16[96,512]{1,0:T(8,128)(2,1)S(1)} collective-permute-done((bf16[96,512]{1,0:T(8,128)(2,1)S(1)}, bf16[96,512]{1,0:T(8,128)(2,1)S(1)}, u32[]{:S(2)}, u32[]{:S(2)}) %collective-permute-start.18) | collective-permute-done | bytes 98336 | tf_op jit(solution)/shard_map/ppermute | solution.py:462
  39.1 0.9 %finish.1 = bf16[128,512]{1,0:T(8,128)(2,1)} custom-call(bf16[128,192]{1,0:T(8,128)(2,1)S(1)} %get-tuple-element.37.refs_0_, f32[128,512]{1,0:T(8,128)S(1)} %combine.1.refs_1_, bf16[96,512]{1,0:T(8,128)(2,1)S(1)} %collective-permute-done.18.refs_2_), custom_call_target="tpu_custom_call" | custom-call | flops 100000000 | bytes 100000 | tf_op jit(solution)/shard_map/finish/pallas_call | solution.py:417
  (9 shorter events, 0.0 us)
Async XLA Ops:
  0.0 2.2 %collective-permute-start = (bf16[128,2048]{1,0:T(8,128)(2,1)}, bf16[128,2048]{1,0:T(8,128)(2,1)S(1)}, u32[]{:S(2)}, u32[]{:S(2)}) collective-permute-start(bf16[128,2048]{1,0:T(8,128)(2,1)} %refs_0_.1), channel_id=1, source_target_pairs={{0,1},{1,0},{2,3},{3,2},{4,5},{5,4},{6,7},{7,6},{8,9},{9,8},{10,11... | collective-permute-start | bytes 1572872 | tf_op jit(solution)/shard_map/ppermute | solution.py:462
  0.5 1.8 %collective-permute-start.1 = (s32[8,128]{1,0:T(8,128)}, s32[8,128]{1,0:T(8,128)S(1)}, u32[]{:S(2)}, u32[]{:S(2)}) collective-permute-start(s32[8,128]{1,0:T(8,128)} %bitcast.16), channel_id=1, source_target_pairs={{0,1},{1,0},{2,3},{3,2},{4,5},{5,4},{6,7},{7,6},{8,9},{9,8},{10,11... | collective-permute-start | bytes 12296 | tf_op jit(solution)/shard_map/ppermute | solution.py:462
  0.5 1.7 %collective-permute-start.2 = (s32[8,128]{1,0:T(8,128)}, s32[8,128]{1,0:T(8,128)S(1)}, u32[]{:S(2)}, u32[]{:S(2)}) collective-permute-start(s32[8,128]{1,0:T(8,128)} %bitcast.18), channel_id=1, source_target_pairs={{0,1},{1,0},{2,3},{3,2},{4,5},{5,4},{6,7},{7,6},{8,9},{9,8},{10,11... | collective-permute-start | bytes 12296 | tf_op jit(solution)/shard_map/ppermute | solution.py:462
  2.7 8.0 %collective-permute-start.3 = (bf16[48,512]{1,0:T(8,128)(2,1)S(1)}, bf16[48,512]{1,0:T(8,128)(2,1)S(1)}, u32[]{:S(2)}, u32[]{:S(2)}) collective-permute-start(bf16[48,512]{1,0:T(8,128)(2,1)S(1)} %get-tuple-element.40.refs_0_), channel_id=1, source_target_pairs={{0,6},{1,7},{2,4},{3,5},{4,2},{5,3},{6,0},{7,1},{8,14},{9,15},{10,... | collective-permute-start | bytes 147464 | tf_op jit(solution)/shard_map/ppermute | solution.py:462
  7.8 5.0 %collective-permute-start.4 = (bf16[48,512]{1,0:T(8,128)(2,1)S(1)}, bf16[48,512]{1,0:T(8,128)(2,1)S(1)}, u32[]{:S(2)}, u32[]{:S(2)}) collective-permute-start(bf16[48,512]{1,0:T(8,128)(2,1)S(1)} %get-tuple-element.44), channel_id=1, source_target_pairs={{0,4},{1,5},{2,6},{3,7},{4,0},{5,1},{6,2},{7,3},{8,12},{9,13},{10,... | collective-permute-start | bytes 147464 | tf_op jit(solution)/shard_map/ppermute | solution.py:462
  12.8 6.2 %collective-permute-start.6 = (bf16[96,512]{1,0:T(8,128)(2,1)S(1)}, bf16[96,512]{1,0:T(8,128)(2,1)S(1)}, u32[]{:S(2)}, u32[]{:S(2)}) collective-permute-start(bf16[96,512]{1,0:T(8,128)(2,1)S(1)} %join_far.1.refs_0_), channel_id=1, source_target_pairs={{0,24},{8,16},{16,8},{24,0},{1,25},{9,17},{17,9},{25,1},{2,26},{10... | collective-permute-start | bytes 294920 | tf_op jit(solution)/shard_map/ppermute | solution.py:459
  15.3 4.7 %collective-permute-start.5 = (bf16[96,512]{1,0:T(8,128)(2,1)S(1)}, bf16[96,512]{1,0:T(8,128)(2,1)S(1)}, u32[]{:S(2)}, u32[]{:S(2)}) collective-permute-start(bf16[96,512]{1,0:T(8,128)(2,1)S(1)} %join_far.1.refs_0_), channel_id=1, source_target_pairs={{0,8},{8,0},{16,24},{24,16},{1,9},{9,1},{17,25},{25,17},{2,10},{10... | collective-permute-start | bytes 294920 | tf_op jit(solution)/shard_map/ppermute | solution.py:459
  15.8 8.9 %collective-permute-start.13 = (bf16[48,2048]{1,0:T(8,128)(2,1)S(1)}, bf16[48,2048]{1,0:T(8,128)(2,1)S(1)}, u32[]{:S(2)}, u32[]{:S(2)}) collective-permute-start(bf16[48,2048]{1,0:T(8,128)(2,1)S(1)} %get-tuple-element.42.refs_0_), channel_id=1, source_target_pairs={{0,2},{1,3},{2,0},{3,1},{4,6},{5,7},{6,4},{7,5},{8,10},{9,11},{10,... | collective-permute-start | bytes 589832 | tf_op jit(solution)/shard_map/ppermute | solution.py:462
  15.8 4.6 %collective-permute-start.7 = (bf16[96,512]{1,0:T(8,128)(2,1)S(1)}, bf16[96,512]{1,0:T(8,128)(2,1)S(1)}, u32[]{:S(2)}, u32[]{:S(2)}) collective-permute-start(bf16[96,512]{1,0:T(8,128)(2,1)S(1)} %join_far.1.refs_0_), channel_id=1, source_target_pairs={{0,16},{8,24},{16,0},{24,8},{1,17},{9,25},{17,1},{25,9},{2,18},{10... | collective-permute-start | bytes 294920 | tf_op jit(solution)/shard_map/ppermute | solution.py:459
  21.1 7.3 %collective-permute-start.8 = (bf16[96,512]{1,0:T(8,128)(2,1)S(1)}, bf16[96,512]{1,0:T(8,128)(2,1)S(1)}, u32[]{:S(2)}, u32[]{:S(2)}) collective-permute-start(bf16[96,512]{1,0:T(8,128)(2,1)S(1)} %get-tuple-element.49), channel_id=1, source_target_pairs={{0,24},{8,16},{16,8},{24,0},{1,25},{9,17},{17,9},{25,1},{2,26},{10... | collective-permute-start | bytes 294920 | tf_op jit(solution)/shard_map/ppermute | solution.py:459
  23.0 6.5 %collective-permute-start.9 = (bf16[96,512]{1,0:T(8,128)(2,1)S(1)}, bf16[96,512]{1,0:T(8,128)(2,1)S(1)}, u32[]{:S(2)}, u32[]{:S(2)}) collective-permute-start(bf16[96,512]{1,0:T(8,128)(2,1)S(1)} %get-tuple-element.50.refs_0_), channel_id=1, source_target_pairs={{0,8},{8,0},{16,24},{24,16},{1,9},{9,1},{17,25},{25,17},{2,10},{10... | collective-permute-start | bytes 294920 | tf_op jit(solution)/shard_map/ppermute | solution.py:459
  23.7 6.2 %collective-permute-start.10 = (bf16[96,512]{1,0:T(8,128)(2,1)S(1)}, bf16[96,512]{1,0:T(8,128)(2,1)S(1)}, u32[]{:S(2)}, u32[]{:S(2)}) collective-permute-start(bf16[96,512]{1,0:T(8,128)(2,1)S(1)} %get-tuple-element.51), channel_id=1, source_target_pairs={{0,16},{8,24},{16,0},{24,8},{1,17},{9,25},{17,1},{25,9},{2,18},{10... | collective-permute-start | bytes 294920 | tf_op jit(solution)/shard_map/ppermute | solution.py:459
  24.7 13.1 %copy-start = (bf16[2048,8]{0,1:T(8,128)(2,1)S(1)}, bf16[2048,8]{0,1:T(8,128)(2,1)}, u32[]{:S(2)}) copy-start(bf16[2048,8]{0,1:T(8,128)(2,1)} %param.11) | copy-start | bytes 98308
  25.9 7.6 %collective-permute-start.14 = (bf16[96,512]{1,0:T(8,128)(2,1)S(1)}, bf16[96,512]{1,0:T(8,128)(2,1)S(1)}, u32[]{:S(2)}, u32[]{:S(2)}) collective-permute-start(bf16[96,512]{1,0:T(8,128)(2,1)S(1)} %get-tuple-element.56), channel_id=1, source_target_pairs={{0,24},{8,16},{16,8},{24,0},{1,25},{9,17},{17,9},{25,1},{2,26},{10... | collective-permute-start | bytes 294920 | tf_op jit(solution)/shard_map/ppermute | solution.py:459
  27.8 5.7 %collective-permute-start.15 = (bf16[96,512]{1,0:T(8,128)(2,1)S(1)}, bf16[96,512]{1,0:T(8,128)(2,1)S(1)}, u32[]{:S(2)}, u32[]{:S(2)}) collective-permute-start(bf16[96,512]{1,0:T(8,128)(2,1)S(1)} %get-tuple-element.57), channel_id=1, source_target_pairs={{0,8},{8,0},{16,24},{24,16},{1,9},{9,1},{17,25},{25,17},{2,10},{10... | collective-permute-start | bytes 294920 | tf_op jit(solution)/shard_map/ppermute | solution.py:459
  28.4 5.0 %collective-permute-start.16 = (bf16[96,512]{1,0:T(8,128)(2,1)S(1)}, bf16[96,512]{1,0:T(8,128)(2,1)S(1)}, u32[]{:S(2)}, u32[]{:S(2)}) collective-permute-start(bf16[96,512]{1,0:T(8,128)(2,1)S(1)} %get-tuple-element.58), channel_id=1, source_target_pairs={{0,16},{8,24},{16,0},{24,8},{1,17},{9,25},{17,1},{25,9},{2,18},{10... | collective-permute-start | bytes 294920 | tf_op jit(solution)/shard_map/ppermute | solution.py:459
  30.0 6.1 %collective-permute-start.11 = (bf16[48,512]{1,0:T(8,128)(2,1)S(1)}, bf16[48,512]{1,0:T(8,128)(2,1)S(1)}, u32[]{:S(2)}, u32[]{:S(2)}) collective-permute-start(bf16[48,512]{1,0:T(8,128)(2,1)S(1)} %get-tuple-element.52.refs_0_), channel_id=1, source_target_pairs={{0,6},{1,7},{2,4},{3,5},{4,2},{5,3},{6,0},{7,1},{8,14},{9,15},{10,... | collective-permute-start | bytes 147464 | tf_op jit(solution)/shard_map/ppermute | solution.py:462
  32.0 5.0 %collective-permute-start.12 = (bf16[48,512]{1,0:T(8,128)(2,1)S(1)}, bf16[48,512]{1,0:T(8,128)(2,1)S(1)}, u32[]{:S(2)}, u32[]{:S(2)}) collective-permute-start(bf16[48,512]{1,0:T(8,128)(2,1)S(1)} %get-tuple-element.53), channel_id=1, source_target_pairs={{0,4},{1,5},{2,6},{3,7},{4,0},{5,1},{6,2},{7,3},{8,12},{9,13},{10,... | collective-permute-start | bytes 147464 | tf_op jit(solution)/shard_map/ppermute | solution.py:462
  33.5 4.2 %collective-permute-start.17 = (bf16[48,512]{1,0:T(8,128)(2,1)S(1)}, bf16[48,512]{1,0:T(8,128)(2,1)S(1)}, u32[]{:S(2)}, u32[]{:S(2)}) collective-permute-start(bf16[48,512]{1,0:T(8,128)(2,1)S(1)} %get-tuple-element.60), channel_id=1, source_target_pairs={{0,2},{1,3},{2,0},{3,1},{4,6},{5,7},{6,4},{7,5},{8,10},{9,11},{10,... | collective-permute-start | bytes 147464 | tf_op jit(solution)/shard_map/ppermute | solution.py:462
  37.7 1.4 %collective-permute-start.18 = (bf16[96,512]{1,0:T(8,128)(2,1)S(1)}, bf16[96,512]{1,0:T(8,128)(2,1)S(1)}, u32[]{:S(2)}, u32[]{:S(2)}) collective-permute-start(bf16[96,512]{1,0:T(8,128)(2,1)S(1)} %flip_back.1), channel_id=1, source_target_pairs={{0,1},{1,0},{2,3},{3,2},{4,5},{5,4},{6,7},{7,6},{8,9},{9,8},{10,11... | collective-permute-start | bytes 294920 | tf_op jit(solution)/shard_map/ppermute | solution.py:462

commit v9 on v8

--- a/solution.py
+++ b/solution.py
@@ -132,7 +132,7 @@
         pltpu.make_async_copy(source, target, arrived.at[index])
         for index, (source, target) in enumerate(zip(in_refs, targets))
     ]
-    for copy in copies:
+    for copy in (*copies[1:], copies[0]):
         copy.start()
     for copy in copies[1:]:
         copy.wait()

time: 40.1 us -> 40.1 us (level)
  transfers between devices with their start and end apart: 19 -> 19, of which waited for: 9 -> 10; matrix products, arithmetic and copies ran while one was open for 0% -> 0% of each run, Pallas kernels for 24% -> 23%
where the time goes in v9:
time: 40.1 us; the launch traced here: 40 us
  starting transfers between devices  21.4 us (53%)
  Pallas kernels  10.8 us (27%)
  waiting for transfers between devices  7.7 us (19%)
    pallas_call x17, Pallas kernels, call(): pl.pallas_call(lambda *refs: kernel(*refs[count:]), in_specs=[pl.BlockSpe...  10.8 us
    ppermute x10, starting transfers between devices, to_peer(): return lax.ppermute(value, 'expert', [(i, i ^ step) for i in range(peers)])  10.7 us
    ppermute x9, starting transfers between devices, to_group(): return lax.ppermute(value, 'dp', [(i, i ^ step) for i in range(groups)])  10.7 us
    ppermute x10, waiting for transfers between devices, to_peer(): return lax.ppermute(value, 'expert', [(i, i ^ step) for i in range(peers)])  5.65 us
    ppermute x9, waiting for transfers between devices, to_group(): return lax.ppermute(value, 'dp', [(i, i ^ step) for i in range(groups)])  2.05 us
  transfers between devices with their start and end apart: 19, of which 10 were waited for; matrix products, arithmetic and copies ran while one was open for 0% of the time, Pallas kernels for 23%

profile of v9, /device:TPU:0, one launch (start us, length us, event | category | flops | bytes accessed | tf_op | source)
XLA Modules:
  0.0 40.0 jit_solution(12052140014771574997)
XLA Ops:
  0.0 0.5 %collective-permute-start = (bf16[128,2048]{1,0:T(8,128)(2,1)}, bf16[128,2048]{1,0:T(8,128)(2,1)S(1)}, u32[]{:S(2)}, u32[]{:S(2)}) collective-permute-start(bf16[128,2048]{1,0:T(8,128)(2,1)} %refs_0_.1), channel_id=1, source_target_pairs={{0,1},{1,0},{2,3},{3,2},{4,5},{5,4},{6,7},{7,6},{8,9},{9,8},{10,11... | collective-permute-start | bytes 1572872 | tf_op jit(solution)/shard_map/ppermute | solution.py:462
  0.5 0.1 collective-permute-start.1
  0.5 0.5 %collective-permute-start.2 = (s32[8,128]{1,0:T(8,128)}, s32[8,128]{1,0:T(8,128)S(1)}, u32[]{:S(2)}, u32[]{:S(2)}) collective-permute-start(s32[8,128]{1,0:T(8,128)} %bitcast.18), channel_id=1, source_target_pairs={{0,1},{1,0},{2,3},{3,2},{4,5},{5,4},{6,7},{7,6},{8,9},{9,8},{10,11... | collective-permute-start | bytes 12296 | tf_op jit(solution)/shard_map/ppermute | solution.py:462
  1.0 1.2 %place.1 = (bf16[128,2048]{1,0:T(8,128)(2,1)S(1)}, bf16[16,128]{1,0:T(8,128)(2,1)S(1)}, s32[1,16]{1,0:T(1,128)S(1)}, s32[1,16]{1,0:T(1,128)S(1)}, f32[16,128]{1,0:T(8,128)S(1)}) custom-call(bf16[128,2048]{1,0:T(8,128)(2,1)} %refs_0_.1, s32[8,128]{1,0:T(8,128)} %bitcast.17, s32[8,128]{1,0:T(8,128)} %bitcast.19, bf16[16,128]{1,0:T(8,128)(2,1)} %bitcast.15, ...), custom_call_target="tpu_custom_call" | custom-call | flops 100000000 | bytes 100000 | tf_op jit(solution)/shard_map/place/pallas_call | solution.py:417
  2.1 0.1 collective-permute-done.1.refs_4_
  2.2 0.0 collective-permute-done.2.refs_5_
  2.2 0.5 %dispatch.1 = (f32[16,128]{1,0:T(8,128)S(1)}, bf16[48,512]{1,0:T(8,128)(2,1)S(1)}, bf16[48,512]{1,0:T(8,128)(2,1)S(1)}) custom-call(bf16[128,2048]{1,0:T(8,128)(2,1)S(1)} %get-tuple-element.33.refs_0_.refs_1_, bf16[128,2048]{1,0:T(8,128)(2,1)S(1)} %collective-permute-done.refs_1_.refs_2_, bf16[16,128]{1,0:T(8,128)(2,1)S(1)} %get-tuple-element.34.refs_1_.refs_2_.refs_3_, ...), custom_call_target="tpu_custom_call" | custom-call | flops 100000000 | bytes 100000 | tf_op jit(solution)/shard_map/dispatch/pallas_call | solution.py:417
  2.7 5.0 %collective-permute-start.3 = (bf16[48,512]{1,0:T(8,128)(2,1)S(1)}, bf16[48,512]{1,0:T(8,128)(2,1)S(1)}, u32[]{:S(2)}, u32[]{:S(2)}) collective-permute-start(bf16[48,512]{1,0:T(8,128)(2,1)S(1)} %get-tuple-element.40.refs_0_), channel_id=1, source_target_pairs={{0,6},{1,7},{2,4},{3,5},{4,2},{5,3},{6,0},{7,1},{8,14},{9,15},{10,... | collective-permute-start | bytes 147464 | tf_op jit(solution)/shard_map/ppermute | solution.py:462
  7.8 0.0 collective-permute-start.4
  7.8 0.6 %dispatch_near.1 = (bf16[48,2048]{1,0:T(8,128)(2,1)S(1)}, bf16[48,2048]{1,0:T(8,128)(2,1)S(1)}) custom-call(bf16[48,512]{1,0:T(8,128)(2,1)S(1)} %get-tuple-element.40.refs_0_, bf16[128,2048]{1,0:T(8,128)(2,1)S(1)} %get-tuple-element.33.refs_0_.refs_1_, bf16[128,2048]{1,0:T(8,128)(2,1)S(1)} %collective-permute-done.refs_1_.refs_2_, ...), custom_call_target="tpu_custom_call" | custom-call | flops 100000000 | bytes 100000 | tf_op jit(solution)/shard_map/dispatch_near/pallas_call | solution.py:417
  8.4 2.3 %split_first.1 = (bf16[2,512,1024]{2,1,0:T(8,128)(2,1)S(1)}, bf16[2,2,2048,128]{3,2,1,0:T(8,128)(2,1)S(1)}) custom-call(bf16[48,2048]{1,0:T(8,128)(2,1)S(1)} %get-tuple-element.42.refs_0_, bf16[2,8192,128]{2,1,0:T(8,128)(2,1)} %bitcast.13), custom_call_target="tpu_custom_call" | custom-call | flops 100000000 | bytes 100000 | tf_op jit(solution)/shard_map/split_first/pallas_call | solution.py:417
  10.7 0.0 collective-permute-done.3.refs_1_
  10.7 2.0 %collective-permute-done.4.refs_2_ = bf16[48,512]{1,0:T(8,128)(2,1)S(1)} collective-permute-done((bf16[48,512]{1,0:T(8,128)(2,1)S(1)}, bf16[48,512]{1,0:T(8,128)(2,1)S(1)}, u32[]{:S(2)}, u32[]{:S(2)}) %collective-permute-start.4) | collective-permute-done | bytes 49184 | tf_op jit(solution)/shard_map/ppermute | solution.py:462
  12.8 2.5 %collective-permute-start.6 = (bf16[96,512]{1,0:T(8,128)(2,1)S(1)}, bf16[96,512]{1,0:T(8,128)(2,1)S(1)}, u32[]{:S(2)}, u32[]{:S(2)}) collective-permute-start(bf16[96,512]{1,0:T(8,128)(2,1)S(1)} %join_far.1.refs_0_), channel_id=1, source_target_pairs={{0,24},{8,16},{16,8},{24,0},{1,25},{9,17},{17,9},{25,1},{2,26},{10... | collective-permute-start | bytes 294920 | tf_op jit(solution)/shard_map/ppermute | solution.py:459
  15.3 0.5 %collective-permute-start.5 = (bf16[96,512]{1,0:T(8,128)(2,1)S(1)}, bf16[96,512]{1,0:T(8,128)(2,1)S(1)}, u32[]{:S(2)}, u32[]{:S(2)}) collective-permute-start(bf16[96,512]{1,0:T(8,128)(2,1)S(1)} %join_far.1.refs_0_), channel_id=1, source_target_pairs={{0,8},{8,0},{16,24},{24,16},{1,9},{9,1},{17,25},{25,17},{2,10},{10... | collective-permute-start | bytes 294920 | tf_op jit(solution)/shard_map/ppermute | solution.py:459
  15.8 0.5 %collective-permute-start.7 = (bf16[96,512]{1,0:T(8,128)(2,1)S(1)}, bf16[96,512]{1,0:T(8,128)(2,1)S(1)}, u32[]{:S(2)}, u32[]{:S(2)}) collective-permute-start(bf16[96,512]{1,0:T(8,128)(2,1)S(1)} %join_far.1.refs_0_), channel_id=1, source_target_pairs={{0,16},{8,24},{16,0},{24,8},{1,17},{9,25},{17,1},{25,9},{2,18},{10... | collective-permute-start | bytes 294920 | tf_op jit(solution)/shard_map/ppermute | solution.py:459
  16.3 0.3 product_far.3.refs_2_
  16.6 1.6 %split_second.1 = (bf16[2,512,1024]{2,1,0:T(8,128)(2,1)S(1)}, bf16[512,2048]{1,0:T(8,128)(2,1)S(1)}) custom-call(bf16[96,512]{1,0:T(8,128)(2,1)S(1)} %join_far.1.refs_0_, bf16[512,2048]{1,0:T(8,128)(2,1)} %bitcast.14, bf16[2,2,2048,128]{3,2,1,0:T(8,128)(2,1)S(1)} %get-tuple-element.45.refs_2_), custom_call_target="tpu_custom_call" | custom-call | flops 100000000 | bytes 100000 | tf_op jit(solution)/shard_map/split_second/pallas_call | solution.py:417
  18.2 0.7 %collective-permute-done.6.refs_0_ = bf16[96,512]{1,0:T(8,128)(2,1)S(1)} collective-permute-done((bf16[96,512]{1,0:T(8,128)(2,1)S(1)}, bf16[96,512]{1,0:T(8,128)(2,1)S(1)}, u32[]{:S(2)}, u32[]{:S(2)}) %collective-permute-start.6) | collective-permute-done | bytes 98336 | tf_op jit(solution)/shard_map/ppermute | solution.py:459
  18.9 0.3 product_far.4.refs_2_
  19.2 0.8 %collective-permute-done.5.refs_0_ = bf16[96,512]{1,0:T(8,128)(2,1)S(1)} collective-permute-done((bf16[96,512]{1,0:T(8,128)(2,1)S(1)}, bf16[96,512]{1,0:T(8,128)(2,1)S(1)}, u32[]{:S(2)}, u32[]{:S(2)}) %collective-permute-start.5) | collective-permute-done | bytes 98336 | tf_op jit(solution)/shard_map/ppermute | solution.py:459
  20.0 0.3 product_far.5.refs_0_
  20.3 0.1 collective-permute-done.7.refs_1_
  20.4 0.7 %expert_far.1 = (bf16[96,512]{1,0:T(8,128)(2,1)S(1)}, bf16[96,512]{1,0:T(8,128)(2,1)S(1)}, bf16[96,512]{1,0:T(8,128)(2,1)S(1)}, bf16[96,512]{1,0:T(8,128)(2,1)S(1)}) custom-call(f32[96,1024]{1,0:T(8,128)S(1)} %product_far.5.refs_0_, bf16[96,512]{1,0:T(8,128)(2,1)S(1)} %collective-permute-done.7.refs_1_, ...), custom_call_target="tpu_custom_call" | custom-call | flops 100000000 | bytes 100000 | tf_op jit(solution)/shard_map/expert_far/pallas_call | solution.py:417
  21.1 1.9 %collective-permute-start.8 = (bf16[96,512]{1,0:T(8,128)(2,1)S(1)}, bf16[96,512]{1,0:T(8,128)(2,1)S(1)}, u32[]{:S(2)}, u32[]{:S(2)}) collective-permute-start(bf16[96,512]{1,0:T(8,128)(2,1)S(1)} %get-tuple-element.49), channel_id=1, source_target_pairs={{0,24},{8,16},{16,8},{24,0},{1,25},{9,17},{17,9},{25,1},{2,26},{10... | collective-permute-start | bytes 294920 | tf_op jit(solution)/shard_map/ppermute | solution.py:459
  23.0 0.7 %collective-permute-start.9 = (bf16[96,512]{1,0:T(8,128)(2,1)S(1)}, bf16[96,512]{1,0:T(8,128)(2,1)S(1)}, u32[]{:S(2)}, u32[]{:S(2)}) collective-permute-start(bf16[96,512]{1,0:T(8,128)(2,1)S(1)} %get-tuple-element.50.refs_0_), channel_id=1, source_target_pairs={{0,8},{8,0},{16,24},{24,16},{1,9},{9,1},{17,25},{25,17},{2,10},{10... | collective-permute-start | bytes 294920 | tf_op jit(solution)/shard_map/ppermute | solution.py:459
  23.7 1.0 %collective-permute-start.10 = (bf16[96,512]{1,0:T(8,128)(2,1)S(1)}, bf16[96,512]{1,0:T(8,128)(2,1)S(1)}, u32[]{:S(2)}, u32[]{:S(2)}) collective-permute-start(bf16[96,512]{1,0:T(8,128)(2,1)S(1)} %get-tuple-element.51), channel_id=1, source_target_pairs={{0,16},{8,24},{16,0},{24,8},{1,17},{9,25},{17,1},{25,9},{2,18},{10... | collective-permute-start | bytes 294920 | tf_op jit(solution)/shard_map/ppermute | solution.py:459
  24.7 0.0 collective-permute-done.13.refs_2_
  24.7 1.2 %expert_near.1 = (bf16[96,512]{1,0:T(8,128)(2,1)S(1)}, bf16[96,512]{1,0:T(8,128)(2,1)S(1)}, bf16[96,512]{1,0:T(8,128)(2,1)S(1)}, bf16[96,512]{1,0:T(8,128)(2,1)S(1)}) custom-call(bf16[96,512]{1,0:T(8,128)(2,1)S(1)} %get-tuple-element.50.refs_0_, bf16[48,2048]{1,0:T(8,128)(2,1)S(1)} %get-tuple-element.54.refs_1_, ...), custom_call_target="tpu_custom_call" | custom-call | flops 100000000 | bytes 100000 | tf_op jit(solution)/shard_map/expert_near/pallas_call | solution.py:417
  25.9 1.9 %collective-permute-start.14 = (bf16[96,512]{1,0:T(8,128)(2,1)S(1)}, bf16[96,512]{1,0:T(8,128)(2,1)S(1)}, u32[]{:S(2)}, u32[]{:S(2)}) collective-permute-start(bf16[96,512]{1,0:T(8,128)(2,1)S(1)} %get-tuple-element.56), channel_id=1, source_target_pairs={{0,24},{8,16},{16,8},{24,0},{1,25},{9,17},{17,9},{25,1},{2,26},{10... | collective-permute-start | bytes 294920 | tf_op jit(solution)/shard_map/ppermute | solution.py:459
  27.8 0.7 %collective-permute-start.15 = (bf16[96,512]{1,0:T(8,128)(2,1)S(1)}, bf16[96,512]{1,0:T(8,128)(2,1)S(1)}, u32[]{:S(2)}, u32[]{:S(2)}) collective-permute-start(bf16[96,512]{1,0:T(8,128)(2,1)S(1)} %get-tuple-element.57), channel_id=1, source_target_pairs={{0,8},{8,0},{16,24},{24,16},{1,9},{9,1},{17,25},{25,17},{2,10},{10... | collective-permute-start | bytes 294920 | tf_op jit(solution)/shard_map/ppermute | solution.py:459
  28.4 1.0 %collective-permute-start.16 = (bf16[96,512]{1,0:T(8,128)(2,1)S(1)}, bf16[96,512]{1,0:T(8,128)(2,1)S(1)}, u32[]{:S(2)}, u32[]{:S(2)}) collective-permute-start(bf16[96,512]{1,0:T(8,128)(2,1)S(1)} %get-tuple-element.58), channel_id=1, source_target_pairs={{0,16},{8,24},{16,0},{24,8},{1,17},{9,25},{17,1},{25,9},{2,18},{10... | collective-permute-start | bytes 294920 | tf_op jit(solution)/shard_map/ppermute | solution.py:459
  29.5 0.0 collective-permute-done.9.refs_2_
  29.5 0.5 %collective-permute-done.10.refs_3_ = bf16[96,512]{1,0:T(8,128)(2,1)S(1)} collective-permute-done((bf16[96,512]{1,0:T(8,128)(2,1)S(1)}, bf16[96,512]{1,0:T(8,128)(2,1)S(1)}, u32[]{:S(2)}, u32[]{:S(2)}) %collective-permute-start.10) | collective-permute-done | bytes 98336 | tf_op jit(solution)/shard_map/ppermute | solution.py:459
  29.9 0.1 sum_far.1
  30.0 2.0 %collective-permute-start.11 = (bf16[48,512]{1,0:T(8,128)(2,1)S(1)}, bf16[48,512]{1,0:T(8,128)(2,1)S(1)}, u32[]{:S(2)}, u32[]{:S(2)}) collective-permute-start(bf16[48,512]{1,0:T(8,128)(2,1)S(1)} %get-tuple-element.52.refs_0_), channel_id=1, source_target_pairs={{0,6},{1,7},{2,4},{3,5},{4,2},{5,3},{6,0},{7,1},{8,14},{9,15},{10,... | collective-permute-start | bytes 147464 | tf_op jit(solution)/shard_map/ppermute | solution.py:462
  32.0 1.5 %collective-permute-start.12 = (bf16[48,512]{1,0:T(8,128)(2,1)S(1)}, bf16[48,512]{1,0:T(8,128)(2,1)S(1)}, u32[]{:S(2)}, u32[]{:S(2)}) collective-permute-start(bf16[48,512]{1,0:T(8,128)(2,1)S(1)} %get-tuple-element.53), channel_id=1, source_target_pairs={{0,4},{1,5},{2,6},{3,7},{4,0},{5,1},{6,2},{7,3},{8,12},{9,13},{10,... | collective-permute-start | bytes 147464 | tf_op jit(solution)/shard_map/ppermute | solution.py:462
  33.5 0.0 collective-permute-done.14.refs_2_
  33.5 0.1 sum_near.1
  33.5 1.2 %collective-permute-start.17 = (bf16[48,512]{1,0:T(8,128)(2,1)S(1)}, bf16[48,512]{1,0:T(8,128)(2,1)S(1)}, u32[]{:S(2)}, u32[]{:S(2)}) collective-permute-start(bf16[48,512]{1,0:T(8,128)(2,1)S(1)} %get-tuple-element.60), channel_id=1, source_target_pairs={{0,2},{1,3},{2,0},{3,1},{4,6},{5,7},{6,4},{7,5},{8,10},{9,11},{10,... | collective-permute-start | bytes 147464 | tf_op jit(solution)/shard_map/ppermute | solution.py:462
  34.7 1.3 %collective-permute-done.11.refs_2_.refs_0_ = bf16[48,512]{1,0:T(8,128)(2,1)S(1)} collective-permute-done((bf16[48,512]{1,0:T(8,128)(2,1)S(1)}, bf16[48,512]{1,0:T(8,128)(2,1)S(1)}, u32[]{:S(2)}, u32[]{:S(2)}) %collective-permute-start.11) | collective-permute-done | bytes 49184 | tf_op jit(solution)/shard_map/ppermute | solution.py:462
  36.0 0.9 %collective-permute-done.12.refs_3_.refs_1_ = bf16[48,512]{1,0:T(8,128)(2,1)S(1)} collective-permute-done((bf16[48,512]{1,0:T(8,128)(2,1)S(1)}, bf16[48,512]{1,0:T(8,128)(2,1)S(1)}, u32[]{:S(2)}, u32[]{:S(2)}) %collective-permute-start.12) | collective-permute-done | bytes 49184 | tf_op jit(solution)/shard_map/ppermute | solution.py:462
  37.0 0.7 %collective-permute-done.17.refs_5_.refs_3_ = bf16[48,512]{1,0:T(8,128)(2,1)S(1)} collective-permute-done((bf16[48,512]{1,0:T(8,128)(2,1)S(1)}, bf16[48,512]{1,0:T(8,128)(2,1)S(1)}, u32[]{:S(2)}, u32[]{:S(2)}) %collective-permute-start.17) | collective-permute-done | bytes 49184 | tf_op jit(solution)/shard_map/ppermute | solution.py:462
  37.7 0.1 collective-permute-start.18
  37.8 0.5 %combine_weights.1 = (bf16[128,192]{1,0:T(8,128)(2,1)S(1)}, bf16[128,512]{1,0:T(8,128)(2,1)S(1)}) custom-call(bf16[128,2048]{1,0:T(8,128)(2,1)S(1)} %get-tuple-element.33.refs_0_.refs_1_, bf16[16,128]{1,0:T(8,128)(2,1)S(1)} %get-tuple-element.34.refs_1_.refs_2_.refs_3_, bf16[8,2048]{1,0:T(8,128)(2,1)S(1)} %bitcast.12, ...), custom_call_target="tpu_custom_call" | custom-call | flops 100000000 | bytes 100000 | tf_op jit(solution)/shard_map/combine_weights/pallas_call | solution.py:417
  38.3 0.2 combine.1.refs_1_
  38.5 0.6 %collective-permute-done.18.refs_2_ = bf16[96,512]{1,0:T(8,128)(2,1)S(1)} collective-permute-done((bf16[96,512]{1,0:T(8,128)(2,1)S(1)}, bf16[96,512]{1,0:T(8,128)(2,1)S(1)}, u32[]{:S(2)}, u32[]{:S(2)}) %collective-permute-start.18) | collective-permute-done | bytes 98336 | tf_op jit(solution)/shard_map/ppermute | solution.py:462
  39.1 0.9 %finish.1 = bf16[128,512]{1,0:T(8,128)(2,1)} custom-call(bf16[128,192]{1,0:T(8,128)(2,1)S(1)} %get-tuple-element.37.refs_0_, f32[128,512]{1,0:T(8,128)S(1)} %combine.1.refs_1_, bf16[96,512]{1,0:T(8,128)(2,1)S(1)} %collective-permute-done.18.refs_2_), custom_call_target="tpu_custom_call" | custom-call | flops 100000000 | bytes 100000 | tf_op jit(solution)/shard_map/finish/pallas_call | solution.py:417
  (9 shorter events, 0.0 us)
Async XLA Ops:
  0.0 2.2 %collective-permute-start = (bf16[128,2048]{1,0:T(8,128)(2,1)}, bf16[128,2048]{1,0:T(8,128)(2,1)S(1)}, u32[]{:S(2)}, u32[]{:S(2)}) collective-permute-start(bf16[128,2048]{1,0:T(8,128)(2,1)} %refs_0_.1), channel_id=1, source_target_pairs={{0,1},{1,0},{2,3},{3,2},{4,5},{5,4},{6,7},{7,6},{8,9},{9,8},{10,11... | collective-permute-start | bytes 1572872 | tf_op jit(solution)/shard_map/ppermute | solution.py:462
  0.5 1.8 %collective-permute-start.1 = (s32[8,128]{1,0:T(8,128)}, s32[8,128]{1,0:T(8,128)S(1)}, u32[]{:S(2)}, u32[]{:S(2)}) collective-permute-start(s32[8,128]{1,0:T(8,128)} %bitcast.16), channel_id=1, source_target_pairs={{0,1},{1,0},{2,3},{3,2},{4,5},{5,4},{6,7},{7,6},{8,9},{9,8},{10,11... | collective-permute-start | bytes 12296 | tf_op jit(solution)/shard_map/ppermute | solution.py:462
  0.5 1.7 %collective-permute-start.2 = (s32[8,128]{1,0:T(8,128)}, s32[8,128]{1,0:T(8,128)S(1)}, u32[]{:S(2)}, u32[]{:S(2)}) collective-permute-start(s32[8,128]{1,0:T(8,128)} %bitcast.18), channel_id=1, source_target_pairs={{0,1},{1,0},{2,3},{3,2},{4,5},{5,4},{6,7},{7,6},{8,9},{9,8},{10,11... | collective-permute-start | bytes 12296 | tf_op jit(solution)/shard_map/ppermute | solution.py:462
  2.7 8.0 %collective-permute-start.3 = (bf16[48,512]{1,0:T(8,128)(2,1)S(1)}, bf16[48,512]{1,0:T(8,128)(2,1)S(1)}, u32[]{:S(2)}, u32[]{:S(2)}) collective-permute-start(bf16[48,512]{1,0:T(8,128)(2,1)S(1)} %get-tuple-element.40.refs_0_), channel_id=1, source_target_pairs={{0,6},{1,7},{2,4},{3,5},{4,2},{5,3},{6,0},{7,1},{8,14},{9,15},{10,... | collective-permute-start | bytes 147464 | tf_op jit(solution)/shard_map/ppermute | solution.py:462
  7.8 5.0 %collective-permute-start.4 = (bf16[48,512]{1,0:T(8,128)(2,1)S(1)}, bf16[48,512]{1,0:T(8,128)(2,1)S(1)}, u32[]{:S(2)}, u32[]{:S(2)}) collective-permute-start(bf16[48,512]{1,0:T(8,128)(2,1)S(1)} %get-tuple-element.44), channel_id=1, source_target_pairs={{0,4},{1,5},{2,6},{3,7},{4,0},{5,1},{6,2},{7,3},{8,12},{9,13},{10,... | collective-permute-start | bytes 147464 | tf_op jit(solution)/shard_map/ppermute | solution.py:462
  12.8 6.2 %collective-permute-start.6 = (bf16[96,512]{1,0:T(8,128)(2,1)S(1)}, bf16[96,512]{1,0:T(8,128)(2,1)S(1)}, u32[]{:S(2)}, u32[]{:S(2)}) collective-permute-start(bf16[96,512]{1,0:T(8,128)(2,1)S(1)} %join_far.1.refs_0_), channel_id=1, source_target_pairs={{0,24},{8,16},{16,8},{24,0},{1,25},{9,17},{17,9},{25,1},{2,26},{10... | collective-permute-start | bytes 294920 | tf_op jit(solution)/shard_map/ppermute | solution.py:459
  15.3 4.7 %collective-permute-start.5 = (bf16[96,512]{1,0:T(8,128)(2,1)S(1)}, bf16[96,512]{1,0:T(8,128)(2,1)S(1)}, u32[]{:S(2)}, u32[]{:S(2)}) collective-permute-start(bf16[96,512]{1,0:T(8,128)(2,1)S(1)} %join_far.1.refs_0_), channel_id=1, source_target_pairs={{0,8},{8,0},{16,24},{24,16},{1,9},{9,1},{17,25},{25,17},{2,10},{10... | collective-permute-start | bytes 294920 | tf_op jit(solution)/shard_map/ppermute | solution.py:459
  15.8 8.9 %collective-permute-start.13 = (bf16[48,2048]{1,0:T(8,128)(2,1)S(1)}, bf16[48,2048]{1,0:T(8,128)(2,1)S(1)}, u32[]{:S(2)}, u32[]{:S(2)}) collective-permute-start(bf16[48,2048]{1,0:T(8,128)(2,1)S(1)} %get-tuple-element.42.refs_0_), channel_id=1, source_target_pairs={{0,2},{1,3},{2,0},{3,1},{4,6},{5,7},{6,4},{7,5},{8,10},{9,11},{10,... | collective-permute-start | bytes 589832 | tf_op jit(solution)/shard_map/ppermute | solution.py:462
  15.8 4.6 %collective-permute-start.7 = (bf16[96,512]{1,0:T(8,128)(2,1)S(1)}, bf16[96,512]{1,0:T(8,128)(2,1)S(1)}, u32[]{:S(2)}, u32[]{:S(2)}) collective-permute-start(bf16[96,512]{1,0:T(8,128)(2,1)S(1)} %join_far.1.refs_0_), channel_id=1, source_target_pairs={{0,16},{8,24},{16,0},{24,8},{1,17},{9,25},{17,1},{25,9},{2,18},{10... | collective-permute-start | bytes 294920 | tf_op jit(solution)/shard_map/ppermute | solution.py:459
  21.1 7.3 %collective-permute-start.8 = (bf16[96,512]{1,0:T(8,128)(2,1)S(1)}, bf16[96,512]{1,0:T(8,128)(2,1)S(1)}, u32[]{:S(2)}, u32[]{:S(2)}) collective-permute-start(bf16[96,512]{1,0:T(8,128)(2,1)S(1)} %get-tuple-element.49), channel_id=1, source_target_pairs={{0,24},{8,16},{16,8},{24,0},{1,25},{9,17},{17,9},{25,1},{2,26},{10... | collective-permute-start | bytes 294920 | tf_op jit(solution)/shard_map/ppermute | solution.py:459
  23.0 6.5 %collective-permute-start.9 = (bf16[96,512]{1,0:T(8,128)(2,1)S(1)}, bf16[96,512]{1,0:T(8,128)(2,1)S(1)}, u32[]{:S(2)}, u32[]{:S(2)}) collective-permute-start(bf16[96,512]{1,0:T(8,128)(2,1)S(1)} %get-tuple-element.50.refs_0_), channel_id=1, source_target_pairs={{0,8},{8,0},{16,24},{24,16},{1,9},{9,1},{17,25},{25,17},{2,10},{10... | collective-permute-start | bytes 294920 | tf_op jit(solution)/shard_map/ppermute | solution.py:459
  23.7 6.3 %collective-permute-start.10 = (bf16[96,512]{1,0:T(8,128)(2,1)S(1)}, bf16[96,512]{1,0:T(8,128)(2,1)S(1)}, u32[]{:S(2)}, u32[]{:S(2)}) collective-permute-start(bf16[96,512]{1,0:T(8,128)(2,1)S(1)} %get-tuple-element.51), channel_id=1, source_target_pairs={{0,16},{8,24},{16,0},{24,8},{1,17},{9,25},{17,1},{25,9},{2,18},{10... | collective-permute-start | bytes 294920 | tf_op jit(solution)/shard_map/ppermute | solution.py:459
  24.7 13.1 %copy-start = (bf16[2048,8]{0,1:T(8,128)(2,1)S(1)}, bf16[2048,8]{0,1:T(8,128)(2,1)}, u32[]{:S(2)}) copy-start(bf16[2048,8]{0,1:T(8,128)(2,1)} %param.11) | copy-start | bytes 98308
  25.9 7.6 %collective-permute-start.14 = (bf16[96,512]{1,0:T(8,128)(2,1)S(1)}, bf16[96,512]{1,0:T(8,128)(2,1)S(1)}, u32[]{:S(2)}, u32[]{:S(2)}) collective-permute-start(bf16[96,512]{1,0:T(8,128)(2,1)S(1)} %get-tuple-element.56), channel_id=1, source_target_pairs={{0,24},{8,16},{16,8},{24,0},{1,25},{9,17},{17,9},{25,1},{2,26},{10... | collective-permute-start | bytes 294920 | tf_op jit(solution)/shard_map/ppermute | solution.py:459
  27.8 5.7 %collective-permute-start.15 = (bf16[96,512]{1,0:T(8,128)(2,1)S(1)}, bf16[96,512]{1,0:T(8,128)(2,1)S(1)}, u32[]{:S(2)}, u32[]{:S(2)}) collective-permute-start(bf16[96,512]{1,0:T(8,128)(2,1)S(1)} %get-tuple-element.57), channel_id=1, source_target_pairs={{0,8},{8,0},{16,24},{24,16},{1,9},{9,1},{17,25},{25,17},{2,10},{10... | collective-permute-start | bytes 294920 | tf_op jit(solution)/shard_map/ppermute | solution.py:459
  28.4 5.0 %collective-permute-start.16 = (bf16[96,512]{1,0:T(8,128)(2,1)S(1)}, bf16[96,512]{1,0:T(8,128)(2,1)S(1)}, u32[]{:S(2)}, u32[]{:S(2)}) collective-permute-start(bf16[96,512]{1,0:T(8,128)(2,1)S(1)} %get-tuple-element.58), channel_id=1, source_target_pairs={{0,16},{8,24},{16,0},{24,8},{1,17},{9,25},{17,1},{25,9},{2,18},{10... | collective-permute-start | bytes 294920 | tf_op jit(solution)/shard_map/ppermute | solution.py:459
  30.0 6.1 %collective-permute-start.11 = (bf16[48,512]{1,0:T(8,128)(2,1)S(1)}, bf16[48,512]{1,0:T(8,128)(2,1)S(1)}, u32[]{:S(2)}, u32[]{:S(2)}) collective-permute-start(bf16[48,512]{1,0:T(8,128)(2,1)S(1)} %get-tuple-element.52.refs_0_), channel_id=1, source_target_pairs={{0,6},{1,7},{2,4},{3,5},{4,2},{5,3},{6,0},{7,1},{8,14},{9,15},{10,... | collective-permute-start | bytes 147464 | tf_op jit(solution)/shard_map/ppermute | solution.py:462
  32.0 5.0 %collective-permute-start.12 = (bf16[48,512]{1,0:T(8,128)(2,1)S(1)}, bf16[48,512]{1,0:T(8,128)(2,1)S(1)}, u32[]{:S(2)}, u32[]{:S(2)}) collective-permute-start(bf16[48,512]{1,0:T(8,128)(2,1)S(1)} %get-tuple-element.53), channel_id=1, source_target_pairs={{0,4},{1,5},{2,6},{3,7},{4,0},{5,1},{6,2},{7,3},{8,12},{9,13},{10,... | collective-permute-start | bytes 147464 | tf_op jit(solution)/shard_map/ppermute | solution.py:462
  33.5 4.2 %collective-permute-start.17 = (bf16[48,512]{1,0:T(8,128)(2,1)S(1)}, bf16[48,512]{1,0:T(8,128)(2,1)S(1)}, u32[]{:S(2)}, u32[]{:S(2)}) collective-permute-start(bf16[48,512]{1,0:T(8,128)(2,1)S(1)} %get-tuple-element.60), channel_id=1, source_target_pairs={{0,2},{1,3},{2,0},{3,1},{4,6},{5,7},{6,4},{7,5},{8,10},{9,11},{10,... | collective-permute-start | bytes 147464 | tf_op jit(solution)/shard_map/ppermute | solution.py:462
  37.7 1.4 %collective-permute-start.18 = (bf16[96,512]{1,0:T(8,128)(2,1)S(1)}, bf16[96,512]{1,0:T(8,128)(2,1)S(1)}, u32[]{:S(2)}, u32[]{:S(2)}) collective-permute-start(bf16[96,512]{1,0:T(8,128)(2,1)S(1)} %flip_back.1), channel_id=1, source_target_pairs={{0,1},{1,0},{2,3},{3,2},{4,5},{5,4},{6,7},{7,6},{8,9},{9,8},{10,11... | collective-permute-start | bytes 294920 | tf_op jit(solution)/shard_map/ppermute | solution.py:462

commit v10 on v8

--- a/solution.py
+++ b/solution.py
@@ -601,7 +601,7 @@
         )
 
     far_back = reduce_groups(far_partials, "sum_far", chips - 2)
-    near_back = reduce_groups(near_partials, "sum_near", 2, far_back[:1])
+    near_back = reduce_groups(near_partials, "sum_near", 2)
     far_back = [to_peer(value, 2 * chip) for chip, value in zip(far, far_back)]
     back = [*far_back, near_back[0], to_peer(near_back[1], 2)]
     (flip_back,) = call(

time: 40.1 us -> 40.1 us (level)
  no operation moved by 1% of the time
where the time goes in v10:
time: 40.1 us; the launch traced here: 40 us
  starting transfers between devices  21.4 us (53%)
  Pallas kernels  10.8 us (27%)
  waiting for transfers between devices  7.63 us (19%)
    pallas_call x17, Pallas kernels, call(): pl.pallas_call(lambda *refs: kernel(*refs[count:]), in_specs=[pl.BlockSpe...  10.8 us
    ppermute x10, starting transfers between devices, to_peer(): return lax.ppermute(value, 'expert', [(i, i ^ step) for i in range(peers)])  10.7 us
    ppermute x9, starting transfers between devices, to_group(): return lax.ppermute(value, 'dp', [(i, i ^ step) for i in range(groups)])  10.7 us
    ppermute x10, waiting for transfers between devices, to_peer(): return lax.ppermute(value, 'expert', [(i, i ^ step) for i in range(peers)])  5.6 us
    ppermute x9, waiting for transfers between devices, to_group(): return lax.ppermute(value, 'dp', [(i, i ^ step) for i in range(groups)])  2.03 us
  transfers between devices with their start and end apart: 19, of which 9 were waited for; matrix products, arithmetic and copies ran while one was open for 0% of the time, Pallas kernels for 24%

profile of v10, /device:TPU:0, one launch (start us, length us, event | category | flops | bytes accessed | tf_op | source)
XLA Modules:
  0.0 40.0 jit_solution(13832152110206469604)
XLA Ops:
  0.0 0.5 %collective-permute-start = (bf16[128,2048]{1,0:T(8,128)(2,1)}, bf16[128,2048]{1,0:T(8,128)(2,1)S(1)}, u32[]{:S(2)}, u32[]{:S(2)}) collective-permute-start(bf16[128,2048]{1,0:T(8,128)(2,1)} %refs_0_.1), channel_id=1, source_target_pairs={{0,1},{1,0},{2,3},{3,2},{4,5},{5,4},{6,7},{7,6},{8,9},{9,8},{10,11... | collective-permute-start | bytes 1572872 | tf_op jit(solution)/shard_map/ppermute | solution.py:462
  0.5 0.1 collective-permute-start.1
  0.5 0.5 %collective-permute-start.2 = (s32[8,128]{1,0:T(8,128)}, s32[8,128]{1,0:T(8,128)S(1)}, u32[]{:S(2)}, u32[]{:S(2)}) collective-permute-start(s32[8,128]{1,0:T(8,128)} %bitcast.18), channel_id=1, source_target_pairs={{0,1},{1,0},{2,3},{3,2},{4,5},{5,4},{6,7},{7,6},{8,9},{9,8},{10,11... | collective-permute-start | bytes 12296 | tf_op jit(solution)/shard_map/ppermute | solution.py:462
  1.0 1.2 %place.1 = (bf16[128,2048]{1,0:T(8,128)(2,1)S(1)}, bf16[16,128]{1,0:T(8,128)(2,1)S(1)}, s32[1,16]{1,0:T(1,128)S(1)}, s32[1,16]{1,0:T(1,128)S(1)}, f32[16,128]{1,0:T(8,128)S(1)}) custom-call(bf16[128,2048]{1,0:T(8,128)(2,1)} %refs_0_.1, s32[8,128]{1,0:T(8,128)} %bitcast.17, s32[8,128]{1,0:T(8,128)} %bitcast.19, bf16[16,128]{1,0:T(8,128)(2,1)} %bitcast.15, ...), custom_call_target="tpu_custom_call" | custom-call | flops 100000000 | bytes 100000 | tf_op jit(solution)/shard_map/place/pallas_call | solution.py:417
  2.2 0.0 collective-permute-done.1.refs_4_
  2.2 0.0 collective-permute-done.2.refs_5_
  2.2 0.0 collective-permute-done.refs_1_.refs_2_
  2.2 0.5 %dispatch.1 = (f32[16,128]{1,0:T(8,128)S(1)}, bf16[48,512]{1,0:T(8,128)(2,1)S(1)}, bf16[48,512]{1,0:T(8,128)(2,1)S(1)}) custom-call(bf16[128,2048]{1,0:T(8,128)(2,1)S(1)} %get-tuple-element.33.refs_0_.refs_1_, bf16[128,2048]{1,0:T(8,128)(2,1)S(1)} %collective-permute-done.refs_1_.refs_2_, bf16[16,128]{1,0:T(8,128)(2,1)S(1)} %get-tuple-element.34.refs_1_.refs_2_.refs_3_, ...), custom_call_target="tpu_custom_call" | custom-call | flops 100000000 | bytes 100000 | tf_op jit(solution)/shard_map/dispatch/pallas_call | solution.py:417
  2.7 5.0 %collective-permute-start.3 = (bf16[48,512]{1,0:T(8,128)(2,1)S(1)}, bf16[48,512]{1,0:T(8,128)(2,1)S(1)}, u32[]{:S(2)}, u32[]{:S(2)}) collective-permute-start(bf16[48,512]{1,0:T(8,128)(2,1)S(1)} %get-tuple-element.40.refs_0_), channel_id=1, source_target_pairs={{0,6},{1,7},{2,4},{3,5},{4,2},{5,3},{6,0},{7,1},{8,14},{9,15},{10,... | collective-permute-start | bytes 147464 | tf_op jit(solution)/shard_map/ppermute | solution.py:462
  7.8 0.0 collective-permute-start.4
  7.8 0.6 %dispatch_near.1 = (bf16[48,2048]{1,0:T(8,128)(2,1)S(1)}, bf16[48,2048]{1,0:T(8,128)(2,1)S(1)}) custom-call(bf16[48,512]{1,0:T(8,128)(2,1)S(1)} %get-tuple-element.40.refs_0_, bf16[128,2048]{1,0:T(8,128)(2,1)S(1)} %get-tuple-element.33.refs_0_.refs_1_, bf16[128,2048]{1,0:T(8,128)(2,1)S(1)} %collective-permute-done.refs_1_.refs_2_, ...), custom_call_target="tpu_custom_call" | custom-call | flops 100000000 | bytes 100000 | tf_op jit(solution)/shard_map/dispatch_near/pallas_call | solution.py:417
  8.4 2.3 %split_first.1 = (bf16[2,512,1024]{2,1,0:T(8,128)(2,1)S(1)}, bf16[2,2,2048,128]{3,2,1,0:T(8,128)(2,1)S(1)}) custom-call(bf16[48,2048]{1,0:T(8,128)(2,1)S(1)} %get-tuple-element.42.refs_0_, bf16[2,8192,128]{2,1,0:T(8,128)(2,1)} %bitcast.13), custom_call_target="tpu_custom_call" | custom-call | flops 100000000 | bytes 100000 | tf_op jit(solution)/shard_map/split_first/pallas_call | solution.py:417
  10.7 0.0 collective-permute-done.3.refs_1_
  10.7 2.0 %collective-permute-done.4.refs_2_ = bf16[48,512]{1,0:T(8,128)(2,1)S(1)} collective-permute-done((bf16[48,512]{1,0:T(8,128)(2,1)S(1)}, bf16[48,512]{1,0:T(8,128)(2,1)S(1)}, u32[]{:S(2)}, u32[]{:S(2)}) %collective-permute-start.4) | collective-permute-done | bytes 49184 | tf_op jit(solution)/shard_map/ppermute | solution.py:462
  12.8 2.5 %collective-permute-start.6 = (bf16[96,512]{1,0:T(8,128)(2,1)S(1)}, bf16[96,512]{1,0:T(8,128)(2,1)S(1)}, u32[]{:S(2)}, u32[]{:S(2)}) collective-permute-start(bf16[96,512]{1,0:T(8,128)(2,1)S(1)} %join_far.1.refs_0_), channel_id=1, source_target_pairs={{0,24},{8,16},{16,8},{24,0},{1,25},{9,17},{17,9},{25,1},{2,26},{10... | collective-permute-start | bytes 294920 | tf_op jit(solution)/shard_map/ppermute | solution.py:459
  15.3 0.5 %collective-permute-start.5 = (bf16[96,512]{1,0:T(8,128)(2,1)S(1)}, bf16[96,512]{1,0:T(8,128)(2,1)S(1)}, u32[]{:S(2)}, u32[]{:S(2)}) collective-permute-start(bf16[96,512]{1,0:T(8,128)(2,1)S(1)} %join_far.1.refs_0_), channel_id=1, source_target_pairs={{0,8},{8,0},{16,24},{24,16},{1,9},{9,1},{17,25},{25,17},{2,10},{10... | collective-permute-start | bytes 294920 | tf_op jit(solution)/shard_map/ppermute | solution.py:459
  15.8 0.0 collective-permute-start.13
  15.8 0.5 %collective-permute-start.7 = (bf16[96,512]{1,0:T(8,128)(2,1)S(1)}, bf16[96,512]{1,0:T(8,128)(2,1)S(1)}, u32[]{:S(2)}, u32[]{:S(2)}) collective-permute-start(bf16[96,512]{1,0:T(8,128)(2,1)S(1)} %join_far.1.refs_0_), channel_id=1, source_target_pairs={{0,16},{8,24},{16,0},{24,8},{1,17},{9,25},{17,1},{25,9},{2,18},{10... | collective-permute-start | bytes 294920 | tf_op jit(solution)/shard_map/ppermute | solution.py:459
  16.3 0.3 product_far.3.refs_2_
  16.6 1.6 %split_second.1 = (bf16[2,512,1024]{2,1,0:T(8,128)(2,1)S(1)}, bf16[512,2048]{1,0:T(8,128)(2,1)S(1)}) custom-call(bf16[96,512]{1,0:T(8,128)(2,1)S(1)} %join_far.1.refs_0_, bf16[512,2048]{1,0:T(8,128)(2,1)} %bitcast.14, bf16[2,2,2048,128]{3,2,1,0:T(8,128)(2,1)S(1)} %get-tuple-element.45.refs_2_), custom_call_target="tpu_custom_call" | custom-call | flops 100000000 | bytes 100000 | tf_op jit(solution)/shard_map/split_second/pallas_call | solution.py:417
  18.2 0.7 %collective-permute-done.6.refs_0_ = bf16[96,512]{1,0:T(8,128)(2,1)S(1)} collective-permute-done((bf16[96,512]{1,0:T(8,128)(2,1)S(1)}, bf16[96,512]{1,0:T(8,128)(2,1)S(1)}, u32[]{:S(2)}, u32[]{:S(2)}) %collective-permute-start.6) | collective-permute-done | bytes 98336 | tf_op jit(solution)/shard_map/ppermute | solution.py:459
  18.9 0.3 product_far.4.refs_2_
  19.2 0.8 %collective-permute-done.5.refs_0_ = bf16[96,512]{1,0:T(8,128)(2,1)S(1)} collective-permute-done((bf16[96,512]{1,0:T(8,128)(2,1)S(1)}, bf16[96,512]{1,0:T(8,128)(2,1)S(1)}, u32[]{:S(2)}, u32[]{:S(2)}) %collective-permute-start.5) | collective-permute-done | bytes 98336 | tf_op jit(solution)/shard_map/ppermute | solution.py:459
  20.0 0.3 product_far.5.refs_0_
  20.3 0.1 collective-permute-done.7.refs_1_
  20.4 0.7 %expert_far.1 = (bf16[96,512]{1,0:T(8,128)(2,1)S(1)}, bf16[96,512]{1,0:T(8,128)(2,1)S(1)}, bf16[96,512]{1,0:T(8,128)(2,1)S(1)}, bf16[96,512]{1,0:T(8,128)(2,1)S(1)}) custom-call(f32[96,1024]{1,0:T(8,128)S(1)} %product_far.5.refs_0_, bf16[96,512]{1,0:T(8,128)(2,1)S(1)} %collective-permute-done.7.refs_1_, ...), custom_call_target="tpu_custom_call" | custom-call | flops 100000000 | bytes 100000 | tf_op jit(solution)/shard_map/expert_far/pallas_call | solution.py:417
  21.1 1.9 %collective-permute-start.8 = (bf16[96,512]{1,0:T(8,128)(2,1)S(1)}, bf16[96,512]{1,0:T(8,128)(2,1)S(1)}, u32[]{:S(2)}, u32[]{:S(2)}) collective-permute-start(bf16[96,512]{1,0:T(8,128)(2,1)S(1)} %get-tuple-element.49), channel_id=1, source_target_pairs={{0,24},{8,16},{16,8},{24,0},{1,25},{9,17},{17,9},{25,1},{2,26},{10... | collective-permute-start | bytes 294920 | tf_op jit(solution)/shard_map/ppermute | solution.py:459
  23.0 0.7 %collective-permute-start.9 = (bf16[96,512]{1,0:T(8,128)(2,1)S(1)}, bf16[96,512]{1,0:T(8,128)(2,1)S(1)}, u32[]{:S(2)}, u32[]{:S(2)}) collective-permute-start(bf16[96,512]{1,0:T(8,128)(2,1)S(1)} %get-tuple-element.50.refs_0_), channel_id=1, source_target_pairs={{0,8},{8,0},{16,24},{24,16},{1,9},{9,1},{17,25},{25,17},{2,10},{10... | collective-permute-start | bytes 294920 | tf_op jit(solution)/shard_map/ppermute | solution.py:459
  23.7 1.0 %collective-permute-start.10 = (bf16[96,512]{1,0:T(8,128)(2,1)S(1)}, bf16[96,512]{1,0:T(8,128)(2,1)S(1)}, u32[]{:S(2)}, u32[]{:S(2)}) collective-permute-start(bf16[96,512]{1,0:T(8,128)(2,1)S(1)} %get-tuple-element.51), channel_id=1, source_target_pairs={{0,16},{8,24},{16,0},{24,8},{1,17},{9,25},{17,1},{25,9},{2,18},{10... | collective-permute-start | bytes 294920 | tf_op jit(solution)/shard_map/ppermute | solution.py:459
  24.7 0.0 collective-permute-done.13.refs_2_
  24.7 1.2 %expert_near.1 = (bf16[96,512]{1,0:T(8,128)(2,1)S(1)}, bf16[96,512]{1,0:T(8,128)(2,1)S(1)}, bf16[96,512]{1,0:T(8,128)(2,1)S(1)}, bf16[96,512]{1,0:T(8,128)(2,1)S(1)}) custom-call(bf16[96,512]{1,0:T(8,128)(2,1)S(1)} %get-tuple-element.50.refs_0_, bf16[48,2048]{1,0:T(8,128)(2,1)S(1)} %get-tuple-element.54.refs_1_, ...), custom_call_target="tpu_custom_call" | custom-call | flops 100000000 | bytes 100000 | tf_op jit(solution)/shard_map/expert_near/pallas_call | solution.py:417
  25.9 1.9 %collective-permute-start.14 = (bf16[96,512]{1,0:T(8,128)(2,1)S(1)}, bf16[96,512]{1,0:T(8,128)(2,1)S(1)}, u32[]{:S(2)}, u32[]{:S(2)}) collective-permute-start(bf16[96,512]{1,0:T(8,128)(2,1)S(1)} %get-tuple-element.56), channel_id=1, source_target_pairs={{0,24},{8,16},{16,8},{24,0},{1,25},{9,17},{17,9},{25,1},{2,26},{10... | collective-permute-start | bytes 294920 | tf_op jit(solution)/shard_map/ppermute | solution.py:459
  27.8 0.6 %collective-permute-start.15 = (bf16[96,512]{1,0:T(8,128)(2,1)S(1)}, bf16[96,512]{1,0:T(8,128)(2,1)S(1)}, u32[]{:S(2)}, u32[]{:S(2)}) collective-permute-start(bf16[96,512]{1,0:T(8,128)(2,1)S(1)} %get-tuple-element.57), channel_id=1, source_target_pairs={{0,8},{8,0},{16,24},{24,16},{1,9},{9,1},{17,25},{25,17},{2,10},{10... | collective-permute-start | bytes 294920 | tf_op jit(solution)/shard_map/ppermute | solution.py:459
  28.4 1.0 %collective-permute-start.16 = (bf16[96,512]{1,0:T(8,128)(2,1)S(1)}, bf16[96,512]{1,0:T(8,128)(2,1)S(1)}, u32[]{:S(2)}, u32[]{:S(2)}) collective-permute-start(bf16[96,512]{1,0:T(8,128)(2,1)S(1)} %get-tuple-element.58), channel_id=1, source_target_pairs={{0,16},{8,24},{16,0},{24,8},{1,17},{9,25},{17,1},{25,9},{2,18},{10... | collective-permute-start | bytes 294920 | tf_op jit(solution)/shard_map/ppermute | solution.py:459
  29.5 0.4 %collective-permute-done.10.refs_3_ = bf16[96,512]{1,0:T(8,128)(2,1)S(1)} collective-permute-done((bf16[96,512]{1,0:T(8,128)(2,1)S(1)}, bf16[96,512]{1,0:T(8,128)(2,1)S(1)}, u32[]{:S(2)}, u32[]{:S(2)}) %collective-permute-start.10) | collective-permute-done | bytes 98336 | tf_op jit(solution)/shard_map/ppermute | solution.py:459
  29.9 0.1 sum_far.1
  30.0 2.0 %collective-permute-start.11 = (bf16[48,512]{1,0:T(8,128)(2,1)S(1)}, bf16[48,512]{1,0:T(8,128)(2,1)S(1)}, u32[]{:S(2)}, u32[]{:S(2)}) collective-permute-start(bf16[48,512]{1,0:T(8,128)(2,1)S(1)} %get-tuple-element.52), channel_id=1, source_target_pairs={{0,6},{1,7},{2,4},{3,5},{4,2},{5,3},{6,0},{7,1},{8,14},{9,15},{10,... | collective-permute-start | bytes 147464 | tf_op jit(solution)/shard_map/ppermute | solution.py:462
  32.0 1.5 %collective-permute-start.12 = (bf16[48,512]{1,0:T(8,128)(2,1)S(1)}, bf16[48,512]{1,0:T(8,128)(2,1)S(1)}, u32[]{:S(2)}, u32[]{:S(2)}) collective-permute-start(bf16[48,512]{1,0:T(8,128)(2,1)S(1)} %get-tuple-element.53), channel_id=1, source_target_pairs={{0,4},{1,5},{2,6},{3,7},{4,0},{5,1},{6,2},{7,3},{8,12},{9,13},{10,... | collective-permute-start | bytes 147464 | tf_op jit(solution)/shard_map/ppermute | solution.py:462
  33.5 0.1 sum_near.1
  33.5 1.2 %collective-permute-start.17 = (bf16[48,512]{1,0:T(8,128)(2,1)S(1)}, bf16[48,512]{1,0:T(8,128)(2,1)S(1)}, u32[]{:S(2)}, u32[]{:S(2)}) collective-permute-start(bf16[48,512]{1,0:T(8,128)(2,1)S(1)} %get-tuple-element.60), channel_id=1, source_target_pairs={{0,2},{1,3},{2,0},{3,1},{4,6},{5,7},{6,4},{7,5},{8,10},{9,11},{10,... | collective-permute-start | bytes 147464 | tf_op jit(solution)/shard_map/ppermute | solution.py:462
  34.7 1.3 %collective-permute-done.11.refs_2_.refs_0_ = bf16[48,512]{1,0:T(8,128)(2,1)S(1)} collective-permute-done((bf16[48,512]{1,0:T(8,128)(2,1)S(1)}, bf16[48,512]{1,0:T(8,128)(2,1)S(1)}, u32[]{:S(2)}, u32[]{:S(2)}) %collective-permute-start.11) | collective-permute-done | bytes 49184 | tf_op jit(solution)/shard_map/ppermute | solution.py:462
  36.0 0.9 %collective-permute-done.12.refs_3_.refs_1_ = bf16[48,512]{1,0:T(8,128)(2,1)S(1)} collective-permute-done((bf16[48,512]{1,0:T(8,128)(2,1)S(1)}, bf16[48,512]{1,0:T(8,128)(2,1)S(1)}, u32[]{:S(2)}, u32[]{:S(2)}) %collective-permute-start.12) | collective-permute-done | bytes 49184 | tf_op jit(solution)/shard_map/ppermute | solution.py:462
  37.0 0.7 %collective-permute-done.17.refs_5_.refs_3_ = bf16[48,512]{1,0:T(8,128)(2,1)S(1)} collective-permute-done((bf16[48,512]{1,0:T(8,128)(2,1)S(1)}, bf16[48,512]{1,0:T(8,128)(2,1)S(1)}, u32[]{:S(2)}, u32[]{:S(2)}) %collective-permute-start.17) | collective-permute-done | bytes 49184 | tf_op jit(solution)/shard_map/ppermute | solution.py:462
  37.7 0.1 collective-permute-start.18
  37.8 0.5 %combine_weights.1 = (bf16[128,192]{1,0:T(8,128)(2,1)S(1)}, bf16[128,512]{1,0:T(8,128)(2,1)S(1)}) custom-call(bf16[128,2048]{1,0:T(8,128)(2,1)S(1)} %get-tuple-element.33.refs_0_.refs_1_, bf16[16,128]{1,0:T(8,128)(2,1)S(1)} %get-tuple-element.34.refs_1_.refs_2_.refs_3_, bf16[8,2048]{1,0:T(8,128)(2,1)S(1)} %bitcast.12, ...), custom_call_target="tpu_custom_call" | custom-call | flops 100000000 | bytes 100000 | tf_op jit(solution)/shard_map/combine_weights/pallas_call | solution.py:417
  38.3 0.2 combine.1.refs_1_
  38.5 0.6 %collective-permute-done.18.refs_2_ = bf16[96,512]{1,0:T(8,128)(2,1)S(1)} collective-permute-done((bf16[96,512]{1,0:T(8,128)(2,1)S(1)}, bf16[96,512]{1,0:T(8,128)(2,1)S(1)}, u32[]{:S(2)}, u32[]{:S(2)}) %collective-permute-start.18) | collective-permute-done | bytes 98336 | tf_op jit(solution)/shard_map/ppermute | solution.py:462
  39.1 0.9 %finish.1 = bf16[128,512]{1,0:T(8,128)(2,1)} custom-call(bf16[128,192]{1,0:T(8,128)(2,1)S(1)} %get-tuple-element.37.refs_0_, f32[128,512]{1,0:T(8,128)S(1)} %combine.1.refs_1_, bf16[96,512]{1,0:T(8,128)(2,1)S(1)} %collective-permute-done.18.refs_2_), custom_call_target="tpu_custom_call" | custom-call | flops 100000000 | bytes 100000 | tf_op jit(solution)/shard_map/finish/pallas_call | solution.py:417
  (9 shorter events, 0.0 us)
Async XLA Ops:
  0.0 2.2 %collective-permute-start = (bf16[128,2048]{1,0:T(8,128)(2,1)}, bf16[128,2048]{1,0:T(8,128)(2,1)S(1)}, u32[]{:S(2)}, u32[]{:S(2)}) collective-permute-start(bf16[128,2048]{1,0:T(8,128)(2,1)} %refs_0_.1), channel_id=1, source_target_pairs={{0,1},{1,0},{2,3},{3,2},{4,5},{5,4},{6,7},{7,6},{8,9},{9,8},{10,11... | collective-permute-start | bytes 1572872 | tf_op jit(solution)/shard_map/ppermute | solution.py:462
  0.5 1.8 %collective-permute-start.1 = (s32[8,128]{1,0:T(8,128)}, s32[8,128]{1,0:T(8,128)S(1)}, u32[]{:S(2)}, u32[]{:S(2)}) collective-permute-start(s32[8,128]{1,0:T(8,128)} %bitcast.16), channel_id=1, source_target_pairs={{0,1},{1,0},{2,3},{3,2},{4,5},{5,4},{6,7},{7,6},{8,9},{9,8},{10,11... | collective-permute-start | bytes 12296 | tf_op jit(solution)/shard_map/ppermute | solution.py:462
  0.5 1.7 %collective-permute-start.2 = (s32[8,128]{1,0:T(8,128)}, s32[8,128]{1,0:T(8,128)S(1)}, u32[]{:S(2)}, u32[]{:S(2)}) collective-permute-start(s32[8,128]{1,0:T(8,128)} %bitcast.18), channel_id=1, source_target_pairs={{0,1},{1,0},{2,3},{3,2},{4,5},{5,4},{6,7},{7,6},{8,9},{9,8},{10,11... | collective-permute-start | bytes 12296 | tf_op jit(solution)/shard_map/ppermute | solution.py:462
  2.7 8.0 %collective-permute-start.3 = (bf16[48,512]{1,0:T(8,128)(2,1)S(1)}, bf16[48,512]{1,0:T(8,128)(2,1)S(1)}, u32[]{:S(2)}, u32[]{:S(2)}) collective-permute-start(bf16[48,512]{1,0:T(8,128)(2,1)S(1)} %get-tuple-element.40.refs_0_), channel_id=1, source_target_pairs={{0,6},{1,7},{2,4},{3,5},{4,2},{5,3},{6,0},{7,1},{8,14},{9,15},{10,... | collective-permute-start | bytes 147464 | tf_op jit(solution)/shard_map/ppermute | solution.py:462
  7.8 5.0 %collective-permute-start.4 = (bf16[48,512]{1,0:T(8,128)(2,1)S(1)}, bf16[48,512]{1,0:T(8,128)(2,1)S(1)}, u32[]{:S(2)}, u32[]{:S(2)}) collective-permute-start(bf16[48,512]{1,0:T(8,128)(2,1)S(1)} %get-tuple-element.44), channel_id=1, source_target_pairs={{0,4},{1,5},{2,6},{3,7},{4,0},{5,1},{6,2},{7,3},{8,12},{9,13},{10,... | collective-permute-start | bytes 147464 | tf_op jit(solution)/shard_map/ppermute | solution.py:462
  12.8 6.2 %collective-permute-start.6 = (bf16[96,512]{1,0:T(8,128)(2,1)S(1)}, bf16[96,512]{1,0:T(8,128)(2,1)S(1)}, u32[]{:S(2)}, u32[]{:S(2)}) collective-permute-start(bf16[96,512]{1,0:T(8,128)(2,1)S(1)} %join_far.1.refs_0_), channel_id=1, source_target_pairs={{0,24},{8,16},{16,8},{24,0},{1,25},{9,17},{17,9},{25,1},{2,26},{10... | collective-permute-start | bytes 294920 | tf_op jit(solution)/shard_map/ppermute | solution.py:459
  15.3 4.7 %collective-permute-start.5 = (bf16[96,512]{1,0:T(8,128)(2,1)S(1)}, bf16[96,512]{1,0:T(8,128)(2,1)S(1)}, u32[]{:S(2)}, u32[]{:S(2)}) collective-permute-start(bf16[96,512]{1,0:T(8,128)(2,1)S(1)} %join_far.1.refs_0_), channel_id=1, source_target_pairs={{0,8},{8,0},{16,24},{24,16},{1,9},{9,1},{17,25},{25,17},{2,10},{10... | collective-permute-start | bytes 294920 | tf_op jit(solution)/shard_map/ppermute | solution.py:459
  15.8 8.9 %collective-permute-start.13 = (bf16[48,2048]{1,0:T(8,128)(2,1)S(1)}, bf16[48,2048]{1,0:T(8,128)(2,1)S(1)}, u32[]{:S(2)}, u32[]{:S(2)}) collective-permute-start(bf16[48,2048]{1,0:T(8,128)(2,1)S(1)} %get-tuple-element.42.refs_0_), channel_id=1, source_target_pairs={{0,2},{1,3},{2,0},{3,1},{4,6},{5,7},{6,4},{7,5},{8,10},{9,11},{10,... | collective-permute-start | bytes 589832 | tf_op jit(solution)/shard_map/ppermute | solution.py:462
  15.8 4.6 %collective-permute-start.7 = (bf16[96,512]{1,0:T(8,128)(2,1)S(1)}, bf16[96,512]{1,0:T(8,128)(2,1)S(1)}, u32[]{:S(2)}, u32[]{:S(2)}) collective-permute-start(bf16[96,512]{1,0:T(8,128)(2,1)S(1)} %join_far.1.refs_0_), channel_id=1, source_target_pairs={{0,16},{8,24},{16,0},{24,8},{1,17},{9,25},{17,1},{25,9},{2,18},{10... | collective-permute-start | bytes 294920 | tf_op jit(solution)/shard_map/ppermute | solution.py:459
  21.1 7.3 %collective-permute-start.8 = (bf16[96,512]{1,0:T(8,128)(2,1)S(1)}, bf16[96,512]{1,0:T(8,128)(2,1)S(1)}, u32[]{:S(2)}, u32[]{:S(2)}) collective-permute-start(bf16[96,512]{1,0:T(8,128)(2,1)S(1)} %get-tuple-element.49), channel_id=1, source_target_pairs={{0,24},{8,16},{16,8},{24,0},{1,25},{9,17},{17,9},{25,1},{2,26},{10... | collective-permute-start | bytes 294920 | tf_op jit(solution)/shard_map/ppermute | solution.py:459
  23.0 6.5 %collective-permute-start.9 = (bf16[96,512]{1,0:T(8,128)(2,1)S(1)}, bf16[96,512]{1,0:T(8,128)(2,1)S(1)}, u32[]{:S(2)}, u32[]{:S(2)}) collective-permute-start(bf16[96,512]{1,0:T(8,128)(2,1)S(1)} %get-tuple-element.50.refs_0_), channel_id=1, source_target_pairs={{0,8},{8,0},{16,24},{24,16},{1,9},{9,1},{17,25},{25,17},{2,10},{10... | collective-permute-start | bytes 294920 | tf_op jit(solution)/shard_map/ppermute | solution.py:459
  23.7 6.2 %collective-permute-start.10 = (bf16[96,512]{1,0:T(8,128)(2,1)S(1)}, bf16[96,512]{1,0:T(8,128)(2,1)S(1)}, u32[]{:S(2)}, u32[]{:S(2)}) collective-permute-start(bf16[96,512]{1,0:T(8,128)(2,1)S(1)} %get-tuple-element.51), channel_id=1, source_target_pairs={{0,16},{8,24},{16,0},{24,8},{1,17},{9,25},{17,1},{25,9},{2,18},{10... | collective-permute-start | bytes 294920 | tf_op jit(solution)/shard_map/ppermute | solution.py:459
  24.7 13.1 %copy-start = (bf16[2048,8]{0,1:T(8,128)(2,1)S(1)}, bf16[2048,8]{0,1:T(8,128)(2,1)}, u32[]{:S(2)}) copy-start(bf16[2048,8]{0,1:T(8,128)(2,1)} %param.11) | copy-start | bytes 98308
  25.9 7.6 %collective-permute-start.14 = (bf16[96,512]{1,0:T(8,128)(2,1)S(1)}, bf16[96,512]{1,0:T(8,128)(2,1)S(1)}, u32[]{:S(2)}, u32[]{:S(2)}) collective-permute-start(bf16[96,512]{1,0:T(8,128)(2,1)S(1)} %get-tuple-element.56), channel_id=1, source_target_pairs={{0,24},{8,16},{16,8},{24,0},{1,25},{9,17},{17,9},{25,1},{2,26},{10... | collective-permute-start | bytes 294920 | tf_op jit(solution)/shard_map/ppermute | solution.py:459
  27.8 5.7 %collective-permute-start.15 = (bf16[96,512]{1,0:T(8,128)(2,1)S(1)}, bf16[96,512]{1,0:T(8,128)(2,1)S(1)}, u32[]{:S(2)}, u32[]{:S(2)}) collective-permute-start(bf16[96,512]{1,0:T(8,128)(2,1)S(1)} %get-tuple-element.57), channel_id=1, source_target_pairs={{0,8},{8,0},{16,24},{24,16},{1,9},{9,1},{17,25},{25,17},{2,10},{10... | collective-permute-start | bytes 294920 | tf_op jit(solution)/shard_map/ppermute | solution.py:459
  28.4 5.0 %collective-permute-start.16 = (bf16[96,512]{1,0:T(8,128)(2,1)S(1)}, bf16[96,512]{1,0:T(8,128)(2,1)S(1)}, u32[]{:S(2)}, u32[]{:S(2)}) collective-permute-start(bf16[96,512]{1,0:T(8,128)(2,1)S(1)} %get-tuple-element.58), channel_id=1, source_target_pairs={{0,16},{8,24},{16,0},{24,8},{1,17},{9,25},{17,1},{25,9},{2,18},{10... | collective-permute-start | bytes 294920 | tf_op jit(solution)/shard_map/ppermute | solution.py:459
  30.0 6.1 %collective-permute-start.11 = (bf16[48,512]{1,0:T(8,128)(2,1)S(1)}, bf16[48,512]{1,0:T(8,128)(2,1)S(1)}, u32[]{:S(2)}, u32[]{:S(2)}) collective-permute-start(bf16[48,512]{1,0:T(8,128)(2,1)S(1)} %get-tuple-element.52), channel_id=1, source_target_pairs={{0,6},{1,7},{2,4},{3,5},{4,2},{5,3},{6,0},{7,1},{8,14},{9,15},{10,... | collective-permute-start | bytes 147464 | tf_op jit(solution)/shard_map/ppermute | solution.py:462
  32.0 5.0 %collective-permute-start.12 = (bf16[48,512]{1,0:T(8,128)(2,1)S(1)}, bf16[48,512]{1,0:T(8,128)(2,1)S(1)}, u32[]{:S(2)}, u32[]{:S(2)}) collective-permute-start(bf16[48,512]{1,0:T(8,128)(2,1)S(1)} %get-tuple-element.53), channel_id=1, source_target_pairs={{0,4},{1,5},{2,6},{3,7},{4,0},{5,1},{6,2},{7,3},{8,12},{9,13},{10,... | collective-permute-start | bytes 147464 | tf_op jit(solution)/shard_map/ppermute | solution.py:462
  33.5 4.2 %collective-permute-start.17 = (bf16[48,512]{1,0:T(8,128)(2,1)S(1)}, bf16[48,512]{1,0:T(8,128)(2,1)S(1)}, u32[]{:S(2)}, u32[]{:S(2)}) collective-permute-start(bf16[48,512]{1,0:T(8,128)(2,1)S(1)} %get-tuple-element.60), channel_id=1, source_target_pairs={{0,2},{1,3},{2,0},{3,1},{4,6},{5,7},{6,4},{7,5},{8,10},{9,11},{10,... | collective-permute-start | bytes 147464 | tf_op jit(solution)/shard_map/ppermute | solution.py:462
  37.7 1.4 %collective-permute-start.18 = (bf16[96,512]{1,0:T(8,128)(2,1)S(1)}, bf16[96,512]{1,0:T(8,128)(2,1)S(1)}, u32[]{:S(2)}, u32[]{:S(2)}) collective-permute-start(bf16[96,512]{1,0:T(8,128)(2,1)S(1)} %flip_back.1), channel_id=1, source_target_pairs={{0,1},{1,0},{2,3},{3,2},{4,5},{5,4},{6,7},{7,6},{8,9},{9,8},{10,11... | collective-permute-start | bytes 294920 | tf_op jit(solution)/shard_map/ppermute | solution.py:462
